TPU v7x, 128 devices: a whole 4x4x4 slice. The times are simulated.
128 devices in a mesh: peer: 2 (over core), dp: 4 (over y), tensor: 16 (over x, z).
Axes of the slice: x: 4, y: 4, z: 4, core: 2. Of those that a mesh axis runs over, the one named last changes fastest.
Arguments:
- hidden: bfloat16 [2, 512, 5120], P('peer', 'dp'), may hold values from -8 to 8
- gain: float32 [2, 5120], P('peer'), may hold values from 0.5 to 1.5
- head: bfloat16 [2, 5120, 81920], P('peer', None, ('dp', 'tensor'))
- targets: int32 [512], P('dp'), may hold values from 0 to 81919
- lengths: int32 [16], P('dp'), may hold values from 1 to 32
Outputs:
- loss: float32 [2], P('peer')
- grad_hidden: bfloat16 [2, 512, 5120], P('peer', 'dp')
Inputs may be any that keep to these rules, and one draw needn't show every extreme that they name: `lengths`: the valid positions of a sequence are its first ones.
All inputs are finite; a program needn't handle non-finite values.
Results may differ from a plain program's by a relative error of at most 0.0071.
Values may be sent and summed in bfloat16 or wider, within the bound.
No kernel may reach another device: no remote copies, remote signals or barrier semaphores. Data moves between devices by JAX's collectives and lax.ppermute only.
A program may use at most 128 MiB of HBM per device.

v0:
```python
import jax
import jax.numpy as jnp
from jax import lax
from jax.sharding import PartitionSpec as P

LEN = 32


kl_weight = 0.5
loss_scale = 64.0
eps_norm = 1e-06


def partner(block, axis, stride):
    count = lax.axis_size(axis)
    route = []
    for low in range(count):
        high = low | 1 << stride
        if high != low and high < count:
            route += [(low, high), (high, low)]
    return lax.ppermute(block, axis, route)


def norm_backward(grad_normed, states, inverse_rms, gain_row):
    scaled = grad_normed * gain_row
    inner = jnp.mean(scaled * states, axis=-1, keepdims=True)
    return (inverse_rms * (scaled - states * inverse_rms * inverse_rms * inner)).astype(
        jnp.bfloat16
    )


def local(hidden, gain, head, targets, lengths):
    states = hidden[0].astype(jnp.float32)
    gain_row = gain[0][None, :]
    matrix = head[0]
    voc_shard = matrix.shape[1]
    tok_group = states.shape[0]
    inverse_rms = lax.rsqrt(jnp.mean(states * states, axis=-1, keepdims=True) + eps_norm)
    normed = (states * inverse_rms * gain_row).astype(jnp.bfloat16)
    logits = jnp.dot(
        lax.all_gather(normed, "dp", axis=0, tiled=True), matrix, preferred_element_type=jnp.float32
    ).astype(jnp.bfloat16)
    all_targets, all_lengths = (
        lax.all_gather(targets, "dp", axis=0, tiled=True),
        lax.all_gather(lengths, "dp", axis=0, tiled=True),
    )
    peer_logits = partner(logits, "peer", 0)
    values = logits.astype(jnp.float32)
    peer_values = peer_logits.astype(jnp.float32)
    own_local = jnp.max(values, axis=-1)
    peer_local = jnp.max(peer_values, axis=-1)
    own_max, peer_max = lax.pmax((own_local, peer_local), ("dp", "tensor"))
    own_sum = jnp.sum(jnp.exp(values - own_max[:, None]), axis=-1)
    peer_sum = jnp.sum(jnp.exp(peer_values - peer_max[:, None]), axis=-1)
    own_total, peer_total = lax.psum((own_sum, peer_sum), ("dp", "tensor"))
    own_log = own_max + jnp.log(own_total)
    peer_log = peer_max + jnp.log(peer_total)
    probs = jnp.exp(values - own_log[:, None])
    peer_probs = jnp.exp(peer_values - peer_log[:, None])
    tok_all = values.shape[0]
    vocab_start = lax.axis_index(("dp", "tensor")) * voc_shard
    columns = vocab_start + lax.broadcasted_iota(jnp.int32, (1, voc_shard), 1)
    onehot = (columns == all_targets[:, None]).astype(jnp.float32)
    position = lax.broadcasted_iota(jnp.int32, (tok_all,), 0)
    limits = jnp.repeat(all_lengths, LEN, total_repeat_length=tok_all)
    weights = (position % LEN < limits).astype(jnp.float32)
    count = jnp.sum(weights)
    shard_terms = -jnp.sum(values * onehot, axis=-1) + kl_weight * jnp.sum(
        peer_probs * (peer_values - values), axis=-1
    )
    partial_loss = jnp.sum(weights * shard_terms)
    total_loss = lax.psum(partial_loss, ("dp", "tensor"))
    local_terms = jnp.sum(weights * ((1.0 + kl_weight) * own_log - kl_weight * peer_log))
    loss = ((total_loss + local_terms) / count).reshape((1,))
    grad_logits = (
        loss_scale
        * weights[:, None]
        * ((1.0 + kl_weight) * probs - onehot - kl_weight * peer_probs)
    ).astype(jnp.bfloat16)
    piece = lax.slice_in_dim(grad_logits, 0, tok_group * lax.axis_size("dp"), axis=0)
    grad_partial = lax.psum_scatter(
        lax.dot_general(
            piece, matrix, (((1,), (1,)), ((), ())), preferred_element_type=jnp.float32
        ),
        "dp",
        scatter_dimension=0,
        tiled=True,
    )
    grad_normed = lax.psum(grad_partial, "tensor")
    grad_hidden = norm_backward(grad_normed, states, inverse_rms, gain_row)
    return (loss, grad_hidden[None])


def solution(mesh):
    return jax.shard_map(
        local,
        mesh=mesh,
        in_specs=(
            P("peer", "dp", None),
            P("peer", None),
            P("peer", None, ("dp", "tensor")),
            P("dp"),
            P("dp"),
        ),
        out_specs=(P("peer"), P("peer", "dp", None)),
        check_vma=False,
    )
```

profile of v0, /device:TPU:0, one launch (start us, length us, event | category | flops | bytes accessed | tf_op | source)
XLA Modules:
  0.0 852.9 jit_solution(12576791177617978660)
XLA Ops:
  7.2 1.7 fusion.24
  8.9 2.8 fusion.9
  11.8 59.5 %all-gather.3.cloned.1.call-done = bf16[512,5120]{1,0:T(8,128)(2,1)} async-done(((bf16[128,5120]{1,0:T(8,128)(2,1)}), bf16[512,5120]{1,0:T(8,128)(2,1)}) %all-gather.3.cloned.1.call-update) | async-done | bytes 5242896 | tf_op jit(solution)/shard_map/all_gather | solution.py:41
  71.3 12.8 %fusion.50 = (bf16[512]{0:T(512)(128)(2,1)S(1)}, bf16[512,1280]{1,0:T(8,128)(2,1)S(1)}) fusion(bf16[512,5120]{1,0:T(8,128)(2,1)} %all-gather.3.cloned.1.call-done, bf16[1,5120,1280]{2,1,0:T(8,128)(2,1)} %param.9), kind=kOutput, calls=%fused_computation.91 | convolution fusion | flops 6712196608 | bytes 19661824 | tf_op jit(solution)/shard_map/dot_general | solution.py:40
  84.2 0.6 dynamic-slice.6
  85.4 0.2 dynamic-update-slice.3
  85.7 8.1 all-reduce
  93.8 8.3 all-gather
  102.1 0.7 fusion.49
  102.9 4.4 compare_select_fusion.1
  107.4 5.7 broadcast_select_fusion
  113.1 0.3 reduce_max.28
  113.4 176.8 %all-reduce.2 = (f32[512]{0:T(512)S(1)}, f32[512]{0:T(512)S(1)}) all-reduce(bf16[512]{0:T(512)(128)(2,1)S(1)} %get-tuple-element.57, bf16[512]{0:T(512)(128)(2,1)S(1)} %reduce_max.28), channel_id=1, replica_groups=mesh['peer'=2,'dp'=4,'tensor'=16] {'dp','tensor'}, use_global_device_ids=true, to_apply=%region_10.11 | all-reduce | flops 1024 | bytes 6144 | tf_op jit(solution)/shard_map/pmax | solution.py:52
  290.2 0.6 fusion.19
  290.8 171.7 %psum.28 = f32[512]{0:T(512)S(1)} all-reduce(f32[512]{0:T(512)S(1)} %fusion.19), channel_id=1, replica_groups=mesh['peer'=2,'dp'=4,'tensor'=16] {'dp','tensor'}, use_global_device_ids=true, to_apply=%region_5.0 | all-reduce | flops 512 | bytes 4096 | tf_op jit(solution)/shard_map/psum | solution.py:55
  462.5 1.7 fusion.28
  464.2 0.6 convert_reduce_fusion
  464.8 174.4 %all-reduce.1 = (f32[]{:T(128)}, f32[512]{0:T(512)S(1)}) all-reduce(f32[]{:T(128)} %get-tuple-element.27, f32[512]{0:T(512)S(1)} %get-tuple-element.14), channel_id=1, replica_groups=mesh['peer'=2,'dp'=4,'tensor'=16] {'dp','tensor'}, use_global_device_ids=true, to_apply=%region_8.0 | all-reduce | flops 513 | bytes 4104 | tf_op jit(solution)/shard_map/psum | solution.py:72
  639.2 0.6 select_reduce_fusion
  639.8 14.1 %fusion = f32[512,5120]{1,0:T(8,128)} fusion(bf16[1,5120,1280]{2,1,0:T(8,128)(2,1)} %param.9, bf16[512,1280]{1,0:T(8,128)(2,1)S(1)} %collective-permute-done, bf16[512,1280]{1,0:T(8,128)(2,1)S(1)} %get-tuple-element.58, f32[512]{0:T(512)S(1)} %get-tuple-element.36, f32[512]{0:T(512)S(1)} %get-tuple-element.32, f32[512]{0:T(512)S(1)} %log_add_fusion.1, ...), kind=kOutput, calls=%fused_computation | convolution fusion | flops 6718750720 | bytes 26227712 | tf_op jit(solution)/shard_map/dot_general | solution.py:82
  654.0 91.0 %reduce-scatter.2.cloned.1.call-done = f32[128,5120]{1,0:T(8,128)} async-done(((f32[512,5120]{1,0:T(8,128)}), f32[128,5120]{1,0:T(8,128)}) %reduce-scatter.2.cloned.1.call-update) | async-done | bytes 2621456 | tf_op jit(solution)/shard_map/reduce_scatter | solution.py:81
  746.9 94.1 %all-reduce.5.cloned.1.call-done = f32[128,5120]{1,0:T(8,128)} async-done(((f32[128,5120]{1,0:T(8,128)}), f32[128,5120]{1,0:T(8,128)}) %all-reduce.5.cloned.1.call-update) | async-done | bytes 2621456 | tf_op jit(solution)/shard_map/psum | solution.py:89
  841.0 2.4 fusion.25
  843.5 1.8 fusion.32
  (30 shorter events, 0.6 us)
Async XLA Ops:
  7.2 64.1 %all-gather.3.cloned.1.call-start = ((), (), s32[]{:S(2)}) async-start(), calls=%async_computation.1 | async-start | bytes 6553600 | tf_op jit(solution)/shard_map/all_gather | solution.py:41
  11.7 72.5 %copy-start.6 = (u32[128]{0:T(128)S(1)}, u32[128]{0:T(128)}, u32[]{:S(2)}) copy-start(u32[128]{0:T(128)} %constant.188) | copy-start | bytes 1540
  11.7 73.8 %copy-start.5 = (s32[4]{0:T(128)S(1)}, s32[4]{0:T(128)}, u32[]{:S(2)}) copy-start(s32[4]{0:T(128)} %param.11) | copy-start | bytes 52
  11.7 82.1 %copy-start.4 = (s32[128]{0:T(128)S(1)}, s32[128]{0:T(128)}, u32[]{:S(2)}) copy-start(s32[128]{0:T(128)} %param.10) | copy-start | bytes 1540
  11.7 91.1 %copy-start.3 = (s32[4,128]{1,0:T(4,128)S(1)}, s32[4,128]{1,0:T(4,128)}, u32[]{:S(2)}) copy-start(s32[4,128]{1,0:T(4,128)} %constant.151.clone.1) | copy-start | bytes 6148
  11.7 733.2 %reduce-scatter.2.cloned.1.call-start = ((), (), s32[]{:S(2)}) async-start(), calls=%async_computation.2 | async-start | bytes 13107200 | tf_op jit(solution)/shard_map/reduce_scatter | solution.py:81
  84.1 29.0 %collective-permute-start = (bf16[512,1280]{1,0:T(8,128)(2,1)S(1)}, bf16[512,1280]{1,0:T(8,128)(2,1)S(1)}, u32[]{:S(2)}, u32[]{:S(2)}) collective-permute-start(bf16[512,1280]{1,0:T(8,128)(2,1)S(1)} %get-tuple-element.58), channel_id=1, source_target_pairs={{0,64},{64,0},{1,65},{65,1},{2,66},{66,2},{3,67},{67,3},{4,68},{68... | collective-permute-start | bytes 3932168 | tf_op jit(solution)/shard_map/ppermute | solution.py:21
  653.9 187.1 %copy-start = (bf16[1,128,5120]{2,1,0:T(8,128)(2,1)S(1)}, bf16[1,128,5120]{2,1,0:T(8,128)(2,1)}, u32[]{:S(2)}) copy-start(bf16[1,128,5120]{2,1,0:T(8,128)(2,1)} %param.7) | copy-start | bytes 3932164
  653.9 187.1 %copy-start.2 = (f32[1,5120]{1,0:T(1,128)S(1)}, f32[1,5120]{1,0:T(1,128)}, u32[]{:S(2)}) copy-start(f32[1,5120]{1,0:T(1,128)} %param.8) | copy-start | bytes 61444
  653.9 187.0 %all-reduce.5.cloned.1.call-start = ((), (), s32[]{:S(2)}) async-start(), calls=%async_computation.3 | async-start | bytes 5242880 | tf_op jit(solution)/shard_map/psum | solution.py:89
  841.0 2.5 copy-start.1
Sparse Core Ops, SparseCore 0:
  11.8 59.4 all-gather.2
  654.0 90.8 reduce-scatter.1
  748.3 92.6 all-reduce.4
where the time goes:
time: 854 us; the launch traced here: 853 us
  blocking collectives  539 us (63%)
  waiting for transfers between devices  245 us (29%)
  matrix products  26.8 us (3%)
  other arithmetic  22.6 us (3%)
  between operations  17.6 us (2%)
    pmax x1, blocking collectives, local(): own_max, peer_max = lax.pmax((own_local, peer_local), ('dp', 'tensor'))  177 us
    psum x1, blocking collectives, local(): total_loss = lax.psum(partial_loss, ('dp', 'tensor'))  174 us
    psum x1, blocking collectives, local(): own_total, peer_total = lax.psum((own_sum, peer_sum), ('dp', 'tensor'))  172 us
    psum x1, waiting for transfers between devices, local(): grad_normed = lax.psum(grad_partial, 'tensor')  94.1 us
    reduce_scatter x1, waiting for transfers between devices, local(): lax.psum_scatter(lax.dot_general(piece, matrix, (((1,), (1,)), ((), ())),...  91 us
    all_gather x1, waiting for transfers between devices, local(): lax.all_gather(normed, 'dp', axis=0, tiled=True)  59.5 us
  transfers between devices with their start and end apart: 4, of which 3 were waited for; matrix products, arithmetic and copies ran while one was open for 1% of the time, Pallas kernels for 0%

commit v1 on v0

v1 whole, which is shorter than its diff:
```python
import jax
import jax.numpy as jnp
from jax import lax
from jax.experimental import pallas as pl
from jax.experimental.pallas import tpu as pltpu
from jax.sharding import Mesh, PartitionSpec as P

LEN = 32
TILE = 128

kl_weight = 0.5
loss_scale = 64.0
eps_norm = 1e-06

ALL = ("peer", "dp", "tx", "tz")

OWN, NEAR, WRAP, FAR = range(4)
FLIP = {1: 1, 2: 3, 3: 2}


def permute(block, move):
    def index(core, y, x, z):
        return ((core * 4 + y) * 4 + x) * 4 + z

    places = [(c, y, x, z) for c in range(2) for y in range(4) for x in range(4) for z in range(4)]
    return lax.ppermute(block, ALL, [(index(*p), index(*move(*p))) for p in places])


def swap_u(block, step):
    return permute(block, lambda c, y, x, z: (c, y, x ^ step, z) if c == 0 else (c, y, x, z ^ step))


def swap_y(block, steps):
    return permute(block, lambda c, y, x, z: (c, y ^ steps[c], x, z))


def core():
    return lax.axis_index("peer")


def by_core(first, second):
    return jnp.where(core() == 0, first, second)


def bits(position):
    return (position ^ (position >> 1)) & 1, position >> 1


def parity():
    return (lax.axis_index("tx") + lax.axis_index("tz")) & 1


def tied(*blocks):
    return lax.optimization_barrier(blocks)


def ring(block, axis):
    near, wrap, far = [lax.ppermute(block, axis, [(i, i ^ s) for i in range(4)]) for s in (1, 3, 2)]
    return [block, near, far, wrap]


def turned(block, step, axis):
    size = block.shape[axis] // 4
    parts = [lax.slice_in_dim(block, p * size, (p + 1) * size, axis=axis) for p in range(4)]
    return jnp.concatenate([parts[p ^ FLIP[step]] for p in range(4)], axis=axis)


def gather_logits(block, gain_row, matrix, ints):
    half = block.shape[0] // 2
    mine = lax.dynamic_slice_in_dim(block, parity() * half, half, axis=0)
    near = swap_y(mine, (1, 1))
    wrap = swap_y(mine, (3, 3))
    ints = ring(ints, "dp")
    logits = add_logits((block,), OWN_PLAN, gain_row, matrix, 3 * 128)
    near, wrap, logits, *ints = tied(near, wrap, logits, *ints)
    far = swap_y(by_core(wrap, near), (1, 3))
    pieces = [slice(k * half // 2, (k + 1) * half // 2) for k in range(2)]
    sides = [swap_u(jnp.concatenate([near[pieces[k]], wrap[pieces[k]]]), (1, 3)[k]) for k in range(2)]
    logits = add_logits((near, wrap), HELD_PLAN, gain_row, matrix, 3 * 128, logits)
    far, logits, *sides = tied(far, logits, *sides)
    far_sides = [swap_u(far[pieces[k]], (1, 3)[k]) for k in range(2)]
    logits = add_logits(sides, OTHER_PLAN, gain_row, matrix, 3 * 128, logits)
    logits, *far_sides = tied(logits, *far_sides)
    far_logits = add_logits((far, *far_sides), FAR_PLAN, gain_row, matrix, 128)
    return logits, far_logits, [ints[s] for s in (0, 1, 3, 2)]


CHUNKS = 10


def make_kernel(count, loads, stores):
    def kernel(*refs):
        sources = refs[:count]
        gain_ref, head_ref = refs[count : count + 2]
        out_ref, held_head, rows, sums, total, block, head_sems, sems = refs[-8:]
        width = rows.shape[1]
        deep = width // CHUNKS
        held = parity() * 64
        shift = {"all": 0, "held": held, "other": 64 - held}
        fetches = []
        for c in range(CHUNKS):
            piece = pl.ds(c * deep, deep)
            fetches.append(pltpu.make_async_copy(head_ref.at[piece], held_head.at[piece], head_sems.at[c]))
        copies = []
        for source, start, length, target, kind in loads:
            to = pl.multiple_of(shift[kind] + target, 16)
            copies.append(
                pltpu.make_async_copy(
                    sources[source].at[pl.ds(start, length)], rows.at[pl.ds(to, length)], sems.at[len(copies)]
                )
            )
        for copy in copies + fetches:
            copy.start()
        for copy in copies:
            copy.wait()

        @pl.loop(0, rows.shape[0] // 16)
        def _(step):
            piece = pl.ds(pl.multiple_of(step * 16, 16), 16)
            lanes = jnp.zeros((16, TILE), jnp.float32)
            for c in range(0, width, TILE):
                states = rows[piece, c : c + TILE].astype(jnp.float32)
                lanes += states * states
            sums[piece, :] = lanes

        mean = jnp.sum(sums[...], axis=-1, keepdims=True) / width
        sums[...] = jnp.broadcast_to(lax.rsqrt(mean + eps_norm), sums.shape)

        @pl.loop(0, rows.shape[0] // 16)
        def _(step):
            piece = pl.ds(pl.multiple_of(step * 16, 16), 16)
            inverse = sums[piece, :]
            for c in range(0, width, TILE):
                states = rows[piece, c : c + TILE].astype(jnp.float32)
                rows[piece, c : c + TILE] = (states * inverse * gain_ref[:, c : c + TILE]).astype(jnp.bfloat16)

        for c in range(0, CHUNKS, 2):
            fetches[c].wait()
            fetches[c + 1].wait()
            columns = slice(c * deep, (c + 2) * deep)
            part = jnp.dot(rows[:, columns], held_head[columns, :], preferred_element_type=jnp.float32)
            if c == 0:
                total[...] = part
            elif c < CHUNKS - 2:
                total[...] += part
            else:
                block[...] = (total[...] + part).astype(jnp.bfloat16)
        copies = []
        for start, length, target, kind in stores:
            to = pl.multiple_of(shift[kind] + target, 16)
            copies.append(
                pltpu.make_async_copy(
                    block.at[pl.ds(start, length)], out_ref.at[pl.ds(to, length)], sems.at[len(copies)]
                )
            )
        for copy in copies:
            copy.start()
        for copy in copies:
            copy.wait()

    return kernel


OWN_PLAN = [(0, 0, 128, 0, "all")], [(0, 128, 0, "all")]
HELD_PLAN = [(0, 0, 64, 0, "all"), (1, 0, 64, 64, "all")], [(0, 64, 128, "held"), (64, 64, 256, "held")]
OTHER_PLAN = (
    [(k, 32 * g, 32, 64 * g + 32 * k, "all") for k in range(2) for g in range(2)],
    [(0, 64, 128, "other"), (64, 64, 256, "other")],
)
FAR_PLAN = [(0, 0, 64, 0, "held")] + [(1 + k, 0, 32, 32 * k, "other") for k in range(2)], [(0, 128, 0, "all")]


def add_logits(sources, plan, gain_row, matrix, tokens, filled=None):
    width, voc = matrix.shape
    anywhere = pl.BlockSpec(memory_space=pl.ANY)
    count = len(sources)
    operands = [*sources, gain_row, matrix] + ([] if filled is None else [filled])
    return pl.pallas_call(
        make_kernel(count, *plan),
        out_shape=jax.ShapeDtypeStruct((tokens, voc), jnp.bfloat16),
        in_specs=[anywhere] * count
        + [pl.BlockSpec(memory_space=pltpu.VMEM), anywhere]
        + ([] if filled is None else [anywhere]),
        out_specs=anywhere,
        scratch_shapes=[
            pltpu.VMEM((width, voc), jnp.bfloat16),
            pltpu.VMEM((128, width), jnp.bfloat16),
            pltpu.VMEM((128, TILE), jnp.float32),
            pltpu.VMEM((128, voc), jnp.float32),
            pltpu.VMEM((128, voc), jnp.bfloat16),
            pltpu.SemaphoreType.DMA((CHUNKS,)),
            pltpu.SemaphoreType.DMA((4,)),
        ],
        input_output_aliases={} if filled is None else {count + 2: 0},
        compiler_params=pltpu.CompilerParams(vmem_limit_bytes=52 * 1024 * 1024),
        cost_estimate=pl.CostEstimate(
            flops=2 * 128 * width * voc, bytes_accessed=2 * width * (voc + 128), transcendentals=0
        ),
    )(*operands)


def merge(stats):
    stats = jnp.stack(stats)
    own_max = jnp.max(stats[:, 0], axis=0)
    peer_max = jnp.max(stats[:, 2], axis=0)
    own_scale = jnp.exp(stats[:, 0] - own_max)
    peer_scale = jnp.exp(stats[:, 2] - peer_max)
    (terms,) = tied(
        jnp.stack([stats[:, 1] * own_scale, stats[:, 3] * peer_scale, stats[:, 4], stats[:, 5] * peer_scale])
    )
    own_sum, peer_sum, target, cross = (terms[:, 0] + terms[:, 1]) + (terms[:, 2] + terms[:, 3])
    return jnp.stack([own_max, own_sum, peer_max, peer_sum, target, cross])


def wide(block):
    return block.astype(jnp.float32)


def narrow(block):
    return block.astype(jnp.bfloat16)


def sum_rows(grad_logits, matrix, later):
    voc = grad_logits.shape[1]
    width = matrix.shape[0] // 4
    at_x, at_z = bits(lax.axis_index("tx")), bits(lax.axis_index("tz"))
    rows = grad_logits.reshape(4, 4, 4, 8, voc)
    for axis in (1, 2):
        rows = jnp.concatenate([lax.slice_in_dim(rows, j, j + 1, axis=axis) for j in (0, 3, 1, 2)], axis=axis)
    rows = rows.reshape(4, 2, 2, 2, 2, 8, voc)
    dims = {"xa": (1, at_x[0], "tx", 1), "xb": (2, at_x[1], "tx", 3), "za": (3, at_z[0], "tz", 1), "zb": (4, at_z[1], "tz", 3)}
    orders = [("xa", "xb", "za", "zb"), ("xb", "xa", "zb", "za"), ("za", "zb", "xa", "xb"), ("zb", "za", "xb", "xa")]

    def product(block, q):
        columns = matrix[q * width : (q + 1) * width]
        out = lax.dot_general(
            block.reshape(-1, voc), columns, (((1,), (1,)), ((), ())), preferred_element_type=jnp.float32
        )
        return out.reshape(block.shape[:-1] + (width,))

    def split(block, name):
        at = dims[name][1]
        away = lax.dynamic_index_in_dim(block, 1 - at, 0, keepdims=False)
        return away, lax.dynamic_index_in_dim(block, at, 0, keepdims=False)

    def swap(block, name):
        axis, step = dims[name][2:]
        return lax.ppermute(block, axis, [(i, i ^ step) for i in range(4)])

    halves = []
    for order in orders:
        turned_rows = jnp.transpose(rows, [dims[name][0] for name in order] + [0, 5, 6])
        halves.append(split(turned_rows, order[0]))
    away = [narrow(product(*tied(halves[q][0]), q)) for q in range(4)]
    *stay, away[3] = tied(*[halves[q][1] for q in range(4)], away[3])
    came = [swap(away[q], orders[q][0]) for q in range(4)]
    kept = [product(stay[q], q) for q in range(4)]
    came[0], later = tied(came[0], later)
    for stage in range(1, 4):
        halves = [
            [k + wide(c) for k, c in zip(split(kept[q], orders[q][stage]), split(came[q], orders[q][stage]))]
            for q in range(4)
        ]
        came = [swap(narrow(halves[q][0]), orders[q][stage]) for q in range(4)]
        kept = [halves[q][1] for q in range(4)]
    state = [kept[q] + wide(came[q]) for q in range(4)]
    done = []
    for pair, first, second, steps in ((state[:2], NEAR, WRAP, (1, 3)), (state[2:], WRAP, NEAR, (3, 1))):
        block = jnp.concatenate(pair, axis=-1)
        came = swap_y(narrow(jnp.stack([block[first], block[FAR]])), (steps[0],) * 2)
        mine = block[OWN] + wide(came[0])
        came = swap_y(narrow(block[second] + wide(came[1])), (steps[1],) * 2)
        done.append(mine + wide(came))
    return jnp.concatenate(done, axis=-1), later


def shard_stats(logits, peer_logits, hit):
    values, peer_values = wide(logits), wide(peer_logits)
    own_max = jnp.max(values, axis=-1)
    peer_max = jnp.max(peer_values, axis=-1)
    peer_exp = jnp.exp(peer_values - peer_max[:, None])
    return jnp.stack(
        [
            own_max,
            jnp.sum(jnp.exp(values - own_max[:, None]), axis=-1),
            peer_max,
            jnp.sum(peer_exp, axis=-1),
            jnp.sum(jnp.where(hit, values, 0.0), axis=-1),
            jnp.sum(peer_exp * (peer_values - values), axis=-1),
        ]
    )


def mean_loss(stats, weights):
    own_log = stats[0] + jnp.log(stats[1])
    peer_log = stats[2] + jnp.log(stats[3])
    per_token = own_log - stats[4] + kl_weight * (stats[5] / stats[3] - peer_log + own_log)
    sums = jnp.sum((weights * per_token).reshape(4, -1), axis=-1)
    total = (sums[OWN] + sums[NEAR]) + (sums[FAR] + sums[WRAP])
    return (total / jnp.sum(weights)).reshape((1,))


def local(hidden, gain, head, targets, lengths):
    block = hidden[0]
    gain_row = gain[0][None, :]
    matrix = head[0]
    group = block.shape[0]
    tokens = 4 * group
    voc_shard = matrix.shape[1]
    first, second, ints = gather_logits(block, gain_row, matrix, jnp.concatenate([targets, lengths]))
    all_targets = jnp.concatenate([part[:group] for part in ints])
    all_lengths = jnp.concatenate([part[group:] for part in ints])
    hit = all_targets[:, None] - lax.axis_index(("dp", "tx", "tz")) * voc_shard
    hit = hit == lax.broadcasted_iota(jnp.int32, (1, voc_shard), 1)
    peer = [(0, 1), (1, 0)]
    first_peer, second_peer = lax.ppermute(first, "peer", peer), lax.ppermute(second, "peer", peer)
    cut = first.shape[0]
    stats = jnp.concatenate(
        [shard_stats(first, first_peer, hit[:cut]), shard_stats(second, second_peer, hit[cut:])], axis=1
    )
    stats = merge(ring(stats, "tz"))
    stats = merge(ring(stats, "tx"))
    stats = ring(stats, "dp")
    stats = merge([stats[0]] + [turned(stats[s], s, 1) for s in (1, 2, 3)])
    own_log = stats[0] + jnp.log(stats[1])
    peer_log = stats[2] + jnp.log(stats[3])
    values = wide(jnp.concatenate([first, second]))
    peer_values = wide(jnp.concatenate([first_peer, second_peer]))
    position = lax.broadcasted_iota(jnp.int32, (tokens // LEN, LEN), 1)
    weights = (position < all_lengths[:, None]).astype(jnp.float32).reshape(tokens)

    grad_logits = (
        loss_scale
        * weights[:, None]
        * (
            (1.0 + kl_weight) * jnp.exp(values - own_log[:, None])
            - hit.astype(jnp.float32)
            - kl_weight * jnp.exp(peer_values - peer_log[:, None])
        )
    ).astype(jnp.bfloat16)
    grad_normed, stats = sum_rows(grad_logits, matrix, stats)
    loss = mean_loss(stats, weights)

    own = wide(lax.dynamic_slice_in_dim(block, lax.axis_index(("tx", "tz")) * 8, 8, axis=0))
    own_inverse = lax.rsqrt(jnp.mean(own * own, axis=-1, keepdims=True) + eps_norm)
    scaled = grad_normed * gain_row
    inner = jnp.mean(scaled * own, axis=-1, keepdims=True)
    rows = narrow(own_inverse * (scaled - own * own_inverse * own_inverse * inner))
    spread = jnp.broadcast_to(rows[None], (16,) + rows.shape)
    grad_hidden = lax.all_to_all(spread, ("tx", "tz"), split_axis=0, concat_axis=0, tiled=True)
    return (loss, grad_hidden.reshape((1,) + block.shape))


def solution(mesh):
    cube = Mesh(mesh.devices.reshape(2, 4, 4, 4), ALL)
    return jax.shard_map(
        local,
        mesh=cube,
        in_specs=(
            P("peer", "dp", None),
            P("peer", None),
            P("peer", None, ("dp", "tx", "tz")),
            P("dp"),
            P("dp"),
        ),
        out_specs=(P("peer"), P("peer", "dp", None)),
        check_vma=False,
    )
```

time: 854 us -> 175 us (0.20)
  blocking collectives: 539 us -> 0 us
  waiting for transfers between devices: 245 us -> 48.5 us
  starting transfers between devices: 0.21 us -> 54.9 us
  Pallas kernels: 0 us -> 27.7 us
  matrix products: 26.8 us -> 10.8 us
  between operations: 17.6 us -> 5.84 us
    psum x2 -> x0, blocking collectives: 346 us -> none  [the longest x1 174 us: local(): total_loss = lax.psum(partial_loss, ('dp', 'tensor'))]
    pmax x1 -> x0, blocking collectives: 177 us -> none  [local(): own_max, peer_max = lax.pmax((own_local, peer_local), ('dp', 'tensor'))]
    psum x1 -> x0, waiting for transfers between devices: 94.1 us -> none  [local(): grad_normed = lax.psum(grad_partial, 'tensor')]
    reduce_scatter x1 -> x0, waiting for transfers between devices: 91 us -> none  [local(): lax.psum_scatter(lax.dot_general(piece, matrix, (((1,), (1,)), ((), ())),...]
    all_gather x1 -> x0, waiting for transfers between devices: 59.5 us -> none  [local(): lax.all_gather(normed, 'dp', axis=0, tiled=True)]
    ppermute x1 -> x41, starting transfers between devices: 0.09 us -> 50.2 us  [the longest x16 18.6 us: swap(): return lax.ppermute(block, axis, [(i, i ^ step) for i in range(4)])]
    ppermute x1 -> x41, waiting for transfers between devices: 0.01 us -> 38.8 us  [the longest x16 17.1 us: swap(): return lax.ppermute(block, axis, [(i, i ^ step) for i in range(4)])]
    pallas_call x0 -> x4, Pallas kernels: none -> 27.7 us  [add_logits(): pl.pallas_call(make_kernel(count, *plan), out_shape=jax.ShapeDtypeStruct(...]
  transfers between devices with their start and end apart: 4 -> 42, of which waited for: 3 -> 23; matrix products, arithmetic and copies ran while one was open for 1% -> 11% of each run, Pallas kernels for 0% -> 16%
where the time goes in v1:
time: 175 us; the launch traced here: 174 us
  starting transfers between devices  54.9 us (31%)
  waiting for transfers between devices  48.5 us (28%)
  Pallas kernels  27.7 us (16%)
  other arithmetic  17.6 us (10%)
  matrix products  10.8 us (6%)
  local copies, waits for them, and re-layouts  8.78 us (5%)
  between operations  5.84 us (3%)
    pallas_call x4, Pallas kernels, add_logits(): pl.pallas_call(make_kernel(count, *plan), out_shape=jax.ShapeDtypeStruct(...  27.7 us
    ppermute x16, starting transfers between devices, swap(): return lax.ppermute(block, axis, [(i, i ^ step) for i in range(4)])  18.6 us
    ppermute x12, starting transfers between devices, ring(): lax.ppermute(block, axis, [(i, i ^ s) for i in range(4)])  18.1 us
    ppermute x16, waiting for transfers between devices, swap(): return lax.ppermute(block, axis, [(i, i ^ step) for i in range(4)])  17.1 us
    ppermute x11, starting transfers between devices, permute(): lax.ppermute(block, ALL, [(index(*p), index(*move(*p))) for p in places])  12.6 us
    ppermute x11, waiting for transfers between devices, permute(): lax.ppermute(block, ALL, [(index(*p), index(*move(*p))) for p in places])  11.5 us
    dot_general x8, matrix products, product(): lax.dot_general(block.reshape(-1, voc), columns, (((1,), (1,)), ((), ()))...  10.8 us
    all_to_all x1, waiting for transfers between devices, local(): lax.all_to_all(spread, ('tx', 'tz'), split_axis=0, concat_axis=0, tiled=T...  9.66 us
  transfers between devices with their start and end apart: 42, of which 23 were waited for; matrix products, arithmetic and copies ran while one was open for 11% of the time, Pallas kernels for 16%

profile of v1, /device:TPU:0, one launch (start us, length us, event | category | flops | bytes accessed | tf_op | source)
XLA Modules:
  0.0 174.2 jit_solution(14545635236991569113)
XLA Ops:
  3.5 2.2 %collective-permute-start.1 = (bf16[64,5120]{1,0:T(8,128)(2,1)S(1)}, bf16[64,5120]{1,0:T(8,128)(2,1)S(1)}, u32[]{:S(2)}, u32[]{:S(2)}) collective-permute-start(bf16[64,5120]{1,0:T(8,128)(2,1)S(1)} %dynamic-slice_bitcast_fusion.8), channel_id=1, source_target_pairs={{0,48},{1,49},{2,50},{3,51},{4,52},{5,53},{6,54},{7,55},{8,56},{9,... | collective-permute-start | bytes 1966088 | tf_op jit(solution)/shard_map/ppermute | solution.py:26
  9.6 2.2 %collective-permute-start.4 = (s32[132]{0:T(256)S(1)}, s32[132]{0:T(256)S(1)}, u32[]{:S(2)}, u32[]{:S(2)}) collective-permute-start(s32[132]{0:T(256)S(1)} %constant_dynamic-update-slice_fusion), channel_id=1, source_target_pairs={{0,48},{16,32},{32,16},{48,0},{1,49},{17,33},{33,17},{49,1},{2,50}... | collective-permute-start | bytes 1592 | tf_op jit(solution)/shard_map/ppermute | solution.py:58
  12.5 8.5 %shard_map.68.refs_4_ = bf16[384,1280]{1,0:T(8,128)(2,1)S(1)} custom-call(bf16[128,5120]{1,0:T(8,128)(2,1)} %bitcast.371, f32[1,5120]{1,0:T(1,128)S(1)} %copy-done.2, bf16[5120,1280]{1,0:T(8,128)(2,1)} %bitcast.358), custom_call_target="tpu_custom_call" | custom-call | flops 1677721600 | bytes 14417920 | tf_op jit(solution)/shard_map/pallas_call | solution.py:178
  26.3 2.1 %collective-permute-start.7 = (bf16[64,5120]{1,0:T(8,128)(2,1)}, bf16[64,5120]{1,0:T(8,128)(2,1)S(1)}, u32[]{:S(2)}, u32[]{:S(2)}) collective-permute-start(bf16[64,5120]{1,0:T(8,128)(2,1)} %pad_maximum_fusion.3), channel_id=1, source_target_pairs={{0,12},{1,13},{2,14},{3,15},{4,8},{5,9},{6,10},{7,11},{8,4},{9,5},... | collective-permute-start | bytes 1966088 | tf_op jit(solution)/shard_map/ppermute | solution.py:26
  28.4 6.6 %shard_map.69.refs_4_ = bf16[384,1280]{1,0:T(8,128)(2,1)} custom-call(bf16[64,5120]{1,0:T(8,128)(2,1)S(1)} %collective-permute-done.refs_0_, bf16[64,5120]{1,0:T(8,128)(2,1)S(1)} %collective-permute-done.1.refs_1_, f32[1,5120]{1,0:T(1,128)S(1)} %copy-done.3, bf16[5120,1280]{1,0:T(8,128)(2,1)} %bitcast.359, ...), custom_call_target="tpu_custom_call", output_to_operand_aliasing={{}: (4, {})} | custom-call | flops 1677721600 | bytes 14417920 | tf_op jit(solution)/shard_map/pallas_call | solution.py:178
  35.0 3.3 %collective-permute-done.7.refs_1_ = bf16[64,5120]{1,0:T(8,128)(2,1)S(1)} collective-permute-done((bf16[64,5120]{1,0:T(8,128)(2,1)}, bf16[64,5120]{1,0:T(8,128)(2,1)S(1)}, u32[]{:S(2)}, u32[]{:S(2)}) %collective-permute-start.7) | collective-permute-done | bytes 655392 | tf_op jit(solution)/shard_map/ppermute | solution.py:26
  38.4 2.2 %collective-permute-start.9 = (bf16[32,5120]{1,0:T(8,128)(2,1)S(1)}, bf16[32,5120]{1,0:T(8,128)(2,1)S(1)}, u32[]{:S(2)}, u32[]{:S(2)}) collective-permute-start(bf16[32,5120]{1,0:T(8,128)(2,1)S(1)} %get-tuple-element.92), channel_id=1, source_target_pairs={{0,12},{1,13},{2,14},{3,15},{4,8},{5,9},{6,10},{7,11},{8,4},{9,5},... | collective-permute-start | bytes 983048 | tf_op jit(solution)/shard_map/ppermute | solution.py:26
  40.6 6.6 %shard_map.70 = bf16[384,1280]{1,0:T(8,128)(2,1)} custom-call(bf16[64,5120]{1,0:T(8,128)(2,1)S(1)} %collective-permute-done.6.refs_0_, bf16[64,5120]{1,0:T(8,128)(2,1)S(1)} %collective-permute-done.7.refs_1_, f32[1,5120]{1,0:T(1,128)S(1)} %copy-done.3, bf16[5120,1280]{1,0:T(8,128)(2,1)} %bitcast.360, ...), custom_call_target="tpu_custom_call", output_to_operand_aliasing={{}: (4, {})} | custom-call | flops 1677721600 | bytes 14417920 | tf_op jit(solution)/shard_map/pallas_call | solution.py:178
  48.8 6.0 %shard_map.71 = bf16[128,1280]{1,0:T(8,128)(2,1)S(1)} custom-call(bf16[64,5120]{1,0:T(8,128)(2,1)S(1)} %collective-permute-done.5.refs_0_, bf16[32,5120]{1,0:T(8,128)(2,1)S(1)} %collective-permute-done.8.refs_1_, bf16[32,5120]{1,0:T(8,128)(2,1)S(1)} %collective-permute-done.9.refs_2_, f32[1,5120]{1,0:T(1,128)S(1)} %copy-done.3, bf16[5120,1280]{1,0:T(8,128)(2,1)} %bitcast.361), custom_call_target="tpu_custom_call" | custom-call | flops 1677721600 | bytes 14417920 | tf_op jit(solution)/shard_map/pallas_call | solution.py:178
  60.0 4.1 %collective-permute-start.14 = (f32[6,512]{1,0:T(8,128)S(1)}, f32[6,512]{1,0:T(8,128)S(1)}, u32[]{:S(2)}, u32[]{:S(2)}) collective-permute-start(f32[6,512]{1,0:T(8,128)S(1)} %get-tuple-element.127), channel_id=1, source_target_pairs={{0,3},{1,2},{2,1},{3,0},{4,7},{5,6},{6,5},{7,4},{8,11},{9,10},{10,... | collective-permute-start | bytes 36872 | tf_op jit(solution)/shard_map/ppermute | solution.py:58
  65.8 3.5 %collective-permute-done.13 = f32[6,512]{1,0:T(8,128)S(1)} collective-permute-done((f32[6,512]{1,0:T(8,128)S(1)}, f32[6,512]{1,0:T(8,128)S(1)}, u32[]{:S(2)}, u32[]{:S(2)}) %collective-permute-start.13) | collective-permute-done | bytes 12320 | tf_op jit(solution)/shard_map/ppermute | solution.py:58
  79.5 2.8 %collective-permute-start.19 = (f32[6,512]{1,0:T(8,128)S(1)}, f32[6,512]{1,0:T(8,128)S(1)}, u32[]{:S(2)}, u32[]{:S(2)}) collective-permute-start(f32[6,512]{1,0:T(8,128)S(1)} %get-tuple-element.129), channel_id=1, source_target_pairs={{0,32},{16,48},{32,0},{48,16},{1,33},{17,49},{33,1},{49,17},{2,34}... | collective-permute-start | bytes 36872 | tf_op jit(solution)/shard_map/ppermute | solution.py:58
  82.4 2.4 %collective-permute-done.19 = f32[6,512]{1,0:T(8,128)S(1)} collective-permute-done((f32[6,512]{1,0:T(8,128)S(1)}, f32[6,512]{1,0:T(8,128)S(1)}, u32[]{:S(2)}, u32[]{:S(2)}) %collective-permute-start.19) | collective-permute-done | bytes 12320 | tf_op jit(solution)/shard_map/ppermute | solution.py:58
  86.8 3.1 %fusion.34 = bf16[4,4,4,8,1280]{4,3,2,1,0:T(8,128)(2,1)S(1)} fusion(bf16[4,4,4,8,1280]{4,3,2,1,0:T(8,128)(2,1)} %bitcast.369, bf16[4,4,4,8,1280]{4,3,2,1,0:T(8,128)(2,1)S(1)} %bitcast.368, f32[4,4,4,8]{3,2,1,0:T(4,128)S(1)} %add.365, s32[4,4,4,8]{3,2,1,0:T(4,128)S(1)} %sub.273, f32[4,4,4,8]{3,2,1,0:T(4,128)S(1)} %add.364, f32[4,4,4,8]{3,2,1,0:T(4,128)S(1)} %fusion.132), kind=kLoop, calls=%fused_computation.42 | loop fusion | flops 7864320 | bytes 3940352 | tf_op jit(solution)/shard_map/convert_element_type | solution.py:340
  90.3 3.1 %fusion.39 = bf16[2,2,2,4,8,1280]{5,4,3,2,1,0:T(8,128)(2,1)S(1)} fusion(bf16[1,5120,1280]{2,1,0:T(8,128)(2,1)} %param.7, bf16[2,2,2,4,8,1280]{5,4,2,1,0,3:T(8,128)(2,1)S(1)} %get-tuple-element.81), kind=kOutput, calls=%fused_computation.50 | convolution fusion | flops 839188480 | bytes 4587520 | tf_op jit(solution)/shard_map/dot_general | solution.py:236
  99.4 2.7 %collective-permute-start.35 = (bf16[2,2,2,4,8,1280]{5,4,3,2,1,0:T(8,128)(2,1)S(1)}, bf16[2,2,2,4,8,1280]{5,4,3,2,1,0:T(8,128)(2,1)S(1)}, u32[]{:S(2)}, u32[]{:S(2)}) collective-permute-start(bf16[2,2,2,4,8,1280]{5,4,3,2,1,0:T(8,128)(2,1)S(1)} %fusion.48), channel_id=1, source_target_pairs={{0,3},{1,2},{2,1},{3,0},{4,7},{5,6},{6,5},{7,4},{8,11},{9,10},{10,... | collective-permute-start | bytes 1966088 | tf_op jit(solution)/shard_map/ppermute | solution.py:248
  106.8 4.2 %collective-permute-done.31 = bf16[2,2,2,4,8,1280]{5,4,3,2,1,0:T(8,128)(2,1)S(1)} collective-permute-done((bf16[2,2,2,4,8,1280]{5,4,3,2,1,0:T(8,128)(2,1)S(1)}, bf16[2,2,2,4,8,1280]{5,4,3,2,1,0:T(8,128)(2,1)S(1)}, u32[]{:S(2)}, u32[]{:S(2)}) %collective-permute-start.31) | collective-permute-done | bytes 655392 | tf_op jit(solution)/shard_map/ppermute | solution.py:248
  112.2 4.4 %collective-permute-done.35 = bf16[2,2,2,4,8,1280]{5,4,3,2,1,0:T(8,128)(2,1)S(1)} collective-permute-done((bf16[2,2,2,4,8,1280]{5,4,3,2,1,0:T(8,128)(2,1)S(1)}, bf16[2,2,2,4,8,1280]{5,4,3,2,1,0:T(8,128)(2,1)S(1)}, u32[]{:S(2)}, u32[]{:S(2)}) %collective-permute-start.35) | collective-permute-done | bytes 655392 | tf_op jit(solution)/shard_map/ppermute | solution.py:248
  121.0 2.1 %collective-permute-start.33 = (bf16[2,4,8,1280]{3,2,1,0:T(8,128)(2,1)S(1)}, bf16[2,4,8,1280]{3,2,1,0:T(8,128)(2,1)S(1)}, u32[]{:S(2)}, u32[]{:S(2)}) collective-permute-start(bf16[2,4,8,1280]{3,2,1,0:T(8,128)(2,1)S(1)} %get-tuple-element.90), channel_id=1, source_target_pairs={{0,4},{4,0},{8,12},{12,8},{1,5},{5,1},{9,13},{13,9},{2,6},{6,2},{1... | collective-permute-start | bytes 491528 | tf_op jit(solution)/shard_map/ppermute | solution.py:248
  128.4 2.1 %collective-permute-start.27 = (bf16[2,4,8,1280]{3,2,1,0:T(8,128)(2,1)S(1)}, bf16[2,4,8,1280]{3,2,1,0:T(8,128)(2,1)S(1)}, u32[]{:S(2)}, u32[]{:S(2)}) collective-permute-start(bf16[2,4,8,1280]{3,2,1,0:T(8,128)(2,1)S(1)} %get-tuple-element.84), channel_id=1, source_target_pairs={{0,3},{1,2},{2,1},{3,0},{4,7},{5,6},{6,5},{7,4},{8,11},{9,10},{10,... | collective-permute-start | bytes 491528 | tf_op jit(solution)/shard_map/ppermute | solution.py:248
  139.9 2.7 %collective-permute-done.39 = bf16[2,8,2560]{2,1,0:T(8,128)(2,1)S(1)} collective-permute-done((bf16[2,8,2560]{2,1,0:T(8,128)(2,1)S(1)}, bf16[2,8,2560]{2,1,0:T(8,128)(2,1)S(1)}, u32[]{:S(2)}, u32[]{:S(2)}) %collective-permute-start.39) | collective-permute-done | bytes 81952 | tf_op jit(solution)/shard_map/ppermute | solution.py:26
  146.7 2.8 %collective-permute-done.30 = bf16[8,2560]{1,0:T(8,128)(2,1)S(1)} collective-permute-done((bf16[8,2560]{1,0:T(8,128)(2,1)S(1)}, bf16[8,2560]{1,0:T(8,128)(2,1)S(1)}, u32[]{:S(2)}, u32[]{:S(2)}) %collective-permute-start.30) | collective-permute-done | bytes 40992 | tf_op jit(solution)/shard_map/ppermute | solution.py:26
  152.8 4.7 %all-to-all-start = ((bf16[16,8,5120]{2,1,0:T(8,128)(2,1)}), bf16[16,8,5120]{2,1,0:T(8,128)(2,1)S(1)}, u32[]{:S(2)}, u32[]{:S(2)}) async-start(bf16[16,8,5120]{2,1,0:T(8,128)(2,1)} %broadcast_in_dim.47), calls=%async_computation | async-start | bytes 2621440 | tf_op jit(solution)/shard_map/all_to_all | solution.py:350
  162.3 9.7 %all-to-all-done = bf16[16,8,5120]{2,1,0:T(8,128)(2,1)S(1)} async-done(((bf16[16,8,5120]{2,1,0:T(8,128)(2,1)}), bf16[16,8,5120]{2,1,0:T(8,128)(2,1)S(1)}, u32[]{:S(2)}, u32[]{:S(2)}) %all-to-all-start) | async-done | bytes 1310752 | tf_op jit(solution)/shard_map/all_to_all | solution.py:350
  (223 shorter events, 74.3 us)
Async XLA Ops:
  1.8 20.2 %collective-permute-start = (bf16[64,5120]{1,0:T(8,128)(2,1)S(1)}, bf16[64,5120]{1,0:T(8,128)(2,1)S(1)}, u32[]{:S(2)}, u32[]{:S(2)}) collective-permute-start(bf16[64,5120]{1,0:T(8,128)(2,1)S(1)} %dynamic-slice_bitcast_fusion.8), channel_id=1, source_target_pairs={{0,16},{1,17},{2,18},{3,19},{4,20},{5,21},{6,22},{7,23},{8,24},{9,... | collective-permute-start | bytes 1966088 | tf_op jit(solution)/shard_map/ppermute | solution.py:26
  3.5 18.5 %collective-permute-start.1 = (bf16[64,5120]{1,0:T(8,128)(2,1)S(1)}, bf16[64,5120]{1,0:T(8,128)(2,1)S(1)}, u32[]{:S(2)}, u32[]{:S(2)}) collective-permute-start(bf16[64,5120]{1,0:T(8,128)(2,1)S(1)} %dynamic-slice_bitcast_fusion.8), channel_id=1, source_target_pairs={{0,48},{1,49},{2,50},{3,51},{4,52},{5,53},{6,54},{7,55},{8,56},{9,... | collective-permute-start | bytes 1966088 | tf_op jit(solution)/shard_map/ppermute | solution.py:26
  7.0 14.9 %collective-permute-start.2 = (s32[132]{0:T(256)S(1)}, s32[132]{0:T(256)S(1)}, u32[]{:S(2)}, u32[]{:S(2)}) collective-permute-start(s32[132]{0:T(256)S(1)} %constant_dynamic-update-slice_fusion), channel_id=1, source_target_pairs={{0,16},{16,0},{32,48},{48,32},{1,17},{17,1},{33,49},{49,33},{2,18}... | collective-permute-start | bytes 1592 | tf_op jit(solution)/shard_map/ppermute | solution.py:58
  7.7 14.3 %collective-permute-start.3 = (s32[132]{0:T(256)S(1)}, s32[132]{0:T(256)S(1)}, u32[]{:S(2)}, u32[]{:S(2)}) collective-permute-start(s32[132]{0:T(256)S(1)} %constant_dynamic-update-slice_fusion), channel_id=1, source_target_pairs={{0,32},{16,48},{32,0},{48,16},{1,33},{17,49},{33,1},{49,17},{2,34}... | collective-permute-start | bytes 1592 | tf_op jit(solution)/shard_map/ppermute | solution.py:58
  9.6 12.4 %collective-permute-start.4 = (s32[132]{0:T(256)S(1)}, s32[132]{0:T(256)S(1)}, u32[]{:S(2)}, u32[]{:S(2)}) collective-permute-start(s32[132]{0:T(256)S(1)} %constant_dynamic-update-slice_fusion), channel_id=1, source_target_pairs={{0,48},{16,32},{32,16},{48,0},{1,49},{17,33},{33,17},{49,1},{2,50}... | collective-permute-start | bytes 1592 | tf_op jit(solution)/shard_map/ppermute | solution.py:58
  23.0 12.0 %collective-permute-start.5 = (bf16[64,5120]{1,0:T(8,128)(2,1)}, bf16[64,5120]{1,0:T(8,128)(2,1)S(1)}, u32[]{:S(2)}, u32[]{:S(2)}) collective-permute-start(bf16[64,5120]{1,0:T(8,128)(2,1)} %broadcast_select_fusion), channel_id=1, source_target_pairs={{0,16},{1,17},{2,18},{3,19},{4,20},{5,21},{6,22},{7,23},{8,24},{9,... | collective-permute-start | bytes 1966088 | tf_op jit(solution)/shard_map/ppermute | solution.py:26
  23.9 11.1 %collective-permute-start.6 = (bf16[64,5120]{1,0:T(8,128)(2,1)}, bf16[64,5120]{1,0:T(8,128)(2,1)S(1)}, u32[]{:S(2)}, u32[]{:S(2)}) collective-permute-start(bf16[64,5120]{1,0:T(8,128)(2,1)} %pad_maximum_fusion.2), channel_id=1, source_target_pairs={{0,4},{1,5},{2,6},{3,7},{4,0},{5,1},{6,2},{7,3},{8,12},{9,13},{10,... | collective-permute-start | bytes 1966088 | tf_op jit(solution)/shard_map/ppermute | solution.py:26
  26.3 12.0 %collective-permute-start.7 = (bf16[64,5120]{1,0:T(8,128)(2,1)}, bf16[64,5120]{1,0:T(8,128)(2,1)S(1)}, u32[]{:S(2)}, u32[]{:S(2)}) collective-permute-start(bf16[64,5120]{1,0:T(8,128)(2,1)} %pad_maximum_fusion.3), channel_id=1, source_target_pairs={{0,12},{1,13},{2,14},{3,15},{4,8},{5,9},{6,10},{7,11},{8,4},{9,5},... | collective-permute-start | bytes 1966088 | tf_op jit(solution)/shard_map/ppermute | solution.py:26
  38.3 8.9 %collective-permute-start.8 = (bf16[32,5120]{1,0:T(8,128)(2,1)S(1)}, bf16[32,5120]{1,0:T(8,128)(2,1)S(1)}, u32[]{:S(2)}, u32[]{:S(2)}) collective-permute-start(bf16[32,5120]{1,0:T(8,128)(2,1)S(1)} %get-tuple-element.93), channel_id=1, source_target_pairs={{0,4},{1,5},{2,6},{3,7},{4,0},{5,1},{6,2},{7,3},{8,12},{9,13},{10,... | collective-permute-start | bytes 983048 | tf_op jit(solution)/shard_map/ppermute | solution.py:26
  38.4 8.8 %collective-permute-start.9 = (bf16[32,5120]{1,0:T(8,128)(2,1)S(1)}, bf16[32,5120]{1,0:T(8,128)(2,1)S(1)}, u32[]{:S(2)}, u32[]{:S(2)}) collective-permute-start(bf16[32,5120]{1,0:T(8,128)(2,1)S(1)} %get-tuple-element.92), channel_id=1, source_target_pairs={{0,12},{1,13},{2,14},{3,15},{4,8},{5,9},{6,10},{7,11},{8,4},{9,5},... | collective-permute-start | bytes 983048 | tf_op jit(solution)/shard_map/ppermute | solution.py:26
  47.3 11.0 %collective-permute-start.10 = (bf16[384,1280]{1,0:T(8,128)(2,1)}, bf16[384,1280]{1,0:T(8,128)(2,1)S(1)}, u32[]{:S(2)}, u32[]{:S(2)}) collective-permute-start(bf16[384,1280]{1,0:T(8,128)(2,1)} %shard_map.70), channel_id=1, source_target_pairs={{0,64},{64,0},{1,65},{65,1},{2,66},{66,2},{3,67},{67,3},{4,68},{68... | collective-permute-start | bytes 2949128 | tf_op jit(solution)/shard_map/ppermute | solution.py:316
  60.0 5.8 %collective-permute-start.14 = (f32[6,512]{1,0:T(8,128)S(1)}, f32[6,512]{1,0:T(8,128)S(1)}, u32[]{:S(2)}, u32[]{:S(2)}) collective-permute-start(f32[6,512]{1,0:T(8,128)S(1)} %get-tuple-element.127), channel_id=1, source_target_pairs={{0,3},{1,2},{2,1},{3,0},{4,7},{5,6},{6,5},{7,4},{8,11},{9,10},{10,... | collective-permute-start | bytes 36872 | tf_op jit(solution)/shard_map/ppermute | solution.py:58
  93.4 13.4 %collective-permute-start.21 = (bf16[2,2,2,4,8,1280]{5,4,3,2,1,0:T(8,128)(2,1)S(1)}, bf16[2,2,2,4,8,1280]{5,4,3,2,1,0:T(8,128)(2,1)S(1)}, u32[]{:S(2)}, u32[]{:S(2)}) collective-permute-start(bf16[2,2,2,4,8,1280]{5,4,3,2,1,0:T(8,128)(2,1)S(1)} %fusion.39), channel_id=1, source_target_pairs={{0,4},{4,0},{8,12},{12,8},{1,5},{5,1},{9,13},{13,9},{2,6},{6,2},{1... | collective-permute-start | bytes 1966088 | tf_op jit(solution)/shard_map/ppermute | solution.py:248
  98.2 12.8 %collective-permute-start.31 = (bf16[2,2,2,4,8,1280]{5,4,3,2,1,0:T(8,128)(2,1)S(1)}, bf16[2,2,2,4,8,1280]{5,4,3,2,1,0:T(8,128)(2,1)S(1)}, u32[]{:S(2)}, u32[]{:S(2)}) collective-permute-start(bf16[2,2,2,4,8,1280]{5,4,3,2,1,0:T(8,128)(2,1)S(1)} %fusion.45), channel_id=1, source_target_pairs={{0,1},{1,0},{2,3},{3,2},{4,5},{5,4},{6,7},{7,6},{8,9},{9,8},{10,11... | collective-permute-start | bytes 1966088 | tf_op jit(solution)/shard_map/ppermute | solution.py:248
  99.4 17.2 %collective-permute-start.35 = (bf16[2,2,2,4,8,1280]{5,4,3,2,1,0:T(8,128)(2,1)S(1)}, bf16[2,2,2,4,8,1280]{5,4,3,2,1,0:T(8,128)(2,1)S(1)}, u32[]{:S(2)}, u32[]{:S(2)}) collective-permute-start(bf16[2,2,2,4,8,1280]{5,4,3,2,1,0:T(8,128)(2,1)S(1)} %fusion.48), channel_id=1, source_target_pairs={{0,3},{1,2},{2,1},{3,0},{4,7},{5,6},{6,5},{7,4},{8,11},{9,10},{10,... | collective-permute-start | bytes 1966088 | tf_op jit(solution)/shard_map/ppermute | solution.py:248
  104.3 16.4 %collective-permute-start.25 = (bf16[2,2,2,4,8,1280]{5,4,3,2,1,0:T(8,128)(2,1)S(1)}, bf16[2,2,2,4,8,1280]{5,4,3,2,1,0:T(8,128)(2,1)S(1)}, u32[]{:S(2)}, u32[]{:S(2)}) collective-permute-start(bf16[2,2,2,4,8,1280]{5,4,3,2,1,0:T(8,128)(2,1)S(1)} %fusion.42), channel_id=1, source_target_pairs={{0,12},{4,8},{8,4},{12,0},{1,13},{5,9},{9,5},{13,1},{2,14},{6,10},... | collective-permute-start | bytes 1966088 | tf_op jit(solution)/shard_map/ppermute | solution.py:248
  111.1 9.8 %collective-permute-start.32 = (bf16[2,2,4,8,1280]{4,3,2,1,0:T(8,128)(2,1)S(1)}, bf16[2,2,4,8,1280]{4,3,2,1,0:T(8,128)(2,1)S(1)}, u32[]{:S(2)}, u32[]{:S(2)}) collective-permute-start(bf16[2,2,4,8,1280]{4,3,2,1,0:T(8,128)(2,1)S(1)} %get-tuple-element.72), channel_id=1, source_target_pairs={{0,3},{1,2},{2,1},{3,0},{4,7},{5,6},{6,5},{7,4},{8,11},{9,10},{10,... | collective-permute-start | bytes 983048 | tf_op jit(solution)/shard_map/ppermute | solution.py:248
  116.7 8.2 %collective-permute-start.36 = (bf16[2,2,4,8,1280]{4,3,2,1,0:T(8,128)(2,1)S(1)}, bf16[2,2,4,8,1280]{4,3,2,1,0:T(8,128)(2,1)S(1)}, u32[]{:S(2)}, u32[]{:S(2)}) collective-permute-start(bf16[2,2,4,8,1280]{4,3,2,1,0:T(8,128)(2,1)S(1)} %get-tuple-element.70), channel_id=1, source_target_pairs={{0,1},{1,0},{2,3},{3,2},{4,5},{5,4},{6,7},{7,6},{8,9},{9,8},{10,11... | collective-permute-start | bytes 983048 | tf_op jit(solution)/shard_map/ppermute | solution.py:248
  117.8 10.2 %collective-permute-start.22 = (bf16[2,2,4,8,1280]{4,3,2,1,0:T(8,128)(2,1)S(1)}, bf16[2,2,4,8,1280]{4,3,2,1,0:T(8,128)(2,1)S(1)}, u32[]{:S(2)}, u32[]{:S(2)}) collective-permute-start(bf16[2,2,4,8,1280]{4,3,2,1,0:T(8,128)(2,1)S(1)} %get-tuple-element.68), channel_id=1, source_target_pairs={{0,12},{4,8},{8,4},{12,0},{1,13},{5,9},{9,5},{13,1},{2,14},{6,10},... | collective-permute-start | bytes 983048 | tf_op jit(solution)/shard_map/ppermute | solution.py:248
  120.8 7.6 %collective-permute-start.26 = (bf16[2,2,4,8,1280]{4,3,2,1,0:T(8,128)(2,1)S(1)}, bf16[2,2,4,8,1280]{4,3,2,1,0:T(8,128)(2,1)S(1)}, u32[]{:S(2)}, u32[]{:S(2)}) collective-permute-start(bf16[2,2,4,8,1280]{4,3,2,1,0:T(8,128)(2,1)S(1)} %get-tuple-element.66), channel_id=1, source_target_pairs={{0,4},{4,0},{8,12},{12,8},{1,5},{5,1},{9,13},{13,9},{2,6},{6,2},{1... | collective-permute-start | bytes 983048 | tf_op jit(solution)/shard_map/ppermute | solution.py:248
  121.0 9.6 %collective-permute-start.33 = (bf16[2,4,8,1280]{3,2,1,0:T(8,128)(2,1)S(1)}, bf16[2,4,8,1280]{3,2,1,0:T(8,128)(2,1)S(1)}, u32[]{:S(2)}, u32[]{:S(2)}) collective-permute-start(bf16[2,4,8,1280]{3,2,1,0:T(8,128)(2,1)S(1)} %get-tuple-element.90), channel_id=1, source_target_pairs={{0,4},{4,0},{8,12},{12,8},{1,5},{5,1},{9,13},{13,9},{2,6},{6,2},{1... | collective-permute-start | bytes 491528 | tf_op jit(solution)/shard_map/ppermute | solution.py:248
  125.0 7.3 %collective-permute-start.37 = (bf16[2,4,8,1280]{3,2,1,0:T(8,128)(2,1)S(1)}, bf16[2,4,8,1280]{3,2,1,0:T(8,128)(2,1)S(1)}, u32[]{:S(2)}, u32[]{:S(2)}) collective-permute-start(bf16[2,4,8,1280]{3,2,1,0:T(8,128)(2,1)S(1)} %get-tuple-element.88), channel_id=1, source_target_pairs={{0,12},{4,8},{8,4},{12,0},{1,13},{5,9},{9,5},{13,1},{2,14},{6,10},... | collective-permute-start | bytes 491528 | tf_op jit(solution)/shard_map/ppermute | solution.py:248
  128.4 6.6 %collective-permute-start.27 = (bf16[2,4,8,1280]{3,2,1,0:T(8,128)(2,1)S(1)}, bf16[2,4,8,1280]{3,2,1,0:T(8,128)(2,1)S(1)}, u32[]{:S(2)}, u32[]{:S(2)}) collective-permute-start(bf16[2,4,8,1280]{3,2,1,0:T(8,128)(2,1)S(1)} %get-tuple-element.84), channel_id=1, source_target_pairs={{0,3},{1,2},{2,1},{3,0},{4,7},{5,6},{6,5},{7,4},{8,11},{9,10},{10,... | collective-permute-start | bytes 491528 | tf_op jit(solution)/shard_map/ppermute | solution.py:248
  152.8 19.2 %all-to-all-start = ((bf16[16,8,5120]{2,1,0:T(8,128)(2,1)}), bf16[16,8,5120]{2,1,0:T(8,128)(2,1)S(1)}, u32[]{:S(2)}, u32[]{:S(2)}) async-start(bf16[16,8,5120]{2,1,0:T(8,128)(2,1)} %broadcast_in_dim.47), calls=%async_computation | async-start | bytes 2621440 | tf_op jit(solution)/shard_map/all_to_all | solution.py:350
  (30 other events, 157.4 us)

commit v2 on v1

--- a/solution.py
+++ b/solution.py
@@ -1,3 +1,5 @@
+import functools
+
 import jax
 import jax.numpy as jnp
 from jax import lax
@@ -67,22 +69,21 @@
 
 def gather_logits(block, gain_row, matrix, ints):
     half = block.shape[0] // 2
+    tokens = 4 * block.shape[0]
     mine = lax.dynamic_slice_in_dim(block, parity() * half, half, axis=0)
-    near = swap_y(mine, (1, 1))
-    wrap = swap_y(mine, (3, 3))
+    p = swap_y(mine, (1, 3))
+    q = swap_y(mine, (3, 1))
     ints = ring(ints, "dp")
-    logits = add_logits((block,), OWN_PLAN, gain_row, matrix, 3 * 128)
-    near, wrap, logits, *ints = tied(near, wrap, logits, *ints)
-    far = swap_y(by_core(wrap, near), (1, 3))
-    pieces = [slice(k * half // 2, (k + 1) * half // 2) for k in range(2)]
-    sides = [swap_u(jnp.concatenate([near[pieces[k]], wrap[pieces[k]]]), (1, 3)[k]) for k in range(2)]
-    logits = add_logits((near, wrap), HELD_PLAN, gain_row, matrix, 3 * 128, logits)
-    far, logits, *sides = tied(far, logits, *sides)
-    far_sides = [swap_u(far[pieces[k]], (1, 3)[k]) for k in range(2)]
-    logits = add_logits(sides, OTHER_PLAN, gain_row, matrix, 3 * 128, logits)
-    logits, *far_sides = tied(logits, *far_sides)
-    far_logits = add_logits((far, *far_sides), FAR_PLAN, gain_row, matrix, 128)
-    return logits, far_logits, [ints[s] for s in (0, 1, 3, 2)]
+    logits = add_logits((block,), OWN_PLAN, gain_row, matrix, tokens)
+    p, q, logits, *ints = tied(p, q, logits, *ints)
+    far = swap_y(q, (1, 3))
+    p_side, q_side = swap_u(p, 1), swap_u(q, 3)
+    logits = add_logits((p, q), HELD_PLAN, gain_row, matrix, tokens, logits)
+    far, logits, p_side, q_side = tied(far, logits, p_side, q_side)
+    far_sides = [swap_u(far[: half // 2], 1), swap_u(far[half // 2 :], 3)]
+    logits = add_logits((p_side, q_side), OTHER_PLAN, gain_row, matrix, tokens, logits)
+    logits = add_logits((far, *far_sides), FAR_PLAN, gain_row, matrix, tokens, logits)
+    return logits, [ints[s] for s in (0, 1, 3, 2)]
 
 
 CHUNKS = 10
@@ -96,7 +97,11 @@
         width = rows.shape[1]
         deep = width // CHUNKS
         held = parity() * 64
+        p_first = 128 * (NEAR + core() * (WRAP - NEAR))
+        q_first = 128 * (NEAR + WRAP) - p_first
         shift = {"all": 0, "held": held, "other": 64 - held}
+        shift |= {"p held": p_first + held, "q held": q_first + held}
+        shift |= {"p other": p_first + 64 - held, "q other": q_first + 64 - held}
         fetches = []
         for c in range(CHUNKS):
             piece = pl.ds(c * deep, deep)
@@ -162,18 +167,19 @@
 
 
 OWN_PLAN = [(0, 0, 128, 0, "all")], [(0, 128, 0, "all")]
-HELD_PLAN = [(0, 0, 64, 0, "all"), (1, 0, 64, 64, "all")], [(0, 64, 128, "held"), (64, 64, 256, "held")]
-OTHER_PLAN = (
-    [(k, 32 * g, 32, 64 * g + 32 * k, "all") for k in range(2) for g in range(2)],
-    [(0, 64, 128, "other"), (64, 64, 256, "other")],
+HELD_PLAN = [(0, 0, 64, 0, "all"), (1, 0, 64, 64, "all")], [(0, 64, 0, "p held"), (64, 64, 0, "q held")]
+OTHER_PLAN = [(0, 0, 64, 0, "all"), (1, 0, 64, 64, "all")], [(0, 64, 0, "p other"), (64, 64, 0, "q other")]
+FAR_PLAN = (
+    [(0, 0, 64, 0, "held")] + [(1 + k, 0, 32, 32 * k, "other") for k in range(2)],
+    [(0, 128, FAR * 128, "all")],
 )
-FAR_PLAN = [(0, 0, 64, 0, "held")] + [(1 + k, 0, 32, 32 * k, "other") for k in range(2)], [(0, 128, 0, "all")]
 
 
 def add_logits(sources, plan, gain_row, matrix, tokens, filled=None):
     width, voc = matrix.shape
     anywhere = pl.BlockSpec(memory_space=pl.ANY)
     count = len(sources)
+    rows = sum(piece[2] for piece in plan[0])
     operands = [*sources, gain_row, matrix] + ([] if filled is None else [filled])
     return pl.pallas_call(
         make_kernel(count, *plan),
@@ -184,17 +190,17 @@
         out_specs=anywhere,
         scratch_shapes=[
             pltpu.VMEM((width, voc), jnp.bfloat16),
-            pltpu.VMEM((128, width), jnp.bfloat16),
-            pltpu.VMEM((128, TILE), jnp.float32),
-            pltpu.VMEM((128, voc), jnp.float32),
-            pltpu.VMEM((128, voc), jnp.bfloat16),
+            pltpu.VMEM((rows, width), jnp.bfloat16),
+            pltpu.VMEM((rows, TILE), jnp.float32),
+            pltpu.VMEM((rows, voc), jnp.float32),
+            pltpu.VMEM((rows, voc), jnp.bfloat16),
             pltpu.SemaphoreType.DMA((CHUNKS,)),
-            pltpu.SemaphoreType.DMA((4,)),
+            pltpu.SemaphoreType.DMA((5,)),
         ],
         input_output_aliases={} if filled is None else {count + 2: 0},
         compiler_params=pltpu.CompilerParams(vmem_limit_bytes=52 * 1024 * 1024),
         cost_estimate=pl.CostEstimate(
-            flops=2 * 128 * width * voc, bytes_accessed=2 * width * (voc + 128), transcendentals=0
+            flops=2 * rows * width * voc, bytes_accessed=2 * width * (voc + rows), transcendentals=0
         ),
     )(*operands)
 
@@ -220,6 +226,55 @@
     return block.astype(jnp.bfloat16)
 
 
+def away_kernel(*refs):
+    sources, head_ref, outs = refs[:4], refs[4], refs[5:9]
+    held_head, blocks, results, head_sems, in_sems, out_sems = refs[9:]
+    deep = head_ref.shape[0] // 8
+    fetches, loads, stores = [], [], []
+    for q in range(4):
+        loads.append(pltpu.make_async_copy(sources[q], blocks.at[q], in_sems.at[q]))
+        for c in (2 * q, 2 * q + 1):
+            piece = pl.ds(c * deep, deep)
+            fetches.append(pltpu.make_async_copy(head_ref.at[piece], held_head.at[piece], head_sems.at[c]))
+    for copy in loads[:1] + fetches[:2] + loads[1:] + fetches[2:]:
+        copy.start()
+    for q in range(4):
+        loads[q].wait()
+        for c in (2 * q, 2 * q + 1):
+            fetches[c].wait()
+        columns = held_head[2 * q * deep : 2 * (q + 1) * deep, :]
+        out = lax.dot_general(blocks[q], columns, (((1,), (1,)), ((), ())), preferred_element_type=jnp.float32)
+        results[q] = narrow(out)
+        stores.append(pltpu.make_async_copy(results.at[q], outs[q], out_sems.at[q]))
+        stores[q].start()
+    for copy in stores:
+        copy.wait()
+
+
+def away_products(blocks, matrix):
+    width, voc = matrix.shape
+    rows, columns = blocks[0].shape[0], width // 4
+    anywhere = pl.BlockSpec(memory_space=pl.ANY)
+    return pl.pallas_call(
+        away_kernel,
+        out_shape=[jax.ShapeDtypeStruct((rows, columns), jnp.bfloat16)] * 4,
+        in_specs=[anywhere] * 5,
+        out_specs=[anywhere] * 4,
+        scratch_shapes=[
+            pltpu.VMEM((width, voc), jnp.bfloat16),
+            pltpu.VMEM((4, rows, voc), jnp.bfloat16),
+            pltpu.VMEM((4, rows, columns), jnp.bfloat16),
+            pltpu.SemaphoreType.DMA((8,)),
+            pltpu.SemaphoreType.DMA((4,)),
+            pltpu.SemaphoreType.DMA((4,)),
+        ],
+        compiler_params=pltpu.CompilerParams(vmem_limit_bytes=52 * 1024 * 1024),
+        cost_estimate=pl.CostEstimate(
+            flops=2 * rows * width * voc, bytes_accessed=2 * (width * voc + rows * (width + 4 * voc)), transcendentals=0
+        ),
+    )(*blocks, matrix)
+
+
 def sum_rows(grad_logits, matrix, later):
     voc = grad_logits.shape[1]
     width = matrix.shape[0] // 4
@@ -247,13 +302,14 @@
         axis, step = dims[name][2:]
         return lax.ppermute(block, axis, [(i, i ^ step) for i in range(4)])
 
-    halves = []
+    away, stay = [], []
     for order in orders:
         turned_rows = jnp.transpose(rows, [dims[name][0] for name in order] + [0, 5, 6])
-        halves.append(split(turned_rows, order[0]))
-    away = [narrow(product(*tied(halves[q][0]), q)) for q in range(4)]
-    *stay, away[3] = tied(*[halves[q][1] for q in range(4)], away[3])
-    came = [swap(away[q], orders[q][0]) for q in range(4)]
+        one, other = split(turned_rows, order[0])
+        away.append(one.reshape(-1, voc))
+        stay.append(other)
+    shape = stay[0].shape[:-1] + (width,)
+    came = [swap(block.reshape(shape), order[0]) for block, order in zip(away_products(away, matrix), orders)]
     kept = [product(stay[q], q) for q in range(4)]
     came[0], later = tied(came[0], later)
     for stage in range(1, 4):
@@ -271,7 +327,7 @@
         mine = block[OWN] + wide(came[0])
         came = swap_y(narrow(block[second] + wide(came[1])), (steps[1],) * 2)
         done.append(mine + wide(came))
-    return jnp.concatenate(done, axis=-1), later
+    return done, later
 
 
 def shard_stats(logits, peer_logits, hit):
@@ -291,6 +347,23 @@
     )
 
 
+def norm_backward_kernel(count, *refs):
+    states_ref, gain_ref, out_ref = refs[count:]
+    states = states_ref[...]
+    width = states.shape[1]
+    inverse = lax.rsqrt(jnp.sum(states * states, axis=-1, keepdims=True) / width + eps_norm)
+    pieces, start = [], 0
+    for ref in refs[:count]:
+        columns = slice(start, start + ref.shape[1])
+        pieces.append((ref[...] * gain_ref[:, columns], columns))
+        start += ref.shape[1]
+    inner = sum(jnp.sum(scaled * states[:, columns], axis=-1, keepdims=True) for scaled, columns in pieces) / width
+    for scaled, columns in pieces:
+        rows = narrow(inverse * (scaled - states[:, columns] * inverse * inverse * inner))
+        for k in range(out_ref.shape[0]):
+            out_ref[k, :, columns] = rows
+
+
 def mean_loss(stats, weights):
     own_log = stats[0] + jnp.log(stats[1])
     peer_log = stats[2] + jnp.log(stats[3])
@@ -307,25 +380,20 @@
     group = block.shape[0]
     tokens = 4 * group
     voc_shard = matrix.shape[1]
-    first, second, ints = gather_logits(block, gain_row, matrix, jnp.concatenate([targets, lengths]))
+    logits, ints = gather_logits(block, gain_row, matrix, jnp.concatenate([targets, lengths]))
     all_targets = jnp.concatenate([part[:group] for part in ints])
     all_lengths = jnp.concatenate([part[group:] for part in ints])
+    peer_logits = lax.ppermute(logits, "peer", [(0, 1), (1, 0)])
     hit = all_targets[:, None] - lax.axis_index(("dp", "tx", "tz")) * voc_shard
     hit = hit == lax.broadcasted_iota(jnp.int32, (1, voc_shard), 1)
-    peer = [(0, 1), (1, 0)]
-    first_peer, second_peer = lax.ppermute(first, "peer", peer), lax.ppermute(second, "peer", peer)
-    cut = first.shape[0]
-    stats = jnp.concatenate(
-        [shard_stats(first, first_peer, hit[:cut]), shard_stats(second, second_peer, hit[cut:])], axis=1
-    )
+    stats = shard_stats(logits, peer_logits, hit)
     stats = merge(ring(stats, "tz"))
     stats = merge(ring(stats, "tx"))
     stats = ring(stats, "dp")
     stats = merge([stats[0]] + [turned(stats[s], s, 1) for s in (1, 2, 3)])
     own_log = stats[0] + jnp.log(stats[1])
     peer_log = stats[2] + jnp.log(stats[3])
-    values = wide(jnp.concatenate([first, second]))
-    peer_values = wide(jnp.concatenate([first_peer, second_peer]))
+    values, peer_values = wide(logits), wide(peer_logits)
     position = lax.broadcasted_iota(jnp.int32, (tokens // LEN, LEN), 1)
     weights = (position < all_lengths[:, None]).astype(jnp.float32).reshape(tokens)
 
@@ -341,12 +409,12 @@
     grad_normed, stats = sum_rows(grad_logits, matrix, stats)
     loss = mean_loss(stats, weights)
 
-    own = wide(lax.dynamic_slice_in_dim(block, lax.axis_index(("tx", "tz")) * 8, 8, axis=0))
-    own_inverse = lax.rsqrt(jnp.mean(own * own, axis=-1, keepdims=True) + eps_norm)
-    scaled = grad_normed * gain_row
-    inner = jnp.mean(scaled * own, axis=-1, keepdims=True)
-    rows = narrow(own_inverse * (scaled - own * own_inverse * own_inverse * inner))
-    spread = jnp.broadcast_to(rows[None], (16,) + rows.shape)
+    own = lax.dynamic_slice_in_dim(block, lax.axis_index(("tx", "tz")) * 8, 8, axis=0)
+    spread = pl.pallas_call(
+        functools.partial(norm_backward_kernel, len(grad_normed)),
+        out_shape=jax.ShapeDtypeStruct((16,) + own.shape, own.dtype),
+        compiler_params=pltpu.CompilerParams(vmem_limit_bytes=16 * 1024 * 1024),
+    )(*grad_normed, wide(own), gain_row)
     grad_hidden = lax.all_to_all(spread, ("tx", "tz"), split_axis=0, concat_axis=0, tiled=True)
     return (loss, grad_hidden.reshape((1,) + block.shape))
 

time: 175 us -> 182 us (1.040)
  Pallas kernels: 27.7 us -> 39.1 us
  other arithmetic: 17.6 us -> 9.45 us
  starting transfers between devices: 54.9 us -> 61 us
  waiting for transfers between devices: 48.5 us -> 43 us
    pallas_call x0 -> x2, Pallas kernels: none -> 10.8 us  [the longest x1 9.49 us: away_products(): pl.pallas_call(away_kernel, out_shape=[jax.ShapeDtypeStruct((rows, column...]
    ppermute x16, waiting for transfers between devices: 17.1 us -> 10.7 us  [swap(): return lax.ppermute(block, axis, [(i, i ^ step) for i in range(4)])]
    concatenate x4 -> x0, other arithmetic: 4.08 us -> none  [the longest x2 1.78 us: gather_logits(): jnp.concatenate([near[pieces[k]], wrap[pieces[k]]])]
    ppermute x16, starting transfers between devices: 18.6 us -> 21.7 us  [swap(): return lax.ppermute(block, axis, [(i, i ^ step) for i in range(4)])]
    dynamic_slice x0 -> x3, local copies, waits for them, and re-layouts: none -> 2.71 us  [split(): away = lax.dynamic_index_in_dim(block, 1 - at, 0, keepdims=False)]
    dot_general x8 -> x4, matrix products: 10.8 us -> 12 us  [product(): lax.dot_general(block.reshape(-1, voc), columns, (((1,), (1,)), ((), ()))...]
  transfers between devices with their start and end apart: 42 -> 41, of which waited for: 23 -> 20; matrix products, arithmetic and copies ran while one was open for 11% -> 10% of each run, Pallas kernels for 16% -> 12%
where the time goes in v2:
time: 182 us; the launch traced here: 181 us
  starting transfers between devices  61 us (34%)
  waiting for transfers between devices  43 us (24%)
  Pallas kernels  39.1 us (21%)
  matrix products  12 us (7%)
  local copies, waits for them, and re-layouts  10.5 us (6%)
  other arithmetic  9.45 us (5%)
  between operations  5.87 us (3%)
    pallas_call x4, Pallas kernels, add_logits(): pl.pallas_call(make_kernel(count, *plan), out_shape=jax.ShapeDtypeStruct(...  28.4 us
    ppermute x16, starting transfers between devices, swap(): return lax.ppermute(block, axis, [(i, i ^ step) for i in range(4)])  21.7 us
    ppermute x12, starting transfers between devices, ring(): lax.ppermute(block, axis, [(i, i ^ s) for i in range(4)])  19.8 us
    ppermute x11, starting transfers between devices, permute(): lax.ppermute(block, ALL, [(index(*p), index(*move(*p))) for p in places])  13.5 us
    dot_general x4, matrix products, product(): lax.dot_general(block.reshape(-1, voc), columns, (((1,), (1,)), ((), ()))...  12 us
    ppermute x11, waiting for transfers between devices, permute(): lax.ppermute(block, ALL, [(index(*p), index(*move(*p))) for p in places])  11.4 us
    ppermute x16, waiting for transfers between devices, swap(): return lax.ppermute(block, axis, [(i, i ^ step) for i in range(4)])  10.7 us
    ppermute x12, waiting for transfers between devices, ring(): lax.ppermute(block, axis, [(i, i ^ s) for i in range(4)])  9.88 us
  transfers between devices with their start and end apart: 41, of which 20 were waited for; matrix products, arithmetic and copies ran while one was open for 10% of the time, Pallas kernels for 12%

profile of v2, /device:TPU:0, one launch (start us, length us, event | category | flops | bytes accessed | tf_op | source)
XLA Modules:
  0.0 181.0 jit_solution(9327802032952039588)
XLA Ops:
  12.5 8.6 %shard_map.68.refs_4_ = bf16[512,1280]{1,0:T(8,128)(2,1)S(1)} custom-call(bf16[128,5120]{1,0:T(8,128)(2,1)} %bitcast.333, f32[1,5120]{1,0:T(1,128)S(1)} %copy-done.2, bf16[5120,1280]{1,0:T(8,128)(2,1)} %bitcast.320), custom_call_target="tpu_custom_call" | custom-call | flops 1677721600 | bytes 14417920 | tf_op jit(solution)/shard_map/pallas_call | solution.py:184
  22.2 2.8 %collective-permute-start.7 = (bf16[64,5120]{1,0:T(8,128)(2,1)S(1)}, bf16[64,5120]{1,0:T(8,128)(2,1)S(1)}, u32[]{:S(2)}, u32[]{:S(2)}) collective-permute-start(bf16[64,5120]{1,0:T(8,128)(2,1)S(1)} %collective-permute-done.1.refs_1_), channel_id=1, source_target_pairs={{0,12},{1,13},{2,14},{3,15},{4,8},{5,9},{6,10},{7,11},{8,4},{9,5},... | collective-permute-start | bytes 1966088 | tf_op jit(solution)/shard_map/ppermute | solution.py:28
  25.3 6.6 %shard_map.69.refs_4_ = bf16[512,1280]{1,0:T(8,128)(2,1)} custom-call(bf16[64,5120]{1,0:T(8,128)(2,1)S(1)} %collective-permute-done.refs_0_, bf16[64,5120]{1,0:T(8,128)(2,1)S(1)} %collective-permute-done.1.refs_1_, f32[1,5120]{1,0:T(1,128)S(1)} %copy-done.2, bf16[5120,1280]{1,0:T(8,128)(2,1)} %bitcast.321, ...), custom_call_target="tpu_custom_call", output_to_operand_aliasing={{}: (4, {})} | custom-call | flops 1677721600 | bytes 14417920 | tf_op jit(solution)/shard_map/pallas_call | solution.py:184
  37.2 6.6 %shard_map.70.refs_5_ = bf16[512,1280]{1,0:T(8,128)(2,1)} custom-call(bf16[64,5120]{1,0:T(8,128)(2,1)S(1)} %collective-permute-done.6.refs_0_, bf16[64,5120]{1,0:T(8,128)(2,1)S(1)} %collective-permute-done.7.refs_1_, f32[1,5120]{1,0:T(1,128)S(1)} %copy-done.2, bf16[5120,1280]{1,0:T(8,128)(2,1)} %bitcast.322, ...), custom_call_target="tpu_custom_call", output_to_operand_aliasing={{}: (4, {})} | custom-call | flops 1677721600 | bytes 14417920 | tf_op jit(solution)/shard_map/pallas_call | solution.py:184
  44.3 6.6 %shard_map.71 = bf16[512,1280]{1,0:T(8,128)(2,1)} custom-call(bf16[64,5120]{1,0:T(8,128)(2,1)S(1)} %collective-permute-done.5.refs_0_, bf16[32,5120]{1,0:T(8,128)(2,1)S(1)} %collective-permute-done.8.refs_1_, bf16[32,5120]{1,0:T(8,128)(2,1)S(1)} %collective-permute-done.9.refs_2_, f32[1,5120]{1,0:T(1,128)S(1)} %copy-done.2, ...), custom_call_target="tpu_custom_call", output_to_operand_aliasing={{}: (5, {})} | custom-call | flops 1677721600 | bytes 14417920 | tf_op jit(solution)/shard_map/pallas_call | solution.py:184
  58.7 3.6 %collective-permute-start.12 = (f32[6,512]{1,0:T(8,128)S(1)}, f32[6,512]{1,0:T(8,128)S(1)}, u32[]{:S(2)}, u32[]{:S(2)}) collective-permute-start(f32[6,512]{1,0:T(8,128)S(1)} %stack.113), channel_id=1, source_target_pairs={{0,2},{1,3},{2,0},{3,1},{4,6},{5,7},{6,4},{7,5},{8,10},{9,11},{10,... | collective-permute-start | bytes 36872 | tf_op jit(solution)/shard_map/ppermute | solution.py:60
  64.2 3.1 %collective-permute-done.13 = f32[6,512]{1,0:T(8,128)S(1)} collective-permute-done((f32[6,512]{1,0:T(8,128)S(1)}, f32[6,512]{1,0:T(8,128)S(1)}, u32[]{:S(2)}, u32[]{:S(2)}) %collective-permute-start.13) | collective-permute-done | bytes 12320 | tf_op jit(solution)/shard_map/ppermute | solution.py:60
  68.3 2.3 %collective-permute-start.15 = (f32[6,512]{1,0:T(8,128)S(1)}, f32[6,512]{1,0:T(8,128)S(1)}, u32[]{:S(2)}, u32[]{:S(2)}) collective-permute-start(f32[6,512]{1,0:T(8,128)S(1)} %get-tuple-element.109), channel_id=1, source_target_pairs={{0,8},{4,12},{8,0},{12,4},{1,9},{5,13},{9,1},{13,5},{2,10},{6,14},... | collective-permute-start | bytes 36872 | tf_op jit(solution)/shard_map/ppermute | solution.py:60
  80.8 2.4 %collective-permute-done.18 = f32[6,512]{1,0:T(8,128)S(1)} collective-permute-done((f32[6,512]{1,0:T(8,128)S(1)}, f32[6,512]{1,0:T(8,128)S(1)}, u32[]{:S(2)}, u32[]{:S(2)}) %collective-permute-start.18) | collective-permute-done | bytes 12320 | tf_op jit(solution)/shard_map/ppermute | solution.py:60
  89.9 9.5 %shard_map.72 = (bf16[256,1280]{1,0:T(8,128)(2,1)S(1)}, bf16[256,1280]{1,0:T(8,128)(2,1)S(1)}, bf16[256,1280]{1,0:T(8,128)(2,1)S(1)}, bf16[256,1280]{1,0:T(8,128)(2,1)}) custom-call(bf16[256,1280]{1,0:T(8,128)(2,1)} %bitcast.337, bf16[256,1280]{1,0:T(8,128)(2,1)} %bitcast.335, bf16[256,1280]{1,0:T(8,128)(2,1)} %bitcast.334, bf16[256,1280]{1,0:T(8,128)(2,1)} %bitcast.336, ...), custom_call_target="tpu_custom_call" | custom-call | flops 3355443200 | bytes 18350080 | tf_op jit(solution)/shard_map/pallas_call | solution.py:258
  99.5 3.0 %fusion = f32[2,2,2,4,8,1280]{5,4,3,2,1,0:T(8,128)S(1)} fusion(bf16[1,5120,1280]{2,1,0:T(8,128)(2,1)} %param.7, bf16[2,2,2,4,8,1280]{5,4,3,0,1,2:T(8,128)(2,1)S(1)} %get-tuple-element.60), kind=kOutput, calls=%fused_computation.8 | convolution fusion | flops 838860800 | bytes 5242880 | tf_op jit(solution)/shard_map/dot_general | solution.py:291
  102.8 3.0 %fusion.2 = f32[2,2,2,4,8,1280]{5,4,3,2,1,0:T(8,128)S(1)} fusion(bf16[1,5120,1280]{2,1,0:T(8,128)(2,1)} %param.7, bf16[2,2,2,4,8,1280]{5,4,3,0,2,1:T(8,128)(2,1)S(1)} %get-tuple-element.62), kind=kOutput, calls=%fused_computation.10 | convolution fusion | flops 838860800 | bytes 5242880 | tf_op jit(solution)/shard_map/dot_general | solution.py:291
  107.5 3.0 %fusion.4 = f32[2,2,2,4,8,1280]{5,4,3,2,1,0:T(8,128)S(1)} fusion(bf16[1,5120,1280]{2,1,0:T(8,128)(2,1)} %param.7, bf16[2,2,2,4,8,1280]{5,4,3,1,2,0:T(8,128)(2,1)S(1)} %get-tuple-element.64), kind=kOutput, calls=%fused_computation.12 | convolution fusion | flops 838860800 | bytes 5242880 | tf_op jit(solution)/shard_map/dot_general | solution.py:291
  110.6 3.0 %fusion.6 = f32[2,2,2,4,8,1280]{5,4,3,2,1,0:T(8,128)S(1)} fusion(bf16[1,5120,1280]{2,1,0:T(8,128)(2,1)} %param.7, bf16[4,2,2,2,2,8,1280]{6,5,0,4,3,2,1:T(8,128)(2,1)S(1)} %bitcast.329, s32[]{:T(128)S(6)} %select_n.95), kind=kOutput, calls=%fused_computation.14 | convolution fusion | flops 838860800 | bytes 5242884 | tf_op jit(solution)/shard_map/dot_general | solution.py:291
  118.0 2.7 %collective-permute-start.31 = (bf16[2,2,4,8,1280]{4,3,2,1,0:T(8,128)(2,1)S(1)}, bf16[2,2,4,8,1280]{4,3,2,1,0:T(8,128)(2,1)S(1)}, u32[]{:S(2)}, u32[]{:S(2)}) collective-permute-start(bf16[2,2,4,8,1280]{4,3,2,1,0:T(8,128)(2,1)S(1)} %get-tuple-element.54), channel_id=1, source_target_pairs={{0,3},{1,2},{2,1},{3,0},{4,7},{5,6},{6,5},{7,4},{8,11},{9,10},{10,... | collective-permute-start | bytes 983048 | tf_op jit(solution)/shard_map/ppermute | solution.py:303
  121.3 6.2 %collective-permute-done.20 = bf16[2,2,2,4,8,1280]{5,4,3,2,1,0:T(8,128)(2,1)S(1)} collective-permute-done((bf16[2,2,2,4,8,1280]{5,4,3,2,1,0:T(8,128)(2,1)S(1)}, bf16[2,2,2,4,8,1280]{5,4,3,2,1,0:T(8,128)(2,1)S(1)}, u32[]{:S(2)}, u32[]{:S(2)}) %collective-permute-start.20) | collective-permute-done | bytes 655392 | tf_op jit(solution)/shard_map/ppermute | solution.py:303
  131.9 2.7 %collective-permute-start.26 = (bf16[2,4,8,1280]{3,2,1,0:T(8,128)(2,1)S(1)}, bf16[2,4,8,1280]{3,2,1,0:T(8,128)(2,1)S(1)}, u32[]{:S(2)}, u32[]{:S(2)}) collective-permute-start(bf16[2,4,8,1280]{3,2,1,0:T(8,128)(2,1)S(1)} %get-tuple-element.72), channel_id=1, source_target_pairs={{0,3},{1,2},{2,1},{3,0},{4,7},{5,6},{6,5},{7,4},{8,11},{9,10},{10,... | collective-permute-start | bytes 491528 | tf_op jit(solution)/shard_map/ppermute | solution.py:303
  141.4 2.7 %collective-permute-start.23 = (bf16[4,8,1280]{2,1,0:T(8,128)(2,1)S(1)}, bf16[4,8,1280]{2,1,0:T(8,128)(2,1)S(1)}, u32[]{:S(2)}, u32[]{:S(2)}) collective-permute-start(bf16[4,8,1280]{2,1,0:T(8,128)(2,1)S(1)} %fusion.69), channel_id=1, source_target_pairs={{0,3},{1,2},{2,1},{3,0},{4,7},{5,6},{6,5},{7,4},{8,11},{9,10},{10,... | collective-permute-start | bytes 245768 | tf_op jit(solution)/shard_map/ppermute | solution.py:303
  144.3 2.3 %collective-permute-start.38 = (bf16[2,8,2560]{2,1,0:T(8,128)(2,1)S(1)}, bf16[2,8,2560]{2,1,0:T(8,128)(2,1)S(1)}, u32[]{:S(2)}, u32[]{:S(2)}) collective-permute-start(bf16[2,8,2560]{2,1,0:T(8,128)(2,1)S(1)} %fusion.64), channel_id=1, source_target_pairs={{0,48},{1,49},{2,50},{3,51},{4,52},{5,53},{6,54},{7,55},{8,56},{9,... | collective-permute-start | bytes 245768 | tf_op jit(solution)/shard_map/ppermute | solution.py:28
  147.5 2.5 %collective-permute-done.38 = bf16[2,8,2560]{2,1,0:T(8,128)(2,1)S(1)} collective-permute-done((bf16[2,8,2560]{2,1,0:T(8,128)(2,1)S(1)}, bf16[2,8,2560]{2,1,0:T(8,128)(2,1)S(1)}, u32[]{:S(2)}, u32[]{:S(2)}) %collective-permute-start.38) | collective-permute-done | bytes 81952 | tf_op jit(solution)/shard_map/ppermute | solution.py:28
  151.8 2.3 %collective-permute-start.29 = (bf16[8,2560]{1,0:T(8,128)(2,1)S(1)}, bf16[8,2560]{1,0:T(8,128)(2,1)S(1)}, u32[]{:S(2)}, u32[]{:S(2)}) collective-permute-start(bf16[8,2560]{1,0:T(8,128)(2,1)S(1)} %fusion.87), channel_id=1, source_target_pairs={{0,48},{1,49},{2,50},{3,51},{4,52},{5,53},{6,54},{7,55},{8,56},{9,... | collective-permute-start | bytes 122888 | tf_op jit(solution)/shard_map/ppermute | solution.py:28
  154.1 3.0 %collective-permute-done.29 = bf16[8,2560]{1,0:T(8,128)(2,1)S(1)} collective-permute-done((bf16[8,2560]{1,0:T(8,128)(2,1)S(1)}, bf16[8,2560]{1,0:T(8,128)(2,1)S(1)}, u32[]{:S(2)}, u32[]{:S(2)}) %collective-permute-start.29) | collective-permute-done | bytes 40992 | tf_op jit(solution)/shard_map/ppermute | solution.py:28
  158.4 5.9 %all-to-all-start = ((bf16[16,8,5120]{2,1,0:T(8,128)(2,1)}), bf16[16,8,5120]{2,1,0:T(8,128)(2,1)S(1)}, u32[]{:S(2)}, u32[]{:S(2)}) async-start(bf16[16,8,5120]{2,1,0:T(8,128)(2,1)} %shard_map.73), calls=%async_computation | async-start | bytes 2621440 | tf_op jit(solution)/shard_map/all_to_all | solution.py:418
  169.3 9.5 %all-to-all-done = bf16[16,8,5120]{2,1,0:T(8,128)(2,1)S(1)} async-done(((bf16[16,8,5120]{2,1,0:T(8,128)(2,1)}), bf16[16,8,5120]{2,1,0:T(8,128)(2,1)S(1)}, u32[]{:S(2)}, u32[]{:S(2)}) %all-to-all-start) | async-done | bytes 1310752 | tf_op jit(solution)/shard_map/all_to_all | solution.py:418
  (179 shorter events, 71.3 us)
Async XLA Ops:
  1.8 20.3 %collective-permute-start = (bf16[64,5120]{1,0:T(8,128)(2,1)S(1)}, bf16[64,5120]{1,0:T(8,128)(2,1)S(1)}, u32[]{:S(2)}, u32[]{:S(2)}) collective-permute-start(bf16[64,5120]{1,0:T(8,128)(2,1)S(1)} %dynamic-slice_bitcast_fusion.6), channel_id=1, source_target_pairs={{0,16},{1,17},{2,18},{3,19},{4,20},{5,21},{6,22},{7,23},{8,24},{9,... | collective-permute-start | bytes 1966088 | tf_op jit(solution)/shard_map/ppermute | solution.py:28
  3.5 18.6 %collective-permute-start.1 = (bf16[64,5120]{1,0:T(8,128)(2,1)S(1)}, bf16[64,5120]{1,0:T(8,128)(2,1)S(1)}, u32[]{:S(2)}, u32[]{:S(2)}) collective-permute-start(bf16[64,5120]{1,0:T(8,128)(2,1)S(1)} %dynamic-slice_bitcast_fusion.6), channel_id=1, source_target_pairs={{0,48},{1,49},{2,50},{3,51},{4,52},{5,53},{6,54},{7,55},{8,56},{9,... | collective-permute-start | bytes 1966088 | tf_op jit(solution)/shard_map/ppermute | solution.py:28
  7.0 15.0 %collective-permute-start.2 = (s32[132]{0:T(256)S(1)}, s32[132]{0:T(256)S(1)}, u32[]{:S(2)}, u32[]{:S(2)}) collective-permute-start(s32[132]{0:T(256)S(1)} %constant_dynamic-update-slice_fusion), channel_id=1, source_target_pairs={{0,16},{16,0},{32,48},{48,32},{1,17},{17,1},{33,49},{49,33},{2,18}... | collective-permute-start | bytes 1592 | tf_op jit(solution)/shard_map/ppermute | solution.py:60
  7.7 14.4 %collective-permute-start.3 = (s32[132]{0:T(256)S(1)}, s32[132]{0:T(256)S(1)}, u32[]{:S(2)}, u32[]{:S(2)}) collective-permute-start(s32[132]{0:T(256)S(1)} %constant_dynamic-update-slice_fusion), channel_id=1, source_target_pairs={{0,32},{16,48},{32,0},{48,16},{1,33},{17,49},{33,1},{49,17},{2,34}... | collective-permute-start | bytes 1592 | tf_op jit(solution)/shard_map/ppermute | solution.py:60
  9.6 12.5 %collective-permute-start.4 = (s32[132]{0:T(256)S(1)}, s32[132]{0:T(256)S(1)}, u32[]{:S(2)}, u32[]{:S(2)}) collective-permute-start(s32[132]{0:T(256)S(1)} %constant_dynamic-update-slice_fusion), channel_id=1, source_target_pairs={{0,48},{16,32},{32,16},{48,0},{1,49},{17,33},{33,17},{49,1},{2,50}... | collective-permute-start | bytes 1592 | tf_op jit(solution)/shard_map/ppermute | solution.py:60
  22.1 10.7 %collective-permute-start.5 = (bf16[64,5120]{1,0:T(8,128)(2,1)S(1)}, bf16[64,5120]{1,0:T(8,128)(2,1)S(1)}, u32[]{:S(2)}, u32[]{:S(2)}) collective-permute-start(bf16[64,5120]{1,0:T(8,128)(2,1)S(1)} %collective-permute-done.1.refs_1_), channel_id=1, source_target_pairs={{0,16},{1,17},{2,18},{3,19},{4,20},{5,21},{6,22},{7,23},{8,24},{9,... | collective-permute-start | bytes 1966088 | tf_op jit(solution)/shard_map/ppermute | solution.py:28
  22.2 11.9 %collective-permute-start.7 = (bf16[64,5120]{1,0:T(8,128)(2,1)S(1)}, bf16[64,5120]{1,0:T(8,128)(2,1)S(1)}, u32[]{:S(2)}, u32[]{:S(2)}) collective-permute-start(bf16[64,5120]{1,0:T(8,128)(2,1)S(1)} %collective-permute-done.1.refs_1_), channel_id=1, source_target_pairs={{0,12},{1,13},{2,14},{3,15},{4,8},{5,9},{6,10},{7,11},{8,4},{9,5},... | collective-permute-start | bytes 1966088 | tf_op jit(solution)/shard_map/ppermute | solution.py:28
  25.0 10.6 %collective-permute-start.6 = (bf16[64,5120]{1,0:T(8,128)(2,1)S(1)}, bf16[64,5120]{1,0:T(8,128)(2,1)S(1)}, u32[]{:S(2)}, u32[]{:S(2)}) collective-permute-start(bf16[64,5120]{1,0:T(8,128)(2,1)S(1)} %collective-permute-done.refs_0_), channel_id=1, source_target_pairs={{0,4},{1,5},{2,6},{3,7},{4,0},{5,1},{6,2},{7,3},{8,12},{9,13},{10,... | collective-permute-start | bytes 1966088 | tf_op jit(solution)/shard_map/ppermute | solution.py:28
  35.7 8.2 %collective-permute-start.8 = (bf16[32,5120]{1,0:T(8,128)(2,1)S(1)}, bf16[32,5120]{1,0:T(8,128)(2,1)S(1)}, u32[]{:S(2)}, u32[]{:S(2)}) collective-permute-start(bf16[32,5120]{1,0:T(8,128)(2,1)S(1)} %get-tuple-element.77), channel_id=1, source_target_pairs={{0,4},{1,5},{2,6},{3,7},{4,0},{5,1},{6,2},{7,3},{8,12},{9,13},{10,... | collective-permute-start | bytes 983048 | tf_op jit(solution)/shard_map/ppermute | solution.py:28
  36.0 8.3 %collective-permute-start.9 = (bf16[32,5120]{1,0:T(8,128)(2,1)S(1)}, bf16[32,5120]{1,0:T(8,128)(2,1)S(1)}, u32[]{:S(2)}, u32[]{:S(2)}) collective-permute-start(bf16[32,5120]{1,0:T(8,128)(2,1)S(1)} %get-tuple-element.76), channel_id=1, source_target_pairs={{0,12},{1,13},{2,14},{3,15},{4,8},{5,9},{6,10},{7,11},{8,4},{9,5},... | collective-permute-start | bytes 983048 | tf_op jit(solution)/shard_map/ppermute | solution.py:28
  56.7 6.6 %collective-permute-start.11 = (f32[6,512]{1,0:T(8,128)S(1)}, f32[6,512]{1,0:T(8,128)S(1)}, u32[]{:S(2)}, u32[]{:S(2)}) collective-permute-start(f32[6,512]{1,0:T(8,128)S(1)} %stack.113), channel_id=1, source_target_pairs={{0,1},{1,0},{2,3},{3,2},{4,5},{5,4},{6,7},{7,6},{8,9},{9,8},{10,11... | collective-permute-start | bytes 36872 | tf_op jit(solution)/shard_map/ppermute | solution.py:60
  99.4 14.3 %collective-permute-start.34 = (bf16[2,2,2,4,8,1280]{5,4,3,2,1,0:T(8,128)(2,1)}, bf16[2,2,2,4,8,1280]{5,4,3,2,1,0:T(8,128)(2,1)S(1)}, u32[]{:S(2)}, u32[]{:S(2)}) collective-permute-start(bf16[2,2,2,4,8,1280]{5,4,3,2,1,0:T(8,128)(2,1)} %bitcast.367), channel_id=1, source_target_pairs={{0,3},{1,2},{2,1},{3,0},{4,7},{5,6},{6,5},{7,4},{8,11},{9,10},{10,... | collective-permute-start | bytes 1966088 | tf_op jit(solution)/shard_map/ppermute | solution.py:303
  102.5 15.4 %collective-permute-start.30 = (bf16[2,2,2,4,8,1280]{5,4,3,2,1,0:T(8,128)(2,1)S(1)}, bf16[2,2,2,4,8,1280]{5,4,3,2,1,0:T(8,128)(2,1)S(1)}, u32[]{:S(2)}, u32[]{:S(2)}) collective-permute-start(bf16[2,2,2,4,8,1280]{5,4,3,2,1,0:T(8,128)(2,1)S(1)} %bitcast.319), channel_id=1, source_target_pairs={{0,1},{1,0},{2,3},{3,2},{4,5},{5,4},{6,7},{7,6},{8,9},{9,8},{10,11... | collective-permute-start | bytes 1966088 | tf_op jit(solution)/shard_map/ppermute | solution.py:303
  105.8 14.9 %collective-permute-start.24 = (bf16[2,2,2,4,8,1280]{5,4,3,2,1,0:T(8,128)(2,1)S(1)}, bf16[2,2,2,4,8,1280]{5,4,3,2,1,0:T(8,128)(2,1)S(1)}, u32[]{:S(2)}, u32[]{:S(2)}) collective-permute-start(bf16[2,2,2,4,8,1280]{5,4,3,2,1,0:T(8,128)(2,1)S(1)} %bitcast.318), channel_id=1, source_target_pairs={{0,12},{4,8},{8,4},{12,0},{1,13},{5,9},{9,5},{13,1},{2,14},{6,10},... | collective-permute-start | bytes 1966088 | tf_op jit(solution)/shard_map/ppermute | solution.py:303
  110.5 17.0 %collective-permute-start.20 = (bf16[2,2,2,4,8,1280]{5,4,3,2,1,0:T(8,128)(2,1)S(1)}, bf16[2,2,2,4,8,1280]{5,4,3,2,1,0:T(8,128)(2,1)S(1)}, u32[]{:S(2)}, u32[]{:S(2)}) collective-permute-start(bf16[2,2,2,4,8,1280]{5,4,3,2,1,0:T(8,128)(2,1)S(1)} %bitcast.317), channel_id=1, source_target_pairs={{0,4},{4,0},{8,12},{12,8},{1,5},{5,1},{9,13},{13,9},{2,6},{6,2},{1... | collective-permute-start | bytes 1966088 | tf_op jit(solution)/shard_map/ppermute | solution.py:303
  113.8 15.5 %collective-permute-start.35 = (bf16[2,2,4,8,1280]{4,3,2,1,0:T(8,128)(2,1)S(1)}, bf16[2,2,4,8,1280]{4,3,2,1,0:T(8,128)(2,1)S(1)}, u32[]{:S(2)}, u32[]{:S(2)}) collective-permute-start(bf16[2,2,4,8,1280]{4,3,2,1,0:T(8,128)(2,1)S(1)} %get-tuple-element.52), channel_id=1, source_target_pairs={{0,1},{1,0},{2,3},{3,2},{4,5},{5,4},{6,7},{7,6},{8,9},{9,8},{10,11... | collective-permute-start | bytes 983048 | tf_op jit(solution)/shard_map/ppermute | solution.py:303
  118.0 13.1 %collective-permute-start.31 = (bf16[2,2,4,8,1280]{4,3,2,1,0:T(8,128)(2,1)S(1)}, bf16[2,2,4,8,1280]{4,3,2,1,0:T(8,128)(2,1)S(1)}, u32[]{:S(2)}, u32[]{:S(2)}) collective-permute-start(bf16[2,2,4,8,1280]{4,3,2,1,0:T(8,128)(2,1)S(1)} %get-tuple-element.54), channel_id=1, source_target_pairs={{0,3},{1,2},{2,1},{3,0},{4,7},{5,6},{6,5},{7,4},{8,11},{9,10},{10,... | collective-permute-start | bytes 983048 | tf_op jit(solution)/shard_map/ppermute | solution.py:303
  120.8 11.0 %collective-permute-start.25 = (bf16[2,2,4,8,1280]{4,3,2,1,0:T(8,128)(2,1)S(1)}, bf16[2,2,4,8,1280]{4,3,2,1,0:T(8,128)(2,1)S(1)}, u32[]{:S(2)}, u32[]{:S(2)}) collective-permute-start(bf16[2,2,4,8,1280]{4,3,2,1,0:T(8,128)(2,1)S(1)} %get-tuple-element.56), channel_id=1, source_target_pairs={{0,4},{4,0},{8,12},{12,8},{1,5},{5,1},{9,13},{13,9},{2,6},{6,2},{1... | collective-permute-start | bytes 983048 | tf_op jit(solution)/shard_map/ppermute | solution.py:303
  127.6 8.4 %collective-permute-start.21 = (bf16[2,2,4,8,1280]{4,3,2,1,0:T(8,128)(2,1)S(1)}, bf16[2,2,4,8,1280]{4,3,2,1,0:T(8,128)(2,1)S(1)}, u32[]{:S(2)}, u32[]{:S(2)}) collective-permute-start(bf16[2,2,4,8,1280]{4,3,2,1,0:T(8,128)(2,1)S(1)} %get-tuple-element.58), channel_id=1, source_target_pairs={{0,12},{4,8},{8,4},{12,0},{1,13},{5,9},{9,5},{13,1},{2,14},{6,10},... | collective-permute-start | bytes 983048 | tf_op jit(solution)/shard_map/ppermute | solution.py:303
  129.3 8.5 %collective-permute-start.36 = (bf16[2,4,8,1280]{3,2,1,0:T(8,128)(2,1)S(1)}, bf16[2,4,8,1280]{3,2,1,0:T(8,128)(2,1)S(1)}, u32[]{:S(2)}, u32[]{:S(2)}) collective-permute-start(bf16[2,4,8,1280]{3,2,1,0:T(8,128)(2,1)S(1)} %get-tuple-element.68), channel_id=1, source_target_pairs={{0,12},{4,8},{8,4},{12,0},{1,13},{5,9},{9,5},{13,1},{2,14},{6,10},... | collective-permute-start | bytes 491528 | tf_op jit(solution)/shard_map/ppermute | solution.py:303
  131.1 6.8 %collective-permute-start.32 = (bf16[2,4,8,1280]{3,2,1,0:T(8,128)(2,1)S(1)}, bf16[2,4,8,1280]{3,2,1,0:T(8,128)(2,1)S(1)}, u32[]{:S(2)}, u32[]{:S(2)}) collective-permute-start(bf16[2,4,8,1280]{3,2,1,0:T(8,128)(2,1)S(1)} %get-tuple-element.70), channel_id=1, source_target_pairs={{0,4},{4,0},{8,12},{12,8},{1,5},{5,1},{9,13},{13,9},{2,6},{6,2},{1... | collective-permute-start | bytes 491528 | tf_op jit(solution)/shard_map/ppermute | solution.py:303
  131.9 7.8 %collective-permute-start.26 = (bf16[2,4,8,1280]{3,2,1,0:T(8,128)(2,1)S(1)}, bf16[2,4,8,1280]{3,2,1,0:T(8,128)(2,1)S(1)}, u32[]{:S(2)}, u32[]{:S(2)}) collective-permute-start(bf16[2,4,8,1280]{3,2,1,0:T(8,128)(2,1)S(1)} %get-tuple-element.72), channel_id=1, source_target_pairs={{0,3},{1,2},{2,1},{3,0},{4,7},{5,6},{6,5},{7,4},{8,11},{9,10},{10,... | collective-permute-start | bytes 491528 | tf_op jit(solution)/shard_map/ppermute | solution.py:303
  139.7 6.8 %collective-permute-start.27 = (bf16[4,8,1280]{2,1,0:T(8,128)(2,1)S(1)}, bf16[4,8,1280]{2,1,0:T(8,128)(2,1)S(1)}, u32[]{:S(2)}, u32[]{:S(2)}) collective-permute-start(bf16[4,8,1280]{2,1,0:T(8,128)(2,1)S(1)} %fusion.70), channel_id=1, source_target_pairs={{0,1},{1,0},{2,3},{3,2},{4,5},{5,4},{6,7},{7,6},{8,9},{9,8},{10,11... | collective-permute-start | bytes 245768 | tf_op jit(solution)/shard_map/ppermute | solution.py:303
  158.4 20.4 %all-to-all-start = ((bf16[16,8,5120]{2,1,0:T(8,128)(2,1)}), bf16[16,8,5120]{2,1,0:T(8,128)(2,1)S(1)}, u32[]{:S(2)}, u32[]{:S(2)}) async-start(bf16[16,8,5120]{2,1,0:T(8,128)(2,1)} %shard_map.73), calls=%async_computation | async-start | bytes 2621440 | tf_op jit(solution)/shard_map/all_to_all | solution.py:418
  (21 other events, 108.4 us)

commit v3 on v2

--- a/solution.py
+++ b/solution.py
@@ -89,11 +89,12 @@
 CHUNKS = 10
 
 
-def make_kernel(count, loads, stores):
+def make_kernel(count, streamed, loads, stores):
     def kernel(*refs):
         sources = refs[:count]
         gain_ref, head_ref = refs[count : count + 2]
-        out_ref, held_head, rows, sums, total, block, head_sems, sems = refs[-8:]
+        out_ref, rows, sums, total, block, sems = refs[len(refs) - 6 :] if not streamed else refs[-8:-2]
+        held_head, head_sems = refs[-2:] if streamed else (head_ref, None)
         width = rows.shape[1]
         deep = width // CHUNKS
         held = parity() * 64
@@ -103,7 +104,7 @@
         shift |= {"p held": p_first + held, "q held": q_first + held}
         shift |= {"p other": p_first + 64 - held, "q other": q_first + 64 - held}
         fetches = []
-        for c in range(CHUNKS):
+        for c in range(CHUNKS if streamed else 0):
             piece = pl.ds(c * deep, deep)
             fetches.append(pltpu.make_async_copy(head_ref.at[piece], held_head.at[piece], head_sems.at[c]))
         copies = []
@@ -140,8 +141,8 @@
                 rows[piece, c : c + TILE] = (states * inverse * gain_ref[:, c : c + TILE]).astype(jnp.bfloat16)
 
         for c in range(0, CHUNKS, 2):
-            fetches[c].wait()
-            fetches[c + 1].wait()
+            for copy in fetches[c : c + 2]:
+                copy.wait()
             columns = slice(c * deep, (c + 2) * deep)
             part = jnp.dot(rows[:, columns], held_head[columns, :], preferred_element_type=jnp.float32)
             if c == 0:
@@ -180,25 +181,25 @@
     anywhere = pl.BlockSpec(memory_space=pl.ANY)
     count = len(sources)
     rows = sum(piece[2] for piece in plan[0])
+    streamed = filled is None
     operands = [*sources, gain_row, matrix] + ([] if filled is None else [filled])
     return pl.pallas_call(
-        make_kernel(count, *plan),
+        make_kernel(count, streamed, *plan),
         out_shape=jax.ShapeDtypeStruct((tokens, voc), jnp.bfloat16),
         in_specs=[anywhere] * count
-        + [pl.BlockSpec(memory_space=pltpu.VMEM), anywhere]
+        + [pl.BlockSpec(memory_space=pltpu.VMEM), anywhere if streamed else pl.BlockSpec(memory_space=pltpu.VMEM)]
         + ([] if filled is None else [anywhere]),
         out_specs=anywhere,
         scratch_shapes=[
-            pltpu.VMEM((width, voc), jnp.bfloat16),
             pltpu.VMEM((rows, width), jnp.bfloat16),
             pltpu.VMEM((rows, TILE), jnp.float32),
             pltpu.VMEM((rows, voc), jnp.float32),
             pltpu.VMEM((rows, voc), jnp.bfloat16),
-            pltpu.SemaphoreType.DMA((CHUNKS,)),
-            pltpu.SemaphoreType.DMA((5,)),
-        ],
+            pltpu.SemaphoreType.DMA((4,)),
+        ]
+        + ([pltpu.VMEM((width, voc), jnp.bfloat16), pltpu.SemaphoreType.DMA((CHUNKS,))] if streamed else []),
         input_output_aliases={} if filled is None else {count + 2: 0},
-        compiler_params=pltpu.CompilerParams(vmem_limit_bytes=52 * 1024 * 1024),
+        compiler_params=pltpu.CompilerParams(vmem_limit_bytes=(52 if streamed else 8) * 1024 * 1024),
         cost_estimate=pl.CostEstimate(
             flops=2 * rows * width * voc, bytes_accessed=2 * width * (voc + rows), transcendentals=0
         ),
@@ -226,55 +227,6 @@
     return block.astype(jnp.bfloat16)
 
 
-def away_kernel(*refs):
-    sources, head_ref, outs = refs[:4], refs[4], refs[5:9]
-    held_head, blocks, results, head_sems, in_sems, out_sems = refs[9:]
-    deep = head_ref.shape[0] // 8
-    fetches, loads, stores = [], [], []
-    for q in range(4):
-        loads.append(pltpu.make_async_copy(sources[q], blocks.at[q], in_sems.at[q]))
-        for c in (2 * q, 2 * q + 1):
-            piece = pl.ds(c * deep, deep)
-            fetches.append(pltpu.make_async_copy(head_ref.at[piece], held_head.at[piece], head_sems.at[c]))
-    for copy in loads[:1] + fetches[:2] + loads[1:] + fetches[2:]:
-        copy.start()
-    for q in range(4):
-        loads[q].wait()
-        for c in (2 * q, 2 * q + 1):
-            fetches[c].wait()
-        columns = held_head[2 * q * deep : 2 * (q + 1) * deep, :]
-        out = lax.dot_general(blocks[q], columns, (((1,), (1,)), ((), ())), preferred_element_type=jnp.float32)
-        results[q] = narrow(out)
-        stores.append(pltpu.make_async_copy(results.at[q], outs[q], out_sems.at[q]))
-        stores[q].start()
-    for copy in stores:
-        copy.wait()
-
-
-def away_products(blocks, matrix):
-    width, voc = matrix.shape
-    rows, columns = blocks[0].shape[0], width // 4
-    anywhere = pl.BlockSpec(memory_space=pl.ANY)
-    return pl.pallas_call(
-        away_kernel,
-        out_shape=[jax.ShapeDtypeStruct((rows, columns), jnp.bfloat16)] * 4,
-        in_specs=[anywhere] * 5,
-        out_specs=[anywhere] * 4,
-        scratch_shapes=[
-            pltpu.VMEM((width, voc), jnp.bfloat16),
-            pltpu.VMEM((4, rows, voc), jnp.bfloat16),
-            pltpu.VMEM((4, rows, columns), jnp.bfloat16),
-            pltpu.SemaphoreType.DMA((8,)),
-            pltpu.SemaphoreType.DMA((4,)),
-            pltpu.SemaphoreType.DMA((4,)),
-        ],
-        compiler_params=pltpu.CompilerParams(vmem_limit_bytes=52 * 1024 * 1024),
-        cost_estimate=pl.CostEstimate(
-            flops=2 * rows * width * voc, bytes_accessed=2 * (width * voc + rows * (width + 4 * voc)), transcendentals=0
-        ),
-    )(*blocks, matrix)
-
-
 def sum_rows(grad_logits, matrix, later):
     voc = grad_logits.shape[1]
     width = matrix.shape[0] // 4
@@ -303,13 +255,13 @@
         return lax.ppermute(block, axis, [(i, i ^ step) for i in range(4)])
 
     away, stay = [], []
-    for order in orders:
+    for q, order in enumerate(orders):
         turned_rows = jnp.transpose(rows, [dims[name][0] for name in order] + [0, 5, 6])
         one, other = split(turned_rows, order[0])
-        away.append(one.reshape(-1, voc))
+        away.append(narrow(product(*tied(one), q)))
         stay.append(other)
-    shape = stay[0].shape[:-1] + (width,)
-    came = [swap(block.reshape(shape), order[0]) for block, order in zip(away_products(away, matrix), orders)]
+    *stay, away[3] = tied(*stay, away[3])
+    came = [swap(away[q], orders[q][0]) for q in range(4)]
     kept = [product(stay[q], q) for q in range(4)]
     came[0], later = tied(came[0], later)
     for stage in range(1, 4):

time: 182 us -> 165 us (0.907)
  Pallas kernels: 39.1 us -> 20.5 us
  waiting for transfers between devices: 43 us -> 50 us
  starting transfers between devices: 61 us -> 57.5 us
    pallas_call x5 -> x4, Pallas kernels: 37.8 us -> 19.2 us  [add_logits(): pl.pallas_call(make_kernel(count, streamed, *plan), out_shape=jax.ShapeDt...]
    ppermute x16, waiting for transfers between devices: 10.7 us -> 17.9 us  [swap(): return lax.ppermute(block, axis, [(i, i ^ step) for i in range(4)])]
    unnamed x11 -> x19, local copies, waits for them, and re-layouts: 3.51 us -> 7.65 us
    dynamic_slice x3 -> x0, local copies, waits for them, and re-layouts: 2.71 us -> none  [split(): away = lax.dynamic_index_in_dim(block, 1 - at, 0, keepdims=False)]
    ppermute x16, starting transfers between devices: 21.7 us -> 19.3 us  [swap(): return lax.ppermute(block, axis, [(i, i ^ step) for i in range(4)])]
    dot_general x4 -> x8, matrix products: 12 us -> 10.6 us  [product(): lax.dot_general(block.reshape(-1, voc), columns, (((1,), (1,)), ((), ()))...]
  transfers between devices with their start and end apart: 41 -> 41, of which waited for: 20 -> 25; matrix products, arithmetic and copies ran while one was open for 10% -> 8% of each run, Pallas kernels for 12% -> 10%
where the time goes in v3:
time: 165 us; the launch traced here: 164 us
  starting transfers between devices  57.5 us (35%)
  waiting for transfers between devices  50 us (30%)
  Pallas kernels  20.5 us (12%)
  local copies, waits for them, and re-layouts  11.9 us (7%)
  matrix products  10.6 us (6%)
  other arithmetic  8.05 us (5%)
  between operations  5.81 us (4%)
    ppermute x16, starting transfers between devices, swap(): return lax.ppermute(block, axis, [(i, i ^ step) for i in range(4)])  19.3 us
    pallas_call x4, Pallas kernels, add_logits(): pl.pallas_call(make_kernel(count, streamed, *plan), out_shape=jax.ShapeDt...  19.2 us
    ppermute x12, starting transfers between devices, ring(): lax.ppermute(block, axis, [(i, i ^ s) for i in range(4)])  18.1 us
    ppermute x16, waiting for transfers between devices, swap(): return lax.ppermute(block, axis, [(i, i ^ step) for i in range(4)])  17.9 us
    ppermute x11, starting transfers between devices, permute(): lax.ppermute(block, ALL, [(index(*p), index(*move(*p))) for p in places])  14.7 us
    dot_general x8, matrix products, product(): lax.dot_general(block.reshape(-1, voc), columns, (((1,), (1,)), ((), ()))...  10.6 us
    ppermute x12, waiting for transfers between devices, ring(): lax.ppermute(block, axis, [(i, i ^ s) for i in range(4)])  9.94 us
    ppermute x11, waiting for transfers between devices, permute(): lax.ppermute(block, ALL, [(index(*p), index(*move(*p))) for p in places])  9.88 us
  transfers between devices with their start and end apart: 41, of which 25 were waited for; matrix products, arithmetic and copies ran while one was open for 8% of the time, Pallas kernels for 10%

profile of v3, /device:TPU:0, one launch (start us, length us, event | category | flops | bytes accessed | tf_op | source)
XLA Modules:
  0.0 164.4 jit_solution(15196229180140769543)
XLA Ops:
  4.3 2.2 %collective-permute-start.1 = (bf16[64,5120]{1,0:T(8,128)(2,1)}, bf16[64,5120]{1,0:T(8,128)(2,1)S(1)}, u32[]{:S(2)}, u32[]{:S(2)}) collective-permute-start(bf16[64,5120]{1,0:T(8,128)(2,1)} %dynamic-slice_bitcast_fusion.8), channel_id=1, source_target_pairs={{0,48},{1,49},{2,50},{3,51},{4,52},{5,53},{6,54},{7,55},{8,56},{9,... | collective-permute-start | bytes 1966088 | tf_op jit(solution)/shard_map/ppermute | solution.py:28
  10.3 2.2 %collective-permute-start.4 = (s32[132]{0:T(256)S(1)}, s32[132]{0:T(256)S(1)}, u32[]{:S(2)}, u32[]{:S(2)}) collective-permute-start(s32[132]{0:T(256)S(1)} %constant_dynamic-update-slice_fusion), channel_id=1, source_target_pairs={{0,48},{16,32},{32,16},{48,0},{1,49},{17,33},{33,17},{49,1},{2,50}... | collective-permute-start | bytes 1592 | tf_op jit(solution)/shard_map/ppermute | solution.py:60
  13.2 8.5 %shard_map.68.refs_4_ = bf16[512,1280]{1,0:T(8,128)(2,1)S(1)} custom-call(bf16[128,5120]{1,0:T(8,128)(2,1)} %bitcast.345, f32[1,5120]{1,0:T(1,128)S(1)} %copy-done.2, bf16[5120,1280]{1,0:T(8,128)(2,1)} %bitcast.332), custom_call_target="tpu_custom_call" | custom-call | flops 1677721600 | bytes 14417920 | tf_op jit(solution)/shard_map/pallas_call | solution.py:186
  25.9 4.7 %copy-done = bf16[1,5120,1280]{2,1,0:T(8,128)(2,1)S(1)} copy-done((bf16[1,5120,1280]{2,1,0:T(8,128)(2,1)S(1)}, bf16[1,5120,1280]{2,1,0:T(8,128)(2,1)}, u32[]{:S(2)}) %copy-start) | copy-done | bytes 13107224
  30.6 3.6 %shard_map.69.refs_4_ = bf16[512,1280]{1,0:T(8,128)(2,1)S(1)} custom-call(bf16[64,5120]{1,0:T(8,128)(2,1)S(1)} %collective-permute-done.refs_0_, bf16[64,5120]{1,0:T(8,128)(2,1)S(1)} %collective-permute-done.1.refs_1_, f32[1,5120]{1,0:T(1,128)S(1)} %copy-done.2, bf16[5120,1280]{1,0:T(8,128)(2,1)S(1)} %bitcast.333, ...), custom_call_target="tpu_custom_call", output_to_operand_aliasing={{}: (4, {})} | custom-call | flops 1677721600 | bytes 14417920 | tf_op jit(solution)/shard_map/pallas_call | solution.py:186
  35.7 2.2 %collective-permute-start.9 = (bf16[32,5120]{1,0:T(8,128)(2,1)S(1)}, bf16[32,5120]{1,0:T(8,128)(2,1)S(1)}, u32[]{:S(2)}, u32[]{:S(2)}) collective-permute-start(bf16[32,5120]{1,0:T(8,128)(2,1)S(1)} %get-tuple-element.80), channel_id=1, source_target_pairs={{0,12},{1,13},{2,14},{3,15},{4,8},{5,9},{6,10},{7,11},{8,4},{9,5},... | collective-permute-start | bytes 983048 | tf_op jit(solution)/shard_map/ppermute | solution.py:28
  37.9 3.7 %shard_map.70.refs_5_ = bf16[512,1280]{1,0:T(8,128)(2,1)S(1)} custom-call(bf16[64,5120]{1,0:T(8,128)(2,1)S(1)} %collective-permute-done.6.refs_0_, bf16[64,5120]{1,0:T(8,128)(2,1)S(1)} %collective-permute-done.7.refs_1_, f32[1,5120]{1,0:T(1,128)S(1)} %copy-done.2, bf16[5120,1280]{1,0:T(8,128)(2,1)S(1)} %bitcast.334, ...), custom_call_target="tpu_custom_call", output_to_operand_aliasing={{}: (4, {})} | custom-call | flops 1677721600 | bytes 14417920 | tf_op jit(solution)/shard_map/pallas_call | solution.py:186
  44.1 3.4 %shard_map.71 = bf16[512,1280]{1,0:T(8,128)(2,1)S(1)} custom-call(bf16[64,5120]{1,0:T(8,128)(2,1)S(1)} %collective-permute-done.5.refs_0_, bf16[32,5120]{1,0:T(8,128)(2,1)S(1)} %collective-permute-done.8.refs_1_, bf16[32,5120]{1,0:T(8,128)(2,1)S(1)} %collective-permute-done.9.refs_2_, f32[1,5120]{1,0:T(1,128)S(1)} %copy-done.2, ...), custom_call_target="tpu_custom_call", output_to_operand_aliasing={{}: (5, {})} | custom-call | flops 1677721600 | bytes 14417920 | tf_op jit(solution)/shard_map/pallas_call | solution.py:186
  48.1 2.7 %collective-permute-done.10 = bf16[512,1280]{1,0:T(8,128)(2,1)S(1)} collective-permute-done((bf16[512,1280]{1,0:T(8,128)(2,1)S(1)}, bf16[512,1280]{1,0:T(8,128)(2,1)S(1)}, u32[]{:S(2)}, u32[]{:S(2)}) %collective-permute-start.10) | collective-permute-done | bytes 1310752 | tf_op jit(solution)/shard_map/ppermute | solution.py:338
  51.0 2.2 %fusion.27 = (f32[512]{0:T(512)S(1)}, f32[512]{0:T(512)S(1)}, f32[512]{0:T(512)S(1)}, f32[512]{0:T(512)S(1)}) fusion(bf16[512,1280]{1,0:T(8,128)(2,1)S(1)} %collective-permute-done.10, bf16[512,1280]{1,0:T(8,128)(2,1)S(1)} %shard_map.71, f32[512]{0:T(512)S(1)} %reduce_max.105, s32[512]{0:T(512)S(1)} %add_subtract_fusion, f32[512]{0:T(512)S(1)} %reduce_max.104), kind=kLoop, calls=%fused_computation.35 | loop fusion | flops 7862272 | bytes 2635776 | tf_op jit(solution)/shard_map/reduce_sum | solution.py:297
  53.2 4.1 %collective-permute-start.13 = (f32[6,512]{1,0:T(8,128)S(1)}, f32[6,512]{1,0:T(8,128)S(1)}, u32[]{:S(2)}, u32[]{:S(2)}) collective-permute-start(f32[6,512]{1,0:T(8,128)S(1)} %stack.113), channel_id=1, source_target_pairs={{0,3},{1,2},{2,1},{3,0},{4,7},{5,6},{6,5},{7,4},{8,11},{9,10},{10,... | collective-permute-start | bytes 36872 | tf_op jit(solution)/shard_map/ppermute | solution.py:60
  59.3 3.3 %collective-permute-done.12 = f32[6,512]{1,0:T(8,128)S(1)} collective-permute-done((f32[6,512]{1,0:T(8,128)S(1)}, f32[6,512]{1,0:T(8,128)S(1)}, u32[]{:S(2)}, u32[]{:S(2)}) %collective-permute-start.12) | collective-permute-done | bytes 12320 | tf_op jit(solution)/shard_map/ppermute | solution.py:60
  62.8 2.2 %collective-permute-start.16 = (f32[6,512]{1,0:T(8,128)S(1)}, f32[6,512]{1,0:T(8,128)S(1)}, u32[]{:S(2)}, u32[]{:S(2)}) collective-permute-start(f32[6,512]{1,0:T(8,128)S(1)} %get-tuple-element.113), channel_id=1, source_target_pairs={{0,12},{4,8},{8,4},{12,0},{1,13},{5,9},{9,5},{13,1},{2,14},{6,10},... | collective-permute-start | bytes 36872 | tf_op jit(solution)/shard_map/ppermute | solution.py:60
  67.8 2.4 %collective-permute-done.15 = f32[6,512]{1,0:T(8,128)S(1)} collective-permute-done((f32[6,512]{1,0:T(8,128)S(1)}, f32[6,512]{1,0:T(8,128)S(1)}, u32[]{:S(2)}, u32[]{:S(2)}) %collective-permute-start.15) | collective-permute-done | bytes 12320 | tf_op jit(solution)/shard_map/ppermute | solution.py:60
  75.4 2.1 %collective-permute-done.18 = f32[6,512]{1,0:T(8,128)S(1)} collective-permute-done((f32[6,512]{1,0:T(8,128)S(1)}, f32[6,512]{1,0:T(8,128)S(1)}, u32[]{:S(2)}, u32[]{:S(2)}) %collective-permute-start.18) | collective-permute-done | bytes 12320 | tf_op jit(solution)/shard_map/ppermute | solution.py:60
  80.7 3.1 %fusion.46 = bf16[2,2,2,4,8,1280]{5,4,3,2,1,0:T(8,128)(2,1)S(1)} fusion(bf16[1,5120,1280]{2,1,0:T(8,128)(2,1)} %param.7, bf16[2,2,2,4,8,1280]{5,4,2,1,0,3:T(8,128)(2,1)S(1)} %get-tuple-element.69), kind=kOutput, calls=%fused_computation.57 | convolution fusion | flops 839188480 | bytes 4587520 | tf_op jit(solution)/shard_map/dot_general | solution.py:243
  94.8 2.7 %collective-permute-start.34 = (bf16[2,2,2,4,8,1280]{5,4,3,2,1,0:T(8,128)(2,1)S(1)}, bf16[2,2,2,4,8,1280]{5,4,3,2,1,0:T(8,128)(2,1)S(1)}, u32[]{:S(2)}, u32[]{:S(2)}) collective-permute-start(bf16[2,2,2,4,8,1280]{5,4,3,2,1,0:T(8,128)(2,1)S(1)} %fusion.55), channel_id=1, source_target_pairs={{0,3},{1,2},{2,1},{3,0},{4,7},{5,6},{6,5},{7,4},{8,11},{9,10},{10,... | collective-permute-start | bytes 1966088 | tf_op jit(solution)/shard_map/ppermute | solution.py:255
  99.2 7.5 %collective-permute-done.24 = bf16[2,2,2,4,8,1280]{5,4,3,2,1,0:T(8,128)(2,1)S(1)} collective-permute-done((bf16[2,2,2,4,8,1280]{5,4,3,2,1,0:T(8,128)(2,1)S(1)}, bf16[2,2,2,4,8,1280]{5,4,3,2,1,0:T(8,128)(2,1)S(1)}, u32[]{:S(2)}, u32[]{:S(2)}) %collective-permute-start.24) | collective-permute-done | bytes 655392 | tf_op jit(solution)/shard_map/ppermute | solution.py:255
  108.2 3.8 %collective-permute-done.34 = bf16[2,2,2,4,8,1280]{5,4,3,2,1,0:T(8,128)(2,1)S(1)} collective-permute-done((bf16[2,2,2,4,8,1280]{5,4,3,2,1,0:T(8,128)(2,1)S(1)}, bf16[2,2,2,4,8,1280]{5,4,3,2,1,0:T(8,128)(2,1)S(1)}, u32[]{:S(2)}, u32[]{:S(2)}) %collective-permute-start.34) | collective-permute-done | bytes 655392 | tf_op jit(solution)/shard_map/ppermute | solution.py:255
  115.1 2.2 %collective-permute-start.26 = (bf16[2,4,8,1280]{3,2,1,0:T(8,128)(2,1)S(1)}, bf16[2,4,8,1280]{3,2,1,0:T(8,128)(2,1)S(1)}, u32[]{:S(2)}, u32[]{:S(2)}) collective-permute-start(bf16[2,4,8,1280]{3,2,1,0:T(8,128)(2,1)S(1)} %get-tuple-element.76), channel_id=1, source_target_pairs={{0,3},{1,2},{2,1},{3,0},{4,7},{5,6},{6,5},{7,4},{8,11},{9,10},{10,... | collective-permute-start | bytes 491528 | tf_op jit(solution)/shard_map/ppermute | solution.py:255
  117.8 2.3 %collective-permute-done.35 = bf16[2,2,4,8,1280]{4,3,2,1,0:T(8,128)(2,1)S(1)} collective-permute-done((bf16[2,2,4,8,1280]{4,3,2,1,0:T(8,128)(2,1)S(1)}, bf16[2,2,4,8,1280]{4,3,2,1,0:T(8,128)(2,1)S(1)}, u32[]{:S(2)}, u32[]{:S(2)}) %collective-permute-start.35) | collective-permute-done | bytes 327712 | tf_op jit(solution)/shard_map/ppermute | solution.py:255
  121.9 2.9 %collective-permute-start.23 = (bf16[4,8,1280]{2,1,0:T(8,128)(2,1)S(1)}, bf16[4,8,1280]{2,1,0:T(8,128)(2,1)S(1)}, u32[]{:S(2)}, u32[]{:S(2)}) collective-permute-start(bf16[4,8,1280]{2,1,0:T(8,128)(2,1)S(1)} %fusion.96), channel_id=1, source_target_pairs={{0,3},{1,2},{2,1},{3,0},{4,7},{5,6},{6,5},{7,4},{8,11},{9,10},{10,... | collective-permute-start | bytes 245768 | tf_op jit(solution)/shard_map/ppermute | solution.py:255
  142.5 5.1 %all-to-all-start = ((bf16[16,8,5120]{2,1,0:T(8,128)(2,1)}), bf16[16,8,5120]{2,1,0:T(8,128)(2,1)S(1)}, u32[]{:S(2)}, u32[]{:S(2)}) async-start(bf16[16,8,5120]{2,1,0:T(8,128)(2,1)} %shard_map.72), calls=%async_computation | async-start | bytes 2621440 | tf_op jit(solution)/shard_map/all_to_all | solution.py:370
  152.6 9.6 %all-to-all-done = bf16[16,8,5120]{2,1,0:T(8,128)(2,1)S(1)} async-done(((bf16[16,8,5120]{2,1,0:T(8,128)(2,1)}), bf16[16,8,5120]{2,1,0:T(8,128)(2,1)S(1)}, u32[]{:S(2)}, u32[]{:S(2)}) %all-to-all-start) | async-done | bytes 1310752 | tf_op jit(solution)/shard_map/all_to_all | solution.py:370
  (187 shorter events, 70.0 us)
Async XLA Ops:
  2.6 19.3 %collective-permute-start = (bf16[64,5120]{1,0:T(8,128)(2,1)}, bf16[64,5120]{1,0:T(8,128)(2,1)S(1)}, u32[]{:S(2)}, u32[]{:S(2)}) collective-permute-start(bf16[64,5120]{1,0:T(8,128)(2,1)} %dynamic-slice_bitcast_fusion.8), channel_id=1, source_target_pairs={{0,16},{1,17},{2,18},{3,19},{4,20},{5,21},{6,22},{7,23},{8,24},{9,... | collective-permute-start | bytes 1966088 | tf_op jit(solution)/shard_map/ppermute | solution.py:28
  4.3 17.6 %collective-permute-start.1 = (bf16[64,5120]{1,0:T(8,128)(2,1)}, bf16[64,5120]{1,0:T(8,128)(2,1)S(1)}, u32[]{:S(2)}, u32[]{:S(2)}) collective-permute-start(bf16[64,5120]{1,0:T(8,128)(2,1)} %dynamic-slice_bitcast_fusion.8), channel_id=1, source_target_pairs={{0,48},{1,49},{2,50},{3,51},{4,52},{5,53},{6,54},{7,55},{8,56},{9,... | collective-permute-start | bytes 1966088 | tf_op jit(solution)/shard_map/ppermute | solution.py:28
  7.8 14.0 %collective-permute-start.2 = (s32[132]{0:T(256)S(1)}, s32[132]{0:T(256)S(1)}, u32[]{:S(2)}, u32[]{:S(2)}) collective-permute-start(s32[132]{0:T(256)S(1)} %constant_dynamic-update-slice_fusion), channel_id=1, source_target_pairs={{0,16},{16,0},{32,48},{48,32},{1,17},{17,1},{33,49},{49,33},{2,18}... | collective-permute-start | bytes 1592 | tf_op jit(solution)/shard_map/ppermute | solution.py:60
  8.5 13.4 %collective-permute-start.3 = (s32[132]{0:T(256)S(1)}, s32[132]{0:T(256)S(1)}, u32[]{:S(2)}, u32[]{:S(2)}) collective-permute-start(s32[132]{0:T(256)S(1)} %constant_dynamic-update-slice_fusion), channel_id=1, source_target_pairs={{0,32},{16,48},{32,0},{48,16},{1,33},{17,49},{33,1},{49,17},{2,34}... | collective-permute-start | bytes 1592 | tf_op jit(solution)/shard_map/ppermute | solution.py:60
  10.3 11.6 %collective-permute-start.4 = (s32[132]{0:T(256)S(1)}, s32[132]{0:T(256)S(1)}, u32[]{:S(2)}, u32[]{:S(2)}) collective-permute-start(s32[132]{0:T(256)S(1)} %constant_dynamic-update-slice_fusion), channel_id=1, source_target_pairs={{0,48},{16,32},{32,16},{48,0},{1,49},{17,33},{33,17},{49,1},{2,50}... | collective-permute-start | bytes 1592 | tf_op jit(solution)/shard_map/ppermute | solution.py:60
  21.9 12.3 %collective-permute-start.5 = (bf16[64,5120]{1,0:T(8,128)(2,1)S(1)}, bf16[64,5120]{1,0:T(8,128)(2,1)S(1)}, u32[]{:S(2)}, u32[]{:S(2)}) collective-permute-start(bf16[64,5120]{1,0:T(8,128)(2,1)S(1)} %collective-permute-done.1.refs_1_), channel_id=1, source_target_pairs={{0,16},{1,17},{2,18},{3,19},{4,20},{5,21},{6,22},{7,23},{8,24},{9,... | collective-permute-start | bytes 1966088 | tf_op jit(solution)/shard_map/ppermute | solution.py:28
  22.3 11.9 %collective-permute-start.6 = (bf16[64,5120]{1,0:T(8,128)(2,1)S(1)}, bf16[64,5120]{1,0:T(8,128)(2,1)S(1)}, u32[]{:S(2)}, u32[]{:S(2)}) collective-permute-start(bf16[64,5120]{1,0:T(8,128)(2,1)S(1)} %collective-permute-done.refs_0_), channel_id=1, source_target_pairs={{0,4},{1,5},{2,6},{3,7},{4,0},{5,1},{6,2},{7,3},{8,12},{9,13},{10,... | collective-permute-start | bytes 1966088 | tf_op jit(solution)/shard_map/ppermute | solution.py:28
  23.8 11.8 %collective-permute-start.7 = (bf16[64,5120]{1,0:T(8,128)(2,1)S(1)}, bf16[64,5120]{1,0:T(8,128)(2,1)S(1)}, u32[]{:S(2)}, u32[]{:S(2)}) collective-permute-start(bf16[64,5120]{1,0:T(8,128)(2,1)S(1)} %collective-permute-done.1.refs_1_), channel_id=1, source_target_pairs={{0,12},{1,13},{2,14},{3,15},{4,8},{5,9},{6,10},{7,11},{8,4},{9,5},... | collective-permute-start | bytes 1966088 | tf_op jit(solution)/shard_map/ppermute | solution.py:28
  35.6 7.2 %collective-permute-start.8 = (bf16[32,5120]{1,0:T(8,128)(2,1)S(1)}, bf16[32,5120]{1,0:T(8,128)(2,1)S(1)}, u32[]{:S(2)}, u32[]{:S(2)}) collective-permute-start(bf16[32,5120]{1,0:T(8,128)(2,1)S(1)} %get-tuple-element.81), channel_id=1, source_target_pairs={{0,4},{1,5},{2,6},{3,7},{4,0},{5,1},{6,2},{7,3},{8,12},{9,13},{10,... | collective-permute-start | bytes 983048 | tf_op jit(solution)/shard_map/ppermute | solution.py:28
  35.7 8.4 %collective-permute-start.9 = (bf16[32,5120]{1,0:T(8,128)(2,1)S(1)}, bf16[32,5120]{1,0:T(8,128)(2,1)S(1)}, u32[]{:S(2)}, u32[]{:S(2)}) collective-permute-start(bf16[32,5120]{1,0:T(8,128)(2,1)S(1)} %get-tuple-element.80), channel_id=1, source_target_pairs={{0,12},{1,13},{2,14},{3,15},{4,8},{5,9},{6,10},{7,11},{8,4},{9,5},... | collective-permute-start | bytes 983048 | tf_op jit(solution)/shard_map/ppermute | solution.py:28
  53.2 6.0 %collective-permute-start.13 = (f32[6,512]{1,0:T(8,128)S(1)}, f32[6,512]{1,0:T(8,128)S(1)}, u32[]{:S(2)}, u32[]{:S(2)}) collective-permute-start(f32[6,512]{1,0:T(8,128)S(1)} %stack.113), channel_id=1, source_target_pairs={{0,3},{1,2},{2,1},{3,0},{4,7},{5,6},{6,5},{7,4},{8,11},{9,10},{10,... | collective-permute-start | bytes 36872 | tf_op jit(solution)/shard_map/ppermute | solution.py:60
  83.8 13.6 %collective-permute-start.20 = (bf16[2,2,2,4,8,1280]{5,4,3,2,1,0:T(8,128)(2,1)S(1)}, bf16[2,2,2,4,8,1280]{5,4,3,2,1,0:T(8,128)(2,1)S(1)}, u32[]{:S(2)}, u32[]{:S(2)}) collective-permute-start(bf16[2,2,2,4,8,1280]{5,4,3,2,1,0:T(8,128)(2,1)S(1)} %fusion.46), channel_id=1, source_target_pairs={{0,4},{4,0},{8,12},{12,8},{1,5},{5,1},{9,13},{13,9},{2,6},{6,2},{1... | collective-permute-start | bytes 1966088 | tf_op jit(solution)/shard_map/ppermute | solution.py:255
  89.5 17.2 %collective-permute-start.24 = (bf16[2,2,2,4,8,1280]{5,4,3,2,1,0:T(8,128)(2,1)S(1)}, bf16[2,2,2,4,8,1280]{5,4,3,2,1,0:T(8,128)(2,1)S(1)}, u32[]{:S(2)}, u32[]{:S(2)}) collective-permute-start(bf16[2,2,2,4,8,1280]{5,4,3,2,1,0:T(8,128)(2,1)S(1)} %fusion.49), channel_id=1, source_target_pairs={{0,12},{4,8},{8,4},{12,0},{1,13},{5,9},{9,5},{13,1},{2,14},{6,10},... | collective-permute-start | bytes 1966088 | tf_op jit(solution)/shard_map/ppermute | solution.py:255
  93.6 13.3 %collective-permute-start.30 = (bf16[2,2,2,4,8,1280]{5,4,3,2,1,0:T(8,128)(2,1)S(1)}, bf16[2,2,2,4,8,1280]{5,4,3,2,1,0:T(8,128)(2,1)S(1)}, u32[]{:S(2)}, u32[]{:S(2)}) collective-permute-start(bf16[2,2,2,4,8,1280]{5,4,3,2,1,0:T(8,128)(2,1)S(1)} %fusion.52), channel_id=1, source_target_pairs={{0,1},{1,0},{2,3},{3,2},{4,5},{5,4},{6,7},{7,6},{8,9},{9,8},{10,11... | collective-permute-start | bytes 1966088 | tf_op jit(solution)/shard_map/ppermute | solution.py:255
  94.8 17.2 %collective-permute-start.34 = (bf16[2,2,2,4,8,1280]{5,4,3,2,1,0:T(8,128)(2,1)S(1)}, bf16[2,2,2,4,8,1280]{5,4,3,2,1,0:T(8,128)(2,1)S(1)}, u32[]{:S(2)}, u32[]{:S(2)}) collective-permute-start(bf16[2,2,2,4,8,1280]{5,4,3,2,1,0:T(8,128)(2,1)S(1)} %fusion.55), channel_id=1, source_target_pairs={{0,3},{1,2},{2,1},{3,0},{4,7},{5,6},{6,5},{7,4},{8,11},{9,10},{10,... | collective-permute-start | bytes 1966088 | tf_op jit(solution)/shard_map/ppermute | solution.py:255
  97.6 15.9 %collective-permute-start.21 = (bf16[2,2,4,8,1280]{4,3,2,1,0:T(8,128)(2,1)S(1)}, bf16[2,2,4,8,1280]{4,3,2,1,0:T(8,128)(2,1)S(1)}, u32[]{:S(2)}, u32[]{:S(2)}) collective-permute-start(bf16[2,2,4,8,1280]{4,3,2,1,0:T(8,128)(2,1)S(1)} %get-tuple-element.60), channel_id=1, source_target_pairs={{0,12},{4,8},{8,4},{12,0},{1,13},{5,9},{9,5},{13,1},{2,14},{6,10},... | collective-permute-start | bytes 983048 | tf_op jit(solution)/shard_map/ppermute | solution.py:255
  106.8 8.2 %collective-permute-start.25 = (bf16[2,2,4,8,1280]{4,3,2,1,0:T(8,128)(2,1)S(1)}, bf16[2,2,4,8,1280]{4,3,2,1,0:T(8,128)(2,1)S(1)}, u32[]{:S(2)}, u32[]{:S(2)}) collective-permute-start(bf16[2,2,4,8,1280]{4,3,2,1,0:T(8,128)(2,1)S(1)} %get-tuple-element.58), channel_id=1, source_target_pairs={{0,4},{4,0},{8,12},{12,8},{1,5},{5,1},{9,13},{13,9},{2,6},{6,2},{1... | collective-permute-start | bytes 983048 | tf_op jit(solution)/shard_map/ppermute | solution.py:255
  107.0 10.2 %collective-permute-start.31 = (bf16[2,2,4,8,1280]{4,3,2,1,0:T(8,128)(2,1)S(1)}, bf16[2,2,4,8,1280]{4,3,2,1,0:T(8,128)(2,1)S(1)}, u32[]{:S(2)}, u32[]{:S(2)}) collective-permute-start(bf16[2,2,4,8,1280]{4,3,2,1,0:T(8,128)(2,1)S(1)} %get-tuple-element.56), channel_id=1, source_target_pairs={{0,3},{1,2},{2,1},{3,0},{4,7},{5,6},{6,5},{7,4},{8,11},{9,10},{10,... | collective-permute-start | bytes 983048 | tf_op jit(solution)/shard_map/ppermute | solution.py:255
  112.1 8.0 %collective-permute-start.35 = (bf16[2,2,4,8,1280]{4,3,2,1,0:T(8,128)(2,1)S(1)}, bf16[2,2,4,8,1280]{4,3,2,1,0:T(8,128)(2,1)S(1)}, u32[]{:S(2)}, u32[]{:S(2)}) collective-permute-start(bf16[2,2,4,8,1280]{4,3,2,1,0:T(8,128)(2,1)S(1)} %get-tuple-element.54), channel_id=1, source_target_pairs={{0,1},{1,0},{2,3},{3,2},{4,5},{5,4},{6,7},{7,6},{8,9},{9,8},{10,11... | collective-permute-start | bytes 983048 | tf_op jit(solution)/shard_map/ppermute | solution.py:255
  113.5 8.4 %collective-permute-start.22 = (bf16[2,4,8,1280]{3,2,1,0:T(8,128)(2,1)S(1)}, bf16[2,4,8,1280]{3,2,1,0:T(8,128)(2,1)S(1)}, u32[]{:S(2)}, u32[]{:S(2)}) collective-permute-start(bf16[2,4,8,1280]{3,2,1,0:T(8,128)(2,1)S(1)} %get-tuple-element.78), channel_id=1, source_target_pairs={{0,1},{1,0},{2,3},{3,2},{4,5},{5,4},{6,7},{7,6},{8,9},{9,8},{10,11... | collective-permute-start | bytes 491528 | tf_op jit(solution)/shard_map/ppermute | solution.py:255
  115.1 9.6 %collective-permute-start.26 = (bf16[2,4,8,1280]{3,2,1,0:T(8,128)(2,1)S(1)}, bf16[2,4,8,1280]{3,2,1,0:T(8,128)(2,1)S(1)}, u32[]{:S(2)}, u32[]{:S(2)}) collective-permute-start(bf16[2,4,8,1280]{3,2,1,0:T(8,128)(2,1)S(1)} %get-tuple-element.76), channel_id=1, source_target_pairs={{0,3},{1,2},{2,1},{3,0},{4,7},{5,6},{6,5},{7,4},{8,11},{9,10},{10,... | collective-permute-start | bytes 491528 | tf_op jit(solution)/shard_map/ppermute | solution.py:255
  117.3 7.5 %collective-permute-start.32 = (bf16[2,4,8,1280]{3,2,1,0:T(8,128)(2,1)S(1)}, bf16[2,4,8,1280]{3,2,1,0:T(8,128)(2,1)S(1)}, u32[]{:S(2)}, u32[]{:S(2)}) collective-permute-start(bf16[2,4,8,1280]{3,2,1,0:T(8,128)(2,1)S(1)} %get-tuple-element.74), channel_id=1, source_target_pairs={{0,4},{4,0},{8,12},{12,8},{1,5},{5,1},{9,13},{13,9},{2,6},{6,2},{1... | collective-permute-start | bytes 491528 | tf_op jit(solution)/shard_map/ppermute | solution.py:255
  120.2 6.6 %collective-permute-start.36 = (bf16[2,4,8,1280]{3,2,1,0:T(8,128)(2,1)S(1)}, bf16[2,4,8,1280]{3,2,1,0:T(8,128)(2,1)S(1)}, u32[]{:S(2)}, u32[]{:S(2)}) collective-permute-start(bf16[2,4,8,1280]{3,2,1,0:T(8,128)(2,1)S(1)} %get-tuple-element.72), channel_id=1, source_target_pairs={{0,12},{4,8},{8,4},{12,0},{1,13},{5,9},{9,5},{13,1},{2,14},{6,10},... | collective-permute-start | bytes 491528 | tf_op jit(solution)/shard_map/ppermute | solution.py:255
  142.5 19.6 %all-to-all-start = ((bf16[16,8,5120]{2,1,0:T(8,128)(2,1)}), bf16[16,8,5120]{2,1,0:T(8,128)(2,1)S(1)}, u32[]{:S(2)}, u32[]{:S(2)}) async-start(bf16[16,8,5120]{2,1,0:T(8,128)(2,1)} %shard_map.72), calls=%async_computation | async-start | bytes 2621440 | tf_op jit(solution)/shard_map/all_to_all | solution.py:370
  (25 other events, 157.8 us)

commit v4 on v3

--- a/solution.py
+++ b/solution.py
@@ -79,34 +79,25 @@
     far = swap_y(q, (1, 3))
     p_side, q_side = swap_u(p, 1), swap_u(q, 3)
     logits = add_logits((p, q), HELD_PLAN, gain_row, matrix, tokens, logits)
-    far, logits, p_side, q_side = tied(far, logits, p_side, q_side)
+    far, logits = tied(far, logits)
     far_sides = [swap_u(far[: half // 2], 1), swap_u(far[half // 2 :], 3)]
     logits = add_logits((p_side, q_side), OTHER_PLAN, gain_row, matrix, tokens, logits)
     logits = add_logits((far, *far_sides), FAR_PLAN, gain_row, matrix, tokens, logits)
     return logits, [ints[s] for s in (0, 1, 3, 2)]
 
 
-CHUNKS = 10
-
-
-def make_kernel(count, streamed, loads, stores):
+def make_kernel(count, loads, stores):
     def kernel(*refs):
         sources = refs[:count]
         gain_ref, head_ref = refs[count : count + 2]
-        out_ref, rows, sums, total, block, sems = refs[len(refs) - 6 :] if not streamed else refs[-8:-2]
-        held_head, head_sems = refs[-2:] if streamed else (head_ref, None)
+        out_ref, rows, sums, total, block, sems = refs[-6:]
         width = rows.shape[1]
-        deep = width // CHUNKS
         held = parity() * 64
         p_first = 128 * (NEAR + core() * (WRAP - NEAR))
         q_first = 128 * (NEAR + WRAP) - p_first
         shift = {"all": 0, "held": held, "other": 64 - held}
         shift |= {"p held": p_first + held, "q held": q_first + held}
         shift |= {"p other": p_first + 64 - held, "q other": q_first + 64 - held}
-        fetches = []
-        for c in range(CHUNKS if streamed else 0):
-            piece = pl.ds(c * deep, deep)
-            fetches.append(pltpu.make_async_copy(head_ref.at[piece], held_head.at[piece], head_sems.at[c]))
         copies = []
         for source, start, length, target, kind in loads:
             to = pl.multiple_of(shift[kind] + target, 16)
@@ -115,7 +106,7 @@
                     sources[source].at[pl.ds(start, length)], rows.at[pl.ds(to, length)], sems.at[len(copies)]
                 )
             )
-        for copy in copies + fetches:
+        for copy in copies:
             copy.start()
         for copy in copies:
             copy.wait()
@@ -140,14 +131,12 @@
                 states = rows[piece, c : c + TILE].astype(jnp.float32)
                 rows[piece, c : c + TILE] = (states * inverse * gain_ref[:, c : c + TILE]).astype(jnp.bfloat16)
 
-        for c in range(0, CHUNKS, 2):
-            for copy in fetches[c : c + 2]:
-                copy.wait()
-            columns = slice(c * deep, (c + 2) * deep)
-            part = jnp.dot(rows[:, columns], held_head[columns, :], preferred_element_type=jnp.float32)
+        depth = 1024
+        for c in range(0, width, depth):
+            part = jnp.dot(rows[:, c : c + depth], head_ref[c : c + depth, :], preferred_element_type=jnp.float32)
             if c == 0:
                 total[...] = part
-            elif c < CHUNKS - 2:
+            elif c + depth < width:
                 total[...] += part
             else:
                 block[...] = (total[...] + part).astype(jnp.bfloat16)
@@ -181,13 +170,12 @@
     anywhere = pl.BlockSpec(memory_space=pl.ANY)
     count = len(sources)
     rows = sum(piece[2] for piece in plan[0])
-    streamed = filled is None
     operands = [*sources, gain_row, matrix] + ([] if filled is None else [filled])
     return pl.pallas_call(
-        make_kernel(count, streamed, *plan),
+        make_kernel(count, *plan),
         out_shape=jax.ShapeDtypeStruct((tokens, voc), jnp.bfloat16),
         in_specs=[anywhere] * count
-        + [pl.BlockSpec(memory_space=pltpu.VMEM), anywhere if streamed else pl.BlockSpec(memory_space=pltpu.VMEM)]
+        + [pl.BlockSpec(memory_space=pltpu.VMEM)] * 2
         + ([] if filled is None else [anywhere]),
         out_specs=anywhere,
         scratch_shapes=[
@@ -196,10 +184,9 @@
             pltpu.VMEM((rows, voc), jnp.float32),
             pltpu.VMEM((rows, voc), jnp.bfloat16),
             pltpu.SemaphoreType.DMA((4,)),
-        ]
-        + ([pltpu.VMEM((width, voc), jnp.bfloat16), pltpu.SemaphoreType.DMA((CHUNKS,))] if streamed else []),
+        ],
         input_output_aliases={} if filled is None else {count + 2: 0},
-        compiler_params=pltpu.CompilerParams(vmem_limit_bytes=(52 if streamed else 8) * 1024 * 1024),
+        compiler_params=pltpu.CompilerParams(vmem_limit_bytes=8 * 1024 * 1024),
         cost_estimate=pl.CostEstimate(
             flops=2 * rows * width * voc, bytes_accessed=2 * width * (voc + rows), transcendentals=0
         ),
@@ -254,17 +241,21 @@
         axis, step = dims[name][2:]
         return lax.ppermute(block, axis, [(i, i ^ step) for i in range(4)])
 
-    away, stay = [], []
+    sent, stay = [], []
     for q, order in enumerate(orders):
         turned_rows = jnp.transpose(rows, [dims[name][0] for name in order] + [0, 5, 6])
         one, other = split(turned_rows, order[0])
-        away.append(narrow(product(*tied(one), q)))
-        stay.append(other)
-    *stay, away[3] = tied(*stay, away[3])
-    came = [swap(away[q], orders[q][0]) for q in range(4)]
-    kept = [product(stay[q], q) for q in range(4)]
+        sent.append(product(*tied(one), q))
+        stay.append(split(other, order[1]))
+    came = [swap(narrow(sent[q]), orders[q][0]) for q in range(4)]
     came[0], later = tied(came[0], later)
-    for stage in range(1, 4):
+    kept = []
+    for q, order in enumerate(orders):
+        pairs = zip(stay[q], split(came[q], order[1]))
+        one, other = [product(block, q) + wide(part) for block, part in pairs]
+        came[q] = swap(narrow(one), order[1])
+        kept.append(other)
+    for stage in range(2, 4):
         halves = [
             [k + wide(c) for k, c in zip(split(kept[q], orders[q][stage]), split(came[q], orders[q][stage]))]
             for q in range(4)

time: 165 us -> 163 us (0.988)
  matrix products: 10.6 us -> 16.2 us
  Pallas kernels: 20.5 us -> 15 us
  starting transfers between devices: 57.5 us -> 54.7 us
  local copies, waits for them, and re-layouts: 11.9 us -> 14.6 us
    ppermute x16, waiting for transfers between devices: 17.9 us -> 11.9 us  [swap(): return lax.ppermute(block, axis, [(i, i ^ step) for i in range(4)])]
    dot_general x8 -> x12, matrix products: 10.6 us -> 16.2 us  [product(): lax.dot_general(block.reshape(-1, voc), columns, (((1,), (1,)), ((), ()))...]
    pallas_call x4, Pallas kernels: 19.2 us -> 13.7 us  [add_logits(): pl.pallas_call(make_kernel(count, *plan), out_shape=jax.ShapeDtypeStruct(...]
    ppermute x11, waiting for transfers between devices: 9.88 us -> 13.7 us  [permute(): lax.ppermute(block, ALL, [(index(*p), index(*move(*p))) for p in places])]
    ppermute x16, starting transfers between devices: 19.3 us -> 15.9 us  [swap(): return lax.ppermute(block, axis, [(i, i ^ step) for i in range(4)])]
    unnamed x19 -> x29, local copies, waits for them, and re-layouts: 7.65 us -> 10.3 us
    ppermute x12, starting transfers between devices: 18.1 us -> 19.8 us  [ring(): lax.ppermute(block, axis, [(i, i ^ s) for i in range(4)])]
  transfers between devices with their start and end apart: 41 -> 41, of which waited for: 25 -> 20; matrix products, arithmetic and copies ran while one was open for 8% -> 11% of each run, Pallas kernels for 10% -> 6%
where the time goes in v4:
time: 163 us; the launch traced here: 162 us
  starting transfers between devices  54.7 us (34%)
  waiting for transfers between devices  48.6 us (30%)
  matrix products  16.2 us (10%)
  Pallas kernels  15 us (9%)
  local copies, waits for them, and re-layouts  14.6 us (9%)
  other arithmetic  7.58 us (5%)
  between operations  5.85 us (4%)
    ppermute x12, starting transfers between devices, ring(): lax.ppermute(block, axis, [(i, i ^ s) for i in range(4)])  19.8 us
    dot_general x12, matrix products, product(): lax.dot_general(block.reshape(-1, voc), columns, (((1,), (1,)), ((), ()))...  16.2 us
    ppermute x16, starting transfers between devices, swap(): return lax.ppermute(block, axis, [(i, i ^ step) for i in range(4)])  15.9 us
    ppermute x11, starting transfers between devices, permute(): lax.ppermute(block, ALL, [(index(*p), index(*move(*p))) for p in places])  15 us
    ppermute x11, waiting for transfers between devices, permute(): lax.ppermute(block, ALL, [(index(*p), index(*move(*p))) for p in places])  13.7 us
    pallas_call x4, Pallas kernels, add_logits(): pl.pallas_call(make_kernel(count, *plan), out_shape=jax.ShapeDtypeStruct(...  13.7 us
    ppermute x16, waiting for transfers between devices, swap(): return lax.ppermute(block, axis, [(i, i ^ step) for i in range(4)])  11.9 us
    ppermute x12, waiting for transfers between devices, ring(): lax.ppermute(block, axis, [(i, i ^ s) for i in range(4)])  10.6 us
  transfers between devices with their start and end apart: 41, of which 20 were waited for; matrix products, arithmetic and copies ran while one was open for 11% of the time, Pallas kernels for 6%

profile of v4, /device:TPU:0, one launch (start us, length us, event | category | flops | bytes accessed | tf_op | source)
XLA Modules:
  0.0 162.5 jit_solution(12141072542570785364)
XLA Ops:
  4.3 2.2 %collective-permute-start.1 = (bf16[64,5120]{1,0:T(8,128)(2,1)}, bf16[64,5120]{1,0:T(8,128)(2,1)S(1)}, u32[]{:S(2)}, u32[]{:S(2)}) collective-permute-start(bf16[64,5120]{1,0:T(8,128)(2,1)} %dynamic-slice_bitcast_fusion.4), channel_id=1, source_target_pairs={{0,48},{1,49},{2,50},{3,51},{4,52},{5,53},{6,54},{7,55},{8,56},{9,... | collective-permute-start | bytes 1966088 | tf_op jit(solution)/shard_map/ppermute | solution.py:28
  10.3 2.2 %collective-permute-start.4 = (s32[132]{0:T(256)S(1)}, s32[132]{0:T(256)S(1)}, u32[]{:S(2)}, u32[]{:S(2)}) collective-permute-start(s32[132]{0:T(256)S(1)} %constant_dynamic-update-slice_fusion), channel_id=1, source_target_pairs={{0,48},{16,32},{32,16},{48,0},{1,49},{17,33},{33,17},{49,1},{2,50}... | collective-permute-start | bytes 1592 | tf_op jit(solution)/shard_map/ppermute | solution.py:60
  12.5 4.7 %copy-done = bf16[1,5120,1280]{2,1,0:T(8,128)(2,1)S(1)} copy-done((bf16[1,5120,1280]{2,1,0:T(8,128)(2,1)S(1)}, bf16[1,5120,1280]{2,1,0:T(8,128)(2,1)}, u32[]{:S(2)}) %copy-start) | copy-done | bytes 13107224
  19.3 3.0 %shard_map.68.refs_4_ = bf16[512,1280]{1,0:T(8,128)(2,1)S(1)} custom-call(bf16[128,5120]{1,0:T(8,128)(2,1)S(1)} %bitcast.387, f32[1,5120]{1,0:T(1,128)S(1)} %copy-done.2, bf16[5120,1280]{1,0:T(8,128)(2,1)S(1)} %bitcast.379), custom_call_target="tpu_custom_call" | custom-call | flops 1677721600 | bytes 14417920 | tf_op jit(solution)/shard_map/pallas_call | solution.py:174
  22.4 2.8 %collective-permute-start.9 = (bf16[64,5120]{1,0:T(8,128)(2,1)S(1)}, bf16[64,5120]{1,0:T(8,128)(2,1)S(1)}, u32[]{:S(2)}, u32[]{:S(2)}) collective-permute-start(bf16[64,5120]{1,0:T(8,128)(2,1)S(1)} %collective-permute-done.1.refs_1_), channel_id=1, source_target_pairs={{0,12},{1,13},{2,14},{3,15},{4,8},{5,9},{6,10},{7,11},{8,4},{9,5},... | collective-permute-start | bytes 1966088 | tf_op jit(solution)/shard_map/ppermute | solution.py:28
  25.5 3.6 %shard_map.69.refs_4_ = bf16[512,1280]{1,0:T(8,128)(2,1)S(1)} custom-call(bf16[64,5120]{1,0:T(8,128)(2,1)S(1)} %collective-permute-done.refs_0_, bf16[64,5120]{1,0:T(8,128)(2,1)S(1)} %collective-permute-done.1.refs_1_, f32[1,5120]{1,0:T(1,128)S(1)} %copy-done.2, bf16[5120,1280]{1,0:T(8,128)(2,1)S(1)} %bitcast.380, ...), custom_call_target="tpu_custom_call", output_to_operand_aliasing={{}: (4, {})} | custom-call | flops 1677721600 | bytes 14417920 | tf_op jit(solution)/shard_map/pallas_call | solution.py:174
  29.1 3.9 %collective-permute-done.5.refs_0_ = bf16[64,5120]{1,0:T(8,128)(2,1)S(1)} collective-permute-done((bf16[64,5120]{1,0:T(8,128)(2,1)S(1)}, bf16[64,5120]{1,0:T(8,128)(2,1)S(1)}, u32[]{:S(2)}, u32[]{:S(2)}) %collective-permute-start.5) | collective-permute-done | bytes 655392 | tf_op jit(solution)/shard_map/ppermute | solution.py:28
  36.7 3.7 %shard_map.70.refs_5_ = bf16[512,1280]{1,0:T(8,128)(2,1)S(1)} custom-call(bf16[64,5120]{1,0:T(8,128)(2,1)S(1)} %collective-permute-done.8.refs_0_, bf16[64,5120]{1,0:T(8,128)(2,1)S(1)} %collective-permute-done.9.refs_1_, f32[1,5120]{1,0:T(1,128)S(1)} %copy-done.2, bf16[5120,1280]{1,0:T(8,128)(2,1)S(1)} %bitcast.383, ...), custom_call_target="tpu_custom_call", output_to_operand_aliasing={{}: (4, {})} | custom-call | flops 1677721600 | bytes 14417920 | tf_op jit(solution)/shard_map/pallas_call | solution.py:174
  40.5 2.4 %collective-permute-done.7.refs_2_ = bf16[32,5120]{1,0:T(8,128)(2,1)S(1)} collective-permute-done((bf16[32,5120]{1,0:T(8,128)(2,1)S(1)}, bf16[32,5120]{1,0:T(8,128)(2,1)S(1)}, u32[]{:S(2)}, u32[]{:S(2)}) %collective-permute-start.7) | collective-permute-done | bytes 327712 | tf_op jit(solution)/shard_map/ppermute | solution.py:28
  42.9 3.4 %shard_map.71 = bf16[512,1280]{1,0:T(8,128)(2,1)S(1)} custom-call(bf16[64,5120]{1,0:T(8,128)(2,1)S(1)} %collective-permute-done.5.refs_0_, bf16[32,5120]{1,0:T(8,128)(2,1)S(1)} %collective-permute-done.6.refs_1_, bf16[32,5120]{1,0:T(8,128)(2,1)S(1)} %collective-permute-done.7.refs_2_, f32[1,5120]{1,0:T(1,128)S(1)} %copy-done.2, ...), custom_call_target="tpu_custom_call", output_to_operand_aliasing={{}: (5, {})} | custom-call | flops 1677721600 | bytes 14417920 | tf_op jit(solution)/shard_map/pallas_call | solution.py:174
  46.9 2.7 %collective-permute-done.10 = bf16[512,1280]{1,0:T(8,128)(2,1)S(1)} collective-permute-done((bf16[512,1280]{1,0:T(8,128)(2,1)S(1)}, bf16[512,1280]{1,0:T(8,128)(2,1)S(1)}, u32[]{:S(2)}, u32[]{:S(2)}) %collective-permute-start.10) | collective-permute-done | bytes 1310752 | tf_op jit(solution)/shard_map/ppermute | solution.py:329
  54.0 3.6 %collective-permute-start.12 = (f32[6,512]{1,0:T(8,128)S(1)}, f32[6,512]{1,0:T(8,128)S(1)}, u32[]{:S(2)}, u32[]{:S(2)}) collective-permute-start(f32[6,512]{1,0:T(8,128)S(1)} %stack.113), channel_id=1, source_target_pairs={{0,2},{1,3},{2,0},{3,1},{4,6},{5,7},{6,4},{7,5},{8,10},{9,11},{10,... | collective-permute-start | bytes 36872 | tf_op jit(solution)/shard_map/ppermute | solution.py:60
  59.5 3.1 %collective-permute-done.13 = f32[6,512]{1,0:T(8,128)S(1)} collective-permute-done((f32[6,512]{1,0:T(8,128)S(1)}, f32[6,512]{1,0:T(8,128)S(1)}, u32[]{:S(2)}, u32[]{:S(2)}) %collective-permute-start.13) | collective-permute-done | bytes 12320 | tf_op jit(solution)/shard_map/ppermute | solution.py:60
  62.9 3.5 %collective-permute-start.15 = (f32[6,512]{1,0:T(8,128)S(1)}, f32[6,512]{1,0:T(8,128)S(1)}, u32[]{:S(2)}, u32[]{:S(2)}) collective-permute-start(f32[6,512]{1,0:T(8,128)S(1)} %get-tuple-element.91), channel_id=1, source_target_pairs={{0,8},{4,12},{8,0},{12,4},{1,9},{5,13},{9,1},{13,5},{2,10},{6,14},... | collective-permute-start | bytes 36872 | tf_op jit(solution)/shard_map/ppermute | solution.py:60
  68.4 3.0 %collective-permute-done.16 = f32[6,512]{1,0:T(8,128)S(1)} collective-permute-done((f32[6,512]{1,0:T(8,128)S(1)}, f32[6,512]{1,0:T(8,128)S(1)}, u32[]{:S(2)}, u32[]{:S(2)}) %collective-permute-start.16) | collective-permute-done | bytes 12320 | tf_op jit(solution)/shard_map/ppermute | solution.py:60
  71.8 2.7 %collective-permute-start.18 = (f32[6,512]{1,0:T(8,128)S(1)}, f32[6,512]{1,0:T(8,128)S(1)}, u32[]{:S(2)}, u32[]{:S(2)}) collective-permute-start(f32[6,512]{1,0:T(8,128)S(1)} %get-tuple-element.89), channel_id=1, source_target_pairs={{0,32},{16,48},{32,0},{48,16},{1,33},{17,49},{33,1},{49,17},{2,34}... | collective-permute-start | bytes 36872 | tf_op jit(solution)/shard_map/ppermute | solution.py:60
  77.1 2.4 %collective-permute-done.19 = f32[6,512]{1,0:T(8,128)S(1)} collective-permute-done((f32[6,512]{1,0:T(8,128)S(1)}, f32[6,512]{1,0:T(8,128)S(1)}, u32[]{:S(2)}, u32[]{:S(2)}) %collective-permute-start.19) | collective-permute-done | bytes 12320 | tf_op jit(solution)/shard_map/ppermute | solution.py:60
  82.3 3.3 %fusion.55 = bf16[2,2,2,4,8,1280]{5,4,3,2,1,0:T(8,128)(2,1)S(1)} fusion(bf16[1,5120,1280]{2,1,0:T(8,128)(2,1)} %param.7, bf16[2,2,2,4,8,1280]{5,4,3,0,1,2:T(8,128)(2,1)S(1)} %dynamic-slice_bitcast_fusion), kind=kOutput, calls=%fused_computation.60 | convolution fusion | flops 839188480 | bytes 4587520 | tf_op jit(solution)/shard_map/dot_general | solution.py:230
  94.9 4.0 %collective-permute-done.34 = bf16[2,2,2,4,8,1280]{5,4,3,2,1,0:T(8,128)(2,1)S(1)} collective-permute-done((bf16[2,2,2,4,8,1280]{5,4,3,2,1,0:T(8,128)(2,1)S(1)}, bf16[2,2,2,4,8,1280]{5,4,3,2,1,0:T(8,128)(2,1)S(1)}, u32[]{:S(2)}, u32[]{:S(2)}) %collective-permute-start.34) | collective-permute-done | bytes 655392 | tf_op jit(solution)/shard_map/ppermute | solution.py:242
  100.2 3.8 %collective-permute-done.30 = bf16[2,2,2,4,8,1280]{5,4,3,2,1,0:T(8,128)(2,1)S(1)} collective-permute-done((bf16[2,2,2,4,8,1280]{5,4,3,2,1,0:T(8,128)(2,1)S(1)}, bf16[2,2,2,4,8,1280]{5,4,3,2,1,0:T(8,128)(2,1)S(1)}, u32[]{:S(2)}, u32[]{:S(2)}) %collective-permute-start.30) | collective-permute-done | bytes 655392 | tf_op jit(solution)/shard_map/ppermute | solution.py:242
  133.1 2.3 %collective-permute-done.28 = bf16[2,8,2560]{2,1,0:T(8,128)(2,1)S(1)} collective-permute-done((bf16[2,8,2560]{2,1,0:T(8,128)(2,1)S(1)}, bf16[2,8,2560]{2,1,0:T(8,128)(2,1)S(1)}, u32[]{:S(2)}, u32[]{:S(2)}) %collective-permute-start.28) | collective-permute-done | bytes 81952 | tf_op jit(solution)/shard_map/ppermute | solution.py:28
  137.5 3.2 %collective-permute-done.29 = bf16[8,2560]{1,0:T(8,128)(2,1)S(1)} collective-permute-done((bf16[8,2560]{1,0:T(8,128)(2,1)S(1)}, bf16[8,2560]{1,0:T(8,128)(2,1)S(1)}, u32[]{:S(2)}, u32[]{:S(2)}) %collective-permute-start.29) | collective-permute-done | bytes 40992 | tf_op jit(solution)/shard_map/ppermute | solution.py:28
  142.1 3.7 %all-to-all-start = ((bf16[16,8,5120]{2,1,0:T(8,128)(2,1)}), bf16[16,8,5120]{2,1,0:T(8,128)(2,1)S(1)}, u32[]{:S(2)}, u32[]{:S(2)}) async-start(bf16[16,8,5120]{2,1,0:T(8,128)(2,1)} %shard_map.72), calls=%async_computation | async-start | bytes 2621440 | tf_op jit(solution)/shard_map/all_to_all | solution.py:361
  150.6 9.7 %all-to-all-done = bf16[16,8,5120]{2,1,0:T(8,128)(2,1)S(1)} async-done(((bf16[16,8,5120]{2,1,0:T(8,128)(2,1)}), bf16[16,8,5120]{2,1,0:T(8,128)(2,1)S(1)}, u32[]{:S(2)}, u32[]{:S(2)}) %all-to-all-start) | async-done | bytes 1310752 | tf_op jit(solution)/shard_map/all_to_all | solution.py:361
  (202 shorter events, 73.8 us)
Async XLA Ops:
  2.6 19.7 %collective-permute-start = (bf16[64,5120]{1,0:T(8,128)(2,1)}, bf16[64,5120]{1,0:T(8,128)(2,1)S(1)}, u32[]{:S(2)}, u32[]{:S(2)}) collective-permute-start(bf16[64,5120]{1,0:T(8,128)(2,1)} %dynamic-slice_bitcast_fusion.4), channel_id=1, source_target_pairs={{0,16},{1,17},{2,18},{3,19},{4,20},{5,21},{6,22},{7,23},{8,24},{9,... | collective-permute-start | bytes 1966088 | tf_op jit(solution)/shard_map/ppermute | solution.py:28
  4.3 18.0 %collective-permute-start.1 = (bf16[64,5120]{1,0:T(8,128)(2,1)}, bf16[64,5120]{1,0:T(8,128)(2,1)S(1)}, u32[]{:S(2)}, u32[]{:S(2)}) collective-permute-start(bf16[64,5120]{1,0:T(8,128)(2,1)} %dynamic-slice_bitcast_fusion.4), channel_id=1, source_target_pairs={{0,48},{1,49},{2,50},{3,51},{4,52},{5,53},{6,54},{7,55},{8,56},{9,... | collective-permute-start | bytes 1966088 | tf_op jit(solution)/shard_map/ppermute | solution.py:28
  7.8 14.5 %collective-permute-start.2 = (s32[132]{0:T(256)S(1)}, s32[132]{0:T(256)S(1)}, u32[]{:S(2)}, u32[]{:S(2)}) collective-permute-start(s32[132]{0:T(256)S(1)} %constant_dynamic-update-slice_fusion), channel_id=1, source_target_pairs={{0,16},{16,0},{32,48},{48,32},{1,17},{17,1},{33,49},{49,33},{2,18}... | collective-permute-start | bytes 1592 | tf_op jit(solution)/shard_map/ppermute | solution.py:60
  8.5 13.8 %collective-permute-start.3 = (s32[132]{0:T(256)S(1)}, s32[132]{0:T(256)S(1)}, u32[]{:S(2)}, u32[]{:S(2)}) collective-permute-start(s32[132]{0:T(256)S(1)} %constant_dynamic-update-slice_fusion), channel_id=1, source_target_pairs={{0,32},{16,48},{32,0},{48,16},{1,33},{17,49},{33,1},{49,17},{2,34}... | collective-permute-start | bytes 1592 | tf_op jit(solution)/shard_map/ppermute | solution.py:60
  10.3 12.0 %collective-permute-start.4 = (s32[132]{0:T(256)S(1)}, s32[132]{0:T(256)S(1)}, u32[]{:S(2)}, u32[]{:S(2)}) collective-permute-start(s32[132]{0:T(256)S(1)} %constant_dynamic-update-slice_fusion), channel_id=1, source_target_pairs={{0,48},{16,32},{32,16},{48,0},{1,49},{17,33},{33,17},{49,1},{2,50}... | collective-permute-start | bytes 1592 | tf_op jit(solution)/shard_map/ppermute | solution.py:60
  22.3 10.7 %collective-permute-start.5 = (bf16[64,5120]{1,0:T(8,128)(2,1)S(1)}, bf16[64,5120]{1,0:T(8,128)(2,1)S(1)}, u32[]{:S(2)}, u32[]{:S(2)}) collective-permute-start(bf16[64,5120]{1,0:T(8,128)(2,1)S(1)} %collective-permute-done.1.refs_1_), channel_id=1, source_target_pairs={{0,16},{1,17},{2,18},{3,19},{4,20},{5,21},{6,22},{7,23},{8,24},{9,... | collective-permute-start | bytes 1966088 | tf_op jit(solution)/shard_map/ppermute | solution.py:28
  22.4 14.3 %collective-permute-start.9 = (bf16[64,5120]{1,0:T(8,128)(2,1)S(1)}, bf16[64,5120]{1,0:T(8,128)(2,1)S(1)}, u32[]{:S(2)}, u32[]{:S(2)}) collective-permute-start(bf16[64,5120]{1,0:T(8,128)(2,1)S(1)} %collective-permute-done.1.refs_1_), channel_id=1, source_target_pairs={{0,12},{1,13},{2,14},{3,15},{4,8},{5,9},{6,10},{7,11},{8,4},{9,5},... | collective-permute-start | bytes 1966088 | tf_op jit(solution)/shard_map/ppermute | solution.py:28
  25.2 11.5 %collective-permute-start.8 = (bf16[64,5120]{1,0:T(8,128)(2,1)S(1)}, bf16[64,5120]{1,0:T(8,128)(2,1)S(1)}, u32[]{:S(2)}, u32[]{:S(2)}) collective-permute-start(bf16[64,5120]{1,0:T(8,128)(2,1)S(1)} %collective-permute-done.refs_0_), channel_id=1, source_target_pairs={{0,4},{1,5},{2,6},{3,7},{4,0},{5,1},{6,2},{7,3},{8,12},{9,13},{10,... | collective-permute-start | bytes 1966088 | tf_op jit(solution)/shard_map/ppermute | solution.py:28
  33.0 7.5 %collective-permute-start.6 = (bf16[32,5120]{1,0:T(8,128)(2,1)S(1)}, bf16[32,5120]{1,0:T(8,128)(2,1)S(1)}, u32[]{:S(2)}, u32[]{:S(2)}) collective-permute-start(bf16[32,5120]{1,0:T(8,128)(2,1)S(1)} %get-tuple-element.59), channel_id=1, source_target_pairs={{0,4},{1,5},{2,6},{3,7},{4,0},{5,1},{6,2},{7,3},{8,12},{9,13},{10,... | collective-permute-start | bytes 983048 | tf_op jit(solution)/shard_map/ppermute | solution.py:28
  34.6 8.3 %collective-permute-start.7 = (bf16[32,5120]{1,0:T(8,128)(2,1)S(1)}, bf16[32,5120]{1,0:T(8,128)(2,1)S(1)}, u32[]{:S(2)}, u32[]{:S(2)}) collective-permute-start(bf16[32,5120]{1,0:T(8,128)(2,1)S(1)} %get-tuple-element.58), channel_id=1, source_target_pairs={{0,12},{1,13},{2,14},{3,15},{4,8},{5,9},{6,10},{7,11},{8,4},{9,5},... | collective-permute-start | bytes 983048 | tf_op jit(solution)/shard_map/ppermute | solution.py:28
  52.0 6.6 %collective-permute-start.11 = (f32[6,512]{1,0:T(8,128)S(1)}, f32[6,512]{1,0:T(8,128)S(1)}, u32[]{:S(2)}, u32[]{:S(2)}) collective-permute-start(f32[6,512]{1,0:T(8,128)S(1)} %stack.113), channel_id=1, source_target_pairs={{0,1},{1,0},{2,3},{3,2},{4,5},{5,4},{6,7},{7,6},{8,9},{9,8},{10,11... | collective-permute-start | bytes 36872 | tf_op jit(solution)/shard_map/ppermute | solution.py:60
  85.6 13.3 %collective-permute-start.34 = (bf16[2,2,2,4,8,1280]{5,4,3,2,1,0:T(8,128)(2,1)S(1)}, bf16[2,2,2,4,8,1280]{5,4,3,2,1,0:T(8,128)(2,1)S(1)}, u32[]{:S(2)}, u32[]{:S(2)}) collective-permute-start(bf16[2,2,2,4,8,1280]{5,4,3,2,1,0:T(8,128)(2,1)S(1)} %fusion.55), channel_id=1, source_target_pairs={{0,3},{1,2},{2,1},{3,0},{4,7},{5,6},{6,5},{7,4},{8,11},{9,10},{10,... | collective-permute-start | bytes 1966088 | tf_op jit(solution)/shard_map/ppermute | solution.py:242
  88.6 15.4 %collective-permute-start.30 = (bf16[2,2,2,4,8,1280]{5,4,3,2,1,0:T(8,128)(2,1)S(1)}, bf16[2,2,2,4,8,1280]{5,4,3,2,1,0:T(8,128)(2,1)S(1)}, u32[]{:S(2)}, u32[]{:S(2)}) collective-permute-start(bf16[2,2,2,4,8,1280]{5,4,3,2,1,0:T(8,128)(2,1)S(1)} %fusion.52), channel_id=1, source_target_pairs={{0,1},{1,0},{2,3},{3,2},{4,5},{5,4},{6,7},{7,6},{8,9},{9,8},{10,11... | collective-permute-start | bytes 1966088 | tf_op jit(solution)/shard_map/ppermute | solution.py:242
  89.7 16.9 %collective-permute-start.24 = (bf16[2,2,2,4,8,1280]{5,4,3,2,1,0:T(8,128)(2,1)S(1)}, bf16[2,2,2,4,8,1280]{5,4,3,2,1,0:T(8,128)(2,1)S(1)}, u32[]{:S(2)}, u32[]{:S(2)}) collective-permute-start(bf16[2,2,2,4,8,1280]{5,4,3,2,1,0:T(8,128)(2,1)S(1)} %fusion.49), channel_id=1, source_target_pairs={{0,12},{4,8},{8,4},{12,0},{1,13},{5,9},{9,5},{13,1},{2,14},{6,10},... | collective-permute-start | bytes 1966088 | tf_op jit(solution)/shard_map/ppermute | solution.py:242
  92.0 15.9 %collective-permute-start.20 = (bf16[2,2,2,4,8,1280]{5,4,3,2,1,0:T(8,128)(2,1)S(1)}, bf16[2,2,2,4,8,1280]{5,4,3,2,1,0:T(8,128)(2,1)S(1)}, u32[]{:S(2)}, u32[]{:S(2)}) collective-permute-start(bf16[2,2,2,4,8,1280]{5,4,3,2,1,0:T(8,128)(2,1)S(1)} %fusion.46), channel_id=1, source_target_pairs={{0,4},{4,0},{8,12},{12,8},{1,5},{5,1},{9,13},{13,9},{2,6},{6,2},{1... | collective-permute-start | bytes 1966088 | tf_op jit(solution)/shard_map/ppermute | solution.py:242
  100.1 13.2 %collective-permute-start.35 = (bf16[2,2,4,8,1280]{4,3,2,1,0:T(8,128)(2,1)S(1)}, bf16[2,2,4,8,1280]{4,3,2,1,0:T(8,128)(2,1)S(1)}, u32[]{:S(2)}, u32[]{:S(2)}) collective-permute-start(bf16[2,2,4,8,1280]{4,3,2,1,0:T(8,128)(2,1)S(1)} %get-tuple-element.54), channel_id=1, source_target_pairs={{0,1},{1,0},{2,3},{3,2},{4,5},{5,4},{6,7},{7,6},{8,9},{9,8},{10,11... | collective-permute-start | bytes 983048 | tf_op jit(solution)/shard_map/ppermute | solution.py:242
  105.2 10.1 %collective-permute-start.31 = (bf16[2,2,4,8,1280]{4,3,2,1,0:T(8,128)(2,1)S(1)}, bf16[2,2,4,8,1280]{4,3,2,1,0:T(8,128)(2,1)S(1)}, u32[]{:S(2)}, u32[]{:S(2)}) collective-permute-start(bf16[2,2,4,8,1280]{4,3,2,1,0:T(8,128)(2,1)S(1)} %fusion.91), channel_id=1, source_target_pairs={{0,3},{1,2},{2,1},{3,0},{4,7},{5,6},{6,5},{7,4},{8,11},{9,10},{10,... | collective-permute-start | bytes 983048 | tf_op jit(solution)/shard_map/ppermute | solution.py:242
  107.8 8.1 %collective-permute-start.25 = (bf16[2,2,4,8,1280]{4,3,2,1,0:T(8,128)(2,1)S(1)}, bf16[2,2,4,8,1280]{4,3,2,1,0:T(8,128)(2,1)S(1)}, u32[]{:S(2)}, u32[]{:S(2)}) collective-permute-start(bf16[2,2,4,8,1280]{4,3,2,1,0:T(8,128)(2,1)S(1)} %get-tuple-element.56), channel_id=1, source_target_pairs={{0,4},{4,0},{8,12},{12,8},{1,5},{5,1},{9,13},{13,9},{2,6},{6,2},{1... | collective-permute-start | bytes 983048 | tf_op jit(solution)/shard_map/ppermute | solution.py:242
  110.4 8.7 %collective-permute-start.21 = (bf16[2,2,4,8,1280]{4,3,2,1,0:T(8,128)(2,1)S(1)}, bf16[2,2,4,8,1280]{4,3,2,1,0:T(8,128)(2,1)S(1)}, u32[]{:S(2)}, u32[]{:S(2)}) collective-permute-start(bf16[2,2,4,8,1280]{4,3,2,1,0:T(8,128)(2,1)S(1)} %fusion.76), channel_id=1, source_target_pairs={{0,12},{4,8},{8,4},{12,0},{1,13},{5,9},{9,5},{13,1},{2,14},{6,10},... | collective-permute-start | bytes 983048 | tf_op jit(solution)/shard_map/ppermute | solution.py:242
  113.4 7.4 %collective-permute-start.36 = (bf16[2,4,8,1280]{3,2,1,0:T(8,128)(2,1)S(1)}, bf16[2,4,8,1280]{3,2,1,0:T(8,128)(2,1)S(1)}, u32[]{:S(2)}, u32[]{:S(2)}) collective-permute-start(bf16[2,4,8,1280]{3,2,1,0:T(8,128)(2,1)S(1)} %get-tuple-element.46), channel_id=1, source_target_pairs={{0,12},{4,8},{8,4},{12,0},{1,13},{5,9},{9,5},{13,1},{2,14},{6,10},... | collective-permute-start | bytes 491528 | tf_op jit(solution)/shard_map/ppermute | solution.py:242
  115.4 6.0 %collective-permute-start.32 = (bf16[2,4,8,1280]{3,2,1,0:T(8,128)(2,1)S(1)}, bf16[2,4,8,1280]{3,2,1,0:T(8,128)(2,1)S(1)}, u32[]{:S(2)}, u32[]{:S(2)}) collective-permute-start(bf16[2,4,8,1280]{3,2,1,0:T(8,128)(2,1)S(1)} %get-tuple-element.48), channel_id=1, source_target_pairs={{0,4},{4,0},{8,12},{12,8},{1,5},{5,1},{9,13},{13,9},{2,6},{6,2},{1... | collective-permute-start | bytes 491528 | tf_op jit(solution)/shard_map/ppermute | solution.py:242
  116.0 7.3 %collective-permute-start.26 = (bf16[2,4,8,1280]{3,2,1,0:T(8,128)(2,1)S(1)}, bf16[2,4,8,1280]{3,2,1,0:T(8,128)(2,1)S(1)}, u32[]{:S(2)}, u32[]{:S(2)}) collective-permute-start(bf16[2,4,8,1280]{3,2,1,0:T(8,128)(2,1)S(1)} %get-tuple-element.50), channel_id=1, source_target_pairs={{0,3},{1,2},{2,1},{3,0},{4,7},{5,6},{6,5},{7,4},{8,11},{9,10},{10,... | collective-permute-start | bytes 491528 | tf_op jit(solution)/shard_map/ppermute | solution.py:242
  119.1 5.9 %collective-permute-start.22 = (bf16[2,4,8,1280]{3,2,1,0:T(8,128)(2,1)S(1)}, bf16[2,4,8,1280]{3,2,1,0:T(8,128)(2,1)S(1)}, u32[]{:S(2)}, u32[]{:S(2)}) collective-permute-start(bf16[2,4,8,1280]{3,2,1,0:T(8,128)(2,1)S(1)} %get-tuple-element.52), channel_id=1, source_target_pairs={{0,1},{1,0},{2,3},{3,2},{4,5},{5,4},{6,7},{7,6},{8,9},{9,8},{10,11... | collective-permute-start | bytes 491528 | tf_op jit(solution)/shard_map/ppermute | solution.py:242
  142.1 18.2 %all-to-all-start = ((bf16[16,8,5120]{2,1,0:T(8,128)(2,1)}), bf16[16,8,5120]{2,1,0:T(8,128)(2,1)S(1)}, u32[]{:S(2)}, u32[]{:S(2)}) async-start(bf16[16,8,5120]{2,1,0:T(8,128)(2,1)} %shard_map.72), calls=%async_computation | async-start | bytes 2621440 | tf_op jit(solution)/shard_map/all_to_all | solution.py:361
  (31 other events, 206.3 us)

commit v5 on v4

--- a/solution.py
+++ b/solution.py
@@ -57,7 +57,7 @@
 
 
 def ring(block, axis):
-    near, wrap, far = [lax.ppermute(block, axis, [(i, i ^ s) for i in range(4)]) for s in (1, 3, 2)]
+    far, near, wrap = [lax.ppermute(block, axis, [(i, i ^ s) for i in range(4)]) for s in (2, 1, 3)]
     return [block, near, far, wrap]
 
 
@@ -251,8 +251,7 @@
     came[0], later = tied(came[0], later)
     kept = []
     for q, order in enumerate(orders):
-        pairs = zip(stay[q], split(came[q], order[1]))
-        one, other = [product(block, q) + wide(part) for block, part in pairs]
+        one, other = [product(part, q) + wide(block) for part, block in zip(stay[q], split(came[q], order[1]))]
         came[q] = swap(narrow(one), order[1])
         kept.append(other)
     for stage in range(2, 4):
@@ -263,31 +262,25 @@
         came = [swap(narrow(halves[q][0]), orders[q][stage]) for q in range(4)]
         kept = [halves[q][1] for q in range(4)]
     state = [kept[q] + wide(came[q]) for q in range(4)]
-    done = []
-    for pair, first, second, steps in ((state[:2], NEAR, WRAP, (1, 3)), (state[2:], WRAP, NEAR, (3, 1))):
-        block = jnp.concatenate(pair, axis=-1)
-        came = swap_y(narrow(jnp.stack([block[first], block[FAR]])), (steps[0],) * 2)
-        mine = block[OWN] + wide(came[0])
-        came = swap_y(narrow(block[second] + wide(came[1])), (steps[1],) * 2)
-        done.append(mine + wide(came))
-    return done, later
+    block = jnp.concatenate(state, axis=-1)
+    first, second = by_core(block[NEAR], block[WRAP]), by_core(block[WRAP], block[NEAR])
+    came = swap_y(narrow(jnp.stack([first, block[FAR]])), (1, 3))
+    mine, rest = block[OWN] + wide(came[0]), second + wide(came[1])
+    return [mine + wide(swap_y(narrow(rest), (3, 1)))], later
 
 
 def shard_stats(logits, peer_logits, hit):
-    values, peer_values = wide(logits), wide(peer_logits)
+    values = wide(logits)
     own_max = jnp.max(values, axis=-1)
+    own_sum = jnp.sum(jnp.exp(values - own_max[:, None]), axis=-1)
+    target = jnp.sum(jnp.where(hit, values, 0.0), axis=-1)
+    own_max, own_sum, target, peer_logits = tied(own_max, own_sum, target, peer_logits)
+    peer_values = wide(peer_logits)
     peer_max = jnp.max(peer_values, axis=-1)
     peer_exp = jnp.exp(peer_values - peer_max[:, None])
-    return jnp.stack(
-        [
-            own_max,
-            jnp.sum(jnp.exp(values - own_max[:, None]), axis=-1),
-            peer_max,
-            jnp.sum(peer_exp, axis=-1),
-            jnp.sum(jnp.where(hit, values, 0.0), axis=-1),
-            jnp.sum(peer_exp * (peer_values - values), axis=-1),
-        ]
-    )
+    peer_sum = jnp.sum(peer_exp, axis=-1)
+    cross = jnp.sum(peer_exp * (peer_values - values), axis=-1)
+    return jnp.stack([own_max, own_sum, peer_max, peer_sum, target, cross]), peer_logits
 
 
 def norm_backward_kernel(count, *refs):
@@ -329,7 +322,7 @@
     peer_logits = lax.ppermute(logits, "peer", [(0, 1), (1, 0)])
     hit = all_targets[:, None] - lax.axis_index(("dp", "tx", "tz")) * voc_shard
     hit = hit == lax.broadcasted_iota(jnp.int32, (1, voc_shard), 1)
-    stats = shard_stats(logits, peer_logits, hit)
+    stats, peer_logits = shard_stats(logits, peer_logits, hit)
     stats = merge(ring(stats, "tz"))
     stats = merge(ring(stats, "tx"))
     stats = ring(stats, "dp")

time: 163 us -> 163 us (level)
    ppermute x11 -> x9, starting transfers between devices: 15 us -> 12.8 us  [permute(): lax.ppermute(block, ALL, [(index(*p), index(*move(*p))) for p in places])]
    ppermute x16, starting transfers between devices: 15.9 us -> 17.8 us  [swap(): return lax.ppermute(block, axis, [(i, i ^ step) for i in range(4)])]
    ppermute x11 -> x9, waiting for transfers between devices: 13.7 us -> 14.4 us  [permute(): lax.ppermute(block, ALL, [(index(*p), index(*move(*p))) for p in places])]
  transfers between devices with their start and end apart: 41 -> 39, of which waited for: 20 -> 18; matrix products, arithmetic and copies ran while one was open for 11% -> 12% of each run, Pallas kernels for 6% -> 6%
where the time goes in v5:
time: 163 us
  starting transfers between devices  55.3 us (34%)
  waiting for transfers between devices  48.7 us (30%)
  matrix products  16.4 us (10%)
  Pallas kernels  15 us (9%)
  local copies, waits for them, and re-layouts  14.4 us (9%)
  other arithmetic  7.49 us (5%)
  between operations  5.79 us (4%)
    ppermute x12, starting transfers between devices, ring(): lax.ppermute(block, axis, [(i, i ^ s) for i in range(4)])  19.8 us
    ppermute x16, starting transfers between devices, swap(): return lax.ppermute(block, axis, [(i, i ^ step) for i in range(4)])  17.8 us
    dot_general x12, matrix products, product(): lax.dot_general(block.reshape(-1, voc), columns, (((1,), (1,)), ((), ()))...  16.4 us
    ppermute x9, waiting for transfers between devices, permute(): lax.ppermute(block, ALL, [(index(*p), index(*move(*p))) for p in places])  14.4 us
    pallas_call x4, Pallas kernels, add_logits(): pl.pallas_call(make_kernel(count, *plan), out_shape=jax.ShapeDtypeStruct(...  13.7 us
    ppermute x9, starting transfers between devices, permute(): lax.ppermute(block, ALL, [(index(*p), index(*move(*p))) for p in places])  12.8 us
    ppermute x12, waiting for transfers between devices, ring(): lax.ppermute(block, axis, [(i, i ^ s) for i in range(4)])  11.5 us
    ppermute x16, waiting for transfers between devices, swap(): return lax.ppermute(block, axis, [(i, i ^ step) for i in range(4)])  11.5 us
  transfers between devices with their start and end apart: 39, of which 18 were waited for; matrix products, arithmetic and copies ran while one was open for 12% of the time, Pallas kernels for 6%

profile of v5, /device:TPU:0, one launch (start us, length us, event | category | flops | bytes accessed | tf_op | source)
XLA Modules:
  0.0 163.0 jit_solution(17001820061106890477)
XLA Ops:
  4.3 2.2 %collective-permute-start.1 = (bf16[64,5120]{1,0:T(8,128)(2,1)}, bf16[64,5120]{1,0:T(8,128)(2,1)S(1)}, u32[]{:S(2)}, u32[]{:S(2)}) collective-permute-start(bf16[64,5120]{1,0:T(8,128)(2,1)} %dynamic-slice_bitcast_fusion.4), channel_id=1, source_target_pairs={{0,48},{1,49},{2,50},{3,51},{4,52},{5,53},{6,54},{7,55},{8,56},{9,... | collective-permute-start | bytes 1966088 | tf_op jit(solution)/shard_map/ppermute | solution.py:28
  12.5 4.7 %copy-done = bf16[1,5120,1280]{2,1,0:T(8,128)(2,1)S(1)} copy-done((bf16[1,5120,1280]{2,1,0:T(8,128)(2,1)S(1)}, bf16[1,5120,1280]{2,1,0:T(8,128)(2,1)}, u32[]{:S(2)}) %copy-start) | copy-done | bytes 13107224
  19.3 3.0 %shard_map.68.refs_4_ = bf16[512,1280]{1,0:T(8,128)(2,1)S(1)} custom-call(bf16[128,5120]{1,0:T(8,128)(2,1)S(1)} %bitcast.381, f32[1,5120]{1,0:T(1,128)S(1)} %copy-done.2, bf16[5120,1280]{1,0:T(8,128)(2,1)S(1)} %bitcast.373), custom_call_target="tpu_custom_call" | custom-call | flops 1677721600 | bytes 14417920 | tf_op jit(solution)/shard_map/pallas_call | solution.py:174
  22.4 2.8 %collective-permute-start.9 = (bf16[64,5120]{1,0:T(8,128)(2,1)S(1)}, bf16[64,5120]{1,0:T(8,128)(2,1)S(1)}, u32[]{:S(2)}, u32[]{:S(2)}) collective-permute-start(bf16[64,5120]{1,0:T(8,128)(2,1)S(1)} %collective-permute-done.1.refs_1_), channel_id=1, source_target_pairs={{0,12},{1,13},{2,14},{3,15},{4,8},{5,9},{6,10},{7,11},{8,4},{9,5},... | collective-permute-start | bytes 1966088 | tf_op jit(solution)/shard_map/ppermute | solution.py:28
  25.5 3.6 %shard_map.69.refs_4_ = bf16[512,1280]{1,0:T(8,128)(2,1)S(1)} custom-call(bf16[64,5120]{1,0:T(8,128)(2,1)S(1)} %collective-permute-done.refs_0_, bf16[64,5120]{1,0:T(8,128)(2,1)S(1)} %collective-permute-done.1.refs_1_, f32[1,5120]{1,0:T(1,128)S(1)} %copy-done.2, bf16[5120,1280]{1,0:T(8,128)(2,1)S(1)} %bitcast.374, ...), custom_call_target="tpu_custom_call", output_to_operand_aliasing={{}: (4, {})} | custom-call | flops 1677721600 | bytes 14417920 | tf_op jit(solution)/shard_map/pallas_call | solution.py:174
  29.1 3.9 %collective-permute-done.5.refs_0_ = bf16[64,5120]{1,0:T(8,128)(2,1)S(1)} collective-permute-done((bf16[64,5120]{1,0:T(8,128)(2,1)S(1)}, bf16[64,5120]{1,0:T(8,128)(2,1)S(1)}, u32[]{:S(2)}, u32[]{:S(2)}) %collective-permute-start.5) | collective-permute-done | bytes 655392 | tf_op jit(solution)/shard_map/ppermute | solution.py:28
  36.7 3.7 %shard_map.70.refs_5_ = bf16[512,1280]{1,0:T(8,128)(2,1)S(1)} custom-call(bf16[64,5120]{1,0:T(8,128)(2,1)S(1)} %collective-permute-done.8.refs_0_, bf16[64,5120]{1,0:T(8,128)(2,1)S(1)} %collective-permute-done.9.refs_1_, f32[1,5120]{1,0:T(1,128)S(1)} %copy-done.2, bf16[5120,1280]{1,0:T(8,128)(2,1)S(1)} %bitcast.377, ...), custom_call_target="tpu_custom_call", output_to_operand_aliasing={{}: (4, {})} | custom-call | flops 1677721600 | bytes 14417920 | tf_op jit(solution)/shard_map/pallas_call | solution.py:174
  40.5 2.4 %collective-permute-done.7.refs_2_ = bf16[32,5120]{1,0:T(8,128)(2,1)S(1)} collective-permute-done((bf16[32,5120]{1,0:T(8,128)(2,1)S(1)}, bf16[32,5120]{1,0:T(8,128)(2,1)S(1)}, u32[]{:S(2)}, u32[]{:S(2)}) %collective-permute-start.7) | collective-permute-done | bytes 327712 | tf_op jit(solution)/shard_map/ppermute | solution.py:28
  42.9 3.4 %shard_map.71 = bf16[512,1280]{1,0:T(8,128)(2,1)S(1)} custom-call(bf16[64,5120]{1,0:T(8,128)(2,1)S(1)} %collective-permute-done.5.refs_0_, bf16[32,5120]{1,0:T(8,128)(2,1)S(1)} %collective-permute-done.6.refs_1_, bf16[32,5120]{1,0:T(8,128)(2,1)S(1)} %collective-permute-done.7.refs_2_, f32[1,5120]{1,0:T(1,128)S(1)} %copy-done.2, ...), custom_call_target="tpu_custom_call", output_to_operand_aliasing={{}: (5, {})} | custom-call | flops 1677721600 | bytes 14417920 | tf_op jit(solution)/shard_map/pallas_call | solution.py:174
  52.8 3.6 %collective-permute-start.12 = (f32[6,512]{1,0:T(8,128)S(1)}, f32[6,512]{1,0:T(8,128)S(1)}, u32[]{:S(2)}, u32[]{:S(2)}) collective-permute-start(f32[6,512]{1,0:T(8,128)S(1)} %stack.114), channel_id=1, source_target_pairs={{0,2},{1,3},{2,0},{3,1},{4,6},{5,7},{6,4},{7,5},{8,10},{9,11},{10,... | collective-permute-start | bytes 36872 | tf_op jit(solution)/shard_map/ppermute | solution.py:60
  58.3 3.1 %collective-permute-done.13 = f32[6,512]{1,0:T(8,128)S(1)} collective-permute-done((f32[6,512]{1,0:T(8,128)S(1)}, f32[6,512]{1,0:T(8,128)S(1)}, u32[]{:S(2)}, u32[]{:S(2)}) %collective-permute-start.13) | collective-permute-done | bytes 12320 | tf_op jit(solution)/shard_map/ppermute | solution.py:60
  61.6 3.5 %collective-permute-start.15 = (f32[6,512]{1,0:T(8,128)S(1)}, f32[6,512]{1,0:T(8,128)S(1)}, u32[]{:S(2)}, u32[]{:S(2)}) collective-permute-start(f32[6,512]{1,0:T(8,128)S(1)} %get-tuple-element.99), channel_id=1, source_target_pairs={{0,8},{4,12},{8,0},{12,4},{1,9},{5,13},{9,1},{13,5},{2,10},{6,14},... | collective-permute-start | bytes 36872 | tf_op jit(solution)/shard_map/ppermute | solution.py:60
  67.2 3.0 %collective-permute-done.16 = f32[6,512]{1,0:T(8,128)S(1)} collective-permute-done((f32[6,512]{1,0:T(8,128)S(1)}, f32[6,512]{1,0:T(8,128)S(1)}, u32[]{:S(2)}, u32[]{:S(2)}) %collective-permute-start.16) | collective-permute-done | bytes 12320 | tf_op jit(solution)/shard_map/ppermute | solution.py:60
  70.6 2.7 %collective-permute-start.18 = (f32[6,512]{1,0:T(8,128)S(1)}, f32[6,512]{1,0:T(8,128)S(1)}, u32[]{:S(2)}, u32[]{:S(2)}) collective-permute-start(f32[6,512]{1,0:T(8,128)S(1)} %get-tuple-element.97), channel_id=1, source_target_pairs={{0,32},{16,48},{32,0},{48,16},{1,33},{17,49},{33,1},{49,17},{2,34}... | collective-permute-start | bytes 36872 | tf_op jit(solution)/shard_map/ppermute | solution.py:60
  75.9 2.4 %collective-permute-done.19 = f32[6,512]{1,0:T(8,128)S(1)} collective-permute-done((f32[6,512]{1,0:T(8,128)S(1)}, f32[6,512]{1,0:T(8,128)S(1)}, u32[]{:S(2)}, u32[]{:S(2)}) %collective-permute-start.19) | collective-permute-done | bytes 12320 | tf_op jit(solution)/shard_map/ppermute | solution.py:60
  82.5 3.5 %fusion.46 = bf16[2,2,2,4,8,1280]{5,4,3,2,1,0:T(8,128)(2,1)S(1)} fusion(bf16[2,2,2,4,8,1280]{5,4,3,2,1,0:T(8,128)(2,1)S(1)} %dynamic-slice_bitcast_fusion.3, bf16[1,5120,1280]{2,1,0:T(8,128)(2,1)} %param.7), kind=kOutput, calls=%fused_computation.57 | convolution fusion | flops 839188480 | bytes 4587520 | tf_op jit(solution)/shard_map/dot_general | solution.py:230
  94.5 3.5 %collective-permute-done.20 = bf16[2,2,2,4,8,1280]{5,4,3,2,1,0:T(8,128)(2,1)S(1)} collective-permute-done((bf16[2,2,2,4,8,1280]{5,4,3,2,1,0:T(8,128)(2,1)S(1)}, bf16[2,2,2,4,8,1280]{5,4,3,2,1,0:T(8,128)(2,1)S(1)}, u32[]{:S(2)}, u32[]{:S(2)}) %collective-permute-start.20) | collective-permute-done | bytes 655392 | tf_op jit(solution)/shard_map/ppermute | solution.py:242
  100.1 3.7 %collective-permute-done.24 = bf16[2,2,2,4,8,1280]{5,4,3,2,1,0:T(8,128)(2,1)S(1)} collective-permute-done((bf16[2,2,2,4,8,1280]{5,4,3,2,1,0:T(8,128)(2,1)S(1)}, bf16[2,2,2,4,8,1280]{5,4,3,2,1,0:T(8,128)(2,1)S(1)}, u32[]{:S(2)}, u32[]{:S(2)}) %collective-permute-start.24) | collective-permute-done | bytes 655392 | tf_op jit(solution)/shard_map/ppermute | solution.py:242
  113.2 3.1 %collective-permute-start.26 = (bf16[2,4,8,1280]{3,2,1,0:T(8,128)(2,1)S(1)}, bf16[2,4,8,1280]{3,2,1,0:T(8,128)(2,1)S(1)}, u32[]{:S(2)}, u32[]{:S(2)}) collective-permute-start(bf16[2,4,8,1280]{3,2,1,0:T(8,128)(2,1)S(1)} %get-tuple-element.56), channel_id=1, source_target_pairs={{0,3},{1,2},{2,1},{3,0},{4,7},{5,6},{6,5},{7,4},{8,11},{9,10},{10,... | collective-permute-start | bytes 491528 | tf_op jit(solution)/shard_map/ppermute | solution.py:242
  119.9 2.7 %collective-permute-start.23 = (bf16[4,8,1280]{2,1,0:T(8,128)(2,1)S(1)}, bf16[4,8,1280]{2,1,0:T(8,128)(2,1)S(1)}, u32[]{:S(2)}, u32[]{:S(2)}) collective-permute-start(bf16[4,8,1280]{2,1,0:T(8,128)(2,1)S(1)} %fusion.127), channel_id=1, source_target_pairs={{0,3},{1,2},{2,1},{3,0},{4,7},{5,6},{6,5},{7,4},{8,11},{9,10},{10,... | collective-permute-start | bytes 245768 | tf_op jit(solution)/shard_map/ppermute | solution.py:242
  129.3 5.3 %collective-permute-done.36 = bf16[2,8,5120]{2,1,0:T(8,128)(2,1)S(1)} collective-permute-done((bf16[2,8,5120]{2,1,0:T(8,128)(2,1)S(1)}, bf16[2,8,5120]{2,1,0:T(8,128)(2,1)S(1)}, u32[]{:S(2)}, u32[]{:S(2)}) %collective-permute-start.36) | collective-permute-done | bytes 163872 | tf_op jit(solution)/shard_map/ppermute | solution.py:28
  137.6 2.8 %collective-permute-done.37 = bf16[8,5120]{1,0:T(8,128)(2,1)S(1)} collective-permute-done((bf16[8,5120]{1,0:T(8,128)(2,1)S(1)}, bf16[8,5120]{1,0:T(8,128)(2,1)S(1)}, u32[]{:S(2)}, u32[]{:S(2)}) %collective-permute-start.37) | collective-permute-done | bytes 81952 | tf_op jit(solution)/shard_map/ppermute | solution.py:28
  141.7 4.6 %all-to-all-start = ((bf16[16,8,5120]{2,1,0:T(8,128)(2,1)}), bf16[16,8,5120]{2,1,0:T(8,128)(2,1)S(1)}, u32[]{:S(2)}, u32[]{:S(2)}) async-start(bf16[16,8,5120]{2,1,0:T(8,128)(2,1)} %shard_map.72), calls=%async_computation | async-start | bytes 2621440 | tf_op jit(solution)/shard_map/all_to_all | solution.py:354
  151.1 9.7 %all-to-all-done = bf16[16,8,5120]{2,1,0:T(8,128)(2,1)S(1)} async-done(((bf16[16,8,5120]{2,1,0:T(8,128)(2,1)}), bf16[16,8,5120]{2,1,0:T(8,128)(2,1)S(1)}, u32[]{:S(2)}, u32[]{:S(2)}) %all-to-all-start) | async-done | bytes 1310752 | tf_op jit(solution)/shard_map/all_to_all | solution.py:354
  (196 shorter events, 70.5 us)
Async XLA Ops:
  2.6 19.7 %collective-permute-start = (bf16[64,5120]{1,0:T(8,128)(2,1)}, bf16[64,5120]{1,0:T(8,128)(2,1)S(1)}, u32[]{:S(2)}, u32[]{:S(2)}) collective-permute-start(bf16[64,5120]{1,0:T(8,128)(2,1)} %dynamic-slice_bitcast_fusion.4), channel_id=1, source_target_pairs={{0,16},{1,17},{2,18},{3,19},{4,20},{5,21},{6,22},{7,23},{8,24},{9,... | collective-permute-start | bytes 1966088 | tf_op jit(solution)/shard_map/ppermute | solution.py:28
  4.3 18.0 %collective-permute-start.1 = (bf16[64,5120]{1,0:T(8,128)(2,1)}, bf16[64,5120]{1,0:T(8,128)(2,1)S(1)}, u32[]{:S(2)}, u32[]{:S(2)}) collective-permute-start(bf16[64,5120]{1,0:T(8,128)(2,1)} %dynamic-slice_bitcast_fusion.4), channel_id=1, source_target_pairs={{0,48},{1,49},{2,50},{3,51},{4,52},{5,53},{6,54},{7,55},{8,56},{9,... | collective-permute-start | bytes 1966088 | tf_op jit(solution)/shard_map/ppermute | solution.py:28
  7.8 14.5 %collective-permute-start.2 = (s32[132]{0:T(256)S(1)}, s32[132]{0:T(256)S(1)}, u32[]{:S(2)}, u32[]{:S(2)}) collective-permute-start(s32[132]{0:T(256)S(1)} %constant_dynamic-update-slice_fusion), channel_id=1, source_target_pairs={{0,16},{16,0},{32,48},{48,32},{1,17},{17,1},{33,49},{49,33},{2,18}... | collective-permute-start | bytes 1592 | tf_op jit(solution)/shard_map/ppermute | solution.py:60
  8.5 13.8 %collective-permute-start.3 = (s32[132]{0:T(256)S(1)}, s32[132]{0:T(256)S(1)}, u32[]{:S(2)}, u32[]{:S(2)}) collective-permute-start(s32[132]{0:T(256)S(1)} %constant_dynamic-update-slice_fusion), channel_id=1, source_target_pairs={{0,32},{16,48},{32,0},{48,16},{1,33},{17,49},{33,1},{49,17},{2,34}... | collective-permute-start | bytes 1592 | tf_op jit(solution)/shard_map/ppermute | solution.py:60
  10.3 12.0 %collective-permute-start.4 = (s32[132]{0:T(256)S(1)}, s32[132]{0:T(256)S(1)}, u32[]{:S(2)}, u32[]{:S(2)}) collective-permute-start(s32[132]{0:T(256)S(1)} %constant_dynamic-update-slice_fusion), channel_id=1, source_target_pairs={{0,48},{16,32},{32,16},{48,0},{1,49},{17,33},{33,17},{49,1},{2,50}... | collective-permute-start | bytes 1592 | tf_op jit(solution)/shard_map/ppermute | solution.py:60
  22.3 10.7 %collective-permute-start.5 = (bf16[64,5120]{1,0:T(8,128)(2,1)S(1)}, bf16[64,5120]{1,0:T(8,128)(2,1)S(1)}, u32[]{:S(2)}, u32[]{:S(2)}) collective-permute-start(bf16[64,5120]{1,0:T(8,128)(2,1)S(1)} %collective-permute-done.1.refs_1_), channel_id=1, source_target_pairs={{0,16},{1,17},{2,18},{3,19},{4,20},{5,21},{6,22},{7,23},{8,24},{9,... | collective-permute-start | bytes 1966088 | tf_op jit(solution)/shard_map/ppermute | solution.py:28
  22.4 14.3 %collective-permute-start.9 = (bf16[64,5120]{1,0:T(8,128)(2,1)S(1)}, bf16[64,5120]{1,0:T(8,128)(2,1)S(1)}, u32[]{:S(2)}, u32[]{:S(2)}) collective-permute-start(bf16[64,5120]{1,0:T(8,128)(2,1)S(1)} %collective-permute-done.1.refs_1_), channel_id=1, source_target_pairs={{0,12},{1,13},{2,14},{3,15},{4,8},{5,9},{6,10},{7,11},{8,4},{9,5},... | collective-permute-start | bytes 1966088 | tf_op jit(solution)/shard_map/ppermute | solution.py:28
  25.2 11.5 %collective-permute-start.8 = (bf16[64,5120]{1,0:T(8,128)(2,1)S(1)}, bf16[64,5120]{1,0:T(8,128)(2,1)S(1)}, u32[]{:S(2)}, u32[]{:S(2)}) collective-permute-start(bf16[64,5120]{1,0:T(8,128)(2,1)S(1)} %collective-permute-done.refs_0_), channel_id=1, source_target_pairs={{0,4},{1,5},{2,6},{3,7},{4,0},{5,1},{6,2},{7,3},{8,12},{9,13},{10,... | collective-permute-start | bytes 1966088 | tf_op jit(solution)/shard_map/ppermute | solution.py:28
  33.0 7.5 %collective-permute-start.6 = (bf16[32,5120]{1,0:T(8,128)(2,1)S(1)}, bf16[32,5120]{1,0:T(8,128)(2,1)S(1)}, u32[]{:S(2)}, u32[]{:S(2)}) collective-permute-start(bf16[32,5120]{1,0:T(8,128)(2,1)S(1)} %get-tuple-element.69), channel_id=1, source_target_pairs={{0,4},{1,5},{2,6},{3,7},{4,0},{5,1},{6,2},{7,3},{8,12},{9,13},{10,... | collective-permute-start | bytes 983048 | tf_op jit(solution)/shard_map/ppermute | solution.py:28
  34.6 8.3 %collective-permute-start.7 = (bf16[32,5120]{1,0:T(8,128)(2,1)S(1)}, bf16[32,5120]{1,0:T(8,128)(2,1)S(1)}, u32[]{:S(2)}, u32[]{:S(2)}) collective-permute-start(bf16[32,5120]{1,0:T(8,128)(2,1)S(1)} %get-tuple-element.68), channel_id=1, source_target_pairs={{0,12},{1,13},{2,14},{3,15},{4,8},{5,9},{6,10},{7,11},{8,4},{9,5},... | collective-permute-start | bytes 983048 | tf_op jit(solution)/shard_map/ppermute | solution.py:28
  85.9 12.1 %collective-permute-start.20 = (bf16[2,2,2,4,8,1280]{5,4,3,2,1,0:T(8,128)(2,1)S(1)}, bf16[2,2,2,4,8,1280]{5,4,3,2,1,0:T(8,128)(2,1)S(1)}, u32[]{:S(2)}, u32[]{:S(2)}) collective-permute-start(bf16[2,2,2,4,8,1280]{5,4,3,2,1,0:T(8,128)(2,1)S(1)} %fusion.46), channel_id=1, source_target_pairs={{0,4},{4,0},{8,12},{12,8},{1,5},{5,1},{9,13},{13,9},{2,6},{6,2},{1... | collective-permute-start | bytes 1966088 | tf_op jit(solution)/shard_map/ppermute | solution.py:242
  87.4 16.4 %collective-permute-start.24 = (bf16[2,2,2,4,8,1280]{5,4,3,2,1,0:T(8,128)(2,1)S(1)}, bf16[2,2,2,4,8,1280]{5,4,3,2,1,0:T(8,128)(2,1)S(1)}, u32[]{:S(2)}, u32[]{:S(2)}) collective-permute-start(bf16[2,2,2,4,8,1280]{5,4,3,2,1,0:T(8,128)(2,1)S(1)} %fusion.49), channel_id=1, source_target_pairs={{0,12},{4,8},{8,4},{12,0},{1,13},{5,9},{9,5},{13,1},{2,14},{6,10},... | collective-permute-start | bytes 1966088 | tf_op jit(solution)/shard_map/ppermute | solution.py:242
  90.9 14.8 %collective-permute-start.28 = (bf16[2,2,2,4,8,1280]{5,4,3,2,1,0:T(8,128)(2,1)S(1)}, bf16[2,2,2,4,8,1280]{5,4,3,2,1,0:T(8,128)(2,1)S(1)}, u32[]{:S(2)}, u32[]{:S(2)}) collective-permute-start(bf16[2,2,2,4,8,1280]{5,4,3,2,1,0:T(8,128)(2,1)S(1)} %fusion.52), channel_id=1, source_target_pairs={{0,1},{1,0},{2,3},{3,2},{4,5},{5,4},{6,7},{7,6},{8,9},{9,8},{10,11... | collective-permute-start | bytes 1966088 | tf_op jit(solution)/shard_map/ppermute | solution.py:242
  92.3 16.2 %collective-permute-start.32 = (bf16[2,2,2,4,8,1280]{5,4,3,2,1,0:T(8,128)(2,1)S(1)}, bf16[2,2,2,4,8,1280]{5,4,3,2,1,0:T(8,128)(2,1)S(1)}, u32[]{:S(2)}, u32[]{:S(2)}) collective-permute-start(bf16[2,2,2,4,8,1280]{5,4,3,2,1,0:T(8,128)(2,1)S(1)} %fusion.55), channel_id=1, source_target_pairs={{0,3},{1,2},{2,1},{3,0},{4,7},{5,6},{6,5},{7,4},{8,11},{9,10},{10,... | collective-permute-start | bytes 1966088 | tf_op jit(solution)/shard_map/ppermute | solution.py:242
  99.2 12.3 %collective-permute-start.21 = (bf16[2,2,4,8,1280]{4,3,2,1,0:T(8,128)(2,1)S(1)}, bf16[2,2,4,8,1280]{4,3,2,1,0:T(8,128)(2,1)S(1)}, u32[]{:S(2)}, u32[]{:S(2)}) collective-permute-start(bf16[2,2,4,8,1280]{4,3,2,1,0:T(8,128)(2,1)S(1)} %fusion.76), channel_id=1, source_target_pairs={{0,12},{4,8},{8,4},{12,0},{1,13},{5,9},{9,5},{13,1},{2,14},{6,10},... | collective-permute-start | bytes 983048 | tf_op jit(solution)/shard_map/ppermute | solution.py:242
  105.0 8.2 %collective-permute-start.25 = (bf16[2,2,4,8,1280]{4,3,2,1,0:T(8,128)(2,1)S(1)}, bf16[2,2,4,8,1280]{4,3,2,1,0:T(8,128)(2,1)S(1)}, u32[]{:S(2)}, u32[]{:S(2)}) collective-permute-start(bf16[2,2,4,8,1280]{4,3,2,1,0:T(8,128)(2,1)S(1)} %get-tuple-element.64), channel_id=1, source_target_pairs={{0,4},{4,0},{8,12},{12,8},{1,5},{5,1},{9,13},{13,9},{2,6},{6,2},{1... | collective-permute-start | bytes 983048 | tf_op jit(solution)/shard_map/ppermute | solution.py:242
  107.0 9.4 %collective-permute-start.29 = (bf16[2,2,4,8,1280]{4,3,2,1,0:T(8,128)(2,1)S(1)}, bf16[2,2,4,8,1280]{4,3,2,1,0:T(8,128)(2,1)S(1)}, u32[]{:S(2)}, u32[]{:S(2)}) collective-permute-start(bf16[2,2,4,8,1280]{4,3,2,1,0:T(8,128)(2,1)S(1)} %fusion.91), channel_id=1, source_target_pairs={{0,3},{1,2},{2,1},{3,0},{4,7},{5,6},{6,5},{7,4},{8,11},{9,10},{10,... | collective-permute-start | bytes 983048 | tf_op jit(solution)/shard_map/ppermute | solution.py:242
  109.7 8.1 %collective-permute-start.33 = (bf16[2,2,4,8,1280]{4,3,2,1,0:T(8,128)(2,1)S(1)}, bf16[2,2,4,8,1280]{4,3,2,1,0:T(8,128)(2,1)S(1)}, u32[]{:S(2)}, u32[]{:S(2)}) collective-permute-start(bf16[2,2,4,8,1280]{4,3,2,1,0:T(8,128)(2,1)S(1)} %get-tuple-element.66), channel_id=1, source_target_pairs={{0,1},{1,0},{2,3},{3,2},{4,5},{5,4},{6,7},{7,6},{8,9},{9,8},{10,11... | collective-permute-start | bytes 983048 | tf_op jit(solution)/shard_map/ppermute | solution.py:242
  111.6 8.3 %collective-permute-start.22 = (bf16[2,4,8,1280]{3,2,1,0:T(8,128)(2,1)S(1)}, bf16[2,4,8,1280]{3,2,1,0:T(8,128)(2,1)S(1)}, u32[]{:S(2)}, u32[]{:S(2)}) collective-permute-start(bf16[2,4,8,1280]{3,2,1,0:T(8,128)(2,1)S(1)} %get-tuple-element.54), channel_id=1, source_target_pairs={{0,1},{1,0},{2,3},{3,2},{4,5},{5,4},{6,7},{7,6},{8,9},{9,8},{10,11... | collective-permute-start | bytes 491528 | tf_op jit(solution)/shard_map/ppermute | solution.py:242
  113.2 9.4 %collective-permute-start.26 = (bf16[2,4,8,1280]{3,2,1,0:T(8,128)(2,1)S(1)}, bf16[2,4,8,1280]{3,2,1,0:T(8,128)(2,1)S(1)}, u32[]{:S(2)}, u32[]{:S(2)}) collective-permute-start(bf16[2,4,8,1280]{3,2,1,0:T(8,128)(2,1)S(1)} %get-tuple-element.56), channel_id=1, source_target_pairs={{0,3},{1,2},{2,1},{3,0},{4,7},{5,6},{6,5},{7,4},{8,11},{9,10},{10,... | collective-permute-start | bytes 491528 | tf_op jit(solution)/shard_map/ppermute | solution.py:242
  116.4 6.3 %collective-permute-start.30 = (bf16[2,4,8,1280]{3,2,1,0:T(8,128)(2,1)S(1)}, bf16[2,4,8,1280]{3,2,1,0:T(8,128)(2,1)S(1)}, u32[]{:S(2)}, u32[]{:S(2)}) collective-permute-start(bf16[2,4,8,1280]{3,2,1,0:T(8,128)(2,1)S(1)} %get-tuple-element.58), channel_id=1, source_target_pairs={{0,4},{4,0},{8,12},{12,8},{1,5},{5,1},{9,13},{13,9},{2,6},{6,2},{1... | collective-permute-start | bytes 491528 | tf_op jit(solution)/shard_map/ppermute | solution.py:242
  117.9 6.6 %collective-permute-start.34 = (bf16[2,4,8,1280]{3,2,1,0:T(8,128)(2,1)S(1)}, bf16[2,4,8,1280]{3,2,1,0:T(8,128)(2,1)S(1)}, u32[]{:S(2)}, u32[]{:S(2)}) collective-permute-start(bf16[2,4,8,1280]{3,2,1,0:T(8,128)(2,1)S(1)} %get-tuple-element.60), channel_id=1, source_target_pairs={{0,12},{4,8},{8,4},{12,0},{1,13},{5,9},{9,5},{13,1},{2,14},{6,10},... | collective-permute-start | bytes 491528 | tf_op jit(solution)/shard_map/ppermute | solution.py:242
  119.9 5.7 %collective-permute-start.23 = (bf16[4,8,1280]{2,1,0:T(8,128)(2,1)S(1)}, bf16[4,8,1280]{2,1,0:T(8,128)(2,1)S(1)}, u32[]{:S(2)}, u32[]{:S(2)}) collective-permute-start(bf16[4,8,1280]{2,1,0:T(8,128)(2,1)S(1)} %fusion.127), channel_id=1, source_target_pairs={{0,3},{1,2},{2,1},{3,0},{4,7},{5,6},{6,5},{7,4},{8,11},{9,10},{10,... | collective-permute-start | bytes 245768 | tf_op jit(solution)/shard_map/ppermute | solution.py:242
  141.7 19.1 %all-to-all-start = ((bf16[16,8,5120]{2,1,0:T(8,128)(2,1)}), bf16[16,8,5120]{2,1,0:T(8,128)(2,1)S(1)}, u32[]{:S(2)}, u32[]{:S(2)}) async-start(bf16[16,8,5120]{2,1,0:T(8,128)(2,1)} %shard_map.72), calls=%async_computation | async-start | bytes 2621440 | tf_op jit(solution)/shard_map/all_to_all | solution.py:354
  (29 other events, 196.3 us)

commit v6 on v5

--- a/solution.py
+++ b/solution.py
@@ -14,6 +14,8 @@
 loss_scale = 64.0
 eps_norm = 1e-06
 
+LOWEST = -3.4e38
+
 ALL = ("peer", "dp", "tx", "tz")
 
 OWN, NEAR, WRAP, FAR = range(4)
@@ -56,8 +58,10 @@
     return lax.optimization_barrier(blocks)
 
 
-def ring(block, axis):
-    far, near, wrap = [lax.ppermute(block, axis, [(i, i ^ s) for i in range(4)]) for s in (2, 1, 3)]
+def ring(block, axis, prepare=lambda block, step: block):
+    far, near, wrap = [
+        lax.ppermute(prepare(block, step), axis, [(i, i ^ step) for i in range(4)]) for step in (2, 1, 3)
+    ]
     return [block, near, far, wrap]
 
 
@@ -271,16 +275,20 @@
 
 def shard_stats(logits, peer_logits, hit):
     values = wide(logits)
-    own_max = jnp.max(values, axis=-1)
+    own_max = jnp.max(jnp.maximum(values, LOWEST), axis=-1)
     own_sum = jnp.sum(jnp.exp(values - own_max[:, None]), axis=-1)
     target = jnp.sum(jnp.where(hit, values, 0.0), axis=-1)
     own_max, own_sum, target, peer_logits = tied(own_max, own_sum, target, peer_logits)
     peer_values = wide(peer_logits)
-    peer_max = jnp.max(peer_values, axis=-1)
+    peer_max = jnp.max(jnp.maximum(peer_values, LOWEST), axis=-1)
     peer_exp = jnp.exp(peer_values - peer_max[:, None])
     peer_sum = jnp.sum(peer_exp, axis=-1)
     cross = jnp.sum(peer_exp * (peer_values - values), axis=-1)
-    return jnp.stack([own_max, own_sum, peer_max, peer_sum, target, cross]), peer_logits
+    row = lax.broadcasted_iota(jnp.int32, (6, own_max.shape[0]), 0)
+    stats = jnp.zeros(row.shape, jnp.float32)
+    for k, part in enumerate((own_max, own_sum, peer_max, peer_sum, target, cross)):
+        stats = jnp.where(row == k, part[None], stats)
+    return stats, peer_logits
 
 
 def norm_backward_kernel(count, *refs):
@@ -325,13 +333,14 @@
     stats, peer_logits = shard_stats(logits, peer_logits, hit)
     stats = merge(ring(stats, "tz"))
     stats = merge(ring(stats, "tx"))
-    stats = ring(stats, "dp")
-    stats = merge([stats[0]] + [turned(stats[s], s, 1) for s in (1, 2, 3)])
+    stats = merge(ring(stats, "dp", lambda block, step: turned(block, step, 1)))
     own_log = stats[0] + jnp.log(stats[1])
     peer_log = stats[2] + jnp.log(stats[3])
     values, peer_values = wide(logits), wide(peer_logits)
-    position = lax.broadcasted_iota(jnp.int32, (tokens // LEN, LEN), 1)
-    weights = (position < all_lengths[:, None]).astype(jnp.float32).reshape(tokens)
+    sequence = lax.broadcasted_iota(jnp.int32, (all_lengths.shape[0], tokens), 0)
+    token = lax.broadcasted_iota(jnp.int32, sequence.shape, 1)
+    limits = jnp.sum(jnp.where(token // LEN == sequence, all_lengths[:, None], 0), axis=0)
+    weights = (lax.broadcasted_iota(jnp.int32, (tokens,), 0) % LEN < limits).astype(jnp.float32)
 
     grad_logits = (
         loss_scale

time: 163 us -> 166 us (1.018)
  waiting for transfers between devices: 48.7 us -> 43.2 us
  local copies, waits for them, and re-layouts: 14.4 us -> 18.8 us
  starting transfers between devices: 55.3 us -> 58.3 us
  matrix products: 16.4 us -> 14.2 us
  Pallas kernels: 15 us -> 17 us
    unnamed x29 -> x25, local copies, waits for them, and re-layouts: 8.8 us -> 13.4 us
    ppermute x9, waiting for transfers between devices: 14.4 us -> 11.7 us  [permute(): lax.ppermute(block, ALL, [(index(*p), index(*move(*p))) for p in places])]
    ppermute x16, starting transfers between devices: 17.8 us -> 20.1 us  [swap(): return lax.ppermute(block, axis, [(i, i ^ step) for i in range(4)])]
    dot_general x12, matrix products: 16.4 us -> 14.2 us  [product(): lax.dot_general(block.reshape(-1, voc), columns, (((1,), (1,)), ((), ()))...]
    pallas_call x4, Pallas kernels: 13.7 us -> 15.7 us  [add_logits(): pl.pallas_call(make_kernel(count, *plan), out_shape=jax.ShapeDtypeStruct(...]
    ppermute x12, waiting for transfers between devices: 11.5 us -> 9.8 us  [ring(): lax.ppermute(prepare(block, step), axis, [(i, i ^ step) for i in range(4)])]
  transfers between devices with their start and end apart: 39 -> 39, of which waited for: 18 -> 20; matrix products, arithmetic and copies ran while one was open for 12% -> 12% of each run, Pallas kernels for 6% -> 7%
where the time goes in v6:
time: 166 us; the launch traced here: 165 us
  starting transfers between devices  58.3 us (35%)
  waiting for transfers between devices  43.2 us (26%)
  local copies, waits for them, and re-layouts  18.8 us (11%)
  Pallas kernels  17 us (10%)
  matrix products  14.2 us (9%)
  other arithmetic  7.77 us (5%)
  between operations  5.74 us (3%)
    ppermute x16, starting transfers between devices, swap(): return lax.ppermute(block, axis, [(i, i ^ step) for i in range(4)])  20.1 us
    ppermute x12, starting transfers between devices, ring(): lax.ppermute(prepare(block, step), axis, [(i, i ^ step) for i in range(4)])  19.8 us
    pallas_call x4, Pallas kernels, add_logits(): pl.pallas_call(make_kernel(count, *plan), out_shape=jax.ShapeDtypeStruct(...  15.7 us
    dot_general x12, matrix products, product(): lax.dot_general(block.reshape(-1, voc), columns, (((1,), (1,)), ((), ()))...  14.2 us
    unnamed x25, local copies, waits for them, and re-layouts  13.4 us
    ppermute x9, starting transfers between devices, permute(): lax.ppermute(block, ALL, [(index(*p), index(*move(*p))) for p in places])  13 us
    ppermute x9, waiting for transfers between devices, permute(): lax.ppermute(block, ALL, [(index(*p), index(*move(*p))) for p in places])  11.7 us
    all_to_all x1, waiting for transfers between devices, local(): lax.all_to_all(spread, ('tx', 'tz'), split_axis=0, concat_axis=0, tiled=T...  10.5 us
  transfers between devices with their start and end apart: 39, of which 20 were waited for; matrix products, arithmetic and copies ran while one was open for 12% of the time, Pallas kernels for 7%

profile of v6, /device:TPU:0, one launch (start us, length us, event | category | flops | bytes accessed | tf_op | source)
XLA Modules:
  0.0 165.1 jit_solution(8473530836417879079)
XLA Ops:
  3.5 2.2 %collective-permute-start.1 = (bf16[64,5120]{1,0:T(8,128)(2,1)S(1)}, bf16[64,5120]{1,0:T(8,128)(2,1)S(1)}, u32[]{:S(2)}, u32[]{:S(2)}) collective-permute-start(bf16[64,5120]{1,0:T(8,128)(2,1)S(1)} %dynamic-slice_bitcast_fusion.4), channel_id=1, source_target_pairs={{0,48},{1,49},{2,50},{3,51},{4,52},{5,53},{6,54},{7,55},{8,56},{9,... | collective-permute-start | bytes 1966088 | tf_op jit(solution)/shard_map/ppermute | solution.py:30
  9.6 2.2 %collective-permute-start.4 = (s32[132]{0:T(256)S(1)}, s32[132]{0:T(256)S(1)}, u32[]{:S(2)}, u32[]{:S(2)}) collective-permute-start(s32[132]{0:T(256)S(1)} %constant_dynamic-update-slice_fusion), channel_id=1, source_target_pairs={{0,48},{16,32},{32,16},{48,0},{1,49},{17,33},{33,17},{49,1},{2,50}... | collective-permute-start | bytes 1592 | tf_op jit(solution)/shard_map/ppermute | solution.py:63
  11.7 4.7 %copy-done = bf16[1,5120,1280]{2,1,0:T(8,128)(2,1)S(1)} copy-done((bf16[1,5120,1280]{2,1,0:T(8,128)(2,1)S(1)}, bf16[1,5120,1280]{2,1,0:T(8,128)(2,1)}, u32[]{:S(2)}) %copy-start) | copy-done | bytes 13107224
  18.5 3.1 %shard_map.68.refs_4_ = bf16[512,1280]{1,0:T(8,128)(2,1)S(1)} custom-call(bf16[128,5120]{1,0:T(8,128)(2,1)S(1)} %bitcast.375, f32[1,5120]{1,0:T(1,128)S(1)} %copy-done.4, bf16[5120,1280]{1,0:T(8,128)(2,1)S(1)} %bitcast.369), custom_call_target="tpu_custom_call" | custom-call | flops 1677721600 | bytes 14417920 | tf_op jit(solution)/shard_map/pallas_call | solution.py:178
  21.7 2.8 %collective-permute-start.9 = (bf16[64,5120]{1,0:T(8,128)(2,1)S(1)}, bf16[64,5120]{1,0:T(8,128)(2,1)}, u32[]{:S(2)}, u32[]{:S(2)}) collective-permute-start(bf16[64,5120]{1,0:T(8,128)(2,1)S(1)} %collective-permute-done.1.refs_1_), channel_id=1, source_target_pairs={{0,12},{1,13},{2,14},{3,15},{4,8},{5,9},{6,10},{7,11},{8,4},{9,5},... | collective-permute-start | bytes 1966088 | tf_op jit(solution)/shard_map/ppermute | solution.py:30
  24.8 3.7 %shard_map.69.refs_4_ = bf16[512,1280]{1,0:T(8,128)(2,1)S(1)} custom-call(bf16[64,5120]{1,0:T(8,128)(2,1)S(1)} %collective-permute-done.refs_0_, bf16[64,5120]{1,0:T(8,128)(2,1)S(1)} %collective-permute-done.1.refs_1_, f32[1,5120]{1,0:T(1,128)S(1)} %copy-done.4, bf16[5120,1280]{1,0:T(8,128)(2,1)S(1)} %bitcast.370, ...), custom_call_target="tpu_custom_call", output_to_operand_aliasing={{}: (4, {})} | custom-call | flops 1677721600 | bytes 14417920 | tf_op jit(solution)/shard_map/pallas_call | solution.py:178
  28.5 3.8 %collective-permute-done.5.refs_0_ = bf16[64,5120]{1,0:T(8,128)(2,1)S(1)} collective-permute-done((bf16[64,5120]{1,0:T(8,128)(2,1)S(1)}, bf16[64,5120]{1,0:T(8,128)(2,1)S(1)}, u32[]{:S(2)}, u32[]{:S(2)}) %collective-permute-start.5) | collective-permute-done | bytes 655392 | tf_op jit(solution)/shard_map/ppermute | solution.py:30
  34.7 2.1 %collective-permute-start.7 = (bf16[32,5120]{1,0:T(8,128)(2,1)}, bf16[32,5120]{1,0:T(8,128)(2,1)}, u32[]{:S(2)}, u32[]{:S(2)}) collective-permute-start(bf16[32,5120]{1,0:T(8,128)(2,1)} %get-tuple-element.68), channel_id=1, source_target_pairs={{0,12},{1,13},{2,14},{3,15},{4,8},{5,9},{6,10},{7,11},{8,4},{9,5},... | collective-permute-start | bytes 983048 | tf_op jit(solution)/shard_map/ppermute | solution.py:30
  36.8 4.7 %copy-done.2 = bf16[1,5120,1280]{2,1,0:T(8,128)(2,1)S(1)} copy-done((bf16[1,5120,1280]{2,1,0:T(8,128)(2,1)S(1)}, bf16[1,5120,1280]{2,1,0:T(8,128)(2,1)}, u32[]{:S(2)}) %copy-start.2) | copy-done | bytes 13107224
  41.5 4.6 %shard_map.70.refs_5_ = bf16[512,1280]{1,0:T(8,128)(2,1)S(1)} custom-call(bf16[64,5120]{1,0:T(8,128)(2,1)} %collective-permute-done.8.refs_0_, bf16[64,5120]{1,0:T(8,128)(2,1)} %collective-permute-done.9.refs_1_, f32[1,5120]{1,0:T(1,128)S(1)} %copy-done.5, bf16[5120,1280]{1,0:T(8,128)(2,1)S(1)} %bitcast.371, ...), custom_call_target="tpu_custom_call", output_to_operand_aliasing={{}: (4, {})} | custom-call | flops 1677721600 | bytes 14417920 | tf_op jit(solution)/shard_map/pallas_call | solution.py:178
  46.2 4.4 %shard_map.71 = bf16[512,1280]{1,0:T(8,128)(2,1)S(1)} custom-call(bf16[64,5120]{1,0:T(8,128)(2,1)S(1)} %collective-permute-done.5.refs_0_, bf16[32,5120]{1,0:T(8,128)(2,1)} %collective-permute-done.6.refs_1_, bf16[32,5120]{1,0:T(8,128)(2,1)} %collective-permute-done.7.refs_2_, f32[1,5120]{1,0:T(1,128)S(1)} %copy-done.5, ...), custom_call_target="tpu_custom_call", output_to_operand_aliasing={{}: (5, {})} | custom-call | flops 1677721600 | bytes 14417920 | tf_op jit(solution)/shard_map/pallas_call | solution.py:178
  57.2 3.6 %collective-permute-start.12 = (f32[6,512]{1,0:T(8,128)S(1)}, f32[6,512]{1,0:T(8,128)S(1)}, u32[]{:S(2)}, u32[]{:S(2)}) collective-permute-start(f32[6,512]{1,0:T(8,128)S(1)} %select_select_fusion), channel_id=1, source_target_pairs={{0,2},{1,3},{2,0},{3,1},{4,6},{5,7},{6,4},{7,5},{8,10},{9,11},{10,... | collective-permute-start | bytes 36872 | tf_op jit(solution)/shard_map/ppermute | solution.py:63
  62.7 3.1 %collective-permute-done.13 = f32[6,512]{1,0:T(8,128)S(1)} collective-permute-done((f32[6,512]{1,0:T(8,128)S(1)}, f32[6,512]{1,0:T(8,128)S(1)}, u32[]{:S(2)}, u32[]{:S(2)}) %collective-permute-start.13) | collective-permute-done | bytes 12320 | tf_op jit(solution)/shard_map/ppermute | solution.py:63
  76.4 2.2 %collective-permute-start.19 = (f32[6,512]{1,0:T(8,128)S(1)}, f32[6,512]{1,0:T(8,128)S(1)}, u32[]{:S(2)}, u32[]{:S(2)}) collective-permute-start(f32[6,512]{1,0:T(8,128)S(1)} %pad_maximum_fusion.10), channel_id=1, source_target_pairs={{0,48},{16,32},{32,16},{48,0},{1,49},{17,33},{33,17},{49,1},{2,50}... | collective-permute-start | bytes 36872 | tf_op jit(solution)/shard_map/ppermute | solution.py:63
  88.0 2.2 %collective-permute-start.24 = (bf16[2,2,2,4,8,1280]{5,4,3,2,1,0:T(8,128)(2,1)S(1)}, bf16[2,2,2,4,8,1280]{5,4,3,2,1,0:T(8,128)(2,1)S(1)}, u32[]{:S(2)}, u32[]{:S(2)}) collective-permute-start(bf16[2,2,2,4,8,1280]{5,4,3,2,1,0:T(8,128)(2,1)S(1)} %fusion.51), channel_id=1, source_target_pairs={{0,12},{4,8},{8,4},{12,0},{1,13},{5,9},{9,5},{13,1},{2,14},{6,10},... | collective-permute-start | bytes 1966088 | tf_op jit(solution)/shard_map/ppermute | solution.py:246
  96.2 2.4 %collective-permute-done.20 = bf16[2,2,2,4,8,1280]{5,4,3,2,1,0:T(8,128)(2,1)S(1)} collective-permute-done((bf16[2,2,2,4,8,1280]{5,4,3,2,1,0:T(8,128)(2,1)S(1)}, bf16[2,2,2,4,8,1280]{5,4,3,2,1,0:T(8,128)(2,1)S(1)}, u32[]{:S(2)}, u32[]{:S(2)}) %collective-permute-start.20) | collective-permute-done | bytes 655392 | tf_op jit(solution)/shard_map/ppermute | solution.py:246
  99.8 2.5 %collective-permute-start.21 = (bf16[2,2,4,8,1280]{4,3,2,1,0:T(8,128)(2,1)S(1)}, bf16[2,2,4,8,1280]{4,3,2,1,0:T(8,128)(2,1)S(1)}, u32[]{:S(2)}, u32[]{:S(2)}) collective-permute-start(bf16[2,2,4,8,1280]{4,3,2,1,0:T(8,128)(2,1)S(1)} %fusion.78), channel_id=1, source_target_pairs={{0,12},{4,8},{8,4},{12,0},{1,13},{5,9},{9,5},{13,1},{2,14},{6,10},... | collective-permute-start | bytes 983048 | tf_op jit(solution)/shard_map/ppermute | solution.py:246
  114.8 2.2 %collective-permute-start.26 = (bf16[2,4,8,1280]{3,2,1,0:T(8,128)(2,1)S(1)}, bf16[2,4,8,1280]{3,2,1,0:T(8,128)(2,1)S(1)}, u32[]{:S(2)}, u32[]{:S(2)}) collective-permute-start(bf16[2,4,8,1280]{3,2,1,0:T(8,128)(2,1)S(1)} %get-tuple-element.56), channel_id=1, source_target_pairs={{0,3},{1,2},{2,1},{3,0},{4,7},{5,6},{6,5},{7,4},{8,11},{9,10},{10,... | collective-permute-start | bytes 491528 | tf_op jit(solution)/shard_map/ppermute | solution.py:246
  121.2 2.8 %collective-permute-start.23 = (bf16[4,8,1280]{2,1,0:T(8,128)(2,1)S(1)}, bf16[4,8,1280]{2,1,0:T(8,128)(2,1)S(1)}, u32[]{:S(2)}, u32[]{:S(2)}) collective-permute-start(bf16[4,8,1280]{2,1,0:T(8,128)(2,1)S(1)} %fusion.129), channel_id=1, source_target_pairs={{0,3},{1,2},{2,1},{3,0},{4,7},{5,6},{6,5},{7,4},{8,11},{9,10},{10,... | collective-permute-start | bytes 245768 | tf_op jit(solution)/shard_map/ppermute | solution.py:246
  130.8 5.3 %collective-permute-done.36 = bf16[2,8,5120]{2,1,0:T(8,128)(2,1)S(1)} collective-permute-done((bf16[2,8,5120]{2,1,0:T(8,128)(2,1)S(1)}, bf16[2,8,5120]{2,1,0:T(8,128)(2,1)S(1)}, u32[]{:S(2)}, u32[]{:S(2)}) %collective-permute-start.36) | collective-permute-done | bytes 163872 | tf_op jit(solution)/shard_map/ppermute | solution.py:30
  136.1 2.2 %collective-permute-start.37 = (bf16[8,5120]{1,0:T(8,128)(2,1)S(1)}, bf16[8,5120]{1,0:T(8,128)(2,1)S(1)}, u32[]{:S(2)}, u32[]{:S(2)}) collective-permute-start(bf16[8,5120]{1,0:T(8,128)(2,1)S(1)} %fusion.128), channel_id=1, source_target_pairs={{0,48},{1,49},{2,50},{3,51},{4,52},{5,53},{6,54},{7,55},{8,56},{9,... | collective-permute-start | bytes 245768 | tf_op jit(solution)/shard_map/ppermute | solution.py:30
  139.3 2.6 %collective-permute-done.37 = bf16[8,5120]{1,0:T(8,128)(2,1)S(1)} collective-permute-done((bf16[8,5120]{1,0:T(8,128)(2,1)S(1)}, bf16[8,5120]{1,0:T(8,128)(2,1)S(1)}, u32[]{:S(2)}, u32[]{:S(2)}) %collective-permute-start.37) | collective-permute-done | bytes 81952 | tf_op jit(solution)/shard_map/ppermute | solution.py:30
  143.2 5.3 %all-to-all-start = ((bf16[16,8,5120]{2,1,0:T(8,128)(2,1)}), bf16[16,8,5120]{2,1,0:T(8,128)(2,1)S(1)}, u32[]{:S(2)}, u32[]{:S(2)}) async-start(bf16[16,8,5120]{2,1,0:T(8,128)(2,1)} %shard_map.72), calls=%async_computation | async-start | bytes 2621440 | tf_op jit(solution)/shard_map/all_to_all | solution.py:363
  152.4 10.5 %all-to-all-done = bf16[16,8,5120]{2,1,0:T(8,128)(2,1)S(1)} async-done(((bf16[16,8,5120]{2,1,0:T(8,128)(2,1)}), bf16[16,8,5120]{2,1,0:T(8,128)(2,1)S(1)}, u32[]{:S(2)}, u32[]{:S(2)}) %all-to-all-start) | async-done | bytes 1310752 | tf_op jit(solution)/shard_map/all_to_all | solution.py:363
  (191 shorter events, 74.4 us)
Async XLA Ops:
  1.8 19.8 %collective-permute-start = (bf16[64,5120]{1,0:T(8,128)(2,1)S(1)}, bf16[64,5120]{1,0:T(8,128)(2,1)S(1)}, u32[]{:S(2)}, u32[]{:S(2)}) collective-permute-start(bf16[64,5120]{1,0:T(8,128)(2,1)S(1)} %dynamic-slice_bitcast_fusion.4), channel_id=1, source_target_pairs={{0,16},{1,17},{2,18},{3,19},{4,20},{5,21},{6,22},{7,23},{8,24},{9,... | collective-permute-start | bytes 1966088 | tf_op jit(solution)/shard_map/ppermute | solution.py:30
  3.5 18.1 %collective-permute-start.1 = (bf16[64,5120]{1,0:T(8,128)(2,1)S(1)}, bf16[64,5120]{1,0:T(8,128)(2,1)S(1)}, u32[]{:S(2)}, u32[]{:S(2)}) collective-permute-start(bf16[64,5120]{1,0:T(8,128)(2,1)S(1)} %dynamic-slice_bitcast_fusion.4), channel_id=1, source_target_pairs={{0,48},{1,49},{2,50},{3,51},{4,52},{5,53},{6,54},{7,55},{8,56},{9,... | collective-permute-start | bytes 1966088 | tf_op jit(solution)/shard_map/ppermute | solution.py:30
  7.0 14.6 %collective-permute-start.2 = (s32[132]{0:T(256)S(1)}, s32[132]{0:T(256)S(1)}, u32[]{:S(2)}, u32[]{:S(2)}) collective-permute-start(s32[132]{0:T(256)S(1)} %constant_dynamic-update-slice_fusion), channel_id=1, source_target_pairs={{0,16},{16,0},{32,48},{48,32},{1,17},{17,1},{33,49},{49,33},{2,18}... | collective-permute-start | bytes 1592 | tf_op jit(solution)/shard_map/ppermute | solution.py:63
  7.7 13.9 %collective-permute-start.3 = (s32[132]{0:T(256)S(1)}, s32[132]{0:T(256)S(1)}, u32[]{:S(2)}, u32[]{:S(2)}) collective-permute-start(s32[132]{0:T(256)S(1)} %constant_dynamic-update-slice_fusion), channel_id=1, source_target_pairs={{0,32},{16,48},{32,0},{48,16},{1,33},{17,49},{33,1},{49,17},{2,34}... | collective-permute-start | bytes 1592 | tf_op jit(solution)/shard_map/ppermute | solution.py:63
  9.6 12.1 %collective-permute-start.4 = (s32[132]{0:T(256)S(1)}, s32[132]{0:T(256)S(1)}, u32[]{:S(2)}, u32[]{:S(2)}) collective-permute-start(s32[132]{0:T(256)S(1)} %constant_dynamic-update-slice_fusion), channel_id=1, source_target_pairs={{0,48},{16,32},{32,16},{48,0},{1,49},{17,33},{33,17},{49,1},{2,50}... | collective-permute-start | bytes 1592 | tf_op jit(solution)/shard_map/ppermute | solution.py:63
  21.6 10.7 %collective-permute-start.5 = (bf16[64,5120]{1,0:T(8,128)(2,1)S(1)}, bf16[64,5120]{1,0:T(8,128)(2,1)S(1)}, u32[]{:S(2)}, u32[]{:S(2)}) collective-permute-start(bf16[64,5120]{1,0:T(8,128)(2,1)S(1)} %collective-permute-done.1.refs_1_), channel_id=1, source_target_pairs={{0,16},{1,17},{2,18},{3,19},{4,20},{5,21},{6,22},{7,23},{8,24},{9,... | collective-permute-start | bytes 1966088 | tf_op jit(solution)/shard_map/ppermute | solution.py:30
  21.7 15.1 %collective-permute-start.9 = (bf16[64,5120]{1,0:T(8,128)(2,1)S(1)}, bf16[64,5120]{1,0:T(8,128)(2,1)}, u32[]{:S(2)}, u32[]{:S(2)}) collective-permute-start(bf16[64,5120]{1,0:T(8,128)(2,1)S(1)} %collective-permute-done.1.refs_1_), channel_id=1, source_target_pairs={{0,12},{1,13},{2,14},{3,15},{4,8},{5,9},{6,10},{7,11},{8,4},{9,5},... | collective-permute-start | bytes 1966088 | tf_op jit(solution)/shard_map/ppermute | solution.py:30
  24.6 12.2 %collective-permute-start.8 = (bf16[64,5120]{1,0:T(8,128)(2,1)S(1)}, bf16[64,5120]{1,0:T(8,128)(2,1)}, u32[]{:S(2)}, u32[]{:S(2)}) collective-permute-start(bf16[64,5120]{1,0:T(8,128)(2,1)S(1)} %collective-permute-done.refs_0_), channel_id=1, source_target_pairs={{0,4},{1,5},{2,6},{3,7},{4,0},{5,1},{6,2},{7,3},{8,12},{9,13},{10,... | collective-permute-start | bytes 1966088 | tf_op jit(solution)/shard_map/ppermute | solution.py:30
  33.2 12.9 %collective-permute-start.6 = (bf16[32,5120]{1,0:T(8,128)(2,1)}, bf16[32,5120]{1,0:T(8,128)(2,1)}, u32[]{:S(2)}, u32[]{:S(2)}) collective-permute-start(bf16[32,5120]{1,0:T(8,128)(2,1)} %get-tuple-element.69), channel_id=1, source_target_pairs={{0,4},{1,5},{2,6},{3,7},{4,0},{5,1},{6,2},{7,3},{8,12},{9,13},{10,... | collective-permute-start | bytes 983048 | tf_op jit(solution)/shard_map/ppermute | solution.py:30
  34.7 11.4 %collective-permute-start.7 = (bf16[32,5120]{1,0:T(8,128)(2,1)}, bf16[32,5120]{1,0:T(8,128)(2,1)}, u32[]{:S(2)}, u32[]{:S(2)}) collective-permute-start(bf16[32,5120]{1,0:T(8,128)(2,1)} %get-tuple-element.68), channel_id=1, source_target_pairs={{0,12},{1,13},{2,14},{3,15},{4,8},{5,9},{6,10},{7,11},{8,4},{9,5},... | collective-permute-start | bytes 983048 | tf_op jit(solution)/shard_map/ppermute | solution.py:30
  86.8 11.7 %collective-permute-start.20 = (bf16[2,2,2,4,8,1280]{5,4,3,2,1,0:T(8,128)(2,1)S(1)}, bf16[2,2,2,4,8,1280]{5,4,3,2,1,0:T(8,128)(2,1)S(1)}, u32[]{:S(2)}, u32[]{:S(2)}) collective-permute-start(bf16[2,2,2,4,8,1280]{5,4,3,2,1,0:T(8,128)(2,1)S(1)} %fusion.48), channel_id=1, source_target_pairs={{0,4},{4,0},{8,12},{12,8},{1,5},{5,1},{9,13},{13,9},{2,6},{6,2},{1... | collective-permute-start | bytes 1966088 | tf_op jit(solution)/shard_map/ppermute | solution.py:246
  88.0 16.1 %collective-permute-start.24 = (bf16[2,2,2,4,8,1280]{5,4,3,2,1,0:T(8,128)(2,1)S(1)}, bf16[2,2,2,4,8,1280]{5,4,3,2,1,0:T(8,128)(2,1)S(1)}, u32[]{:S(2)}, u32[]{:S(2)}) collective-permute-start(bf16[2,2,2,4,8,1280]{5,4,3,2,1,0:T(8,128)(2,1)S(1)} %fusion.51), channel_id=1, source_target_pairs={{0,12},{4,8},{8,4},{12,0},{1,13},{5,9},{9,5},{13,1},{2,14},{6,10},... | collective-permute-start | bytes 1966088 | tf_op jit(solution)/shard_map/ppermute | solution.py:246
  92.6 13.8 %collective-permute-start.28 = (bf16[2,2,2,4,8,1280]{5,4,3,2,1,0:T(8,128)(2,1)S(1)}, bf16[2,2,2,4,8,1280]{5,4,3,2,1,0:T(8,128)(2,1)S(1)}, u32[]{:S(2)}, u32[]{:S(2)}) collective-permute-start(bf16[2,2,2,4,8,1280]{5,4,3,2,1,0:T(8,128)(2,1)S(1)} %fusion.54), channel_id=1, source_target_pairs={{0,1},{1,0},{2,3},{3,2},{4,5},{5,4},{6,7},{7,6},{8,9},{9,8},{10,11... | collective-permute-start | bytes 1966088 | tf_op jit(solution)/shard_map/ppermute | solution.py:246
  94.0 16.1 %collective-permute-start.32 = (bf16[2,2,2,4,8,1280]{5,4,3,2,1,0:T(8,128)(2,1)S(1)}, bf16[2,2,2,4,8,1280]{5,4,3,2,1,0:T(8,128)(2,1)S(1)}, u32[]{:S(2)}, u32[]{:S(2)}) collective-permute-start(bf16[2,2,2,4,8,1280]{5,4,3,2,1,0:T(8,128)(2,1)S(1)} %fusion.57), channel_id=1, source_target_pairs={{0,3},{1,2},{2,1},{3,0},{4,7},{5,6},{6,5},{7,4},{8,11},{9,10},{10,... | collective-permute-start | bytes 1966088 | tf_op jit(solution)/shard_map/ppermute | solution.py:246
  99.8 14.5 %collective-permute-start.21 = (bf16[2,2,4,8,1280]{4,3,2,1,0:T(8,128)(2,1)S(1)}, bf16[2,2,4,8,1280]{4,3,2,1,0:T(8,128)(2,1)S(1)}, u32[]{:S(2)}, u32[]{:S(2)}) collective-permute-start(bf16[2,2,4,8,1280]{4,3,2,1,0:T(8,128)(2,1)S(1)} %fusion.78), channel_id=1, source_target_pairs={{0,12},{4,8},{8,4},{12,0},{1,13},{5,9},{9,5},{13,1},{2,14},{6,10},... | collective-permute-start | bytes 983048 | tf_op jit(solution)/shard_map/ppermute | solution.py:246
  105.3 9.5 %collective-permute-start.25 = (bf16[2,2,4,8,1280]{4,3,2,1,0:T(8,128)(2,1)S(1)}, bf16[2,2,4,8,1280]{4,3,2,1,0:T(8,128)(2,1)S(1)}, u32[]{:S(2)}, u32[]{:S(2)}) collective-permute-start(bf16[2,2,4,8,1280]{4,3,2,1,0:T(8,128)(2,1)S(1)} %get-tuple-element.64), channel_id=1, source_target_pairs={{0,4},{4,0},{8,12},{12,8},{1,5},{5,1},{9,13},{13,9},{2,6},{6,2},{1... | collective-permute-start | bytes 983048 | tf_op jit(solution)/shard_map/ppermute | solution.py:246
  107.6 9.4 %collective-permute-start.29 = (bf16[2,2,4,8,1280]{4,3,2,1,0:T(8,128)(2,1)S(1)}, bf16[2,2,4,8,1280]{4,3,2,1,0:T(8,128)(2,1)S(1)}, u32[]{:S(2)}, u32[]{:S(2)}) collective-permute-start(bf16[2,2,4,8,1280]{4,3,2,1,0:T(8,128)(2,1)S(1)} %fusion.93), channel_id=1, source_target_pairs={{0,3},{1,2},{2,1},{3,0},{4,7},{5,6},{6,5},{7,4},{8,11},{9,10},{10,... | collective-permute-start | bytes 983048 | tf_op jit(solution)/shard_map/ppermute | solution.py:246
  111.3 8.0 %collective-permute-start.33 = (bf16[2,2,4,8,1280]{4,3,2,1,0:T(8,128)(2,1)S(1)}, bf16[2,2,4,8,1280]{4,3,2,1,0:T(8,128)(2,1)S(1)}, u32[]{:S(2)}, u32[]{:S(2)}) collective-permute-start(bf16[2,2,4,8,1280]{4,3,2,1,0:T(8,128)(2,1)S(1)} %get-tuple-element.66), channel_id=1, source_target_pairs={{0,1},{1,0},{2,3},{3,2},{4,5},{5,4},{6,7},{7,6},{8,9},{9,8},{10,11... | collective-permute-start | bytes 983048 | tf_op jit(solution)/shard_map/ppermute | solution.py:246
  114.4 6.8 %collective-permute-start.22 = (bf16[2,4,8,1280]{3,2,1,0:T(8,128)(2,1)S(1)}, bf16[2,4,8,1280]{3,2,1,0:T(8,128)(2,1)S(1)}, u32[]{:S(2)}, u32[]{:S(2)}) collective-permute-start(bf16[2,4,8,1280]{3,2,1,0:T(8,128)(2,1)S(1)} %get-tuple-element.54), channel_id=1, source_target_pairs={{0,1},{1,0},{2,3},{3,2},{4,5},{5,4},{6,7},{7,6},{8,9},{9,8},{10,11... | collective-permute-start | bytes 491528 | tf_op jit(solution)/shard_map/ppermute | solution.py:246
  114.8 9.2 %collective-permute-start.26 = (bf16[2,4,8,1280]{3,2,1,0:T(8,128)(2,1)S(1)}, bf16[2,4,8,1280]{3,2,1,0:T(8,128)(2,1)S(1)}, u32[]{:S(2)}, u32[]{:S(2)}) collective-permute-start(bf16[2,4,8,1280]{3,2,1,0:T(8,128)(2,1)S(1)} %get-tuple-element.56), channel_id=1, source_target_pairs={{0,3},{1,2},{2,1},{3,0},{4,7},{5,6},{6,5},{7,4},{8,11},{9,10},{10,... | collective-permute-start | bytes 491528 | tf_op jit(solution)/shard_map/ppermute | solution.py:246
  117.1 7.1 %collective-permute-start.30 = (bf16[2,4,8,1280]{3,2,1,0:T(8,128)(2,1)S(1)}, bf16[2,4,8,1280]{3,2,1,0:T(8,128)(2,1)S(1)}, u32[]{:S(2)}, u32[]{:S(2)}) collective-permute-start(bf16[2,4,8,1280]{3,2,1,0:T(8,128)(2,1)S(1)} %get-tuple-element.58), channel_id=1, source_target_pairs={{0,4},{4,0},{8,12},{12,8},{1,5},{5,1},{9,13},{13,9},{2,6},{6,2},{1... | collective-permute-start | bytes 491528 | tf_op jit(solution)/shard_map/ppermute | solution.py:246
  119.4 6.6 %collective-permute-start.34 = (bf16[2,4,8,1280]{3,2,1,0:T(8,128)(2,1)S(1)}, bf16[2,4,8,1280]{3,2,1,0:T(8,128)(2,1)S(1)}, u32[]{:S(2)}, u32[]{:S(2)}) collective-permute-start(bf16[2,4,8,1280]{3,2,1,0:T(8,128)(2,1)S(1)} %get-tuple-element.60), channel_id=1, source_target_pairs={{0,12},{4,8},{8,4},{12,0},{1,13},{5,9},{9,5},{13,1},{2,14},{6,10},... | collective-permute-start | bytes 491528 | tf_op jit(solution)/shard_map/ppermute | solution.py:246
  121.2 5.7 %collective-permute-start.23 = (bf16[4,8,1280]{2,1,0:T(8,128)(2,1)S(1)}, bf16[4,8,1280]{2,1,0:T(8,128)(2,1)S(1)}, u32[]{:S(2)}, u32[]{:S(2)}) collective-permute-start(bf16[4,8,1280]{2,1,0:T(8,128)(2,1)S(1)} %fusion.129), channel_id=1, source_target_pairs={{0,3},{1,2},{2,1},{3,0},{4,7},{5,6},{6,5},{7,4},{8,11},{9,10},{10,... | collective-permute-start | bytes 245768 | tf_op jit(solution)/shard_map/ppermute | solution.py:246
  143.2 19.8 %all-to-all-start = ((bf16[16,8,5120]{2,1,0:T(8,128)(2,1)}), bf16[16,8,5120]{2,1,0:T(8,128)(2,1)S(1)}, u32[]{:S(2)}, u32[]{:S(2)}) async-start(bf16[16,8,5120]{2,1,0:T(8,128)(2,1)} %shard_map.72), calls=%async_computation | async-start | bytes 2621440 | tf_op jit(solution)/shard_map/all_to_all | solution.py:363
  (27 other events, 224.7 us)

commit v7 on v6

--- a/solution.py
+++ b/solution.py
@@ -78,23 +78,23 @@
     p = swap_y(mine, (1, 3))
     q = swap_y(mine, (3, 1))
     ints = ring(ints, "dp")
-    logits = add_logits((block,), OWN_PLAN, gain_row, matrix, tokens)
+    logits, matrix = add_logits((block,), OWN_PLAN, gain_row, matrix, tokens)
     p, q, logits, *ints = tied(p, q, logits, *ints)
     far = swap_y(q, (1, 3))
     p_side, q_side = swap_u(p, 1), swap_u(q, 3)
-    logits = add_logits((p, q), HELD_PLAN, gain_row, matrix, tokens, logits)
+    logits, matrix = add_logits((p, q), HELD_PLAN, gain_row, matrix, tokens, logits)
     far, logits = tied(far, logits)
     far_sides = [swap_u(far[: half // 2], 1), swap_u(far[half // 2 :], 3)]
-    logits = add_logits((p_side, q_side), OTHER_PLAN, gain_row, matrix, tokens, logits)
-    logits = add_logits((far, *far_sides), FAR_PLAN, gain_row, matrix, tokens, logits)
-    return logits, [ints[s] for s in (0, 1, 3, 2)]
-
-
-def make_kernel(count, loads, stores):
+    logits, matrix = add_logits((p_side, q_side), OTHER_PLAN, gain_row, matrix, tokens, logits)
+    logits, matrix = add_logits((far, *far_sides), FAR_PLAN, gain_row, matrix, tokens, logits)
+    return logits, matrix, [ints[s] for s in (0, 1, 3, 2)]
+
+
+def make_kernel(count, streamed, loads, stores):
     def kernel(*refs):
         sources = refs[:count]
         gain_ref, head_ref = refs[count : count + 2]
-        out_ref, rows, sums, total, block, sems = refs[-6:]
+        out_ref, held_head, rows, sums, total, block, sems, head_sems = refs[-8:]
         width = rows.shape[1]
         held = parity() * 64
         p_first = 128 * (NEAR + core() * (WRAP - NEAR))
@@ -110,7 +110,15 @@
                     sources[source].at[pl.ds(start, length)], rows.at[pl.ds(to, length)], sems.at[len(copies)]
                 )
             )
-        for copy in copies:
+        depth = 1024
+        fetches = []
+        if streamed:
+            for c in range(0, width, depth // 2):
+                piece = pl.ds(c, depth // 2)
+                fetches.append(
+                    pltpu.make_async_copy(head_ref.at[piece], held_head.at[piece], head_sems.at[len(fetches)])
+                )
+        for copy in copies + fetches:
             copy.start()
         for copy in copies:
             copy.wait()
@@ -135,9 +143,10 @@
                 states = rows[piece, c : c + TILE].astype(jnp.float32)
                 rows[piece, c : c + TILE] = (states * inverse * gain_ref[:, c : c + TILE]).astype(jnp.bfloat16)
 
-        depth = 1024
         for c in range(0, width, depth):
-            part = jnp.dot(rows[:, c : c + depth], head_ref[c : c + depth, :], preferred_element_type=jnp.float32)
+            for copy in fetches[2 * c // depth : 2 * c // depth + 2]:
+                copy.wait()
+            part = jnp.dot(rows[:, c : c + depth], held_head[c : c + depth, :], preferred_element_type=jnp.float32)
             if c == 0:
                 total[...] = part
             elif c + depth < width:
@@ -174,22 +183,27 @@
     anywhere = pl.BlockSpec(memory_space=pl.ANY)
     count = len(sources)
     rows = sum(piece[2] for piece in plan[0])
+    streamed = filled is None
     operands = [*sources, gain_row, matrix] + ([] if filled is None else [filled])
     return pl.pallas_call(
-        make_kernel(count, *plan),
-        out_shape=jax.ShapeDtypeStruct((tokens, voc), jnp.bfloat16),
+        make_kernel(count, streamed, *plan),
+        out_shape=(
+            jax.ShapeDtypeStruct((tokens, voc), jnp.bfloat16),
+            jax.ShapeDtypeStruct(matrix.shape, matrix.dtype),
+        ),
         in_specs=[anywhere] * count
-        + [pl.BlockSpec(memory_space=pltpu.VMEM)] * 2
+        + [pl.BlockSpec(memory_space=pltpu.VMEM), anywhere if streamed else pl.BlockSpec(memory_space=pltpu.VMEM)]
         + ([] if filled is None else [anywhere]),
-        out_specs=anywhere,
+        out_specs=(anywhere, pl.BlockSpec(memory_space=pltpu.VMEM)),
         scratch_shapes=[
             pltpu.VMEM((rows, width), jnp.bfloat16),
             pltpu.VMEM((rows, TILE), jnp.float32),
             pltpu.VMEM((rows, voc), jnp.float32),
             pltpu.VMEM((rows, voc), jnp.bfloat16),
             pltpu.SemaphoreType.DMA((4,)),
+            pltpu.SemaphoreType.DMA((10,)),
         ],
-        input_output_aliases={} if filled is None else {count + 2: 0},
+        input_output_aliases={} if streamed else {count + 1: 1, count + 2: 0},
         compiler_params=pltpu.CompilerParams(vmem_limit_bytes=8 * 1024 * 1024),
         cost_estimate=pl.CostEstimate(
             flops=2 * rows * width * voc, bytes_accessed=2 * width * (voc + rows), transcendentals=0
@@ -308,11 +322,8 @@
             out_ref[k, :, columns] = rows
 
 
-def mean_loss(stats, weights):
-    own_log = stats[0] + jnp.log(stats[1])
-    peer_log = stats[2] + jnp.log(stats[3])
-    per_token = own_log - stats[4] + kl_weight * (stats[5] / stats[3] - peer_log + own_log)
-    sums = jnp.sum((weights * per_token).reshape(4, -1), axis=-1)
+def mean_loss(per_token, weights):
+    sums = jnp.sum(per_token.reshape(4, -1), axis=-1)
     total = (sums[OWN] + sums[NEAR]) + (sums[FAR] + sums[WRAP])
     return (total / jnp.sum(weights)).reshape((1,))
 
@@ -324,7 +335,7 @@
     group = block.shape[0]
     tokens = 4 * group
     voc_shard = matrix.shape[1]
-    logits, ints = gather_logits(block, gain_row, matrix, jnp.concatenate([targets, lengths]))
+    logits, matrix, ints = gather_logits(block, gain_row, matrix, jnp.concatenate([targets, lengths]))
     all_targets = jnp.concatenate([part[:group] for part in ints])
     all_lengths = jnp.concatenate([part[group:] for part in ints])
     peer_logits = lax.ppermute(logits, "peer", [(0, 1), (1, 0)])
@@ -351,8 +362,9 @@
             - kl_weight * jnp.exp(peer_values - peer_log[:, None])
         )
     ).astype(jnp.bfloat16)
-    grad_normed, stats = sum_rows(grad_logits, matrix, stats)
-    loss = mean_loss(stats, weights)
+    per_token = own_log - stats[4] + kl_weight * (stats[5] / stats[3] - peer_log + own_log)
+    grad_normed, per_token = sum_rows(grad_logits, matrix, weights * per_token)
+    loss = mean_loss(per_token, weights)
 
     own = lax.dynamic_slice_in_dim(block, lax.axis_index(("tx", "tz")) * 8, 8, axis=0)
     spread = pl.pallas_call(

time: 166 us -> 171 us (1.030)
  waiting for transfers between devices: 43.2 us -> 52.3 us
  starting transfers between devices: 58.3 us -> 53.1 us
    ppermute x16, waiting for transfers between devices: 9.91 us -> 15.7 us  [swap(): return lax.ppermute(block, axis, [(i, i ^ step) for i in range(4)])]
    ppermute x16, starting transfers between devices: 20.1 us -> 15.7 us  [swap(): return lax.ppermute(block, axis, [(i, i ^ step) for i in range(4)])]
    unnamed x25 -> x14, local copies, waits for them, and re-layouts: 13.4 us -> 17.3 us
    ppermute x9, waiting for transfers between devices: 11.7 us -> 13.9 us  [permute(): lax.ppermute(block, ALL, [(index(*p), index(*move(*p))) for p in places])]
  transfers between devices with their start and end apart: 39 -> 39, of which waited for: 20 -> 19; matrix products, arithmetic and copies ran while one was open for 12% -> 11% of each run, Pallas kernels for 7% -> 7%
where the time goes in v7:
time: 171 us
  starting transfers between devices  53.1 us (31%)
  waiting for transfers between devices  52.3 us (31%)
  local copies, waits for them, and re-layouts  20.4 us (12%)
  Pallas kernels  17.2 us (10%)
  matrix products  14.2 us (8%)
  other arithmetic  7.71 us (5%)
  between operations  5.63 us (3%)
    ppermute x12, starting transfers between devices, ring(): lax.ppermute(prepare(block, step), axis, [(i, i ^ step) for i in range(4)])  19.8 us
    unnamed x14, local copies, waits for them, and re-layouts  17.3 us
    pallas_call x4, Pallas kernels, add_logits(): pl.pallas_call(make_kernel(count, streamed, *plan), out_shape=(jax.ShapeD...  15.9 us
    ppermute x16, waiting for transfers between devices, swap(): return lax.ppermute(block, axis, [(i, i ^ step) for i in range(4)])  15.7 us
    ppermute x16, starting transfers between devices, swap(): return lax.ppermute(block, axis, [(i, i ^ step) for i in range(4)])  15.7 us
    dot_general x12, matrix products, product(): lax.dot_general(block.reshape(-1, voc), columns, (((1,), (1,)), ((), ()))...  14.2 us
    ppermute x9, waiting for transfers between devices, permute(): lax.ppermute(block, ALL, [(index(*p), index(*move(*p))) for p in places])  13.9 us
    ppermute x9, starting transfers between devices, permute(): lax.ppermute(block, ALL, [(index(*p), index(*move(*p))) for p in places])  13.1 us
  transfers between devices with their start and end apart: 39, of which 19 were waited for; matrix products, arithmetic and copies ran while one was open for 11% of the time, Pallas kernels for 7%

profile of v7, /device:TPU:0, one launch (start us, length us, event | category | flops | bytes accessed | tf_op | source)
XLA Modules:
  0.0 170.5 jit_solution(7749110167806330563)
XLA Ops:
  11.7 4.7 %copy-done.2 = bf16[1,5120,1280]{2,1,0:T(8,128)(2,1)S(1)} copy-done((bf16[1,5120,1280]{2,1,0:T(8,128)(2,1)S(1)}, bf16[1,5120,1280]{2,1,0:T(8,128)(2,1)}, u32[]{:S(2)}) %copy-start.2) | copy-done | bytes 13107224
  18.5 4.8 %shard_map.68 = (bf16[512,1280]{1,0:T(8,128)(2,1)S(1)}, bf16[5120,1280]{1,0:T(8,128)(2,1)S(1)}) custom-call(bf16[128,5120]{1,0:T(8,128)(2,1)S(1)} %bitcast.354, f32[1,5120]{1,0:T(1,128)S(1)} %copy-done.4, bf16[5120,1280]{1,0:T(8,128)(2,1)S(1)} %bitcast.353), custom_call_target="tpu_custom_call" | custom-call | flops 1677721600 | bytes 14417920 | tf_op jit(solution)/shard_map/pallas_call | solution.py:188
  23.5 2.8 %collective-permute-start.9 = (bf16[64,5120]{1,0:T(8,128)(2,1)S(1)}, bf16[64,5120]{1,0:T(8,128)(2,1)S(1)}, u32[]{:S(2)}, u32[]{:S(2)}) collective-permute-start(bf16[64,5120]{1,0:T(8,128)(2,1)S(1)} %collective-permute-done.1.refs_1_), channel_id=1, source_target_pairs={{0,12},{1,13},{2,14},{3,15},{4,8},{5,9},{6,10},{7,11},{8,4},{9,5},... | collective-permute-start | bytes 1966088 | tf_op jit(solution)/shard_map/ppermute | solution.py:30
  26.5 3.8 %shard_map.69 = (bf16[512,1280]{1,0:T(8,128)(2,1)S(1)}, bf16[5120,1280]{1,0:T(8,128)(2,1)S(1)}) custom-call(bf16[64,5120]{1,0:T(8,128)(2,1)S(1)} %collective-permute-done.refs_0_, bf16[64,5120]{1,0:T(8,128)(2,1)S(1)} %collective-permute-done.1.refs_1_, f32[1,5120]{1,0:T(1,128)S(1)} %copy-done.4, ...), custom_call_target="tpu_custom_call", output_to_operand_aliasing={{1}: (3, {}), {0}: (4, {})} | custom-call | flops 1677721600 | bytes 14417920 | tf_op jit(solution)/shard_map/pallas_call | solution.py:188
  30.3 3.7 %collective-permute-done.5.refs_0_ = bf16[64,5120]{1,0:T(8,128)(2,1)S(1)} collective-permute-done((bf16[64,5120]{1,0:T(8,128)(2,1)S(1)}, bf16[64,5120]{1,0:T(8,128)(2,1)S(1)}, u32[]{:S(2)}, u32[]{:S(2)}) %collective-permute-start.5) | collective-permute-done | bytes 655392 | tf_op jit(solution)/shard_map/ppermute | solution.py:30
  37.8 3.8 %shard_map.70 = (bf16[512,1280]{1,0:T(8,128)(2,1)S(1)}, bf16[5120,1280]{1,0:T(8,128)(2,1)S(1)}) custom-call(bf16[64,5120]{1,0:T(8,128)(2,1)S(1)} %collective-permute-done.8.refs_0_, bf16[64,5120]{1,0:T(8,128)(2,1)S(1)} %collective-permute-done.9.refs_1_, f32[1,5120]{1,0:T(1,128)S(1)} %copy-done.5, ...), custom_call_target="tpu_custom_call", output_to_operand_aliasing={{1}: (3, {}), {0}: (4, {})} | custom-call | flops 1677721600 | bytes 14417920 | tf_op jit(solution)/shard_map/pallas_call | solution.py:188
  41.6 2.3 %collective-permute-done.7.refs_2_ = bf16[32,5120]{1,0:T(8,128)(2,1)S(1)} collective-permute-done((bf16[32,5120]{1,0:T(8,128)(2,1)S(1)}, bf16[32,5120]{1,0:T(8,128)(2,1)S(1)}, u32[]{:S(2)}, u32[]{:S(2)}) %collective-permute-start.7) | collective-permute-done | bytes 327712 | tf_op jit(solution)/shard_map/ppermute | solution.py:30
  43.9 3.5 %shard_map.71 = (bf16[512,1280]{1,0:T(8,128)(2,1)S(1)}, bf16[5120,1280]{1,0:T(8,128)(2,1)S(1)}) custom-call(bf16[64,5120]{1,0:T(8,128)(2,1)S(1)} %collective-permute-done.5.refs_0_, bf16[32,5120]{1,0:T(8,128)(2,1)S(1)} %collective-permute-done.6.refs_1_, ...), custom_call_target="tpu_custom_call", output_to_operand_aliasing={{1}: (4, {}), {0}: (5, {})} | custom-call | flops 1677721600 | bytes 14417920 | tf_op jit(solution)/shard_map/pallas_call | solution.py:188
  47.4 4.7 %copy-done = bf16[5120,1280]{1,0:T(8,128)(2,1)} copy-done((bf16[5120,1280]{1,0:T(8,128)(2,1)}, bf16[5120,1280]{1,0:T(8,128)(2,1)S(1)}, u32[]{:S(2)}) %copy-start) | copy-done | bytes 13107224
  58.5 3.6 %collective-permute-start.12 = (f32[6,512]{1,0:T(8,128)S(1)}, f32[6,512]{1,0:T(8,128)S(1)}, u32[]{:S(2)}, u32[]{:S(2)}) collective-permute-start(f32[6,512]{1,0:T(8,128)S(1)} %select_select_fusion), channel_id=1, source_target_pairs={{0,2},{1,3},{2,0},{3,1},{4,6},{5,7},{6,4},{7,5},{8,10},{9,11},{10,... | collective-permute-start | bytes 36872 | tf_op jit(solution)/shard_map/ppermute | solution.py:63
  64.0 3.1 %collective-permute-done.13 = f32[6,512]{1,0:T(8,128)S(1)} collective-permute-done((f32[6,512]{1,0:T(8,128)S(1)}, f32[6,512]{1,0:T(8,128)S(1)}, u32[]{:S(2)}, u32[]{:S(2)}) %collective-permute-start.13) | collective-permute-done | bytes 12320 | tf_op jit(solution)/shard_map/ppermute | solution.py:63
  67.3 3.5 %collective-permute-start.15 = (f32[6,512]{1,0:T(8,128)S(1)}, f32[6,512]{1,0:T(8,128)S(1)}, u32[]{:S(2)}, u32[]{:S(2)}) collective-permute-start(f32[6,512]{1,0:T(8,128)S(1)} %get-tuple-element.112), channel_id=1, source_target_pairs={{0,8},{4,12},{8,0},{12,4},{1,9},{5,13},{9,1},{13,5},{2,10},{6,14},... | collective-permute-start | bytes 36872 | tf_op jit(solution)/shard_map/ppermute | solution.py:63
  72.8 3.0 %collective-permute-done.16 = f32[6,512]{1,0:T(8,128)S(1)} collective-permute-done((f32[6,512]{1,0:T(8,128)S(1)}, f32[6,512]{1,0:T(8,128)S(1)}, u32[]{:S(2)}, u32[]{:S(2)}) %collective-permute-start.16) | collective-permute-done | bytes 12320 | tf_op jit(solution)/shard_map/ppermute | solution.py:63
  76.1 2.5 %collective-permute-start.18 = (f32[6,512]{1,0:T(8,128)S(1)}, f32[6,512]{1,0:T(8,128)S(1)}, u32[]{:S(2)}, u32[]{:S(2)}) collective-permute-start(f32[6,512]{1,0:T(8,128)S(1)} %get-tuple-element.102), channel_id=1, source_target_pairs={{0,32},{16,48},{32,0},{48,16},{1,33},{17,49},{33,1},{49,17},{2,34}... | collective-permute-start | bytes 36872 | tf_op jit(solution)/shard_map/ppermute | solution.py:63
  86.3 4.1 %copy-done.1 = bf16[5120,1280]{1,0:T(8,128)(2,1)S(1)} copy-done((bf16[5120,1280]{1,0:T(8,128)(2,1)S(1)}, bf16[5120,1280]{1,0:T(8,128)(2,1)}, u32[]{:S(2)}) %copy-start.1) | copy-done | bytes 13107224
  97.5 6.1 %collective-permute-done.20 = bf16[2,2,2,4,8,1280]{5,4,3,2,1,0:T(8,128)(2,1)S(1)} collective-permute-done((bf16[2,2,2,4,8,1280]{5,4,3,2,1,0:T(8,128)(2,1)S(1)}, bf16[2,2,2,4,8,1280]{5,4,3,2,1,0:T(8,128)(2,1)S(1)}, u32[]{:S(2)}, u32[]{:S(2)}) %collective-permute-start.20) | collective-permute-done | bytes 655392 | tf_op jit(solution)/shard_map/ppermute | solution.py:260
  105.7 3.1 %collective-permute-done.24 = bf16[2,2,2,4,8,1280]{5,4,3,2,1,0:T(8,128)(2,1)S(1)} collective-permute-done((bf16[2,2,2,4,8,1280]{5,4,3,2,1,0:T(8,128)(2,1)S(1)}, bf16[2,2,2,4,8,1280]{5,4,3,2,1,0:T(8,128)(2,1)S(1)}, u32[]{:S(2)}, u32[]{:S(2)}) %collective-permute-start.24) | collective-permute-done | bytes 655392 | tf_op jit(solution)/shard_map/ppermute | solution.py:260
  121.3 3.1 %collective-permute-start.26 = (bf16[2,4,8,1280]{3,2,1,0:T(8,128)(2,1)S(1)}, bf16[2,4,8,1280]{3,2,1,0:T(8,128)(2,1)S(1)}, u32[]{:S(2)}, u32[]{:S(2)}) collective-permute-start(bf16[2,4,8,1280]{3,2,1,0:T(8,128)(2,1)S(1)} %get-tuple-element.75), channel_id=1, source_target_pairs={{0,3},{1,2},{2,1},{3,0},{4,7},{5,6},{6,5},{7,4},{8,11},{9,10},{10,... | collective-permute-start | bytes 491528 | tf_op jit(solution)/shard_map/ppermute | solution.py:260
  132.5 3.1 %collective-permute-done.31 = bf16[4,8,1280]{2,1,0:T(8,128)(2,1)S(1)} collective-permute-done((bf16[4,8,1280]{2,1,0:T(8,128)(2,1)S(1)}, bf16[4,8,1280]{2,1,0:T(8,128)(2,1)S(1)}, u32[]{:S(2)}, u32[]{:S(2)}) %collective-permute-start.31) | collective-permute-done | bytes 81952 | tf_op jit(solution)/shard_map/ppermute | solution.py:260
  136.8 5.3 %collective-permute-done.36 = bf16[2,8,5120]{2,1,0:T(8,128)(2,1)S(1)} collective-permute-done((bf16[2,8,5120]{2,1,0:T(8,128)(2,1)S(1)}, bf16[2,8,5120]{2,1,0:T(8,128)(2,1)S(1)}, u32[]{:S(2)}, u32[]{:S(2)}) %collective-permute-start.36) | collective-permute-done | bytes 163872 | tf_op jit(solution)/shard_map/ppermute | solution.py:30
  142.1 2.3 %collective-permute-start.37 = (bf16[8,5120]{1,0:T(8,128)(2,1)S(1)}, bf16[8,5120]{1,0:T(8,128)(2,1)S(1)}, u32[]{:S(2)}, u32[]{:S(2)}) collective-permute-start(bf16[8,5120]{1,0:T(8,128)(2,1)S(1)} %fusion.144), channel_id=1, source_target_pairs={{0,48},{1,49},{2,50},{3,51},{4,52},{5,53},{6,54},{7,55},{8,56},{9,... | collective-permute-start | bytes 245768 | tf_op jit(solution)/shard_map/ppermute | solution.py:30
  145.3 2.6 %collective-permute-done.37 = bf16[8,5120]{1,0:T(8,128)(2,1)S(1)} collective-permute-done((bf16[8,5120]{1,0:T(8,128)(2,1)S(1)}, bf16[8,5120]{1,0:T(8,128)(2,1)S(1)}, u32[]{:S(2)}, u32[]{:S(2)}) %collective-permute-start.37) | collective-permute-done | bytes 81952 | tf_op jit(solution)/shard_map/ppermute | solution.py:30
  149.2 4.6 %all-to-all-start = ((bf16[16,8,5120]{2,1,0:T(8,128)(2,1)}), bf16[16,8,5120]{2,1,0:T(8,128)(2,1)S(1)}, u32[]{:S(2)}, u32[]{:S(2)}) async-start(bf16[16,8,5120]{2,1,0:T(8,128)(2,1)} %shard_map.72), calls=%async_computation | async-start | bytes 2621440 | tf_op jit(solution)/shard_map/all_to_all | solution.py:375
  157.8 10.6 %all-to-all-done = bf16[16,8,5120]{2,1,0:T(8,128)(2,1)S(1)} async-done(((bf16[16,8,5120]{2,1,0:T(8,128)(2,1)}), bf16[16,8,5120]{2,1,0:T(8,128)(2,1)S(1)}, u32[]{:S(2)}, u32[]{:S(2)}) %all-to-all-start) | async-done | bytes 1310752 | tf_op jit(solution)/shard_map/all_to_all | solution.py:375
  (172 shorter events, 70.2 us)
Async XLA Ops:
  1.8 21.6 %collective-permute-start = (bf16[64,5120]{1,0:T(8,128)(2,1)S(1)}, bf16[64,5120]{1,0:T(8,128)(2,1)S(1)}, u32[]{:S(2)}, u32[]{:S(2)}) collective-permute-start(bf16[64,5120]{1,0:T(8,128)(2,1)S(1)} %dynamic-slice_bitcast_fusion.4), channel_id=1, source_target_pairs={{0,16},{1,17},{2,18},{3,19},{4,20},{5,21},{6,22},{7,23},{8,24},{9,... | collective-permute-start | bytes 1966088 | tf_op jit(solution)/shard_map/ppermute | solution.py:30
  3.5 19.8 %collective-permute-start.1 = (bf16[64,5120]{1,0:T(8,128)(2,1)S(1)}, bf16[64,5120]{1,0:T(8,128)(2,1)S(1)}, u32[]{:S(2)}, u32[]{:S(2)}) collective-permute-start(bf16[64,5120]{1,0:T(8,128)(2,1)S(1)} %dynamic-slice_bitcast_fusion.4), channel_id=1, source_target_pairs={{0,48},{1,49},{2,50},{3,51},{4,52},{5,53},{6,54},{7,55},{8,56},{9,... | collective-permute-start | bytes 1966088 | tf_op jit(solution)/shard_map/ppermute | solution.py:30
  7.0 16.3 %collective-permute-start.2 = (s32[132]{0:T(256)S(1)}, s32[132]{0:T(256)S(1)}, u32[]{:S(2)}, u32[]{:S(2)}) collective-permute-start(s32[132]{0:T(256)S(1)} %constant_dynamic-update-slice_fusion), channel_id=1, source_target_pairs={{0,16},{16,0},{32,48},{48,32},{1,17},{17,1},{33,49},{49,33},{2,18}... | collective-permute-start | bytes 1592 | tf_op jit(solution)/shard_map/ppermute | solution.py:63
  7.7 15.6 %collective-permute-start.3 = (s32[132]{0:T(256)S(1)}, s32[132]{0:T(256)S(1)}, u32[]{:S(2)}, u32[]{:S(2)}) collective-permute-start(s32[132]{0:T(256)S(1)} %constant_dynamic-update-slice_fusion), channel_id=1, source_target_pairs={{0,32},{16,48},{32,0},{48,16},{1,33},{17,49},{33,1},{49,17},{2,34}... | collective-permute-start | bytes 1592 | tf_op jit(solution)/shard_map/ppermute | solution.py:63
  9.6 13.8 %collective-permute-start.4 = (s32[132]{0:T(256)S(1)}, s32[132]{0:T(256)S(1)}, u32[]{:S(2)}, u32[]{:S(2)}) collective-permute-start(s32[132]{0:T(256)S(1)} %constant_dynamic-update-slice_fusion), channel_id=1, source_target_pairs={{0,48},{16,32},{32,16},{48,0},{1,49},{17,33},{33,17},{49,1},{2,50}... | collective-permute-start | bytes 1592 | tf_op jit(solution)/shard_map/ppermute | solution.py:63
  23.4 10.7 %collective-permute-start.5 = (bf16[64,5120]{1,0:T(8,128)(2,1)S(1)}, bf16[64,5120]{1,0:T(8,128)(2,1)S(1)}, u32[]{:S(2)}, u32[]{:S(2)}) collective-permute-start(bf16[64,5120]{1,0:T(8,128)(2,1)S(1)} %collective-permute-done.1.refs_1_), channel_id=1, source_target_pairs={{0,16},{1,17},{2,18},{3,19},{4,20},{5,21},{6,22},{7,23},{8,24},{9,... | collective-permute-start | bytes 1966088 | tf_op jit(solution)/shard_map/ppermute | solution.py:30
  23.5 14.3 %collective-permute-start.9 = (bf16[64,5120]{1,0:T(8,128)(2,1)S(1)}, bf16[64,5120]{1,0:T(8,128)(2,1)S(1)}, u32[]{:S(2)}, u32[]{:S(2)}) collective-permute-start(bf16[64,5120]{1,0:T(8,128)(2,1)S(1)} %collective-permute-done.1.refs_1_), channel_id=1, source_target_pairs={{0,12},{1,13},{2,14},{3,15},{4,8},{5,9},{6,10},{7,11},{8,4},{9,5},... | collective-permute-start | bytes 1966088 | tf_op jit(solution)/shard_map/ppermute | solution.py:30
  26.3 11.5 %collective-permute-start.8 = (bf16[64,5120]{1,0:T(8,128)(2,1)S(1)}, bf16[64,5120]{1,0:T(8,128)(2,1)S(1)}, u32[]{:S(2)}, u32[]{:S(2)}) collective-permute-start(bf16[64,5120]{1,0:T(8,128)(2,1)S(1)} %collective-permute-done.refs_0_), channel_id=1, source_target_pairs={{0,4},{1,5},{2,6},{3,7},{4,0},{5,1},{6,2},{7,3},{8,12},{9,13},{10,... | collective-permute-start | bytes 1966088 | tf_op jit(solution)/shard_map/ppermute | solution.py:30
  34.1 7.5 %collective-permute-start.6 = (bf16[32,5120]{1,0:T(8,128)(2,1)S(1)}, bf16[32,5120]{1,0:T(8,128)(2,1)S(1)}, u32[]{:S(2)}, u32[]{:S(2)}) collective-permute-start(bf16[32,5120]{1,0:T(8,128)(2,1)S(1)} %get-tuple-element.84), channel_id=1, source_target_pairs={{0,4},{1,5},{2,6},{3,7},{4,0},{5,1},{6,2},{7,3},{8,12},{9,13},{10,... | collective-permute-start | bytes 983048 | tf_op jit(solution)/shard_map/ppermute | solution.py:30
  35.6 8.3 %collective-permute-start.7 = (bf16[32,5120]{1,0:T(8,128)(2,1)S(1)}, bf16[32,5120]{1,0:T(8,128)(2,1)S(1)}, u32[]{:S(2)}, u32[]{:S(2)}) collective-permute-start(bf16[32,5120]{1,0:T(8,128)(2,1)S(1)} %get-tuple-element.83), channel_id=1, source_target_pairs={{0,12},{1,13},{2,14},{3,15},{4,8},{5,9},{6,10},{7,11},{8,4},{9,5},... | collective-permute-start | bytes 983048 | tf_op jit(solution)/shard_map/ppermute | solution.py:30
  91.5 12.1 %collective-permute-start.20 = (bf16[2,2,2,4,8,1280]{5,4,3,2,1,0:T(8,128)(2,1)S(1)}, bf16[2,2,2,4,8,1280]{5,4,3,2,1,0:T(8,128)(2,1)S(1)}, u32[]{:S(2)}, u32[]{:S(2)}) collective-permute-start(bf16[2,2,2,4,8,1280]{5,4,3,2,1,0:T(8,128)(2,1)S(1)} %fusion.48), channel_id=1, source_target_pairs={{0,4},{4,0},{8,12},{12,8},{1,5},{5,1},{9,13},{13,9},{2,6},{6,2},{1... | collective-permute-start | bytes 1966088 | tf_op jit(solution)/shard_map/ppermute | solution.py:260
  92.7 16.1 %collective-permute-start.24 = (bf16[2,2,2,4,8,1280]{5,4,3,2,1,0:T(8,128)(2,1)S(1)}, bf16[2,2,2,4,8,1280]{5,4,3,2,1,0:T(8,128)(2,1)S(1)}, u32[]{:S(2)}, u32[]{:S(2)}) collective-permute-start(bf16[2,2,2,4,8,1280]{5,4,3,2,1,0:T(8,128)(2,1)S(1)} %fusion.51), channel_id=1, source_target_pairs={{0,12},{4,8},{8,4},{12,0},{1,13},{5,9},{9,5},{13,1},{2,14},{6,10},... | collective-permute-start | bytes 1966088 | tf_op jit(solution)/shard_map/ppermute | solution.py:260
  95.0 16.3 %collective-permute-start.28 = (bf16[2,2,2,4,8,1280]{5,4,3,2,1,0:T(8,128)(2,1)S(1)}, bf16[2,2,2,4,8,1280]{5,4,3,2,1,0:T(8,128)(2,1)S(1)}, u32[]{:S(2)}, u32[]{:S(2)}) collective-permute-start(bf16[2,2,2,4,8,1280]{5,4,3,2,1,0:T(8,128)(2,1)S(1)} %fusion.54), channel_id=1, source_target_pairs={{0,1},{1,0},{2,3},{3,2},{4,5},{5,4},{6,7},{7,6},{8,9},{9,8},{10,11... | collective-permute-start | bytes 1966088 | tf_op jit(solution)/shard_map/ppermute | solution.py:260
  96.2 16.6 %collective-permute-start.32 = (bf16[2,2,2,4,8,1280]{5,4,3,2,1,0:T(8,128)(2,1)S(1)}, bf16[2,2,2,4,8,1280]{5,4,3,2,1,0:T(8,128)(2,1)S(1)}, u32[]{:S(2)}, u32[]{:S(2)}) collective-permute-start(bf16[2,2,2,4,8,1280]{5,4,3,2,1,0:T(8,128)(2,1)S(1)} %fusion.57), channel_id=1, source_target_pairs={{0,3},{1,2},{2,1},{3,0},{4,7},{5,6},{6,5},{7,4},{8,11},{9,10},{10,... | collective-permute-start | bytes 1966088 | tf_op jit(solution)/shard_map/ppermute | solution.py:260
  104.8 14.5 %collective-permute-start.21 = (bf16[2,2,4,8,1280]{4,3,2,1,0:T(8,128)(2,1)S(1)}, bf16[2,2,4,8,1280]{4,3,2,1,0:T(8,128)(2,1)S(1)}, u32[]{:S(2)}, u32[]{:S(2)}) collective-permute-start(bf16[2,2,4,8,1280]{4,3,2,1,0:T(8,128)(2,1)S(1)} %fusion.105), channel_id=1, source_target_pairs={{0,12},{4,8},{8,4},{12,0},{1,13},{5,9},{9,5},{13,1},{2,14},{6,10},... | collective-permute-start | bytes 983048 | tf_op jit(solution)/shard_map/ppermute | solution.py:260
  110.0 11.2 %collective-permute-start.25 = (bf16[2,2,4,8,1280]{4,3,2,1,0:T(8,128)(2,1)S(1)}, bf16[2,2,4,8,1280]{4,3,2,1,0:T(8,128)(2,1)S(1)}, u32[]{:S(2)}, u32[]{:S(2)}) collective-permute-start(bf16[2,2,4,8,1280]{4,3,2,1,0:T(8,128)(2,1)S(1)} %fusion.102), channel_id=1, source_target_pairs={{0,4},{4,0},{8,12},{12,8},{1,5},{5,1},{9,13},{13,9},{2,6},{6,2},{1... | collective-permute-start | bytes 983048 | tf_op jit(solution)/shard_map/ppermute | solution.py:260
  112.5 11.8 %collective-permute-start.29 = (bf16[2,2,4,8,1280]{4,3,2,1,0:T(8,128)(2,1)S(1)}, bf16[2,2,4,8,1280]{4,3,2,1,0:T(8,128)(2,1)S(1)}, u32[]{:S(2)}, u32[]{:S(2)}) collective-permute-start(bf16[2,2,4,8,1280]{4,3,2,1,0:T(8,128)(2,1)S(1)} %fusion.99), channel_id=1, source_target_pairs={{0,3},{1,2},{2,1},{3,0},{4,7},{5,6},{6,5},{7,4},{8,11},{9,10},{10,... | collective-permute-start | bytes 983048 | tf_op jit(solution)/shard_map/ppermute | solution.py:260
  114.1 11.2 %collective-permute-start.33 = (bf16[2,2,4,8,1280]{4,3,2,1,0:T(8,128)(2,1)S(1)}, bf16[2,2,4,8,1280]{4,3,2,1,0:T(8,128)(2,1)S(1)}, u32[]{:S(2)}, u32[]{:S(2)}) collective-permute-start(bf16[2,2,4,8,1280]{4,3,2,1,0:T(8,128)(2,1)S(1)} %fusion.96), channel_id=1, source_target_pairs={{0,1},{1,0},{2,3},{3,2},{4,5},{5,4},{6,7},{7,6},{8,9},{9,8},{10,11... | collective-permute-start | bytes 983048 | tf_op jit(solution)/shard_map/ppermute | solution.py:260
  119.4 7.2 %collective-permute-start.22 = (bf16[2,4,8,1280]{3,2,1,0:T(8,128)(2,1)S(1)}, bf16[2,4,8,1280]{3,2,1,0:T(8,128)(2,1)S(1)}, u32[]{:S(2)}, u32[]{:S(2)}) collective-permute-start(bf16[2,4,8,1280]{3,2,1,0:T(8,128)(2,1)S(1)} %get-tuple-element.73), channel_id=1, source_target_pairs={{0,1},{1,0},{2,3},{3,2},{4,5},{5,4},{6,7},{7,6},{8,9},{9,8},{10,11... | collective-permute-start | bytes 491528 | tf_op jit(solution)/shard_map/ppermute | solution.py:260
  121.3 6.6 %collective-permute-start.26 = (bf16[2,4,8,1280]{3,2,1,0:T(8,128)(2,1)S(1)}, bf16[2,4,8,1280]{3,2,1,0:T(8,128)(2,1)S(1)}, u32[]{:S(2)}, u32[]{:S(2)}) collective-permute-start(bf16[2,4,8,1280]{3,2,1,0:T(8,128)(2,1)S(1)} %get-tuple-element.75), channel_id=1, source_target_pairs={{0,3},{1,2},{2,1},{3,0},{4,7},{5,6},{6,5},{7,4},{8,11},{9,10},{10,... | collective-permute-start | bytes 491528 | tf_op jit(solution)/shard_map/ppermute | solution.py:260
  125.4 6.6 %collective-permute-start.34 = (bf16[2,4,8,1280]{3,2,1,0:T(8,128)(2,1)S(1)}, bf16[2,4,8,1280]{3,2,1,0:T(8,128)(2,1)S(1)}, u32[]{:S(2)}, u32[]{:S(2)}) collective-permute-start(bf16[2,4,8,1280]{3,2,1,0:T(8,128)(2,1)S(1)} %get-tuple-element.79), channel_id=1, source_target_pairs={{0,12},{4,8},{8,4},{12,0},{1,13},{5,9},{9,5},{13,1},{2,14},{6,10},... | collective-permute-start | bytes 491528 | tf_op jit(solution)/shard_map/ppermute | solution.py:260
  126.7 5.7 %collective-permute-start.23 = (bf16[4,8,1280]{2,1,0:T(8,128)(2,1)S(1)}, bf16[4,8,1280]{2,1,0:T(8,128)(2,1)S(1)}, u32[]{:S(2)}, u32[]{:S(2)}) collective-permute-start(bf16[4,8,1280]{2,1,0:T(8,128)(2,1)S(1)} %fusion.145), channel_id=1, source_target_pairs={{0,3},{1,2},{2,1},{3,0},{4,7},{5,6},{6,5},{7,4},{8,11},{9,10},{10,... | collective-permute-start | bytes 245768 | tf_op jit(solution)/shard_map/ppermute | solution.py:260
  129.9 5.7 %collective-permute-start.31 = (bf16[4,8,1280]{2,1,0:T(8,128)(2,1)S(1)}, bf16[4,8,1280]{2,1,0:T(8,128)(2,1)S(1)}, u32[]{:S(2)}, u32[]{:S(2)}) collective-permute-start(bf16[4,8,1280]{2,1,0:T(8,128)(2,1)S(1)} %fusion.147), channel_id=1, source_target_pairs={{0,12},{4,8},{8,4},{12,0},{1,13},{5,9},{9,5},{13,1},{2,14},{6,10},... | collective-permute-start | bytes 245768 | tf_op jit(solution)/shard_map/ppermute | solution.py:260
  149.2 19.1 %all-to-all-start = ((bf16[16,8,5120]{2,1,0:T(8,128)(2,1)}), bf16[16,8,5120]{2,1,0:T(8,128)(2,1)S(1)}, u32[]{:S(2)}, u32[]{:S(2)}) async-start(bf16[16,8,5120]{2,1,0:T(8,128)(2,1)} %shard_map.72), calls=%async_computation | async-start | bytes 2621440 | tf_op jit(solution)/shard_map/all_to_all | solution.py:375
  (21 other events, 103.1 us)

commit v8 on v7

--- a/solution.py
+++ b/solution.py
@@ -86,8 +86,8 @@
     far, logits = tied(far, logits)
     far_sides = [swap_u(far[: half // 2], 1), swap_u(far[half // 2 :], 3)]
     logits, matrix = add_logits((p_side, q_side), OTHER_PLAN, gain_row, matrix, tokens, logits)
-    logits, matrix = add_logits((far, *far_sides), FAR_PLAN, gain_row, matrix, tokens, logits)
-    return logits, matrix, [ints[s] for s in (0, 1, 3, 2)]
+    logits, _ = add_logits((far, *far_sides), FAR_PLAN, gain_row, matrix, tokens, logits)
+    return logits, [ints[s] for s in (0, 1, 3, 2)]
 
 
 def make_kernel(count, streamed, loads, stores):
@@ -335,7 +335,7 @@
     group = block.shape[0]
     tokens = 4 * group
     voc_shard = matrix.shape[1]
-    logits, matrix, ints = gather_logits(block, gain_row, matrix, jnp.concatenate([targets, lengths]))
+    logits, ints = gather_logits(block, gain_row, matrix, jnp.concatenate([targets, lengths]))
     all_targets = jnp.concatenate([part[:group] for part in ints])
     all_lengths = jnp.concatenate([part[group:] for part in ints])
     peer_logits = lax.ppermute(logits, "peer", [(0, 1), (1, 0)])

time: 171 us -> 163 us (0.953)
  local copies, waits for them, and re-layouts: 20.4 us -> 12.3 us
  waiting for transfers between devices: 52.3 us -> 50.1 us
  matrix products: 14.2 us -> 16.3 us
    unnamed x14 -> x18, local copies, waits for them, and re-layouts: 17.3 us -> 9.17 us
    ppermute x16, waiting for transfers between devices: 15.7 us -> 13.4 us  [swap(): return lax.ppermute(block, axis, [(i, i ^ step) for i in range(4)])]
    dot_general x12, matrix products: 14.2 us -> 16.3 us  [product(): lax.dot_general(block.reshape(-1, voc), columns, (((1,), (1,)), ((), ()))...]
  transfers between devices with their start and end apart: 39 -> 39, of which waited for: 19 -> 20; matrix products, arithmetic and copies ran while one was open for 11% -> 12% of each run, Pallas kernels for 7% -> 7%
where the time goes in v8:
time: 163 us
  starting transfers between devices  53.6 us (33%)
  waiting for transfers between devices  50.1 us (31%)
  Pallas kernels  16.9 us (10%)
  matrix products  16.3 us (10%)
  local copies, waits for them, and re-layouts  12.3 us (8%)
  other arithmetic  7.7 us (5%)
  between operations  5.77 us (4%)
    ppermute x12, starting transfers between devices, ring(): lax.ppermute(prepare(block, step), axis, [(i, i ^ step) for i in range(4)])  19.8 us
    dot_general x12, matrix products, product(): lax.dot_general(block.reshape(-1, voc), columns, (((1,), (1,)), ((), ()))...  16.3 us
    ppermute x16, starting transfers between devices, swap(): return lax.ppermute(block, axis, [(i, i ^ step) for i in range(4)])  16.2 us
    pallas_call x4, Pallas kernels, add_logits(): pl.pallas_call(make_kernel(count, streamed, *plan), out_shape=(jax.ShapeD...  15.6 us
    ppermute x9, waiting for transfers between devices, permute(): lax.ppermute(block, ALL, [(index(*p), index(*move(*p))) for p in places])  14.1 us
    ppermute x16, waiting for transfers between devices, swap(): return lax.ppermute(block, axis, [(i, i ^ step) for i in range(4)])  13.4 us
    ppermute x9, starting transfers between devices, permute(): lax.ppermute(block, ALL, [(index(*p), index(*move(*p))) for p in places])  13.1 us
    ppermute x12, waiting for transfers between devices, ring(): lax.ppermute(prepare(block, step), axis, [(i, i ^ step) for i in range(4)])  10.7 us
  transfers between devices with their start and end apart: 39, of which 20 were waited for; matrix products, arithmetic and copies ran while one was open for 12% of the time, Pallas kernels for 7%

profile of v8, /device:TPU:0, one launch (start us, length us, event | category | flops | bytes accessed | tf_op | source)
XLA Modules:
  0.0 162.6 jit_solution(15196353799259776260)
XLA Ops:
  11.7 4.7 %copy-done = bf16[1,5120,1280]{2,1,0:T(8,128)(2,1)S(1)} copy-done((bf16[1,5120,1280]{2,1,0:T(8,128)(2,1)S(1)}, bf16[1,5120,1280]{2,1,0:T(8,128)(2,1)}, u32[]{:S(2)}) %copy-start) | copy-done | bytes 13107224
  18.5 4.8 %shard_map.68 = (bf16[512,1280]{1,0:T(8,128)(2,1)S(1)}, bf16[5120,1280]{1,0:T(8,128)(2,1)S(1)}) custom-call(bf16[128,5120]{1,0:T(8,128)(2,1)S(1)} %bitcast.362, f32[1,5120]{1,0:T(1,128)S(1)} %copy-done.2, bf16[5120,1280]{1,0:T(8,128)(2,1)S(1)} %bitcast.359), custom_call_target="tpu_custom_call" | custom-call | flops 1677721600 | bytes 14417920 | tf_op jit(solution)/shard_map/pallas_call | solution.py:188
  23.4 2.8 %collective-permute-start.9 = (bf16[64,5120]{1,0:T(8,128)(2,1)S(1)}, bf16[64,5120]{1,0:T(8,128)(2,1)S(1)}, u32[]{:S(2)}, u32[]{:S(2)}) collective-permute-start(bf16[64,5120]{1,0:T(8,128)(2,1)S(1)} %collective-permute-done.1.refs_1_), channel_id=1, source_target_pairs={{0,12},{1,13},{2,14},{3,15},{4,8},{5,9},{6,10},{7,11},{8,4},{9,5},... | collective-permute-start | bytes 1966088 | tf_op jit(solution)/shard_map/ppermute | solution.py:30
  26.5 3.7 %shard_map.69 = (bf16[512,1280]{1,0:T(8,128)(2,1)S(1)}, bf16[5120,1280]{1,0:T(8,128)(2,1)S(1)}) custom-call(bf16[64,5120]{1,0:T(8,128)(2,1)S(1)} %collective-permute-done.refs_0_, bf16[64,5120]{1,0:T(8,128)(2,1)S(1)} %collective-permute-done.1.refs_1_, f32[1,5120]{1,0:T(1,128)S(1)} %copy-done.2, ...), custom_call_target="tpu_custom_call", output_to_operand_aliasing={{1}: (3, {}), {0}: (4, {})} | custom-call | flops 1677721600 | bytes 14417920 | tf_op jit(solution)/shard_map/pallas_call | solution.py:188
  30.2 3.8 %collective-permute-done.5.refs_0_ = bf16[64,5120]{1,0:T(8,128)(2,1)S(1)} collective-permute-done((bf16[64,5120]{1,0:T(8,128)(2,1)S(1)}, bf16[64,5120]{1,0:T(8,128)(2,1)S(1)}, u32[]{:S(2)}, u32[]{:S(2)}) %collective-permute-start.5) | collective-permute-done | bytes 655392 | tf_op jit(solution)/shard_map/ppermute | solution.py:30
  37.7 3.7 %shard_map.70 = (bf16[512,1280]{1,0:T(8,128)(2,1)S(1)}, bf16[5120,1280]{1,0:T(8,128)(2,1)S(1)}) custom-call(bf16[64,5120]{1,0:T(8,128)(2,1)S(1)} %collective-permute-done.8.refs_0_, bf16[64,5120]{1,0:T(8,128)(2,1)S(1)} %collective-permute-done.9.refs_1_, f32[1,5120]{1,0:T(1,128)S(1)} %copy-done.3, ...), custom_call_target="tpu_custom_call", output_to_operand_aliasing={{1}: (3, {}), {0}: (4, {})} | custom-call | flops 1677721600 | bytes 14417920 | tf_op jit(solution)/shard_map/pallas_call | solution.py:188
  41.4 2.4 %collective-permute-done.7.refs_2_ = bf16[32,5120]{1,0:T(8,128)(2,1)S(1)} collective-permute-done((bf16[32,5120]{1,0:T(8,128)(2,1)S(1)}, bf16[32,5120]{1,0:T(8,128)(2,1)S(1)}, u32[]{:S(2)}, u32[]{:S(2)}) %collective-permute-start.7) | collective-permute-done | bytes 327712 | tf_op jit(solution)/shard_map/ppermute | solution.py:30
  43.9 3.4 %shard_map.71 = (bf16[512,1280]{1,0:T(8,128)(2,1)S(1)}, bf16[5120,1280]{1,0:T(8,128)(2,1)S(1)}) custom-call(bf16[64,5120]{1,0:T(8,128)(2,1)S(1)} %collective-permute-done.5.refs_0_, bf16[32,5120]{1,0:T(8,128)(2,1)S(1)} %collective-permute-done.6.refs_1_, ...), custom_call_target="tpu_custom_call", output_to_operand_aliasing={{1}: (4, {}), {0}: (5, {})} | custom-call | flops 1677721600 | bytes 14417920 | tf_op jit(solution)/shard_map/pallas_call | solution.py:188
  53.9 3.6 %collective-permute-start.12 = (f32[6,512]{1,0:T(8,128)S(1)}, f32[6,512]{1,0:T(8,128)S(1)}, u32[]{:S(2)}, u32[]{:S(2)}) collective-permute-start(f32[6,512]{1,0:T(8,128)S(1)} %select_select_fusion), channel_id=1, source_target_pairs={{0,2},{1,3},{2,0},{3,1},{4,6},{5,7},{6,4},{7,5},{8,10},{9,11},{10,... | collective-permute-start | bytes 36872 | tf_op jit(solution)/shard_map/ppermute | solution.py:63
  59.4 3.1 %collective-permute-done.13 = f32[6,512]{1,0:T(8,128)S(1)} collective-permute-done((f32[6,512]{1,0:T(8,128)S(1)}, f32[6,512]{1,0:T(8,128)S(1)}, u32[]{:S(2)}, u32[]{:S(2)}) %collective-permute-start.13) | collective-permute-done | bytes 12320 | tf_op jit(solution)/shard_map/ppermute | solution.py:63
  62.7 3.6 %collective-permute-start.15 = (f32[6,512]{1,0:T(8,128)S(1)}, f32[6,512]{1,0:T(8,128)S(1)}, u32[]{:S(2)}, u32[]{:S(2)}) collective-permute-start(f32[6,512]{1,0:T(8,128)S(1)} %get-tuple-element.114), channel_id=1, source_target_pairs={{0,8},{4,12},{8,0},{12,4},{1,9},{5,13},{9,1},{13,5},{2,10},{6,14},... | collective-permute-start | bytes 36872 | tf_op jit(solution)/shard_map/ppermute | solution.py:63
  68.3 3.0 %collective-permute-done.16 = f32[6,512]{1,0:T(8,128)S(1)} collective-permute-done((f32[6,512]{1,0:T(8,128)S(1)}, f32[6,512]{1,0:T(8,128)S(1)}, u32[]{:S(2)}, u32[]{:S(2)}) %collective-permute-start.16) | collective-permute-done | bytes 12320 | tf_op jit(solution)/shard_map/ppermute | solution.py:63
  71.5 2.5 %collective-permute-start.18 = (f32[6,512]{1,0:T(8,128)S(1)}, f32[6,512]{1,0:T(8,128)S(1)}, u32[]{:S(2)}, u32[]{:S(2)}) collective-permute-start(f32[6,512]{1,0:T(8,128)S(1)} %get-tuple-element.104), channel_id=1, source_target_pairs={{0,32},{16,48},{32,0},{48,16},{1,33},{17,49},{33,1},{49,17},{2,34}... | collective-permute-start | bytes 36872 | tf_op jit(solution)/shard_map/ppermute | solution.py:63
  74.0 2.2 %collective-permute-start.19 = (f32[6,512]{1,0:T(8,128)S(1)}, f32[6,512]{1,0:T(8,128)S(1)}, u32[]{:S(2)}, u32[]{:S(2)}) collective-permute-start(f32[6,512]{1,0:T(8,128)S(1)} %pad_maximum_fusion.10), channel_id=1, source_target_pairs={{0,48},{16,32},{32,16},{48,0},{1,49},{17,33},{33,17},{49,1},{2,50}... | collective-permute-start | bytes 36872 | tf_op jit(solution)/shard_map/ppermute | solution.py:63
  81.8 3.3 %fusion.48 = bf16[2,2,2,4,8,1280]{5,4,3,2,1,0:T(8,128)(2,1)S(1)} fusion(bf16[2,2,2,4,8,1280]{5,4,3,2,1,0:T(8,128)(2,1)S(1)} %dynamic-slice_bitcast_fusion.3, bf16[1,5120,1280]{2,1,0:T(8,128)(2,1)} %param.7), kind=kOutput, calls=%fused_computation.61 | convolution fusion | flops 839188480 | bytes 4587520 | tf_op jit(solution)/shard_map/dot_general | solution.py:248
  94.1 3.0 %collective-permute-done.20 = bf16[2,2,2,4,8,1280]{5,4,3,2,1,0:T(8,128)(2,1)S(1)} collective-permute-done((bf16[2,2,2,4,8,1280]{5,4,3,2,1,0:T(8,128)(2,1)S(1)}, bf16[2,2,2,4,8,1280]{5,4,3,2,1,0:T(8,128)(2,1)S(1)}, u32[]{:S(2)}, u32[]{:S(2)}) %collective-permute-start.20) | collective-permute-done | bytes 655392 | tf_op jit(solution)/shard_map/ppermute | solution.py:260
  99.2 4.5 %collective-permute-done.24 = bf16[2,2,2,4,8,1280]{5,4,3,2,1,0:T(8,128)(2,1)S(1)} collective-permute-done((bf16[2,2,2,4,8,1280]{5,4,3,2,1,0:T(8,128)(2,1)S(1)}, bf16[2,2,2,4,8,1280]{5,4,3,2,1,0:T(8,128)(2,1)S(1)}, u32[]{:S(2)}, u32[]{:S(2)}) %collective-permute-start.24) | collective-permute-done | bytes 655392 | tf_op jit(solution)/shard_map/ppermute | solution.py:260
  113.3 2.4 %collective-permute-start.26 = (bf16[2,4,8,1280]{3,2,1,0:T(8,128)(2,1)S(1)}, bf16[2,4,8,1280]{3,2,1,0:T(8,128)(2,1)S(1)}, u32[]{:S(2)}, u32[]{:S(2)}) collective-permute-start(bf16[2,4,8,1280]{3,2,1,0:T(8,128)(2,1)S(1)} %get-tuple-element.73), channel_id=1, source_target_pairs={{0,3},{1,2},{2,1},{3,0},{4,7},{5,6},{6,5},{7,4},{8,11},{9,10},{10,... | collective-permute-start | bytes 491528 | tf_op jit(solution)/shard_map/ppermute | solution.py:260
  119.5 2.4 %collective-permute-start.23 = (bf16[4,8,1280]{2,1,0:T(8,128)(2,1)S(1)}, bf16[4,8,1280]{2,1,0:T(8,128)(2,1)S(1)}, u32[]{:S(2)}, u32[]{:S(2)}) collective-permute-start(bf16[4,8,1280]{2,1,0:T(8,128)(2,1)S(1)} %fusion.129), channel_id=1, source_target_pairs={{0,3},{1,2},{2,1},{3,0},{4,7},{5,6},{6,5},{7,4},{8,11},{9,10},{10,... | collective-permute-start | bytes 245768 | tf_op jit(solution)/shard_map/ppermute | solution.py:260
  129.3 5.3 %collective-permute-done.36 = bf16[2,8,5120]{2,1,0:T(8,128)(2,1)S(1)} collective-permute-done((bf16[2,8,5120]{2,1,0:T(8,128)(2,1)S(1)}, bf16[2,8,5120]{2,1,0:T(8,128)(2,1)S(1)}, u32[]{:S(2)}, u32[]{:S(2)}) %collective-permute-start.36) | collective-permute-done | bytes 163872 | tf_op jit(solution)/shard_map/ppermute | solution.py:30
  134.6 2.3 %collective-permute-start.37 = (bf16[8,5120]{1,0:T(8,128)(2,1)S(1)}, bf16[8,5120]{1,0:T(8,128)(2,1)S(1)}, u32[]{:S(2)}, u32[]{:S(2)}) collective-permute-start(bf16[8,5120]{1,0:T(8,128)(2,1)S(1)} %fusion.128), channel_id=1, source_target_pairs={{0,48},{1,49},{2,50},{3,51},{4,52},{5,53},{6,54},{7,55},{8,56},{9,... | collective-permute-start | bytes 245768 | tf_op jit(solution)/shard_map/ppermute | solution.py:30
  137.8 2.6 %collective-permute-done.37 = bf16[8,5120]{1,0:T(8,128)(2,1)S(1)} collective-permute-done((bf16[8,5120]{1,0:T(8,128)(2,1)S(1)}, bf16[8,5120]{1,0:T(8,128)(2,1)S(1)}, u32[]{:S(2)}, u32[]{:S(2)}) %collective-permute-start.37) | collective-permute-done | bytes 81952 | tf_op jit(solution)/shard_map/ppermute | solution.py:30
  141.7 4.3 %all-to-all-start = ((bf16[16,8,5120]{2,1,0:T(8,128)(2,1)}), bf16[16,8,5120]{2,1,0:T(8,128)(2,1)S(1)}, u32[]{:S(2)}, u32[]{:S(2)}) async-start(bf16[16,8,5120]{2,1,0:T(8,128)(2,1)} %shard_map.72), calls=%async_computation | async-start | bytes 2621440 | tf_op jit(solution)/shard_map/all_to_all | solution.py:375
  149.8 10.6 %all-to-all-done = bf16[16,8,5120]{2,1,0:T(8,128)(2,1)S(1)} async-done(((bf16[16,8,5120]{2,1,0:T(8,128)(2,1)}), bf16[16,8,5120]{2,1,0:T(8,128)(2,1)S(1)}, u32[]{:S(2)}, u32[]{:S(2)}) %all-to-all-start) | async-done | bytes 1310752 | tf_op jit(solution)/shard_map/all_to_all | solution.py:375
  (177 shorter events, 69.2 us)
Async XLA Ops:
  1.8 21.5 %collective-permute-start = (bf16[64,5120]{1,0:T(8,128)(2,1)S(1)}, bf16[64,5120]{1,0:T(8,128)(2,1)S(1)}, u32[]{:S(2)}, u32[]{:S(2)}) collective-permute-start(bf16[64,5120]{1,0:T(8,128)(2,1)S(1)} %dynamic-slice_bitcast_fusion.4), channel_id=1, source_target_pairs={{0,16},{1,17},{2,18},{3,19},{4,20},{5,21},{6,22},{7,23},{8,24},{9,... | collective-permute-start | bytes 1966088 | tf_op jit(solution)/shard_map/ppermute | solution.py:30
  3.5 19.8 %collective-permute-start.1 = (bf16[64,5120]{1,0:T(8,128)(2,1)S(1)}, bf16[64,5120]{1,0:T(8,128)(2,1)S(1)}, u32[]{:S(2)}, u32[]{:S(2)}) collective-permute-start(bf16[64,5120]{1,0:T(8,128)(2,1)S(1)} %dynamic-slice_bitcast_fusion.4), channel_id=1, source_target_pairs={{0,48},{1,49},{2,50},{3,51},{4,52},{5,53},{6,54},{7,55},{8,56},{9,... | collective-permute-start | bytes 1966088 | tf_op jit(solution)/shard_map/ppermute | solution.py:30
  7.0 16.2 %collective-permute-start.2 = (s32[132]{0:T(256)S(1)}, s32[132]{0:T(256)S(1)}, u32[]{:S(2)}, u32[]{:S(2)}) collective-permute-start(s32[132]{0:T(256)S(1)} %constant_dynamic-update-slice_fusion), channel_id=1, source_target_pairs={{0,16},{16,0},{32,48},{48,32},{1,17},{17,1},{33,49},{49,33},{2,18}... | collective-permute-start | bytes 1592 | tf_op jit(solution)/shard_map/ppermute | solution.py:63
  7.7 15.6 %collective-permute-start.3 = (s32[132]{0:T(256)S(1)}, s32[132]{0:T(256)S(1)}, u32[]{:S(2)}, u32[]{:S(2)}) collective-permute-start(s32[132]{0:T(256)S(1)} %constant_dynamic-update-slice_fusion), channel_id=1, source_target_pairs={{0,32},{16,48},{32,0},{48,16},{1,33},{17,49},{33,1},{49,17},{2,34}... | collective-permute-start | bytes 1592 | tf_op jit(solution)/shard_map/ppermute | solution.py:63
  9.6 13.7 %collective-permute-start.4 = (s32[132]{0:T(256)S(1)}, s32[132]{0:T(256)S(1)}, u32[]{:S(2)}, u32[]{:S(2)}) collective-permute-start(s32[132]{0:T(256)S(1)} %constant_dynamic-update-slice_fusion), channel_id=1, source_target_pairs={{0,48},{16,32},{32,16},{48,0},{1,49},{17,33},{33,17},{49,1},{2,50}... | collective-permute-start | bytes 1592 | tf_op jit(solution)/shard_map/ppermute | solution.py:63
  23.3 10.7 %collective-permute-start.5 = (bf16[64,5120]{1,0:T(8,128)(2,1)S(1)}, bf16[64,5120]{1,0:T(8,128)(2,1)S(1)}, u32[]{:S(2)}, u32[]{:S(2)}) collective-permute-start(bf16[64,5120]{1,0:T(8,128)(2,1)S(1)} %collective-permute-done.1.refs_1_), channel_id=1, source_target_pairs={{0,16},{1,17},{2,18},{3,19},{4,20},{5,21},{6,22},{7,23},{8,24},{9,... | collective-permute-start | bytes 1966088 | tf_op jit(solution)/shard_map/ppermute | solution.py:30
  23.4 14.3 %collective-permute-start.9 = (bf16[64,5120]{1,0:T(8,128)(2,1)S(1)}, bf16[64,5120]{1,0:T(8,128)(2,1)S(1)}, u32[]{:S(2)}, u32[]{:S(2)}) collective-permute-start(bf16[64,5120]{1,0:T(8,128)(2,1)S(1)} %collective-permute-done.1.refs_1_), channel_id=1, source_target_pairs={{0,12},{1,13},{2,14},{3,15},{4,8},{5,9},{6,10},{7,11},{8,4},{9,5},... | collective-permute-start | bytes 1966088 | tf_op jit(solution)/shard_map/ppermute | solution.py:30
  26.2 11.5 %collective-permute-start.8 = (bf16[64,5120]{1,0:T(8,128)(2,1)S(1)}, bf16[64,5120]{1,0:T(8,128)(2,1)S(1)}, u32[]{:S(2)}, u32[]{:S(2)}) collective-permute-start(bf16[64,5120]{1,0:T(8,128)(2,1)S(1)} %collective-permute-done.refs_0_), channel_id=1, source_target_pairs={{0,4},{1,5},{2,6},{3,7},{4,0},{5,1},{6,2},{7,3},{8,12},{9,13},{10,... | collective-permute-start | bytes 1966088 | tf_op jit(solution)/shard_map/ppermute | solution.py:30
  34.0 7.4 %collective-permute-start.6 = (bf16[32,5120]{1,0:T(8,128)(2,1)S(1)}, bf16[32,5120]{1,0:T(8,128)(2,1)S(1)}, u32[]{:S(2)}, u32[]{:S(2)}) collective-permute-start(bf16[32,5120]{1,0:T(8,128)(2,1)S(1)} %get-tuple-element.86), channel_id=1, source_target_pairs={{0,4},{1,5},{2,6},{3,7},{4,0},{5,1},{6,2},{7,3},{8,12},{9,13},{10,... | collective-permute-start | bytes 983048 | tf_op jit(solution)/shard_map/ppermute | solution.py:30
  35.6 8.3 %collective-permute-start.7 = (bf16[32,5120]{1,0:T(8,128)(2,1)S(1)}, bf16[32,5120]{1,0:T(8,128)(2,1)S(1)}, u32[]{:S(2)}, u32[]{:S(2)}) collective-permute-start(bf16[32,5120]{1,0:T(8,128)(2,1)S(1)} %get-tuple-element.85), channel_id=1, source_target_pairs={{0,12},{1,13},{2,14},{3,15},{4,8},{5,9},{6,10},{7,11},{8,4},{9,5},... | collective-permute-start | bytes 983048 | tf_op jit(solution)/shard_map/ppermute | solution.py:30
  85.0 12.1 %collective-permute-start.20 = (bf16[2,2,2,4,8,1280]{5,4,3,2,1,0:T(8,128)(2,1)S(1)}, bf16[2,2,2,4,8,1280]{5,4,3,2,1,0:T(8,128)(2,1)S(1)}, u32[]{:S(2)}, u32[]{:S(2)}) collective-permute-start(bf16[2,2,2,4,8,1280]{5,4,3,2,1,0:T(8,128)(2,1)S(1)} %fusion.48), channel_id=1, source_target_pairs={{0,4},{4,0},{8,12},{12,8},{1,5},{5,1},{9,13},{13,9},{2,6},{6,2},{1... | collective-permute-start | bytes 1966088 | tf_op jit(solution)/shard_map/ppermute | solution.py:260
  86.9 16.8 %collective-permute-start.24 = (bf16[2,2,2,4,8,1280]{5,4,3,2,1,0:T(8,128)(2,1)S(1)}, bf16[2,2,2,4,8,1280]{5,4,3,2,1,0:T(8,128)(2,1)S(1)}, u32[]{:S(2)}, u32[]{:S(2)}) collective-permute-start(bf16[2,2,2,4,8,1280]{5,4,3,2,1,0:T(8,128)(2,1)S(1)} %fusion.51), channel_id=1, source_target_pairs={{0,12},{4,8},{8,4},{12,0},{1,13},{5,9},{9,5},{13,1},{2,14},{6,10},... | collective-permute-start | bytes 1966088 | tf_op jit(solution)/shard_map/ppermute | solution.py:260
  90.5 14.5 %collective-permute-start.28 = (bf16[2,2,2,4,8,1280]{5,4,3,2,1,0:T(8,128)(2,1)S(1)}, bf16[2,2,2,4,8,1280]{5,4,3,2,1,0:T(8,128)(2,1)S(1)}, u32[]{:S(2)}, u32[]{:S(2)}) collective-permute-start(bf16[2,2,2,4,8,1280]{5,4,3,2,1,0:T(8,128)(2,1)S(1)} %fusion.54), channel_id=1, source_target_pairs={{0,1},{1,0},{2,3},{3,2},{4,5},{5,4},{6,7},{7,6},{8,9},{9,8},{10,11... | collective-permute-start | bytes 1966088 | tf_op jit(solution)/shard_map/ppermute | solution.py:260
  91.9 16.1 %collective-permute-start.32 = (bf16[2,2,2,4,8,1280]{5,4,3,2,1,0:T(8,128)(2,1)S(1)}, bf16[2,2,2,4,8,1280]{5,4,3,2,1,0:T(8,128)(2,1)S(1)}, u32[]{:S(2)}, u32[]{:S(2)}) collective-permute-start(bf16[2,2,2,4,8,1280]{5,4,3,2,1,0:T(8,128)(2,1)S(1)} %fusion.57), channel_id=1, source_target_pairs={{0,3},{1,2},{2,1},{3,0},{4,7},{5,6},{6,5},{7,4},{8,11},{9,10},{10,... | collective-permute-start | bytes 1966088 | tf_op jit(solution)/shard_map/ppermute | solution.py:260
  98.3 12.9 %collective-permute-start.21 = (bf16[2,2,4,8,1280]{4,3,2,1,0:T(8,128)(2,1)S(1)}, bf16[2,2,4,8,1280]{4,3,2,1,0:T(8,128)(2,1)S(1)}, u32[]{:S(2)}, u32[]{:S(2)}) collective-permute-start(bf16[2,2,4,8,1280]{4,3,2,1,0:T(8,128)(2,1)S(1)} %fusion.78), channel_id=1, source_target_pairs={{0,12},{4,8},{8,4},{12,0},{1,13},{5,9},{9,5},{13,1},{2,14},{6,10},... | collective-permute-start | bytes 983048 | tf_op jit(solution)/shard_map/ppermute | solution.py:260
  104.9 8.3 %collective-permute-start.25 = (bf16[2,2,4,8,1280]{4,3,2,1,0:T(8,128)(2,1)S(1)}, bf16[2,2,4,8,1280]{4,3,2,1,0:T(8,128)(2,1)S(1)}, u32[]{:S(2)}, u32[]{:S(2)}) collective-permute-start(bf16[2,2,4,8,1280]{4,3,2,1,0:T(8,128)(2,1)S(1)} %get-tuple-element.81), channel_id=1, source_target_pairs={{0,4},{4,0},{8,12},{12,8},{1,5},{5,1},{9,13},{13,9},{2,6},{6,2},{1... | collective-permute-start | bytes 983048 | tf_op jit(solution)/shard_map/ppermute | solution.py:260
  106.3 9.4 %collective-permute-start.29 = (bf16[2,2,4,8,1280]{4,3,2,1,0:T(8,128)(2,1)S(1)}, bf16[2,2,4,8,1280]{4,3,2,1,0:T(8,128)(2,1)S(1)}, u32[]{:S(2)}, u32[]{:S(2)}) collective-permute-start(bf16[2,2,4,8,1280]{4,3,2,1,0:T(8,128)(2,1)S(1)} %fusion.93), channel_id=1, source_target_pairs={{0,3},{1,2},{2,1},{3,0},{4,7},{5,6},{6,5},{7,4},{8,11},{9,10},{10,... | collective-permute-start | bytes 983048 | tf_op jit(solution)/shard_map/ppermute | solution.py:260
  109.3 8.5 %collective-permute-start.33 = (bf16[2,2,4,8,1280]{4,3,2,1,0:T(8,128)(2,1)S(1)}, bf16[2,2,4,8,1280]{4,3,2,1,0:T(8,128)(2,1)S(1)}, u32[]{:S(2)}, u32[]{:S(2)}) collective-permute-start(bf16[2,2,4,8,1280]{4,3,2,1,0:T(8,128)(2,1)S(1)} %get-tuple-element.83), channel_id=1, source_target_pairs={{0,1},{1,0},{2,3},{3,2},{4,5},{5,4},{6,7},{7,6},{8,9},{9,8},{10,11... | collective-permute-start | bytes 983048 | tf_op jit(solution)/shard_map/ppermute | solution.py:260
  111.3 8.2 %collective-permute-start.22 = (bf16[2,4,8,1280]{3,2,1,0:T(8,128)(2,1)S(1)}, bf16[2,4,8,1280]{3,2,1,0:T(8,128)(2,1)S(1)}, u32[]{:S(2)}, u32[]{:S(2)}) collective-permute-start(bf16[2,4,8,1280]{3,2,1,0:T(8,128)(2,1)S(1)} %get-tuple-element.71), channel_id=1, source_target_pairs={{0,1},{1,0},{2,3},{3,2},{4,5},{5,4},{6,7},{7,6},{8,9},{9,8},{10,11... | collective-permute-start | bytes 491528 | tf_op jit(solution)/shard_map/ppermute | solution.py:260
  113.3 8.6 %collective-permute-start.26 = (bf16[2,4,8,1280]{3,2,1,0:T(8,128)(2,1)S(1)}, bf16[2,4,8,1280]{3,2,1,0:T(8,128)(2,1)S(1)}, u32[]{:S(2)}, u32[]{:S(2)}) collective-permute-start(bf16[2,4,8,1280]{3,2,1,0:T(8,128)(2,1)S(1)} %get-tuple-element.73), channel_id=1, source_target_pairs={{0,3},{1,2},{2,1},{3,0},{4,7},{5,6},{6,5},{7,4},{8,11},{9,10},{10,... | collective-permute-start | bytes 491528 | tf_op jit(solution)/shard_map/ppermute | solution.py:260
  115.7 6.3 %collective-permute-start.30 = (bf16[2,4,8,1280]{3,2,1,0:T(8,128)(2,1)S(1)}, bf16[2,4,8,1280]{3,2,1,0:T(8,128)(2,1)S(1)}, u32[]{:S(2)}, u32[]{:S(2)}) collective-permute-start(bf16[2,4,8,1280]{3,2,1,0:T(8,128)(2,1)S(1)} %get-tuple-element.75), channel_id=1, source_target_pairs={{0,4},{4,0},{8,12},{12,8},{1,5},{5,1},{9,13},{13,9},{2,6},{6,2},{1... | collective-permute-start | bytes 491528 | tf_op jit(solution)/shard_map/ppermute | solution.py:260
  117.9 6.6 %collective-permute-start.34 = (bf16[2,4,8,1280]{3,2,1,0:T(8,128)(2,1)S(1)}, bf16[2,4,8,1280]{3,2,1,0:T(8,128)(2,1)S(1)}, u32[]{:S(2)}, u32[]{:S(2)}) collective-permute-start(bf16[2,4,8,1280]{3,2,1,0:T(8,128)(2,1)S(1)} %get-tuple-element.77), channel_id=1, source_target_pairs={{0,12},{4,8},{8,4},{12,0},{1,13},{5,9},{9,5},{13,1},{2,14},{6,10},... | collective-permute-start | bytes 491528 | tf_op jit(solution)/shard_map/ppermute | solution.py:260
  119.5 5.7 %collective-permute-start.23 = (bf16[4,8,1280]{2,1,0:T(8,128)(2,1)S(1)}, bf16[4,8,1280]{2,1,0:T(8,128)(2,1)S(1)}, u32[]{:S(2)}, u32[]{:S(2)}) collective-permute-start(bf16[4,8,1280]{2,1,0:T(8,128)(2,1)S(1)} %fusion.129), channel_id=1, source_target_pairs={{0,3},{1,2},{2,1},{3,0},{4,7},{5,6},{6,5},{7,4},{8,11},{9,10},{10,... | collective-permute-start | bytes 245768 | tf_op jit(solution)/shard_map/ppermute | solution.py:260
  141.7 18.8 %all-to-all-start = ((bf16[16,8,5120]{2,1,0:T(8,128)(2,1)}), bf16[16,8,5120]{2,1,0:T(8,128)(2,1)S(1)}, u32[]{:S(2)}, u32[]{:S(2)}) async-start(bf16[16,8,5120]{2,1,0:T(8,128)(2,1)} %shard_map.72), calls=%async_computation | async-start | bytes 2621440 | tf_op jit(solution)/shard_map/all_to_all | solution.py:375
  (23 other events, 120.4 us)

commit v9 on v8

--- a/solution.py
+++ b/solution.py
@@ -85,8 +85,8 @@
     logits, matrix = add_logits((p, q), HELD_PLAN, gain_row, matrix, tokens, logits)
     far, logits = tied(far, logits)
     far_sides = [swap_u(far[: half // 2], 1), swap_u(far[half // 2 :], 3)]
-    logits, matrix = add_logits((p_side, q_side), OTHER_PLAN, gain_row, matrix, tokens, logits)
-    logits, _ = add_logits((far, *far_sides), FAR_PLAN, gain_row, matrix, tokens, logits)
+    logits, matrix = add_logits((p_side, q_side, far), OTHER_PLAN, gain_row, matrix, tokens, logits)
+    logits, _ = add_logits(far_sides, LAST_PLAN, gain_row, matrix, tokens, logits)
     return logits, [ints[s] for s in (0, 1, 3, 2)]
 
 
@@ -171,11 +171,11 @@
 
 OWN_PLAN = [(0, 0, 128, 0, "all")], [(0, 128, 0, "all")]
 HELD_PLAN = [(0, 0, 64, 0, "all"), (1, 0, 64, 64, "all")], [(0, 64, 0, "p held"), (64, 64, 0, "q held")]
-OTHER_PLAN = [(0, 0, 64, 0, "all"), (1, 0, 64, 64, "all")], [(0, 64, 0, "p other"), (64, 64, 0, "q other")]
-FAR_PLAN = (
-    [(0, 0, 64, 0, "held")] + [(1 + k, 0, 32, 32 * k, "other") for k in range(2)],
-    [(0, 128, FAR * 128, "all")],
+OTHER_PLAN = (
+    [(0, 0, 64, 0, "all"), (1, 0, 64, 64, "all"), (2, 0, 64, 128, "all")],
+    [(0, 64, 0, "p other"), (64, 64, 0, "q other"), (128, 64, FAR * 128, "held")],
 )
+LAST_PLAN = [(k, 0, 32, 32 * k, "all") for k in range(2)], [(0, 64, FAR * 128, "other")]
 
 
 def add_logits(sources, plan, gain_row, matrix, tokens, filled=None):
@@ -281,10 +281,10 @@
         kept = [halves[q][1] for q in range(4)]
     state = [kept[q] + wide(came[q]) for q in range(4)]
     block = jnp.concatenate(state, axis=-1)
-    first, second = by_core(block[NEAR], block[WRAP]), by_core(block[WRAP], block[NEAR])
-    came = swap_y(narrow(jnp.stack([first, block[FAR]])), (1, 3))
-    mine, rest = block[OWN] + wide(came[0]), second + wide(came[1])
-    return [mine + wide(swap_y(narrow(rest), (3, 1)))], later
+    mine = block[OWN]
+    for group, step in ((FAR, 2), (NEAR, 1), (WRAP, 3)):
+        mine = mine + wide(swap_y(narrow(block[group]), (step, step)))
+    return [mine], later
 
 
 def shard_stats(logits, peer_logits, hit):

time: 163 us -> 173 us (1.061)
  local copies, waits for them, and re-layouts: 12.3 us -> 31.1 us
  waiting for transfers between devices: 50.1 us -> 40.8 us
  matrix products: 16.3 us -> 14.2 us
  Pallas kernels: 16.9 us -> 18.8 us
    unnamed x18 -> x26, local copies, waits for them, and re-layouts: 9.17 us -> 27.9 us
    ppermute x9 -> x10, waiting for transfers between devices: 14.1 us -> 4.56 us  [permute(): lax.ppermute(block, ALL, [(index(*p), index(*move(*p))) for p in places])]
    dot_general x12, matrix products: 16.3 us -> 14.2 us  [product(): lax.dot_general(block.reshape(-1, voc), columns, (((1,), (1,)), ((), ()))...]
    pallas_call x4, Pallas kernels: 15.6 us -> 17.5 us  [add_logits(): pl.pallas_call(make_kernel(count, streamed, *plan), out_shape=(jax.ShapeD...]
    ppermute x9 -> x10, starting transfers between devices: 13.1 us -> 13.6 us  [permute(): lax.ppermute(block, ALL, [(index(*p), index(*move(*p))) for p in places])]
  transfers between devices with their start and end apart: 39 -> 40, of which waited for: 20 -> 19; matrix products, arithmetic and copies ran while one was open for 12% -> 11% of each run, Pallas kernels for 7% -> 8%
where the time goes in v9:
time: 173 us; the launch traced here: 172 us
  starting transfers between devices  54.4 us (31%)
  waiting for transfers between devices  40.8 us (24%)
  local copies, waits for them, and re-layouts  31.1 us (18%)
  Pallas kernels  18.8 us (11%)
  matrix products  14.2 us (8%)
  other arithmetic  7.68 us (4%)
  between operations  5.71 us (3%)
    unnamed x26, local copies, waits for them, and re-layouts  27.9 us
    ppermute x12, starting transfers between devices, ring(): lax.ppermute(prepare(block, step), axis, [(i, i ^ step) for i in range(4)])  19.8 us
    pallas_call x4, Pallas kernels, add_logits(): pl.pallas_call(make_kernel(count, streamed, *plan), out_shape=(jax.ShapeD...  17.5 us
    ppermute x16, starting transfers between devices, swap(): return lax.ppermute(block, axis, [(i, i ^ step) for i in range(4)])  16.2 us
    dot_general x12, matrix products, product(): lax.dot_general(block.reshape(-1, voc), columns, (((1,), (1,)), ((), ()))...  14.2 us
    ppermute x16, waiting for transfers between devices, swap(): return lax.ppermute(block, axis, [(i, i ^ step) for i in range(4)])  13.7 us
    ppermute x10, starting transfers between devices, permute(): lax.ppermute(block, ALL, [(index(*p), index(*move(*p))) for p in places])  13.6 us
    ppermute x12, waiting for transfers between devices, ring(): lax.ppermute(prepare(block, step), axis, [(i, i ^ step) for i in range(4)])  11.4 us
  transfers between devices with their start and end apart: 40, of which 19 were waited for; matrix products, arithmetic and copies ran while one was open for 11% of the time, Pallas kernels for 8%

profile of v9, /device:TPU:0, one launch (start us, length us, event | category | flops | bytes accessed | tf_op | source)
XLA Modules:
  0.0 172.5 jit_solution(3013727007896736874)
XLA Ops:
  3.5 2.2 %collective-permute-start.1 = (bf16[64,5120]{1,0:T(8,128)(2,1)S(1)}, bf16[64,5120]{1,0:T(8,128)(2,1)S(1)}, u32[]{:S(2)}, u32[]{:S(2)}) collective-permute-start(bf16[64,5120]{1,0:T(8,128)(2,1)S(1)} %dynamic-slice_bitcast_fusion.4), channel_id=1, source_target_pairs={{0,48},{1,49},{2,50},{3,51},{4,52},{5,53},{6,54},{7,55},{8,56},{9,... | collective-permute-start | bytes 1966088 | tf_op jit(solution)/shard_map/ppermute | solution.py:30
  9.6 2.2 %collective-permute-start.4 = (s32[132]{0:T(256)S(1)}, s32[132]{0:T(256)S(1)}, u32[]{:S(2)}, u32[]{:S(2)}) collective-permute-start(s32[132]{0:T(256)S(1)} %constant_dynamic-update-slice_fusion), channel_id=1, source_target_pairs={{0,48},{16,32},{32,16},{48,0},{1,49},{17,33},{33,17},{49,1},{2,50}... | collective-permute-start | bytes 1592 | tf_op jit(solution)/shard_map/ppermute | solution.py:63
  11.7 4.7 %copy-done.4 = bf16[1,5120,1280]{2,1,0:T(8,128)(2,1)S(1)} copy-done((bf16[1,5120,1280]{2,1,0:T(8,128)(2,1)S(1)}, bf16[1,5120,1280]{2,1,0:T(8,128)(2,1)}, u32[]{:S(2)}) %copy-start.4) | copy-done | bytes 13107224
  18.5 4.8 %shard_map.68 = (bf16[512,1280]{1,0:T(8,128)(2,1)S(1)}, bf16[5120,1280]{1,0:T(8,128)(2,1)S(1)}) custom-call(bf16[128,5120]{1,0:T(8,128)(2,1)S(1)} %bitcast.370, f32[1,5120]{1,0:T(1,128)S(1)} %copy-done.6, bf16[5120,1280]{1,0:T(8,128)(2,1)S(1)} %bitcast.367), custom_call_target="tpu_custom_call" | custom-call | flops 1677721600 | bytes 14417920 | tf_op jit(solution)/shard_map/pallas_call | solution.py:188
  23.3 4.7 %copy-done = bf16[5120,1280]{1,0:T(8,128)(2,1)} copy-done((bf16[5120,1280]{1,0:T(8,128)(2,1)}, bf16[5120,1280]{1,0:T(8,128)(2,1)S(1)}, u32[]{:S(2)}) %copy-start) | copy-done | bytes 13107224
  28.3 2.8 %collective-permute-start.9 = (bf16[64,5120]{1,0:T(8,128)(2,1)S(1)}, bf16[64,5120]{1,0:T(8,128)(2,1)S(1)}, u32[]{:S(2)}, u32[]{:S(2)}) collective-permute-start(bf16[64,5120]{1,0:T(8,128)(2,1)S(1)} %collective-permute-done.1.refs_1_), channel_id=1, source_target_pairs={{0,12},{1,13},{2,14},{3,15},{4,8},{5,9},{6,10},{7,11},{8,4},{9,5},... | collective-permute-start | bytes 1966088 | tf_op jit(solution)/shard_map/ppermute | solution.py:30
  31.4 4.7 %copy-done.1 = bf16[5120,1280]{1,0:T(8,128)(2,1)S(1)} copy-done((bf16[5120,1280]{1,0:T(8,128)(2,1)S(1)}, bf16[5120,1280]{1,0:T(8,128)(2,1)}, u32[]{:S(2)}) %copy-start.1) | copy-done | bytes 13107224
  36.1 3.8 %shard_map.69 = (bf16[512,1280]{1,0:T(8,128)(2,1)S(1)}, bf16[5120,1280]{1,0:T(8,128)(2,1)S(1)}) custom-call(bf16[64,5120]{1,0:T(8,128)(2,1)S(1)} %collective-permute-done.refs_0_, bf16[64,5120]{1,0:T(8,128)(2,1)S(1)} %collective-permute-done.1.refs_1_, f32[1,5120]{1,0:T(1,128)S(1)} %copy-done.7, ...), custom_call_target="tpu_custom_call", output_to_operand_aliasing={{1}: (3, {}), {0}: (4, {})} | custom-call | flops 1677721600 | bytes 14417920 | tf_op jit(solution)/shard_map/pallas_call | solution.py:188
  39.9 4.7 %copy-done.2 = bf16[5120,1280]{1,0:T(8,128)(2,1)} copy-done((bf16[5120,1280]{1,0:T(8,128)(2,1)}, bf16[5120,1280]{1,0:T(8,128)(2,1)S(1)}, u32[]{:S(2)}) %copy-start.2) | copy-done | bytes 13107224
  47.1 4.7 %copy-done.3 = bf16[5120,1280]{1,0:T(8,128)(2,1)S(1)} copy-done((bf16[5120,1280]{1,0:T(8,128)(2,1)S(1)}, bf16[5120,1280]{1,0:T(8,128)(2,1)}, u32[]{:S(2)}) %copy-start.3) | copy-done | bytes 13107224
  51.8 5.5 %shard_map.70 = (bf16[512,1280]{1,0:T(8,128)(2,1)S(1)}, bf16[5120,1280]{1,0:T(8,128)(2,1)S(1)}) custom-call(bf16[64,5120]{1,0:T(8,128)(2,1)S(1)} %collective-permute-done.8.refs_0_, bf16[64,5120]{1,0:T(8,128)(2,1)S(1)} %collective-permute-done.9.refs_1_, ...), custom_call_target="tpu_custom_call", output_to_operand_aliasing={{1}: (4, {}), {0}: (5, {})} | custom-call | flops 2516582400 | bytes 15073280 | tf_op jit(solution)/shard_map/pallas_call | solution.py:188
  57.3 3.4 %shard_map.71 = (bf16[512,1280]{1,0:T(8,128)(2,1)S(1)}, bf16[5120,1280]{1,0:T(8,128)(2,1)S(1)}) custom-call(bf16[32,5120]{1,0:T(8,128)(2,1)S(1)} %collective-permute-done.6.refs_0_, bf16[32,5120]{1,0:T(8,128)(2,1)S(1)} %collective-permute-done.7.refs_1_, f32[1,5120]{1,0:T(1,128)S(1)} %copy-done.7, ...), custom_call_target="tpu_custom_call", output_to_operand_aliasing={{1}: (3, {}), {0}: (4, {})} | custom-call | flops 838860800 | bytes 13762560 | tf_op jit(solution)/shard_map/pallas_call | solution.py:188
  67.1 3.6 %collective-permute-start.12 = (f32[6,512]{1,0:T(8,128)S(1)}, f32[6,512]{1,0:T(8,128)S(1)}, u32[]{:S(2)}, u32[]{:S(2)}) collective-permute-start(f32[6,512]{1,0:T(8,128)S(1)} %select_select_fusion), channel_id=1, source_target_pairs={{0,2},{1,3},{2,0},{3,1},{4,6},{5,7},{6,4},{7,5},{8,10},{9,11},{10,... | collective-permute-start | bytes 36872 | tf_op jit(solution)/shard_map/ppermute | solution.py:63
  72.6 3.1 %collective-permute-done.13 = f32[6,512]{1,0:T(8,128)S(1)} collective-permute-done((f32[6,512]{1,0:T(8,128)S(1)}, f32[6,512]{1,0:T(8,128)S(1)}, u32[]{:S(2)}, u32[]{:S(2)}) %collective-permute-start.13) | collective-permute-done | bytes 12320 | tf_op jit(solution)/shard_map/ppermute | solution.py:63
  76.2 3.9 %collective-permute-start.15 = (f32[6,512]{1,0:T(8,128)S(1)}, f32[6,512]{1,0:T(8,128)S(1)}, u32[]{:S(2)}, u32[]{:S(2)}) collective-permute-start(f32[6,512]{1,0:T(8,128)S(1)} %get-tuple-element.115), channel_id=1, source_target_pairs={{0,8},{4,12},{8,0},{12,4},{1,9},{5,13},{9,1},{13,5},{2,10},{6,14},... | collective-permute-start | bytes 36872 | tf_op jit(solution)/shard_map/ppermute | solution.py:63
  82.2 3.0 %collective-permute-done.16 = f32[6,512]{1,0:T(8,128)S(1)} collective-permute-done((f32[6,512]{1,0:T(8,128)S(1)}, f32[6,512]{1,0:T(8,128)S(1)}, u32[]{:S(2)}, u32[]{:S(2)}) %collective-permute-start.16) | collective-permute-done | bytes 12320 | tf_op jit(solution)/shard_map/ppermute | solution.py:63
  88.0 2.2 %collective-permute-start.19 = (f32[6,512]{1,0:T(8,128)S(1)}, f32[6,512]{1,0:T(8,128)S(1)}, u32[]{:S(2)}, u32[]{:S(2)}) collective-permute-start(f32[6,512]{1,0:T(8,128)S(1)} %pad_maximum_fusion.9), channel_id=1, source_target_pairs={{0,48},{16,32},{32,16},{48,0},{1,49},{17,33},{33,17},{49,1},{2,50}... | collective-permute-start | bytes 36872 | tf_op jit(solution)/shard_map/ppermute | solution.py:63
  105.2 4.5 %collective-permute-done.20 = bf16[2,2,2,4,8,1280]{5,4,3,2,1,0:T(8,128)(2,1)S(1)} collective-permute-done((bf16[2,2,2,4,8,1280]{5,4,3,2,1,0:T(8,128)(2,1)S(1)}, bf16[2,2,2,4,8,1280]{5,4,3,2,1,0:T(8,128)(2,1)S(1)}, u32[]{:S(2)}, u32[]{:S(2)}) %collective-permute-start.20) | collective-permute-done | bytes 655392 | tf_op jit(solution)/shard_map/ppermute | solution.py:260
  111.0 3.5 %collective-permute-done.24 = bf16[2,2,2,4,8,1280]{5,4,3,2,1,0:T(8,128)(2,1)S(1)} collective-permute-done((bf16[2,2,2,4,8,1280]{5,4,3,2,1,0:T(8,128)(2,1)S(1)}, bf16[2,2,2,4,8,1280]{5,4,3,2,1,0:T(8,128)(2,1)S(1)}, u32[]{:S(2)}, u32[]{:S(2)}) %collective-permute-start.24) | collective-permute-done | bytes 655392 | tf_op jit(solution)/shard_map/ppermute | solution.py:260
  125.1 3.1 %collective-permute-start.26 = (bf16[2,4,8,1280]{3,2,1,0:T(8,128)(2,1)S(1)}, bf16[2,4,8,1280]{3,2,1,0:T(8,128)(2,1)S(1)}, u32[]{:S(2)}, u32[]{:S(2)}) collective-permute-start(bf16[2,4,8,1280]{3,2,1,0:T(8,128)(2,1)S(1)} %get-tuple-element.73), channel_id=1, source_target_pairs={{0,3},{1,2},{2,1},{3,0},{4,7},{5,6},{6,5},{7,4},{8,11},{9,10},{10,... | collective-permute-start | bytes 491528 | tf_op jit(solution)/shard_map/ppermute | solution.py:260
  131.4 3.1 %collective-permute-start.23 = (bf16[4,8,1280]{2,1,0:T(8,128)(2,1)S(1)}, bf16[4,8,1280]{2,1,0:T(8,128)(2,1)S(1)}, u32[]{:S(2)}, u32[]{:S(2)}) collective-permute-start(bf16[4,8,1280]{2,1,0:T(8,128)(2,1)S(1)} %fusion.129), channel_id=1, source_target_pairs={{0,3},{1,2},{2,1},{3,0},{4,7},{5,6},{6,5},{7,4},{8,11},{9,10},{10,... | collective-permute-start | bytes 245768 | tf_op jit(solution)/shard_map/ppermute | solution.py:260
  147.4 2.4 %collective-permute-done.38 = bf16[8,5120]{1,0:T(8,128)(2,1)S(1)} collective-permute-done((bf16[8,5120]{1,0:T(8,128)(2,1)S(1)}, bf16[8,5120]{1,0:T(8,128)(2,1)S(1)}, u32[]{:S(2)}, u32[]{:S(2)}) %collective-permute-start.38) | collective-permute-done | bytes 81952 | tf_op jit(solution)/shard_map/ppermute | solution.py:30
  151.1 4.6 %all-to-all-start = ((bf16[16,8,5120]{2,1,0:T(8,128)(2,1)}), bf16[16,8,5120]{2,1,0:T(8,128)(2,1)S(1)}, u32[]{:S(2)}, u32[]{:S(2)}) async-start(bf16[16,8,5120]{2,1,0:T(8,128)(2,1)} %shard_map.72), calls=%async_computation | async-start | bytes 2621440 | tf_op jit(solution)/shard_map/all_to_all | solution.py:375
  159.7 10.6 %all-to-all-done = bf16[16,8,5120]{2,1,0:T(8,128)(2,1)S(1)} async-done(((bf16[16,8,5120]{2,1,0:T(8,128)(2,1)}), bf16[16,8,5120]{2,1,0:T(8,128)(2,1)S(1)}, u32[]{:S(2)}, u32[]{:S(2)}) %all-to-all-start) | async-done | bytes 1310752 | tf_op jit(solution)/shard_map/all_to_all | solution.py:375
  (186 shorter events, 70.9 us)
Async XLA Ops:
  1.8 26.3 %collective-permute-start = (bf16[64,5120]{1,0:T(8,128)(2,1)S(1)}, bf16[64,5120]{1,0:T(8,128)(2,1)S(1)}, u32[]{:S(2)}, u32[]{:S(2)}) collective-permute-start(bf16[64,5120]{1,0:T(8,128)(2,1)S(1)} %dynamic-slice_bitcast_fusion.4), channel_id=1, source_target_pairs={{0,16},{1,17},{2,18},{3,19},{4,20},{5,21},{6,22},{7,23},{8,24},{9,... | collective-permute-start | bytes 1966088 | tf_op jit(solution)/shard_map/ppermute | solution.py:30
  3.5 24.6 %collective-permute-start.1 = (bf16[64,5120]{1,0:T(8,128)(2,1)S(1)}, bf16[64,5120]{1,0:T(8,128)(2,1)S(1)}, u32[]{:S(2)}, u32[]{:S(2)}) collective-permute-start(bf16[64,5120]{1,0:T(8,128)(2,1)S(1)} %dynamic-slice_bitcast_fusion.4), channel_id=1, source_target_pairs={{0,48},{1,49},{2,50},{3,51},{4,52},{5,53},{6,54},{7,55},{8,56},{9,... | collective-permute-start | bytes 1966088 | tf_op jit(solution)/shard_map/ppermute | solution.py:30
  7.0 21.0 %collective-permute-start.2 = (s32[132]{0:T(256)S(1)}, s32[132]{0:T(256)S(1)}, u32[]{:S(2)}, u32[]{:S(2)}) collective-permute-start(s32[132]{0:T(256)S(1)} %constant_dynamic-update-slice_fusion), channel_id=1, source_target_pairs={{0,16},{16,0},{32,48},{48,32},{1,17},{17,1},{33,49},{49,33},{2,18}... | collective-permute-start | bytes 1592 | tf_op jit(solution)/shard_map/ppermute | solution.py:63
  7.7 20.4 %collective-permute-start.3 = (s32[132]{0:T(256)S(1)}, s32[132]{0:T(256)S(1)}, u32[]{:S(2)}, u32[]{:S(2)}) collective-permute-start(s32[132]{0:T(256)S(1)} %constant_dynamic-update-slice_fusion), channel_id=1, source_target_pairs={{0,32},{16,48},{32,0},{48,16},{1,33},{17,49},{33,1},{49,17},{2,34}... | collective-permute-start | bytes 1592 | tf_op jit(solution)/shard_map/ppermute | solution.py:63
  9.6 18.5 %collective-permute-start.4 = (s32[132]{0:T(256)S(1)}, s32[132]{0:T(256)S(1)}, u32[]{:S(2)}, u32[]{:S(2)}) collective-permute-start(s32[132]{0:T(256)S(1)} %constant_dynamic-update-slice_fusion), channel_id=1, source_target_pairs={{0,48},{16,32},{32,16},{48,0},{1,49},{17,33},{33,17},{49,1},{2,50}... | collective-permute-start | bytes 1592 | tf_op jit(solution)/shard_map/ppermute | solution.py:63
  28.1 16.5 %collective-permute-start.5 = (bf16[64,5120]{1,0:T(8,128)(2,1)S(1)}, bf16[64,5120]{1,0:T(8,128)(2,1)S(1)}, u32[]{:S(2)}, u32[]{:S(2)}) collective-permute-start(bf16[64,5120]{1,0:T(8,128)(2,1)S(1)} %collective-permute-done.1.refs_1_), channel_id=1, source_target_pairs={{0,16},{1,17},{2,18},{3,19},{4,20},{5,21},{6,22},{7,23},{8,24},{9,... | collective-permute-start | bytes 1966088 | tf_op jit(solution)/shard_map/ppermute | solution.py:30
  28.3 18.8 %collective-permute-start.9 = (bf16[64,5120]{1,0:T(8,128)(2,1)S(1)}, bf16[64,5120]{1,0:T(8,128)(2,1)S(1)}, u32[]{:S(2)}, u32[]{:S(2)}) collective-permute-start(bf16[64,5120]{1,0:T(8,128)(2,1)S(1)} %collective-permute-done.1.refs_1_), channel_id=1, source_target_pairs={{0,12},{1,13},{2,14},{3,15},{4,8},{5,9},{6,10},{7,11},{8,4},{9,5},... | collective-permute-start | bytes 1966088 | tf_op jit(solution)/shard_map/ppermute | solution.py:30
  31.1 15.9 %collective-permute-start.8 = (bf16[64,5120]{1,0:T(8,128)(2,1)S(1)}, bf16[64,5120]{1,0:T(8,128)(2,1)S(1)}, u32[]{:S(2)}, u32[]{:S(2)}) collective-permute-start(bf16[64,5120]{1,0:T(8,128)(2,1)S(1)} %collective-permute-done.refs_0_), channel_id=1, source_target_pairs={{0,4},{1,5},{2,6},{3,7},{4,0},{5,1},{6,2},{7,3},{8,12},{9,13},{10,... | collective-permute-start | bytes 1966088 | tf_op jit(solution)/shard_map/ppermute | solution.py:30
  44.7 12.6 %collective-permute-start.6 = (bf16[32,5120]{1,0:T(8,128)(2,1)S(1)}, bf16[32,5120]{1,0:T(8,128)(2,1)S(1)}, u32[]{:S(2)}, u32[]{:S(2)}) collective-permute-start(bf16[32,5120]{1,0:T(8,128)(2,1)S(1)} %get-tuple-element.84), channel_id=1, source_target_pairs={{0,4},{1,5},{2,6},{3,7},{4,0},{5,1},{6,2},{7,3},{8,12},{9,13},{10,... | collective-permute-start | bytes 983048 | tf_op jit(solution)/shard_map/ppermute | solution.py:30
  46.6 10.7 %collective-permute-start.7 = (bf16[32,5120]{1,0:T(8,128)(2,1)S(1)}, bf16[32,5120]{1,0:T(8,128)(2,1)S(1)}, u32[]{:S(2)}, u32[]{:S(2)}) collective-permute-start(bf16[32,5120]{1,0:T(8,128)(2,1)S(1)} %get-tuple-element.83), channel_id=1, source_target_pairs={{0,12},{1,13},{2,14},{3,15},{4,8},{5,9},{6,10},{7,11},{8,4},{9,5},... | collective-permute-start | bytes 983048 | tf_op jit(solution)/shard_map/ppermute | solution.py:30
  97.3 12.3 %collective-permute-start.20 = (bf16[2,2,2,4,8,1280]{5,4,3,2,1,0:T(8,128)(2,1)S(1)}, bf16[2,2,2,4,8,1280]{5,4,3,2,1,0:T(8,128)(2,1)S(1)}, u32[]{:S(2)}, u32[]{:S(2)}) collective-permute-start(bf16[2,2,2,4,8,1280]{5,4,3,2,1,0:T(8,128)(2,1)S(1)} %fusion.48), channel_id=1, source_target_pairs={{0,4},{4,0},{8,12},{12,8},{1,5},{5,1},{9,13},{13,9},{2,6},{6,2},{1... | collective-permute-start | bytes 1966088 | tf_op jit(solution)/shard_map/ppermute | solution.py:260
  98.5 16.1 %collective-permute-start.24 = (bf16[2,2,2,4,8,1280]{5,4,3,2,1,0:T(8,128)(2,1)S(1)}, bf16[2,2,2,4,8,1280]{5,4,3,2,1,0:T(8,128)(2,1)S(1)}, u32[]{:S(2)}, u32[]{:S(2)}) collective-permute-start(bf16[2,2,2,4,8,1280]{5,4,3,2,1,0:T(8,128)(2,1)S(1)} %fusion.51), channel_id=1, source_target_pairs={{0,12},{4,8},{8,4},{12,0},{1,13},{5,9},{9,5},{13,1},{2,14},{6,10},... | collective-permute-start | bytes 1966088 | tf_op jit(solution)/shard_map/ppermute | solution.py:260
  101.8 15.6 %collective-permute-start.28 = (bf16[2,2,2,4,8,1280]{5,4,3,2,1,0:T(8,128)(2,1)S(1)}, bf16[2,2,2,4,8,1280]{5,4,3,2,1,0:T(8,128)(2,1)S(1)}, u32[]{:S(2)}, u32[]{:S(2)}) collective-permute-start(bf16[2,2,2,4,8,1280]{5,4,3,2,1,0:T(8,128)(2,1)S(1)} %fusion.54), channel_id=1, source_target_pairs={{0,1},{1,0},{2,3},{3,2},{4,5},{5,4},{6,7},{7,6},{8,9},{9,8},{10,11... | collective-permute-start | bytes 1966088 | tf_op jit(solution)/shard_map/ppermute | solution.py:260
  103.0 17.4 %collective-permute-start.32 = (bf16[2,2,2,4,8,1280]{5,4,3,2,1,0:T(8,128)(2,1)S(1)}, bf16[2,2,2,4,8,1280]{5,4,3,2,1,0:T(8,128)(2,1)S(1)}, u32[]{:S(2)}, u32[]{:S(2)}) collective-permute-start(bf16[2,2,2,4,8,1280]{5,4,3,2,1,0:T(8,128)(2,1)S(1)} %fusion.57), channel_id=1, source_target_pairs={{0,3},{1,2},{2,1},{3,0},{4,7},{5,6},{6,5},{7,4},{8,11},{9,10},{10,... | collective-permute-start | bytes 1966088 | tf_op jit(solution)/shard_map/ppermute | solution.py:260
  110.8 12.1 %collective-permute-start.21 = (bf16[2,2,4,8,1280]{4,3,2,1,0:T(8,128)(2,1)S(1)}, bf16[2,2,4,8,1280]{4,3,2,1,0:T(8,128)(2,1)S(1)}, u32[]{:S(2)}, u32[]{:S(2)}) collective-permute-start(bf16[2,2,4,8,1280]{4,3,2,1,0:T(8,128)(2,1)S(1)} %fusion.78), channel_id=1, source_target_pairs={{0,12},{4,8},{8,4},{12,0},{1,13},{5,9},{9,5},{13,1},{2,14},{6,10},... | collective-permute-start | bytes 983048 | tf_op jit(solution)/shard_map/ppermute | solution.py:260
  115.8 9.3 %collective-permute-start.25 = (bf16[2,2,4,8,1280]{4,3,2,1,0:T(8,128)(2,1)S(1)}, bf16[2,2,4,8,1280]{4,3,2,1,0:T(8,128)(2,1)S(1)}, u32[]{:S(2)}, u32[]{:S(2)}) collective-permute-start(bf16[2,2,4,8,1280]{4,3,2,1,0:T(8,128)(2,1)S(1)} %get-tuple-element.79), channel_id=1, source_target_pairs={{0,4},{4,0},{8,12},{12,8},{1,5},{5,1},{9,13},{13,9},{2,6},{6,2},{1... | collective-permute-start | bytes 983048 | tf_op jit(solution)/shard_map/ppermute | solution.py:260
  118.6 9.7 %collective-permute-start.29 = (bf16[2,2,4,8,1280]{4,3,2,1,0:T(8,128)(2,1)S(1)}, bf16[2,2,4,8,1280]{4,3,2,1,0:T(8,128)(2,1)S(1)}, u32[]{:S(2)}, u32[]{:S(2)}) collective-permute-start(bf16[2,2,4,8,1280]{4,3,2,1,0:T(8,128)(2,1)S(1)} %fusion.93), channel_id=1, source_target_pairs={{0,3},{1,2},{2,1},{3,0},{4,7},{5,6},{6,5},{7,4},{8,11},{9,10},{10,... | collective-permute-start | bytes 983048 | tf_op jit(solution)/shard_map/ppermute | solution.py:260
  121.6 8.0 %collective-permute-start.33 = (bf16[2,2,4,8,1280]{4,3,2,1,0:T(8,128)(2,1)S(1)}, bf16[2,2,4,8,1280]{4,3,2,1,0:T(8,128)(2,1)S(1)}, u32[]{:S(2)}, u32[]{:S(2)}) collective-permute-start(bf16[2,2,4,8,1280]{4,3,2,1,0:T(8,128)(2,1)S(1)} %get-tuple-element.81), channel_id=1, source_target_pairs={{0,1},{1,0},{2,3},{3,2},{4,5},{5,4},{6,7},{7,6},{8,9},{9,8},{10,11... | collective-permute-start | bytes 983048 | tf_op jit(solution)/shard_map/ppermute | solution.py:260
  123.0 8.4 %collective-permute-start.22 = (bf16[2,4,8,1280]{3,2,1,0:T(8,128)(2,1)S(1)}, bf16[2,4,8,1280]{3,2,1,0:T(8,128)(2,1)S(1)}, u32[]{:S(2)}, u32[]{:S(2)}) collective-permute-start(bf16[2,4,8,1280]{3,2,1,0:T(8,128)(2,1)S(1)} %get-tuple-element.71), channel_id=1, source_target_pairs={{0,1},{1,0},{2,3},{3,2},{4,5},{5,4},{6,7},{7,6},{8,9},{9,8},{10,11... | collective-permute-start | bytes 491528 | tf_op jit(solution)/shard_map/ppermute | solution.py:260
  125.1 9.4 %collective-permute-start.26 = (bf16[2,4,8,1280]{3,2,1,0:T(8,128)(2,1)S(1)}, bf16[2,4,8,1280]{3,2,1,0:T(8,128)(2,1)S(1)}, u32[]{:S(2)}, u32[]{:S(2)}) collective-permute-start(bf16[2,4,8,1280]{3,2,1,0:T(8,128)(2,1)S(1)} %get-tuple-element.73), channel_id=1, source_target_pairs={{0,3},{1,2},{2,1},{3,0},{4,7},{5,6},{6,5},{7,4},{8,11},{9,10},{10,... | collective-permute-start | bytes 491528 | tf_op jit(solution)/shard_map/ppermute | solution.py:260
  128.3 6.3 %collective-permute-start.30 = (bf16[2,4,8,1280]{3,2,1,0:T(8,128)(2,1)S(1)}, bf16[2,4,8,1280]{3,2,1,0:T(8,128)(2,1)S(1)}, u32[]{:S(2)}, u32[]{:S(2)}) collective-permute-start(bf16[2,4,8,1280]{3,2,1,0:T(8,128)(2,1)S(1)} %get-tuple-element.75), channel_id=1, source_target_pairs={{0,4},{4,0},{8,12},{12,8},{1,5},{5,1},{9,13},{13,9},{2,6},{6,2},{1... | collective-permute-start | bytes 491528 | tf_op jit(solution)/shard_map/ppermute | solution.py:260
  129.7 6.7 %collective-permute-start.34 = (bf16[2,4,8,1280]{3,2,1,0:T(8,128)(2,1)S(1)}, bf16[2,4,8,1280]{3,2,1,0:T(8,128)(2,1)S(1)}, u32[]{:S(2)}, u32[]{:S(2)}) collective-permute-start(bf16[2,4,8,1280]{3,2,1,0:T(8,128)(2,1)S(1)} %get-tuple-element.77), channel_id=1, source_target_pairs={{0,12},{4,8},{8,4},{12,0},{1,13},{5,9},{9,5},{13,1},{2,14},{6,10},... | collective-permute-start | bytes 491528 | tf_op jit(solution)/shard_map/ppermute | solution.py:260
  141.0 6.0 %collective-permute-start.36 = (bf16[8,5120]{1,0:T(8,128)(2,1)S(1)}, bf16[8,5120]{1,0:T(8,128)(2,1)S(1)}, u32[]{:S(2)}, u32[]{:S(2)}) collective-permute-start(bf16[8,5120]{1,0:T(8,128)(2,1)S(1)} %get-tuple-element.85), channel_id=1, source_target_pairs={{0,32},{1,33},{2,34},{3,35},{4,36},{5,37},{6,38},{7,39},{8,40},{9,... | collective-permute-start | bytes 245768 | tf_op jit(solution)/shard_map/ppermute | solution.py:30
  151.1 19.2 %all-to-all-start = ((bf16[16,8,5120]{2,1,0:T(8,128)(2,1)}), bf16[16,8,5120]{2,1,0:T(8,128)(2,1)S(1)}, u32[]{:S(2)}, u32[]{:S(2)}) async-start(bf16[16,8,5120]{2,1,0:T(8,128)(2,1)} %shard_map.72), calls=%async_computation | async-start | bytes 2621440 | tf_op jit(solution)/shard_map/all_to_all | solution.py:375
  (28 other events, 229.5 us)

commit v10 on v8

--- a/solution.py
+++ b/solution.py
@@ -281,10 +281,10 @@
         kept = [halves[q][1] for q in range(4)]
     state = [kept[q] + wide(came[q]) for q in range(4)]
     block = jnp.concatenate(state, axis=-1)
-    first, second = by_core(block[NEAR], block[WRAP]), by_core(block[WRAP], block[NEAR])
-    came = swap_y(narrow(jnp.stack([first, block[FAR]])), (1, 3))
-    mine, rest = block[OWN] + wide(came[0]), second + wide(came[1])
-    return [mine + wide(swap_y(narrow(rest), (3, 1)))], later
+    mine = block[OWN]
+    for group, step in ((FAR, 2), (NEAR, 1), (WRAP, 3)):
+        mine = mine + wide(swap_y(narrow(block[group]), (step, step)))
+    return [mine], later
 
 
 def shard_stats(logits, peer_logits, hit):

time: 163 us -> 173 us (1.061)
  local copies, waits for them, and re-layouts: 12.3 us -> 32.2 us
  waiting for transfers between devices: 50.1 us -> 39.8 us
  matrix products: 16.3 us -> 14.2 us
    unnamed x18 -> x26, local copies, waits for them, and re-layouts: 9.17 us -> 29.1 us
    ppermute x9 -> x10, waiting for transfers between devices: 14.1 us -> 4.57 us  [permute(): lax.ppermute(block, ALL, [(index(*p), index(*move(*p))) for p in places])]
    dot_general x12, matrix products: 16.3 us -> 14.2 us  [product(): lax.dot_general(block.reshape(-1, voc), columns, (((1,), (1,)), ((), ()))...]
    ppermute x9 -> x10, starting transfers between devices: 13.1 us -> 13.6 us  [permute(): lax.ppermute(block, ALL, [(index(*p), index(*move(*p))) for p in places])]
  transfers between devices with their start and end apart: 39 -> 40, of which waited for: 20 -> 18; matrix products, arithmetic and copies ran while one was open for 12% -> 11% of each run, Pallas kernels for 7% -> 7%
where the time goes in v10:
time: 173 us; the launch traced here: 172 us
  starting transfers between devices  55.2 us (32%)
  waiting for transfers between devices  39.8 us (23%)
  local copies, waits for them, and re-layouts  32.2 us (19%)
  Pallas kernels  17.2 us (10%)
  matrix products  14.2 us (8%)
  other arithmetic  7.68 us (4%)
  between operations  5.71 us (3%)
    unnamed x26, local copies, waits for them, and re-layouts  29.1 us
    ppermute x12, starting transfers between devices, ring(): lax.ppermute(prepare(block, step), axis, [(i, i ^ step) for i in range(4)])  19.8 us
    ppermute x16, starting transfers between devices, swap(): return lax.ppermute(block, axis, [(i, i ^ step) for i in range(4)])  16.9 us
    pallas_call x4, Pallas kernels, add_logits(): pl.pallas_call(make_kernel(count, streamed, *plan), out_shape=(jax.ShapeD...  15.9 us
    dot_general x12, matrix products, product(): lax.dot_general(block.reshape(-1, voc), columns, (((1,), (1,)), ((), ()))...  14.2 us
    ppermute x10, starting transfers between devices, permute(): lax.ppermute(block, ALL, [(index(*p), index(*move(*p))) for p in places])  13.6 us
    ppermute x16, waiting for transfers between devices, swap(): return lax.ppermute(block, axis, [(i, i ^ step) for i in range(4)])  12.8 us
    ppermute x12, waiting for transfers between devices, ring(): lax.ppermute(prepare(block, step), axis, [(i, i ^ step) for i in range(4)])  11.4 us
  transfers between devices with their start and end apart: 40, of which 18 were waited for; matrix products, arithmetic and copies ran while one was open for 11% of the time, Pallas kernels for 7%

profile of v10, /device:TPU:0, one launch (start us, length us, event | category | flops | bytes accessed | tf_op | source)
XLA Modules:
  0.0 172.0 jit_solution(1986998250862603858)
XLA Ops:
  3.5 2.2 %collective-permute-start.1 = (bf16[64,5120]{1,0:T(8,128)(2,1)S(1)}, bf16[64,5120]{1,0:T(8,128)(2,1)S(1)}, u32[]{:S(2)}, u32[]{:S(2)}) collective-permute-start(bf16[64,5120]{1,0:T(8,128)(2,1)S(1)} %dynamic-slice_bitcast_fusion.4), channel_id=1, source_target_pairs={{0,48},{1,49},{2,50},{3,51},{4,52},{5,53},{6,54},{7,55},{8,56},{9,... | collective-permute-start | bytes 1966088 | tf_op jit(solution)/shard_map/ppermute | solution.py:30
  9.6 2.2 %collective-permute-start.4 = (s32[132]{0:T(256)S(1)}, s32[132]{0:T(256)S(1)}, u32[]{:S(2)}, u32[]{:S(2)}) collective-permute-start(s32[132]{0:T(256)S(1)} %constant_dynamic-update-slice_fusion), channel_id=1, source_target_pairs={{0,48},{16,32},{32,16},{48,0},{1,49},{17,33},{33,17},{49,1},{2,50}... | collective-permute-start | bytes 1592 | tf_op jit(solution)/shard_map/ppermute | solution.py:63
  11.7 4.7 %copy-done.4 = bf16[1,5120,1280]{2,1,0:T(8,128)(2,1)S(1)} copy-done((bf16[1,5120,1280]{2,1,0:T(8,128)(2,1)S(1)}, bf16[1,5120,1280]{2,1,0:T(8,128)(2,1)}, u32[]{:S(2)}) %copy-start.4) | copy-done | bytes 13107224
  18.5 4.8 %shard_map.68 = (bf16[512,1280]{1,0:T(8,128)(2,1)S(1)}, bf16[5120,1280]{1,0:T(8,128)(2,1)S(1)}) custom-call(bf16[128,5120]{1,0:T(8,128)(2,1)S(1)} %bitcast.370, f32[1,5120]{1,0:T(1,128)S(1)} %copy-done.6, bf16[5120,1280]{1,0:T(8,128)(2,1)S(1)} %bitcast.367), custom_call_target="tpu_custom_call" | custom-call | flops 1677721600 | bytes 14417920 | tf_op jit(solution)/shard_map/pallas_call | solution.py:188
  23.3 4.7 %copy-done = bf16[5120,1280]{1,0:T(8,128)(2,1)} copy-done((bf16[5120,1280]{1,0:T(8,128)(2,1)}, bf16[5120,1280]{1,0:T(8,128)(2,1)S(1)}, u32[]{:S(2)}) %copy-start) | copy-done | bytes 13107224
  28.3 2.8 %collective-permute-start.9 = (bf16[64,5120]{1,0:T(8,128)(2,1)S(1)}, bf16[64,5120]{1,0:T(8,128)(2,1)S(1)}, u32[]{:S(2)}, u32[]{:S(2)}) collective-permute-start(bf16[64,5120]{1,0:T(8,128)(2,1)S(1)} %collective-permute-done.1.refs_1_), channel_id=1, source_target_pairs={{0,12},{1,13},{2,14},{3,15},{4,8},{5,9},{6,10},{7,11},{8,4},{9,5},... | collective-permute-start | bytes 1966088 | tf_op jit(solution)/shard_map/ppermute | solution.py:30
  31.3 4.7 %copy-done.1 = bf16[5120,1280]{1,0:T(8,128)(2,1)S(1)} copy-done((bf16[5120,1280]{1,0:T(8,128)(2,1)S(1)}, bf16[5120,1280]{1,0:T(8,128)(2,1)}, u32[]{:S(2)}) %copy-start.1) | copy-done | bytes 13107224
  36.1 3.8 %shard_map.69 = (bf16[512,1280]{1,0:T(8,128)(2,1)S(1)}, bf16[5120,1280]{1,0:T(8,128)(2,1)S(1)}) custom-call(bf16[64,5120]{1,0:T(8,128)(2,1)S(1)} %collective-permute-done.refs_0_, bf16[64,5120]{1,0:T(8,128)(2,1)S(1)} %collective-permute-done.1.refs_1_, f32[1,5120]{1,0:T(1,128)S(1)} %copy-done.7, ...), custom_call_target="tpu_custom_call", output_to_operand_aliasing={{1}: (3, {}), {0}: (4, {})} | custom-call | flops 1677721600 | bytes 14417920 | tf_op jit(solution)/shard_map/pallas_call | solution.py:188
  39.9 4.7 %copy-done.2 = bf16[5120,1280]{1,0:T(8,128)(2,1)} copy-done((bf16[5120,1280]{1,0:T(8,128)(2,1)}, bf16[5120,1280]{1,0:T(8,128)(2,1)S(1)}, u32[]{:S(2)}) %copy-start.2) | copy-done | bytes 13107224
  47.1 4.7 %copy-done.3 = bf16[5120,1280]{1,0:T(8,128)(2,1)S(1)} copy-done((bf16[5120,1280]{1,0:T(8,128)(2,1)S(1)}, bf16[5120,1280]{1,0:T(8,128)(2,1)}, u32[]{:S(2)}) %copy-start.3) | copy-done | bytes 13107224
  51.8 3.8 %shard_map.70 = (bf16[512,1280]{1,0:T(8,128)(2,1)S(1)}, bf16[5120,1280]{1,0:T(8,128)(2,1)S(1)}) custom-call(bf16[64,5120]{1,0:T(8,128)(2,1)S(1)} %collective-permute-done.8.refs_0_, bf16[64,5120]{1,0:T(8,128)(2,1)S(1)} %collective-permute-done.9.refs_1_, f32[1,5120]{1,0:T(1,128)S(1)} %copy-done.7, ...), custom_call_target="tpu_custom_call", output_to_operand_aliasing={{1}: (3, {}), {0}: (4, {})} | custom-call | flops 1677721600 | bytes 14417920 | tf_op jit(solution)/shard_map/pallas_call | solution.py:188
  55.6 3.5 %shard_map.71 = (bf16[512,1280]{1,0:T(8,128)(2,1)S(1)}, bf16[5120,1280]{1,0:T(8,128)(2,1)S(1)}) custom-call(bf16[64,5120]{1,0:T(8,128)(2,1)S(1)} %collective-permute-done.5.refs_0_, bf16[32,5120]{1,0:T(8,128)(2,1)S(1)} %collective-permute-done.6.refs_1_, ...), custom_call_target="tpu_custom_call", output_to_operand_aliasing={{1}: (4, {}), {0}: (5, {})} | custom-call | flops 1677721600 | bytes 14417920 | tf_op jit(solution)/shard_map/pallas_call | solution.py:188
  65.7 3.6 %collective-permute-start.12 = (f32[6,512]{1,0:T(8,128)S(1)}, f32[6,512]{1,0:T(8,128)S(1)}, u32[]{:S(2)}, u32[]{:S(2)}) collective-permute-start(f32[6,512]{1,0:T(8,128)S(1)} %select_select_fusion), channel_id=1, source_target_pairs={{0,2},{1,3},{2,0},{3,1},{4,6},{5,7},{6,4},{7,5},{8,10},{9,11},{10,... | collective-permute-start | bytes 36872 | tf_op jit(solution)/shard_map/ppermute | solution.py:63
  71.2 3.1 %collective-permute-done.13 = f32[6,512]{1,0:T(8,128)S(1)} collective-permute-done((f32[6,512]{1,0:T(8,128)S(1)}, f32[6,512]{1,0:T(8,128)S(1)}, u32[]{:S(2)}, u32[]{:S(2)}) %collective-permute-start.13) | collective-permute-done | bytes 12320 | tf_op jit(solution)/shard_map/ppermute | solution.py:63
  74.8 3.9 %collective-permute-start.15 = (f32[6,512]{1,0:T(8,128)S(1)}, f32[6,512]{1,0:T(8,128)S(1)}, u32[]{:S(2)}, u32[]{:S(2)}) collective-permute-start(f32[6,512]{1,0:T(8,128)S(1)} %get-tuple-element.115), channel_id=1, source_target_pairs={{0,8},{4,12},{8,0},{12,4},{1,9},{5,13},{9,1},{13,5},{2,10},{6,14},... | collective-permute-start | bytes 36872 | tf_op jit(solution)/shard_map/ppermute | solution.py:63
  80.8 3.0 %collective-permute-done.16 = f32[6,512]{1,0:T(8,128)S(1)} collective-permute-done((f32[6,512]{1,0:T(8,128)S(1)}, f32[6,512]{1,0:T(8,128)S(1)}, u32[]{:S(2)}, u32[]{:S(2)}) %collective-permute-start.16) | collective-permute-done | bytes 12320 | tf_op jit(solution)/shard_map/ppermute | solution.py:63
  86.6 2.2 %collective-permute-start.19 = (f32[6,512]{1,0:T(8,128)S(1)}, f32[6,512]{1,0:T(8,128)S(1)}, u32[]{:S(2)}, u32[]{:S(2)}) collective-permute-start(f32[6,512]{1,0:T(8,128)S(1)} %pad_maximum_fusion.9), channel_id=1, source_target_pairs={{0,48},{16,32},{32,16},{48,0},{1,49},{17,33},{33,17},{49,1},{2,50}... | collective-permute-start | bytes 36872 | tf_op jit(solution)/shard_map/ppermute | solution.py:63
  105.1 4.2 %collective-permute-done.20 = bf16[2,2,2,4,8,1280]{5,4,3,2,1,0:T(8,128)(2,1)S(1)} collective-permute-done((bf16[2,2,2,4,8,1280]{5,4,3,2,1,0:T(8,128)(2,1)S(1)}, bf16[2,2,2,4,8,1280]{5,4,3,2,1,0:T(8,128)(2,1)S(1)}, u32[]{:S(2)}, u32[]{:S(2)}) %collective-permute-start.20) | collective-permute-done | bytes 655392 | tf_op jit(solution)/shard_map/ppermute | solution.py:260
  110.8 3.5 %collective-permute-done.24 = bf16[2,2,2,4,8,1280]{5,4,3,2,1,0:T(8,128)(2,1)S(1)} collective-permute-done((bf16[2,2,2,4,8,1280]{5,4,3,2,1,0:T(8,128)(2,1)S(1)}, bf16[2,2,2,4,8,1280]{5,4,3,2,1,0:T(8,128)(2,1)S(1)}, u32[]{:S(2)}, u32[]{:S(2)}) %collective-permute-start.24) | collective-permute-done | bytes 655392 | tf_op jit(solution)/shard_map/ppermute | solution.py:260
  124.6 3.1 %collective-permute-start.26 = (bf16[2,4,8,1280]{3,2,1,0:T(8,128)(2,1)S(1)}, bf16[2,4,8,1280]{3,2,1,0:T(8,128)(2,1)S(1)}, u32[]{:S(2)}, u32[]{:S(2)}) collective-permute-start(bf16[2,4,8,1280]{3,2,1,0:T(8,128)(2,1)S(1)} %get-tuple-element.73), channel_id=1, source_target_pairs={{0,3},{1,2},{2,1},{3,0},{4,7},{5,6},{6,5},{7,4},{8,11},{9,10},{10,... | collective-permute-start | bytes 491528 | tf_op jit(solution)/shard_map/ppermute | solution.py:260
  130.9 3.1 %collective-permute-start.23 = (bf16[4,8,1280]{2,1,0:T(8,128)(2,1)S(1)}, bf16[4,8,1280]{2,1,0:T(8,128)(2,1)S(1)}, u32[]{:S(2)}, u32[]{:S(2)}) collective-permute-start(bf16[4,8,1280]{2,1,0:T(8,128)(2,1)S(1)} %fusion.129), channel_id=1, source_target_pairs={{0,3},{1,2},{2,1},{3,0},{4,7},{5,6},{6,5},{7,4},{8,11},{9,10},{10,... | collective-permute-start | bytes 245768 | tf_op jit(solution)/shard_map/ppermute | solution.py:260
  146.9 2.4 %collective-permute-done.38 = bf16[8,5120]{1,0:T(8,128)(2,1)S(1)} collective-permute-done((bf16[8,5120]{1,0:T(8,128)(2,1)S(1)}, bf16[8,5120]{1,0:T(8,128)(2,1)S(1)}, u32[]{:S(2)}, u32[]{:S(2)}) %collective-permute-start.38) | collective-permute-done | bytes 81952 | tf_op jit(solution)/shard_map/ppermute | solution.py:30
  150.6 4.6 %all-to-all-start = ((bf16[16,8,5120]{2,1,0:T(8,128)(2,1)}), bf16[16,8,5120]{2,1,0:T(8,128)(2,1)S(1)}, u32[]{:S(2)}, u32[]{:S(2)}) async-start(bf16[16,8,5120]{2,1,0:T(8,128)(2,1)} %shard_map.72), calls=%async_computation | async-start | bytes 2621440 | tf_op jit(solution)/shard_map/all_to_all | solution.py:375
  159.2 10.6 %all-to-all-done = bf16[16,8,5120]{2,1,0:T(8,128)(2,1)S(1)} async-done(((bf16[16,8,5120]{2,1,0:T(8,128)(2,1)}), bf16[16,8,5120]{2,1,0:T(8,128)(2,1)S(1)}, u32[]{:S(2)}, u32[]{:S(2)}) %all-to-all-start) | async-done | bytes 1310752 | tf_op jit(solution)/shard_map/all_to_all | solution.py:375
  (186 shorter events, 72.2 us)
Async XLA Ops:
  1.8 26.3 %collective-permute-start = (bf16[64,5120]{1,0:T(8,128)(2,1)S(1)}, bf16[64,5120]{1,0:T(8,128)(2,1)S(1)}, u32[]{:S(2)}, u32[]{:S(2)}) collective-permute-start(bf16[64,5120]{1,0:T(8,128)(2,1)S(1)} %dynamic-slice_bitcast_fusion.4), channel_id=1, source_target_pairs={{0,16},{1,17},{2,18},{3,19},{4,20},{5,21},{6,22},{7,23},{8,24},{9,... | collective-permute-start | bytes 1966088 | tf_op jit(solution)/shard_map/ppermute | solution.py:30
  3.5 24.6 %collective-permute-start.1 = (bf16[64,5120]{1,0:T(8,128)(2,1)S(1)}, bf16[64,5120]{1,0:T(8,128)(2,1)S(1)}, u32[]{:S(2)}, u32[]{:S(2)}) collective-permute-start(bf16[64,5120]{1,0:T(8,128)(2,1)S(1)} %dynamic-slice_bitcast_fusion.4), channel_id=1, source_target_pairs={{0,48},{1,49},{2,50},{3,51},{4,52},{5,53},{6,54},{7,55},{8,56},{9,... | collective-permute-start | bytes 1966088 | tf_op jit(solution)/shard_map/ppermute | solution.py:30
  7.0 21.0 %collective-permute-start.2 = (s32[132]{0:T(256)S(1)}, s32[132]{0:T(256)S(1)}, u32[]{:S(2)}, u32[]{:S(2)}) collective-permute-start(s32[132]{0:T(256)S(1)} %constant_dynamic-update-slice_fusion), channel_id=1, source_target_pairs={{0,16},{16,0},{32,48},{48,32},{1,17},{17,1},{33,49},{49,33},{2,18}... | collective-permute-start | bytes 1592 | tf_op jit(solution)/shard_map/ppermute | solution.py:63
  7.7 20.4 %collective-permute-start.3 = (s32[132]{0:T(256)S(1)}, s32[132]{0:T(256)S(1)}, u32[]{:S(2)}, u32[]{:S(2)}) collective-permute-start(s32[132]{0:T(256)S(1)} %constant_dynamic-update-slice_fusion), channel_id=1, source_target_pairs={{0,32},{16,48},{32,0},{48,16},{1,33},{17,49},{33,1},{49,17},{2,34}... | collective-permute-start | bytes 1592 | tf_op jit(solution)/shard_map/ppermute | solution.py:63
  9.6 18.5 %collective-permute-start.4 = (s32[132]{0:T(256)S(1)}, s32[132]{0:T(256)S(1)}, u32[]{:S(2)}, u32[]{:S(2)}) collective-permute-start(s32[132]{0:T(256)S(1)} %constant_dynamic-update-slice_fusion), channel_id=1, source_target_pairs={{0,48},{16,32},{32,16},{48,0},{1,49},{17,33},{33,17},{49,1},{2,50}... | collective-permute-start | bytes 1592 | tf_op jit(solution)/shard_map/ppermute | solution.py:63
  28.1 16.5 %collective-permute-start.5 = (bf16[64,5120]{1,0:T(8,128)(2,1)S(1)}, bf16[64,5120]{1,0:T(8,128)(2,1)S(1)}, u32[]{:S(2)}, u32[]{:S(2)}) collective-permute-start(bf16[64,5120]{1,0:T(8,128)(2,1)S(1)} %collective-permute-done.1.refs_1_), channel_id=1, source_target_pairs={{0,16},{1,17},{2,18},{3,19},{4,20},{5,21},{6,22},{7,23},{8,24},{9,... | collective-permute-start | bytes 1966088 | tf_op jit(solution)/shard_map/ppermute | solution.py:30
  28.3 18.8 %collective-permute-start.9 = (bf16[64,5120]{1,0:T(8,128)(2,1)S(1)}, bf16[64,5120]{1,0:T(8,128)(2,1)S(1)}, u32[]{:S(2)}, u32[]{:S(2)}) collective-permute-start(bf16[64,5120]{1,0:T(8,128)(2,1)S(1)} %collective-permute-done.1.refs_1_), channel_id=1, source_target_pairs={{0,12},{1,13},{2,14},{3,15},{4,8},{5,9},{6,10},{7,11},{8,4},{9,5},... | collective-permute-start | bytes 1966088 | tf_op jit(solution)/shard_map/ppermute | solution.py:30
  31.1 15.9 %collective-permute-start.8 = (bf16[64,5120]{1,0:T(8,128)(2,1)S(1)}, bf16[64,5120]{1,0:T(8,128)(2,1)S(1)}, u32[]{:S(2)}, u32[]{:S(2)}) collective-permute-start(bf16[64,5120]{1,0:T(8,128)(2,1)S(1)} %collective-permute-done.refs_0_), channel_id=1, source_target_pairs={{0,4},{1,5},{2,6},{3,7},{4,0},{5,1},{6,2},{7,3},{8,12},{9,13},{10,... | collective-permute-start | bytes 1966088 | tf_op jit(solution)/shard_map/ppermute | solution.py:30
  44.7 10.9 %collective-permute-start.6 = (bf16[32,5120]{1,0:T(8,128)(2,1)S(1)}, bf16[32,5120]{1,0:T(8,128)(2,1)S(1)}, u32[]{:S(2)}, u32[]{:S(2)}) collective-permute-start(bf16[32,5120]{1,0:T(8,128)(2,1)S(1)} %get-tuple-element.84), channel_id=1, source_target_pairs={{0,4},{1,5},{2,6},{3,7},{4,0},{5,1},{6,2},{7,3},{8,12},{9,13},{10,... | collective-permute-start | bytes 983048 | tf_op jit(solution)/shard_map/ppermute | solution.py:30
  46.6 9.0 %collective-permute-start.7 = (bf16[32,5120]{1,0:T(8,128)(2,1)S(1)}, bf16[32,5120]{1,0:T(8,128)(2,1)S(1)}, u32[]{:S(2)}, u32[]{:S(2)}) collective-permute-start(bf16[32,5120]{1,0:T(8,128)(2,1)S(1)} %get-tuple-element.83), channel_id=1, source_target_pairs={{0,12},{1,13},{2,14},{3,15},{4,8},{5,9},{6,10},{7,11},{8,4},{9,5},... | collective-permute-start | bytes 983048 | tf_op jit(solution)/shard_map/ppermute | solution.py:30
  97.0 12.3 %collective-permute-start.20 = (bf16[2,2,2,4,8,1280]{5,4,3,2,1,0:T(8,128)(2,1)S(1)}, bf16[2,2,2,4,8,1280]{5,4,3,2,1,0:T(8,128)(2,1)S(1)}, u32[]{:S(2)}, u32[]{:S(2)}) collective-permute-start(bf16[2,2,2,4,8,1280]{5,4,3,2,1,0:T(8,128)(2,1)S(1)} %fusion.48), channel_id=1, source_target_pairs={{0,4},{4,0},{8,12},{12,8},{1,5},{5,1},{9,13},{13,9},{2,6},{6,2},{1... | collective-permute-start | bytes 1966088 | tf_op jit(solution)/shard_map/ppermute | solution.py:260
  98.2 16.1 %collective-permute-start.24 = (bf16[2,2,2,4,8,1280]{5,4,3,2,1,0:T(8,128)(2,1)S(1)}, bf16[2,2,2,4,8,1280]{5,4,3,2,1,0:T(8,128)(2,1)S(1)}, u32[]{:S(2)}, u32[]{:S(2)}) collective-permute-start(bf16[2,2,2,4,8,1280]{5,4,3,2,1,0:T(8,128)(2,1)S(1)} %fusion.51), channel_id=1, source_target_pairs={{0,12},{4,8},{8,4},{12,0},{1,13},{5,9},{9,5},{13,1},{2,14},{6,10},... | collective-permute-start | bytes 1966088 | tf_op jit(solution)/shard_map/ppermute | solution.py:260
  101.5 15.6 %collective-permute-start.28 = (bf16[2,2,2,4,8,1280]{5,4,3,2,1,0:T(8,128)(2,1)S(1)}, bf16[2,2,2,4,8,1280]{5,4,3,2,1,0:T(8,128)(2,1)S(1)}, u32[]{:S(2)}, u32[]{:S(2)}) collective-permute-start(bf16[2,2,2,4,8,1280]{5,4,3,2,1,0:T(8,128)(2,1)S(1)} %fusion.54), channel_id=1, source_target_pairs={{0,1},{1,0},{2,3},{3,2},{4,5},{5,4},{6,7},{7,6},{8,9},{9,8},{10,11... | collective-permute-start | bytes 1966088 | tf_op jit(solution)/shard_map/ppermute | solution.py:260
  102.9 16.9 %collective-permute-start.32 = (bf16[2,2,2,4,8,1280]{5,4,3,2,1,0:T(8,128)(2,1)S(1)}, bf16[2,2,2,4,8,1280]{5,4,3,2,1,0:T(8,128)(2,1)S(1)}, u32[]{:S(2)}, u32[]{:S(2)}) collective-permute-start(bf16[2,2,2,4,8,1280]{5,4,3,2,1,0:T(8,128)(2,1)S(1)} %fusion.57), channel_id=1, source_target_pairs={{0,3},{1,2},{2,1},{3,0},{4,7},{5,6},{6,5},{7,4},{8,11},{9,10},{10,... | collective-permute-start | bytes 1966088 | tf_op jit(solution)/shard_map/ppermute | solution.py:260
  110.6 11.9 %collective-permute-start.21 = (bf16[2,2,4,8,1280]{4,3,2,1,0:T(8,128)(2,1)S(1)}, bf16[2,2,4,8,1280]{4,3,2,1,0:T(8,128)(2,1)S(1)}, u32[]{:S(2)}, u32[]{:S(2)}) collective-permute-start(bf16[2,2,4,8,1280]{4,3,2,1,0:T(8,128)(2,1)S(1)} %fusion.78), channel_id=1, source_target_pairs={{0,12},{4,8},{8,4},{12,0},{1,13},{5,9},{9,5},{13,1},{2,14},{6,10},... | collective-permute-start | bytes 983048 | tf_op jit(solution)/shard_map/ppermute | solution.py:260
  115.6 9.0 %collective-permute-start.25 = (bf16[2,2,4,8,1280]{4,3,2,1,0:T(8,128)(2,1)S(1)}, bf16[2,2,4,8,1280]{4,3,2,1,0:T(8,128)(2,1)S(1)}, u32[]{:S(2)}, u32[]{:S(2)}) collective-permute-start(bf16[2,2,4,8,1280]{4,3,2,1,0:T(8,128)(2,1)S(1)} %get-tuple-element.79), channel_id=1, source_target_pairs={{0,4},{4,0},{8,12},{12,8},{1,5},{5,1},{9,13},{13,9},{2,6},{6,2},{1... | collective-permute-start | bytes 983048 | tf_op jit(solution)/shard_map/ppermute | solution.py:260
  118.3 9.4 %collective-permute-start.29 = (bf16[2,2,4,8,1280]{4,3,2,1,0:T(8,128)(2,1)S(1)}, bf16[2,2,4,8,1280]{4,3,2,1,0:T(8,128)(2,1)S(1)}, u32[]{:S(2)}, u32[]{:S(2)}) collective-permute-start(bf16[2,2,4,8,1280]{4,3,2,1,0:T(8,128)(2,1)S(1)} %fusion.93), channel_id=1, source_target_pairs={{0,3},{1,2},{2,1},{3,0},{4,7},{5,6},{6,5},{7,4},{8,11},{9,10},{10,... | collective-permute-start | bytes 983048 | tf_op jit(solution)/shard_map/ppermute | solution.py:260
  121.1 8.0 %collective-permute-start.33 = (bf16[2,2,4,8,1280]{4,3,2,1,0:T(8,128)(2,1)S(1)}, bf16[2,2,4,8,1280]{4,3,2,1,0:T(8,128)(2,1)S(1)}, u32[]{:S(2)}, u32[]{:S(2)}) collective-permute-start(bf16[2,2,4,8,1280]{4,3,2,1,0:T(8,128)(2,1)S(1)} %get-tuple-element.81), channel_id=1, source_target_pairs={{0,1},{1,0},{2,3},{3,2},{4,5},{5,4},{6,7},{7,6},{8,9},{9,8},{10,11... | collective-permute-start | bytes 983048 | tf_op jit(solution)/shard_map/ppermute | solution.py:260
  122.5 8.3 %collective-permute-start.22 = (bf16[2,4,8,1280]{3,2,1,0:T(8,128)(2,1)S(1)}, bf16[2,4,8,1280]{3,2,1,0:T(8,128)(2,1)S(1)}, u32[]{:S(2)}, u32[]{:S(2)}) collective-permute-start(bf16[2,4,8,1280]{3,2,1,0:T(8,128)(2,1)S(1)} %get-tuple-element.71), channel_id=1, source_target_pairs={{0,1},{1,0},{2,3},{3,2},{4,5},{5,4},{6,7},{7,6},{8,9},{9,8},{10,11... | collective-permute-start | bytes 491528 | tf_op jit(solution)/shard_map/ppermute | solution.py:260
  124.6 9.4 %collective-permute-start.26 = (bf16[2,4,8,1280]{3,2,1,0:T(8,128)(2,1)S(1)}, bf16[2,4,8,1280]{3,2,1,0:T(8,128)(2,1)S(1)}, u32[]{:S(2)}, u32[]{:S(2)}) collective-permute-start(bf16[2,4,8,1280]{3,2,1,0:T(8,128)(2,1)S(1)} %get-tuple-element.73), channel_id=1, source_target_pairs={{0,3},{1,2},{2,1},{3,0},{4,7},{5,6},{6,5},{7,4},{8,11},{9,10},{10,... | collective-permute-start | bytes 491528 | tf_op jit(solution)/shard_map/ppermute | solution.py:260
  127.8 6.3 %collective-permute-start.30 = (bf16[2,4,8,1280]{3,2,1,0:T(8,128)(2,1)S(1)}, bf16[2,4,8,1280]{3,2,1,0:T(8,128)(2,1)S(1)}, u32[]{:S(2)}, u32[]{:S(2)}) collective-permute-start(bf16[2,4,8,1280]{3,2,1,0:T(8,128)(2,1)S(1)} %get-tuple-element.75), channel_id=1, source_target_pairs={{0,4},{4,0},{8,12},{12,8},{1,5},{5,1},{9,13},{13,9},{2,6},{6,2},{1... | collective-permute-start | bytes 491528 | tf_op jit(solution)/shard_map/ppermute | solution.py:260
  129.2 6.7 %collective-permute-start.34 = (bf16[2,4,8,1280]{3,2,1,0:T(8,128)(2,1)S(1)}, bf16[2,4,8,1280]{3,2,1,0:T(8,128)(2,1)S(1)}, u32[]{:S(2)}, u32[]{:S(2)}) collective-permute-start(bf16[2,4,8,1280]{3,2,1,0:T(8,128)(2,1)S(1)} %get-tuple-element.77), channel_id=1, source_target_pairs={{0,12},{4,8},{8,4},{12,0},{1,13},{5,9},{9,5},{13,1},{2,14},{6,10},... | collective-permute-start | bytes 491528 | tf_op jit(solution)/shard_map/ppermute | solution.py:260
  140.5 6.0 %collective-permute-start.36 = (bf16[8,5120]{1,0:T(8,128)(2,1)S(1)}, bf16[8,5120]{1,0:T(8,128)(2,1)S(1)}, u32[]{:S(2)}, u32[]{:S(2)}) collective-permute-start(bf16[8,5120]{1,0:T(8,128)(2,1)S(1)} %get-tuple-element.85), channel_id=1, source_target_pairs={{0,32},{1,33},{2,34},{3,35},{4,36},{5,37},{6,38},{7,39},{8,40},{9,... | collective-permute-start | bytes 245768 | tf_op jit(solution)/shard_map/ppermute | solution.py:30
  150.6 19.2 %all-to-all-start = ((bf16[16,8,5120]{2,1,0:T(8,128)(2,1)}), bf16[16,8,5120]{2,1,0:T(8,128)(2,1)S(1)}, u32[]{:S(2)}, u32[]{:S(2)}) async-start(bf16[16,8,5120]{2,1,0:T(8,128)(2,1)} %shard_map.72), calls=%async_computation | async-start | bytes 2621440 | tf_op jit(solution)/shard_map/all_to_all | solution.py:375
  (28 other events, 231.3 us)

commit v11 on v5

--- a/solution.py
+++ b/solution.py
@@ -263,10 +263,10 @@
         kept = [halves[q][1] for q in range(4)]
     state = [kept[q] + wide(came[q]) for q in range(4)]
     block = jnp.concatenate(state, axis=-1)
-    first, second = by_core(block[NEAR], block[WRAP]), by_core(block[WRAP], block[NEAR])
-    came = swap_y(narrow(jnp.stack([first, block[FAR]])), (1, 3))
-    mine, rest = block[OWN] + wide(came[0]), second + wide(came[1])
-    return [mine + wide(swap_y(narrow(rest), (3, 1)))], later
+    mine = block[OWN]
+    for group, step in ((FAR, 2), (NEAR, 1), (WRAP, 3)):
+        mine = mine + wide(swap_y(narrow(block[group]), (step, step)))
+    return [mine], later
 
 
 def shard_stats(logits, peer_logits, hit):

time: 163 us -> 161 us (0.988)
  waiting for transfers between devices: 48.7 us -> 43.9 us
  starting transfers between devices: 55.3 us -> 57.4 us
    ppermute x9 -> x10, waiting for transfers between devices: 14.4 us -> 10.6 us  [permute(): lax.ppermute(block, ALL, [(index(*p), index(*move(*p))) for p in places])]
    ppermute x9 -> x10, starting transfers between devices: 12.8 us -> 14.8 us  [permute(): lax.ppermute(block, ALL, [(index(*p), index(*move(*p))) for p in places])]
  transfers between devices with their start and end apart: 39 -> 40, of which waited for: 18 -> 19; matrix products, arithmetic and copies ran while one was open for 12% -> 12% of each run, Pallas kernels for 6% -> 6%
where the time goes in v11:
time: 161 us; the launch traced here: 160 us
  starting transfers between devices  57.4 us (36%)
  waiting for transfers between devices  43.9 us (27%)
  matrix products  16.4 us (10%)
  Pallas kernels  15 us (9%)
  local copies, waits for them, and re-layouts  14.4 us (9%)
  other arithmetic  7.46 us (5%)
  between operations  5.81 us (4%)
    ppermute x12, starting transfers between devices, ring(): lax.ppermute(block, axis, [(i, i ^ s) for i in range(4)])  19.8 us
    ppermute x16, starting transfers between devices, swap(): return lax.ppermute(block, axis, [(i, i ^ step) for i in range(4)])  17.8 us
    dot_general x12, matrix products, product(): lax.dot_general(block.reshape(-1, voc), columns, (((1,), (1,)), ((), ()))...  16.4 us
    ppermute x10, starting transfers between devices, permute(): lax.ppermute(block, ALL, [(index(*p), index(*move(*p))) for p in places])  14.8 us
    pallas_call x4, Pallas kernels, add_logits(): pl.pallas_call(make_kernel(count, *plan), out_shape=jax.ShapeDtypeStruct(...  13.7 us
    ppermute x16, waiting for transfers between devices, swap(): return lax.ppermute(block, axis, [(i, i ^ step) for i in range(4)])  11.4 us
    ppermute x10, waiting for transfers between devices, permute(): lax.ppermute(block, ALL, [(index(*p), index(*move(*p))) for p in places])  10.6 us
    ppermute x12, waiting for transfers between devices, ring(): lax.ppermute(block, axis, [(i, i ^ s) for i in range(4)])  10.6 us
  transfers between devices with their start and end apart: 40, of which 19 were waited for; matrix products, arithmetic and copies ran while one was open for 12% of the time, Pallas kernels for 6%

profile of v11, /device:TPU:0, one launch (start us, length us, event | category | flops | bytes accessed | tf_op | source)
XLA Modules:
  0.0 160.4 jit_solution(4525120782824325096)
XLA Ops:
  4.3 2.2 %collective-permute-start.1 = (bf16[64,5120]{1,0:T(8,128)(2,1)}, bf16[64,5120]{1,0:T(8,128)(2,1)S(1)}, u32[]{:S(2)}, u32[]{:S(2)}) collective-permute-start(bf16[64,5120]{1,0:T(8,128)(2,1)} %dynamic-slice_bitcast_fusion.4), channel_id=1, source_target_pairs={{0,48},{1,49},{2,50},{3,51},{4,52},{5,53},{6,54},{7,55},{8,56},{9,... | collective-permute-start | bytes 1966088 | tf_op jit(solution)/shard_map/ppermute | solution.py:28
  10.3 2.2 %collective-permute-start.4 = (s32[132]{0:T(256)S(1)}, s32[132]{0:T(256)S(1)}, u32[]{:S(2)}, u32[]{:S(2)}) collective-permute-start(s32[132]{0:T(256)S(1)} %constant_dynamic-update-slice_fusion), channel_id=1, source_target_pairs={{0,48},{16,32},{32,16},{48,0},{1,49},{17,33},{33,17},{49,1},{2,50}... | collective-permute-start | bytes 1592 | tf_op jit(solution)/shard_map/ppermute | solution.py:60
  12.5 4.7 %copy-done = bf16[1,5120,1280]{2,1,0:T(8,128)(2,1)S(1)} copy-done((bf16[1,5120,1280]{2,1,0:T(8,128)(2,1)S(1)}, bf16[1,5120,1280]{2,1,0:T(8,128)(2,1)}, u32[]{:S(2)}) %copy-start) | copy-done | bytes 13107224
  19.3 3.0 %shard_map.68.refs_4_ = bf16[512,1280]{1,0:T(8,128)(2,1)S(1)} custom-call(bf16[128,5120]{1,0:T(8,128)(2,1)S(1)} %bitcast.389, f32[1,5120]{1,0:T(1,128)S(1)} %copy-done.2, bf16[5120,1280]{1,0:T(8,128)(2,1)S(1)} %bitcast.381), custom_call_target="tpu_custom_call" | custom-call | flops 1677721600 | bytes 14417920 | tf_op jit(solution)/shard_map/pallas_call | solution.py:174
  22.4 2.8 %collective-permute-start.9 = (bf16[64,5120]{1,0:T(8,128)(2,1)S(1)}, bf16[64,5120]{1,0:T(8,128)(2,1)S(1)}, u32[]{:S(2)}, u32[]{:S(2)}) collective-permute-start(bf16[64,5120]{1,0:T(8,128)(2,1)S(1)} %collective-permute-done.1.refs_1_), channel_id=1, source_target_pairs={{0,12},{1,13},{2,14},{3,15},{4,8},{5,9},{6,10},{7,11},{8,4},{9,5},... | collective-permute-start | bytes 1966088 | tf_op jit(solution)/shard_map/ppermute | solution.py:28
  25.5 3.6 %shard_map.69.refs_4_ = bf16[512,1280]{1,0:T(8,128)(2,1)S(1)} custom-call(bf16[64,5120]{1,0:T(8,128)(2,1)S(1)} %collective-permute-done.refs_0_, bf16[64,5120]{1,0:T(8,128)(2,1)S(1)} %collective-permute-done.1.refs_1_, f32[1,5120]{1,0:T(1,128)S(1)} %copy-done.2, bf16[5120,1280]{1,0:T(8,128)(2,1)S(1)} %bitcast.382, ...), custom_call_target="tpu_custom_call", output_to_operand_aliasing={{}: (4, {})} | custom-call | flops 1677721600 | bytes 14417920 | tf_op jit(solution)/shard_map/pallas_call | solution.py:174
  29.1 3.9 %collective-permute-done.5.refs_0_ = bf16[64,5120]{1,0:T(8,128)(2,1)S(1)} collective-permute-done((bf16[64,5120]{1,0:T(8,128)(2,1)S(1)}, bf16[64,5120]{1,0:T(8,128)(2,1)S(1)}, u32[]{:S(2)}, u32[]{:S(2)}) %collective-permute-start.5) | collective-permute-done | bytes 655392 | tf_op jit(solution)/shard_map/ppermute | solution.py:28
  36.7 3.7 %shard_map.70.refs_5_ = bf16[512,1280]{1,0:T(8,128)(2,1)S(1)} custom-call(bf16[64,5120]{1,0:T(8,128)(2,1)S(1)} %collective-permute-done.8.refs_0_, bf16[64,5120]{1,0:T(8,128)(2,1)S(1)} %collective-permute-done.9.refs_1_, f32[1,5120]{1,0:T(1,128)S(1)} %copy-done.2, bf16[5120,1280]{1,0:T(8,128)(2,1)S(1)} %bitcast.385, ...), custom_call_target="tpu_custom_call", output_to_operand_aliasing={{}: (4, {})} | custom-call | flops 1677721600 | bytes 14417920 | tf_op jit(solution)/shard_map/pallas_call | solution.py:174
  40.5 2.4 %collective-permute-done.7.refs_2_ = bf16[32,5120]{1,0:T(8,128)(2,1)S(1)} collective-permute-done((bf16[32,5120]{1,0:T(8,128)(2,1)S(1)}, bf16[32,5120]{1,0:T(8,128)(2,1)S(1)}, u32[]{:S(2)}, u32[]{:S(2)}) %collective-permute-start.7) | collective-permute-done | bytes 327712 | tf_op jit(solution)/shard_map/ppermute | solution.py:28
  42.9 3.4 %shard_map.71 = bf16[512,1280]{1,0:T(8,128)(2,1)S(1)} custom-call(bf16[64,5120]{1,0:T(8,128)(2,1)S(1)} %collective-permute-done.5.refs_0_, bf16[32,5120]{1,0:T(8,128)(2,1)S(1)} %collective-permute-done.6.refs_1_, bf16[32,5120]{1,0:T(8,128)(2,1)S(1)} %collective-permute-done.7.refs_2_, f32[1,5120]{1,0:T(1,128)S(1)} %copy-done.2, ...), custom_call_target="tpu_custom_call", output_to_operand_aliasing={{}: (5, {})} | custom-call | flops 1677721600 | bytes 14417920 | tf_op jit(solution)/shard_map/pallas_call | solution.py:174
  52.8 3.6 %collective-permute-start.12 = (f32[6,512]{1,0:T(8,128)S(1)}, f32[6,512]{1,0:T(8,128)S(1)}, u32[]{:S(2)}, u32[]{:S(2)}) collective-permute-start(f32[6,512]{1,0:T(8,128)S(1)} %stack.109), channel_id=1, source_target_pairs={{0,2},{1,3},{2,0},{3,1},{4,6},{5,7},{6,4},{7,5},{8,10},{9,11},{10,... | collective-permute-start | bytes 36872 | tf_op jit(solution)/shard_map/ppermute | solution.py:60
  58.3 3.1 %collective-permute-done.13 = f32[6,512]{1,0:T(8,128)S(1)} collective-permute-done((f32[6,512]{1,0:T(8,128)S(1)}, f32[6,512]{1,0:T(8,128)S(1)}, u32[]{:S(2)}, u32[]{:S(2)}) %collective-permute-start.13) | collective-permute-done | bytes 12320 | tf_op jit(solution)/shard_map/ppermute | solution.py:60
  61.6 3.5 %collective-permute-start.15 = (f32[6,512]{1,0:T(8,128)S(1)}, f32[6,512]{1,0:T(8,128)S(1)}, u32[]{:S(2)}, u32[]{:S(2)}) collective-permute-start(f32[6,512]{1,0:T(8,128)S(1)} %get-tuple-element.100), channel_id=1, source_target_pairs={{0,8},{4,12},{8,0},{12,4},{1,9},{5,13},{9,1},{13,5},{2,10},{6,14},... | collective-permute-start | bytes 36872 | tf_op jit(solution)/shard_map/ppermute | solution.py:60
  67.2 3.0 %collective-permute-done.16 = f32[6,512]{1,0:T(8,128)S(1)} collective-permute-done((f32[6,512]{1,0:T(8,128)S(1)}, f32[6,512]{1,0:T(8,128)S(1)}, u32[]{:S(2)}, u32[]{:S(2)}) %collective-permute-start.16) | collective-permute-done | bytes 12320 | tf_op jit(solution)/shard_map/ppermute | solution.py:60
  70.6 2.7 %collective-permute-start.18 = (f32[6,512]{1,0:T(8,128)S(1)}, f32[6,512]{1,0:T(8,128)S(1)}, u32[]{:S(2)}, u32[]{:S(2)}) collective-permute-start(f32[6,512]{1,0:T(8,128)S(1)} %get-tuple-element.98), channel_id=1, source_target_pairs={{0,32},{16,48},{32,0},{48,16},{1,33},{17,49},{33,1},{49,17},{2,34}... | collective-permute-start | bytes 36872 | tf_op jit(solution)/shard_map/ppermute | solution.py:60
  75.9 2.4 %collective-permute-done.19 = f32[6,512]{1,0:T(8,128)S(1)} collective-permute-done((f32[6,512]{1,0:T(8,128)S(1)}, f32[6,512]{1,0:T(8,128)S(1)}, u32[]{:S(2)}, u32[]{:S(2)}) %collective-permute-start.19) | collective-permute-done | bytes 12320 | tf_op jit(solution)/shard_map/ppermute | solution.py:60
  82.5 3.5 %fusion.46 = bf16[2,2,2,4,8,1280]{5,4,3,2,1,0:T(8,128)(2,1)S(1)} fusion(bf16[2,2,2,4,8,1280]{5,4,3,2,1,0:T(8,128)(2,1)S(1)} %dynamic-slice_bitcast_fusion.3, bf16[1,5120,1280]{2,1,0:T(8,128)(2,1)} %param.7), kind=kOutput, calls=%fused_computation.57 | convolution fusion | flops 839188480 | bytes 4587520 | tf_op jit(solution)/shard_map/dot_general | solution.py:230
  94.5 3.5 %collective-permute-done.20 = bf16[2,2,2,4,8,1280]{5,4,3,2,1,0:T(8,128)(2,1)S(1)} collective-permute-done((bf16[2,2,2,4,8,1280]{5,4,3,2,1,0:T(8,128)(2,1)S(1)}, bf16[2,2,2,4,8,1280]{5,4,3,2,1,0:T(8,128)(2,1)S(1)}, u32[]{:S(2)}, u32[]{:S(2)}) %collective-permute-start.20) | collective-permute-done | bytes 655392 | tf_op jit(solution)/shard_map/ppermute | solution.py:242
  100.1 3.7 %collective-permute-done.24 = bf16[2,2,2,4,8,1280]{5,4,3,2,1,0:T(8,128)(2,1)S(1)} collective-permute-done((bf16[2,2,2,4,8,1280]{5,4,3,2,1,0:T(8,128)(2,1)S(1)}, bf16[2,2,2,4,8,1280]{5,4,3,2,1,0:T(8,128)(2,1)S(1)}, u32[]{:S(2)}, u32[]{:S(2)}) %collective-permute-start.24) | collective-permute-done | bytes 655392 | tf_op jit(solution)/shard_map/ppermute | solution.py:242
  113.2 3.1 %collective-permute-start.26 = (bf16[2,4,8,1280]{3,2,1,0:T(8,128)(2,1)S(1)}, bf16[2,4,8,1280]{3,2,1,0:T(8,128)(2,1)S(1)}, u32[]{:S(2)}, u32[]{:S(2)}) collective-permute-start(bf16[2,4,8,1280]{3,2,1,0:T(8,128)(2,1)S(1)} %get-tuple-element.56), channel_id=1, source_target_pairs={{0,3},{1,2},{2,1},{3,0},{4,7},{5,6},{6,5},{7,4},{8,11},{9,10},{10,... | collective-permute-start | bytes 491528 | tf_op jit(solution)/shard_map/ppermute | solution.py:242
  119.9 2.7 %collective-permute-start.23 = (bf16[4,8,1280]{2,1,0:T(8,128)(2,1)S(1)}, bf16[4,8,1280]{2,1,0:T(8,128)(2,1)S(1)}, u32[]{:S(2)}, u32[]{:S(2)}) collective-permute-start(bf16[4,8,1280]{2,1,0:T(8,128)(2,1)S(1)} %fusion.127), channel_id=1, source_target_pairs={{0,3},{1,2},{2,1},{3,0},{4,7},{5,6},{6,5},{7,4},{8,11},{9,10},{10,... | collective-permute-start | bytes 245768 | tf_op jit(solution)/shard_map/ppermute | solution.py:242
  135.3 2.4 %collective-permute-done.38 = bf16[8,5120]{1,0:T(8,128)(2,1)S(1)} collective-permute-done((bf16[8,5120]{1,0:T(8,128)(2,1)S(1)}, bf16[8,5120]{1,0:T(8,128)(2,1)S(1)}, u32[]{:S(2)}, u32[]{:S(2)}) %collective-permute-start.38) | collective-permute-done | bytes 81952 | tf_op jit(solution)/shard_map/ppermute | solution.py:28
  139.0 4.7 %all-to-all-start = ((bf16[16,8,5120]{2,1,0:T(8,128)(2,1)}), bf16[16,8,5120]{2,1,0:T(8,128)(2,1)S(1)}, u32[]{:S(2)}, u32[]{:S(2)}) async-start(bf16[16,8,5120]{2,1,0:T(8,128)(2,1)} %shard_map.72), calls=%async_computation | async-start | bytes 2621440 | tf_op jit(solution)/shard_map/all_to_all | solution.py:354
  148.5 9.7 %all-to-all-done = bf16[16,8,5120]{2,1,0:T(8,128)(2,1)S(1)} async-done(((bf16[16,8,5120]{2,1,0:T(8,128)(2,1)}), bf16[16,8,5120]{2,1,0:T(8,128)(2,1)S(1)}, u32[]{:S(2)}, u32[]{:S(2)}) %all-to-all-start) | async-done | bytes 1310752 | tf_op jit(solution)/shard_map/all_to_all | solution.py:354
  (197 shorter events, 71.3 us)
Async XLA Ops:
  2.6 19.7 %collective-permute-start = (bf16[64,5120]{1,0:T(8,128)(2,1)}, bf16[64,5120]{1,0:T(8,128)(2,1)S(1)}, u32[]{:S(2)}, u32[]{:S(2)}) collective-permute-start(bf16[64,5120]{1,0:T(8,128)(2,1)} %dynamic-slice_bitcast_fusion.4), channel_id=1, source_target_pairs={{0,16},{1,17},{2,18},{3,19},{4,20},{5,21},{6,22},{7,23},{8,24},{9,... | collective-permute-start | bytes 1966088 | tf_op jit(solution)/shard_map/ppermute | solution.py:28
  4.3 18.0 %collective-permute-start.1 = (bf16[64,5120]{1,0:T(8,128)(2,1)}, bf16[64,5120]{1,0:T(8,128)(2,1)S(1)}, u32[]{:S(2)}, u32[]{:S(2)}) collective-permute-start(bf16[64,5120]{1,0:T(8,128)(2,1)} %dynamic-slice_bitcast_fusion.4), channel_id=1, source_target_pairs={{0,48},{1,49},{2,50},{3,51},{4,52},{5,53},{6,54},{7,55},{8,56},{9,... | collective-permute-start | bytes 1966088 | tf_op jit(solution)/shard_map/ppermute | solution.py:28
  7.8 14.5 %collective-permute-start.2 = (s32[132]{0:T(256)S(1)}, s32[132]{0:T(256)S(1)}, u32[]{:S(2)}, u32[]{:S(2)}) collective-permute-start(s32[132]{0:T(256)S(1)} %constant_dynamic-update-slice_fusion), channel_id=1, source_target_pairs={{0,16},{16,0},{32,48},{48,32},{1,17},{17,1},{33,49},{49,33},{2,18}... | collective-permute-start | bytes 1592 | tf_op jit(solution)/shard_map/ppermute | solution.py:60
  8.5 13.8 %collective-permute-start.3 = (s32[132]{0:T(256)S(1)}, s32[132]{0:T(256)S(1)}, u32[]{:S(2)}, u32[]{:S(2)}) collective-permute-start(s32[132]{0:T(256)S(1)} %constant_dynamic-update-slice_fusion), channel_id=1, source_target_pairs={{0,32},{16,48},{32,0},{48,16},{1,33},{17,49},{33,1},{49,17},{2,34}... | collective-permute-start | bytes 1592 | tf_op jit(solution)/shard_map/ppermute | solution.py:60
  10.3 12.0 %collective-permute-start.4 = (s32[132]{0:T(256)S(1)}, s32[132]{0:T(256)S(1)}, u32[]{:S(2)}, u32[]{:S(2)}) collective-permute-start(s32[132]{0:T(256)S(1)} %constant_dynamic-update-slice_fusion), channel_id=1, source_target_pairs={{0,48},{16,32},{32,16},{48,0},{1,49},{17,33},{33,17},{49,1},{2,50}... | collective-permute-start | bytes 1592 | tf_op jit(solution)/shard_map/ppermute | solution.py:60
  22.3 10.7 %collective-permute-start.5 = (bf16[64,5120]{1,0:T(8,128)(2,1)S(1)}, bf16[64,5120]{1,0:T(8,128)(2,1)S(1)}, u32[]{:S(2)}, u32[]{:S(2)}) collective-permute-start(bf16[64,5120]{1,0:T(8,128)(2,1)S(1)} %collective-permute-done.1.refs_1_), channel_id=1, source_target_pairs={{0,16},{1,17},{2,18},{3,19},{4,20},{5,21},{6,22},{7,23},{8,24},{9,... | collective-permute-start | bytes 1966088 | tf_op jit(solution)/shard_map/ppermute | solution.py:28
  22.4 14.3 %collective-permute-start.9 = (bf16[64,5120]{1,0:T(8,128)(2,1)S(1)}, bf16[64,5120]{1,0:T(8,128)(2,1)S(1)}, u32[]{:S(2)}, u32[]{:S(2)}) collective-permute-start(bf16[64,5120]{1,0:T(8,128)(2,1)S(1)} %collective-permute-done.1.refs_1_), channel_id=1, source_target_pairs={{0,12},{1,13},{2,14},{3,15},{4,8},{5,9},{6,10},{7,11},{8,4},{9,5},... | collective-permute-start | bytes 1966088 | tf_op jit(solution)/shard_map/ppermute | solution.py:28
  25.2 11.5 %collective-permute-start.8 = (bf16[64,5120]{1,0:T(8,128)(2,1)S(1)}, bf16[64,5120]{1,0:T(8,128)(2,1)S(1)}, u32[]{:S(2)}, u32[]{:S(2)}) collective-permute-start(bf16[64,5120]{1,0:T(8,128)(2,1)S(1)} %collective-permute-done.refs_0_), channel_id=1, source_target_pairs={{0,4},{1,5},{2,6},{3,7},{4,0},{5,1},{6,2},{7,3},{8,12},{9,13},{10,... | collective-permute-start | bytes 1966088 | tf_op jit(solution)/shard_map/ppermute | solution.py:28
  33.0 7.5 %collective-permute-start.6 = (bf16[32,5120]{1,0:T(8,128)(2,1)S(1)}, bf16[32,5120]{1,0:T(8,128)(2,1)S(1)}, u32[]{:S(2)}, u32[]{:S(2)}) collective-permute-start(bf16[32,5120]{1,0:T(8,128)(2,1)S(1)} %get-tuple-element.67), channel_id=1, source_target_pairs={{0,4},{1,5},{2,6},{3,7},{4,0},{5,1},{6,2},{7,3},{8,12},{9,13},{10,... | collective-permute-start | bytes 983048 | tf_op jit(solution)/shard_map/ppermute | solution.py:28
  34.6 8.3 %collective-permute-start.7 = (bf16[32,5120]{1,0:T(8,128)(2,1)S(1)}, bf16[32,5120]{1,0:T(8,128)(2,1)S(1)}, u32[]{:S(2)}, u32[]{:S(2)}) collective-permute-start(bf16[32,5120]{1,0:T(8,128)(2,1)S(1)} %get-tuple-element.66), channel_id=1, source_target_pairs={{0,12},{1,13},{2,14},{3,15},{4,8},{5,9},{6,10},{7,11},{8,4},{9,5},... | collective-permute-start | bytes 983048 | tf_op jit(solution)/shard_map/ppermute | solution.py:28
  50.8 6.6 %collective-permute-start.11 = (f32[6,512]{1,0:T(8,128)S(1)}, f32[6,512]{1,0:T(8,128)S(1)}, u32[]{:S(2)}, u32[]{:S(2)}) collective-permute-start(f32[6,512]{1,0:T(8,128)S(1)} %stack.109), channel_id=1, source_target_pairs={{0,1},{1,0},{2,3},{3,2},{4,5},{5,4},{6,7},{7,6},{8,9},{9,8},{10,11... | collective-permute-start | bytes 36872 | tf_op jit(solution)/shard_map/ppermute | solution.py:60
  85.9 12.1 %collective-permute-start.20 = (bf16[2,2,2,4,8,1280]{5,4,3,2,1,0:T(8,128)(2,1)S(1)}, bf16[2,2,2,4,8,1280]{5,4,3,2,1,0:T(8,128)(2,1)S(1)}, u32[]{:S(2)}, u32[]{:S(2)}) collective-permute-start(bf16[2,2,2,4,8,1280]{5,4,3,2,1,0:T(8,128)(2,1)S(1)} %fusion.46), channel_id=1, source_target_pairs={{0,4},{4,0},{8,12},{12,8},{1,5},{5,1},{9,13},{13,9},{2,6},{6,2},{1... | collective-permute-start | bytes 1966088 | tf_op jit(solution)/shard_map/ppermute | solution.py:242
  87.4 16.4 %collective-permute-start.24 = (bf16[2,2,2,4,8,1280]{5,4,3,2,1,0:T(8,128)(2,1)S(1)}, bf16[2,2,2,4,8,1280]{5,4,3,2,1,0:T(8,128)(2,1)S(1)}, u32[]{:S(2)}, u32[]{:S(2)}) collective-permute-start(bf16[2,2,2,4,8,1280]{5,4,3,2,1,0:T(8,128)(2,1)S(1)} %fusion.49), channel_id=1, source_target_pairs={{0,12},{4,8},{8,4},{12,0},{1,13},{5,9},{9,5},{13,1},{2,14},{6,10},... | collective-permute-start | bytes 1966088 | tf_op jit(solution)/shard_map/ppermute | solution.py:242
  90.9 14.8 %collective-permute-start.28 = (bf16[2,2,2,4,8,1280]{5,4,3,2,1,0:T(8,128)(2,1)S(1)}, bf16[2,2,2,4,8,1280]{5,4,3,2,1,0:T(8,128)(2,1)S(1)}, u32[]{:S(2)}, u32[]{:S(2)}) collective-permute-start(bf16[2,2,2,4,8,1280]{5,4,3,2,1,0:T(8,128)(2,1)S(1)} %fusion.52), channel_id=1, source_target_pairs={{0,1},{1,0},{2,3},{3,2},{4,5},{5,4},{6,7},{7,6},{8,9},{9,8},{10,11... | collective-permute-start | bytes 1966088 | tf_op jit(solution)/shard_map/ppermute | solution.py:242
  92.3 16.1 %collective-permute-start.32 = (bf16[2,2,2,4,8,1280]{5,4,3,2,1,0:T(8,128)(2,1)S(1)}, bf16[2,2,2,4,8,1280]{5,4,3,2,1,0:T(8,128)(2,1)S(1)}, u32[]{:S(2)}, u32[]{:S(2)}) collective-permute-start(bf16[2,2,2,4,8,1280]{5,4,3,2,1,0:T(8,128)(2,1)S(1)} %fusion.55), channel_id=1, source_target_pairs={{0,3},{1,2},{2,1},{3,0},{4,7},{5,6},{6,5},{7,4},{8,11},{9,10},{10,... | collective-permute-start | bytes 1966088 | tf_op jit(solution)/shard_map/ppermute | solution.py:242
  99.2 12.3 %collective-permute-start.21 = (bf16[2,2,4,8,1280]{4,3,2,1,0:T(8,128)(2,1)S(1)}, bf16[2,2,4,8,1280]{4,3,2,1,0:T(8,128)(2,1)S(1)}, u32[]{:S(2)}, u32[]{:S(2)}) collective-permute-start(bf16[2,2,4,8,1280]{4,3,2,1,0:T(8,128)(2,1)S(1)} %fusion.76), channel_id=1, source_target_pairs={{0,12},{4,8},{8,4},{12,0},{1,13},{5,9},{9,5},{13,1},{2,14},{6,10},... | collective-permute-start | bytes 983048 | tf_op jit(solution)/shard_map/ppermute | solution.py:242
  105.0 8.2 %collective-permute-start.25 = (bf16[2,2,4,8,1280]{4,3,2,1,0:T(8,128)(2,1)S(1)}, bf16[2,2,4,8,1280]{4,3,2,1,0:T(8,128)(2,1)S(1)}, u32[]{:S(2)}, u32[]{:S(2)}) collective-permute-start(bf16[2,2,4,8,1280]{4,3,2,1,0:T(8,128)(2,1)S(1)} %get-tuple-element.62), channel_id=1, source_target_pairs={{0,4},{4,0},{8,12},{12,8},{1,5},{5,1},{9,13},{13,9},{2,6},{6,2},{1... | collective-permute-start | bytes 983048 | tf_op jit(solution)/shard_map/ppermute | solution.py:242
  106.9 9.4 %collective-permute-start.29 = (bf16[2,2,4,8,1280]{4,3,2,1,0:T(8,128)(2,1)S(1)}, bf16[2,2,4,8,1280]{4,3,2,1,0:T(8,128)(2,1)S(1)}, u32[]{:S(2)}, u32[]{:S(2)}) collective-permute-start(bf16[2,2,4,8,1280]{4,3,2,1,0:T(8,128)(2,1)S(1)} %fusion.91), channel_id=1, source_target_pairs={{0,3},{1,2},{2,1},{3,0},{4,7},{5,6},{6,5},{7,4},{8,11},{9,10},{10,... | collective-permute-start | bytes 983048 | tf_op jit(solution)/shard_map/ppermute | solution.py:242
  109.7 8.1 %collective-permute-start.33 = (bf16[2,2,4,8,1280]{4,3,2,1,0:T(8,128)(2,1)S(1)}, bf16[2,2,4,8,1280]{4,3,2,1,0:T(8,128)(2,1)S(1)}, u32[]{:S(2)}, u32[]{:S(2)}) collective-permute-start(bf16[2,2,4,8,1280]{4,3,2,1,0:T(8,128)(2,1)S(1)} %get-tuple-element.64), channel_id=1, source_target_pairs={{0,1},{1,0},{2,3},{3,2},{4,5},{5,4},{6,7},{7,6},{8,9},{9,8},{10,11... | collective-permute-start | bytes 983048 | tf_op jit(solution)/shard_map/ppermute | solution.py:242
  111.6 8.3 %collective-permute-start.22 = (bf16[2,4,8,1280]{3,2,1,0:T(8,128)(2,1)S(1)}, bf16[2,4,8,1280]{3,2,1,0:T(8,128)(2,1)S(1)}, u32[]{:S(2)}, u32[]{:S(2)}) collective-permute-start(bf16[2,4,8,1280]{3,2,1,0:T(8,128)(2,1)S(1)} %get-tuple-element.54), channel_id=1, source_target_pairs={{0,1},{1,0},{2,3},{3,2},{4,5},{5,4},{6,7},{7,6},{8,9},{9,8},{10,11... | collective-permute-start | bytes 491528 | tf_op jit(solution)/shard_map/ppermute | solution.py:242
  113.2 9.4 %collective-permute-start.26 = (bf16[2,4,8,1280]{3,2,1,0:T(8,128)(2,1)S(1)}, bf16[2,4,8,1280]{3,2,1,0:T(8,128)(2,1)S(1)}, u32[]{:S(2)}, u32[]{:S(2)}) collective-permute-start(bf16[2,4,8,1280]{3,2,1,0:T(8,128)(2,1)S(1)} %get-tuple-element.56), channel_id=1, source_target_pairs={{0,3},{1,2},{2,1},{3,0},{4,7},{5,6},{6,5},{7,4},{8,11},{9,10},{10,... | collective-permute-start | bytes 491528 | tf_op jit(solution)/shard_map/ppermute | solution.py:242
  116.4 6.3 %collective-permute-start.30 = (bf16[2,4,8,1280]{3,2,1,0:T(8,128)(2,1)S(1)}, bf16[2,4,8,1280]{3,2,1,0:T(8,128)(2,1)S(1)}, u32[]{:S(2)}, u32[]{:S(2)}) collective-permute-start(bf16[2,4,8,1280]{3,2,1,0:T(8,128)(2,1)S(1)} %get-tuple-element.58), channel_id=1, source_target_pairs={{0,4},{4,0},{8,12},{12,8},{1,5},{5,1},{9,13},{13,9},{2,6},{6,2},{1... | collective-permute-start | bytes 491528 | tf_op jit(solution)/shard_map/ppermute | solution.py:242
  117.9 6.6 %collective-permute-start.34 = (bf16[2,4,8,1280]{3,2,1,0:T(8,128)(2,1)S(1)}, bf16[2,4,8,1280]{3,2,1,0:T(8,128)(2,1)S(1)}, u32[]{:S(2)}, u32[]{:S(2)}) collective-permute-start(bf16[2,4,8,1280]{3,2,1,0:T(8,128)(2,1)S(1)} %get-tuple-element.60), channel_id=1, source_target_pairs={{0,12},{4,8},{8,4},{12,0},{1,13},{5,9},{9,5},{13,1},{2,14},{6,10},... | collective-permute-start | bytes 491528 | tf_op jit(solution)/shard_map/ppermute | solution.py:242
  139.0 19.2 %all-to-all-start = ((bf16[16,8,5120]{2,1,0:T(8,128)(2,1)}), bf16[16,8,5120]{2,1,0:T(8,128)(2,1)S(1)}, u32[]{:S(2)}, u32[]{:S(2)}) async-start(bf16[16,8,5120]{2,1,0:T(8,128)(2,1)} %shard_map.72), calls=%async_computation | async-start | bytes 2621440 | tf_op jit(solution)/shard_map/all_to_all | solution.py:354
  (30 other events, 199.8 us)
